TPU v7x, 32 devices: a whole 2x2x4 slice. The times are simulated.
32 devices in a mesh: dp: 8 (over z, y), ctx: 4 (over x, core).
Axes of the slice: x: 2, y: 2, z: 4, core: 2. Of those that a mesh axis runs over, the one named last changes fastest.
Arguments:
- tokens: bfloat16 [8, 1376, 1024], P('dp', 'ctx'), may hold values from -6 to 6
- counts: int32 [8, 4], P('dp', 'ctx'), may hold values from 301 to 344, as said below
- w_qkv: bfloat16 [1024, 3072], P(('dp', 'ctx')), may hold values from -0.1875 to 0.1875
- w_proj: bfloat16 [1024, 1024], P(None, ('dp', 'ctx')), may hold values from -2.5 to 2.5
- w_fc1: bfloat16 [1024, 4096], P(('dp', 'ctx')), may hold values from -0.1875 to 0.1875
- fc1_bias: bfloat16 [4096], P(('dp', 'ctx')), may hold values from -3 to 3
- w_fc2: bfloat16 [4096, 1024], P(None, ('dp', 'ctx')), may hold values from -0.09375 to 0.09375
- vectors: bfloat16 [10, 1024], P(None, ('dp', 'ctx')), as said below
- cotangent: bfloat16 [8, 1376, 1024], P('dp', 'ctx'), may hold values from -6 to 6
Outputs:
- output: bfloat16 [8, 1376, 1024], P('dp', 'ctx')
- input_grad: bfloat16 [8, 1376, 1024], P('dp', 'ctx')
- grad_qkv: float32 [1024, 3072], P(('dp', 'ctx'))
- grad_proj: float32 [1024, 1024], P(None, ('dp', 'ctx'))
- grad_fc1: float32 [1024, 4096], P(('dp', 'ctx'))
- grad_fc1_bias: float32 [4096], P(('dp', 'ctx'))
- grad_fc2: float32 [4096, 1024], P(None, ('dp', 'ctx'))
- grad_vectors: float32 [10, 1024], P(None, ('dp', 'ctx'))
Inputs may be any that keep to these rules, and one draw needn't show every extreme that they name: `counts`: in every image one device holds 344 live tokens and another 344 - 344 // 8. `vectors`: rows 0, 5, 6 and 9 are positive.
All inputs are finite; a program needn't handle non-finite values.
Results may differ from a plain program's by a relative error of at most 0.017.
Values may be sent and summed in bfloat16 or wider, within the bound.
No kernel may reach another device: no remote copies, remote signals or barrier semaphores. Data moves between devices by JAX's collectives and lax.ppermute only.
A program may use at most 192 MiB of HBM per device.

v0:
```python
import jax
import jax.numpy as jnp
from jax import lax
from jax.experimental import pallas as pl
from jax.experimental.pallas import tpu as pltpu
from jax.sharding import PartitionSpec as P

HD = 64
PAIR = 2 * HD
EXTRA = 128
EPSILON = 1e-06
MASKED_SCORE = -1e30
SQRT_HALF = 0.7071067811865476
INV_ROOT_TWO_PI = 0.3989422804014327
BF = jnp.bfloat16
F32 = jnp.float32
PARAMS = pltpu.CompilerParams(vmem_limit_bytes=60 * 1024 * 1024)
VMEM = pl.BlockSpec(memory_space=pltpu.VMEM)
SMEM = pl.BlockSpec(memory_space=pltpu.SMEM)


def shaped(shape, dtype):
    return jax.ShapeDtypeStruct(shape, dtype)


def dot(left, right, left_dim, right_dim):
    return lax.dot_general(
        left, right, (((left_dim,), (right_dim,)), ((), ())), preferred_element_type=F32
    )


def lanes(start, size):
    return pl.ds(pl.multiple_of(start, 128), size)


def unit_rows(inputs):
    centered = inputs - jnp.mean(inputs, axis=-1, keepdims=True)
    spread = jnp.mean(centered * centered, axis=-1, keepdims=True)
    inverse = lax.rsqrt(spread + EPSILON)
    return (centered * inverse, inverse)


def norm_back(grad_in, unit, inverse, gain):
    scaled = grad_in * gain
    inner = (
        scaled
        - jnp.mean(scaled, axis=-1, keepdims=True)
        - unit * jnp.mean(scaled * unit, axis=-1, keepdims=True)
    )
    return inner * inverse


def cut_kernel(ids_ref, count_ref, qkv_ref, proj_ref, fc1_ref, fc2_ref, vec_ref, bias_ref, *rest):
    outs, extra_ref = rest[:-1], rest[-1]
    group = len(outs) // 2
    place = ids_ref[0]
    width = proj_ref.shape[1]
    part = width // group
    hidden_part = fc1_ref.shape[1] // group
    vector_count, bias_cols = vec_ref.shape[0], bias_ref.shape[0]
    column = vector_count + bias_cols
    lane = lax.broadcasted_iota(jnp.int32, extra_ref.shape, 1)
    count = count_ref[0, 0]
    high = (count >> 7).astype(F32)
    low = (count & 127).astype(F32)
    extra_ref[...] = jnp.where(lane == column, high, jnp.where(lane == column + 1, low, 0.0))
    extra_ref[:, :vector_count] = vec_ref[...].astype(F32).T
    extra_ref[:, vector_count:column] = bias_ref[...].astype(F32).T
    extra = extra_ref[...].astype(BF)
    for k in range(group):
        target = place ^ k
        first, second = outs[k], outs[group + k]
        for third in range(3):
            for pair in range(part // PAIR):
                spot = (pair * 3 + third) * PAIR
                first[:, spot : spot + PAIR] = qkv_ref[
                    :, lanes(third * width + target * part + pair * PAIR, PAIR)
                ]
        first[:, 3 * part : 4 * part] = proj_ref[:, lanes(target * part, part)]
        first[:, 4 * part :] = extra
        second[:, :hidden_part] = fc1_ref[:, lanes(target * hidden_part, hidden_part)]
        second[:, hidden_part:] = fc2_ref[:, lanes(target * hidden_part, hidden_part)]


def cut(ids, counts, w_qkv, w_proj_t, w_fc1, w_fc2_t, vectors, bias, group):
    rows, width = w_proj_t.shape
    part, hidden_part = width // group, w_fc1.shape[1] // group
    return pl.pallas_call(
        cut_kernel,
        in_specs=[SMEM, SMEM] + [VMEM] * 6,
        out_specs=[VMEM] * (2 * group),
        out_shape=[shaped((rows, 4 * part + EXTRA), BF)] * group
        + [shaped((rows, 2 * hidden_part), BF)] * group,
        scratch_shapes=[pltpu.VMEM((rows, EXTRA), F32)],
        compiler_params=PARAMS,
        name="cut",
    )(ids, counts, w_qkv, w_proj_t, w_fc1, w_fc2_t, vectors, bias)


def project_kernel(ordered, group, ids_ref, *rest):
    tokens, pieces, outs = rest[:group], rest[group:-11], rest[-11:]
    qkv_w, proj_w, rows_ref, normed_ref, out_ref, mean_ref, inv_ref, fc1_ref = outs[:8]
    extra_ref, bias_ref, small_ref = outs[8:]
    place, row = ids_ref[0], ids_ref[1]
    capacity, width = tokens[0].shape
    part = proj_w.shape[1]
    size = pieces[0].shape[0]

    def lay(block, start, count):
        where = pl.ds(start, count)
        qkv_w[where, :] = block[:, : 3 * part]
        proj_w[where, :] = block[:, 3 * part : 4 * part]
        extra_ref[where, :] = block[:, 4 * part :].astype(F32)

    if ordered:
        lay(pieces[0], 0, size)
        shard = ordered
    else:
        sub = shard = size // group
        for m, piece in enumerate(pieces):
            for j in range(group):
                start = (row ^ m) * size + (place ^ j) * sub
                lay(piece.at[j * sub : (j + 1) * sub], pl.multiple_of(start, sub), sub)
    turned = extra_ref[...].T
    rows_ref[...] = turned[: rows_ref.shape[0]]
    bias_ref[...] = jnp.zeros(bias_ref.shape, F32)
    for pair in range(part // PAIR):
        for third, line in ((0, 2), (2, 3)):
            spot = (pair * 3 + third) * PAIR
            bias_ref[0:1, spot : spot + PAIR] = rows_ref[
                line : line + 1, lanes(place * part + pair * PAIR, PAIR)
            ]
    cols = fc1_ref.shape[1] // part
    small_ref[0:cols, :] = rows_ref[10 : 10 + cols, lanes(place * part, part)]
    for owner in range(part // shard):
        for line in range(cols):
            spot = (owner * cols + line) * shard
            fc1_ref[0:1, spot : spot + shard] = small_ref[
                line : line + 1, owner * shard : (owner + 1) * shard
            ]
    gain, shift, bias = rows_ref[0:1, :], rows_ref[1:2, :], bias_ref[0:1, :]
    for first in range(0, group, 2):
        span = slice(first * capacity, (first + 2) * capacity)
        inputs = jnp.concatenate([tokens[first][...].astype(F32), tokens[first + 1][...].astype(F32)])
        mean = jnp.mean(inputs, axis=-1, keepdims=True)
        centered = inputs - mean
        inverse = lax.rsqrt(jnp.mean(centered * centered, axis=-1, keepdims=True) + EPSILON)
        normed = (centered * inverse * gain + shift).astype(BF)
        normed_ref[span, :] = normed
        mean_ref[span, :] = mean
        inv_ref[span, :] = inverse
        out_ref[span, :] = (dot(normed, qkv_w[...], 1, 0) + bias).astype(BF)


def project(ids, tokens, pieces, hidden_part, ordered):
    capacity, width = tokens[0].shape
    group = len(tokens)
    length = group * capacity
    part = width // group
    return pl.pallas_call(
        lambda *refs: project_kernel(ordered, group, *refs),
        in_specs=[SMEM] + [VMEM] * (group + len(pieces)),
        out_specs=[VMEM] * 8,
        out_shape=[
            shaped((width, 3 * part), BF),
            shaped((width, part), BF),
            shaped((16, width), F32),
            shaped((length, width), BF),
            shaped((length, 3 * part), BF),
            shaped((length, 1), F32),
            shaped((length, 1), F32),
            shaped((1, hidden_part), F32),
        ],
        scratch_shapes=[
            pltpu.VMEM((width, EXTRA), F32),
            pltpu.VMEM((8, 3 * part), F32),
            pltpu.VMEM((8, part), F32),
        ],
        compiler_params=PARAMS,
        cost_estimate=pl.CostEstimate(
            flops=6 * length * width * part, bytes_accessed=12_000_000, transcendentals=0
        ),
        name="project",
    )(ids, *tokens, *pieces)


def query_chunks(length):
    step = 512
    return [(start, min(step, length - start)) for start in range(0, length, step)]


def attend_kernel(qkv_ref, bias_ref, out_ref, low_ref, lse_ref):
    length = qkv_ref.shape[0]
    key_bias = bias_ref[...]
    for head in range(2):
        keys = qkv_ref[:, PAIR + head * HD : PAIR + (head + 1) * HD]
        values = qkv_ref[:, 2 * PAIR + head * HD : 2 * PAIR + (head + 1) * HD]
        for start, size in query_chunks(length):
            queries = qkv_ref[start : start + size, head * HD : (head + 1) * HD]
            queries = queries * jnp.asarray(HD**-0.5, BF)
            scores = dot(keys, queries, 1, 1) + key_bias
            top = jnp.max(scores, axis=0, keepdims=True)
            expo = jnp.exp(scores - top)
            total = jnp.sum(expo, axis=0, keepdims=True)
            mixed = (dot(values, expo.astype(BF), 0, 0) / total).T
            out_ref[start : start + size, head * HD : (head + 1) * HD] = mixed
            low_ref[start : start + size, head * HD : (head + 1) * HD] = mixed.astype(BF)
            lse_ref[0, head : head + 1, start : start + size] = top + jnp.log(total)


def attend(qkv, key_bias):
    length, columns = qkv.shape
    pairs = columns // (3 * PAIR)
    return pl.pallas_call(
        attend_kernel,
        grid=(pairs,),
        in_specs=[
            pl.BlockSpec((length, 3 * PAIR), lambda p: (0, p)),
            pl.BlockSpec((length, 1), lambda p: (0, 0)),
        ],
        out_specs=[
            pl.BlockSpec((length, PAIR), lambda p: (0, p)),
            pl.BlockSpec((length, PAIR), lambda p: (0, p)),
            pl.BlockSpec((1, 2, length), lambda p: (p, 0, 0)),
        ],
        out_shape=[
            shaped((length, pairs * PAIR), F32),
            shaped((length, pairs * PAIR), BF),
            shaped((pairs, 2, length), F32),
        ],
        compiler_params=PARAMS,
        cost_estimate=pl.CostEstimate(
            flops=pairs * 2 * 4 * length * length * 256,
            bytes_accessed=length * columns * 4,
            transcendentals=pairs * 2 * length * length,
        ),
        name="attend",
    )(qkv, key_bias)


def attend_back_kernel(qkv_ref, bias_ref, att_ref, lse_ref, *rest):
    pieces, (out_ref, sums_ref, grad_ref) = rest[:-3], rest[-3:]
    length = qkv_ref.shape[0]
    size = pieces[0].shape[0]
    factor = HD**-0.5
    key_bias = bias_ref[...]
    for j, piece in enumerate(pieces):
        grad_ref[j * size : (j + 1) * size, :] = piece[...].astype(F32)
    for head in range(2):
        low, high = head * HD, (head + 1) * HD
        keys = qkv_ref[:, PAIR + low : PAIR + high]
        values = qkv_ref[:, 2 * PAIR + low : 2 * PAIR + high]
        key_grad = jnp.zeros((length, HD), F32)
        value_grad = jnp.zeros((length, HD), F32)
        for start, size in query_chunks(length):
            rows = slice(start, start + size)
            queries = qkv_ref[rows, low:high] * jnp.asarray(factor, BF)
            product = grad_ref[rows, low:high] * att_ref[rows, low:high]
            grads = grad_ref[rows, low:high].astype(BF)
            delta = jnp.sum(product.T, axis=0, keepdims=True)
            scores = dot(keys, queries, 1, 1) + key_bias
            probs = jnp.exp(scores - lse_ref[0, head : head + 1, rows])
            value_grad += dot(probs.astype(BF), grads, 1, 0)
            raw = (probs * (dot(values, grads, 1, 1) - delta)).astype(BF)
            key_grad += dot(raw, queries, 1, 0)
            query_grad = dot(keys, raw, 0, 0).T * factor
            out_ref[rows, low:high] = query_grad.astype(BF)
        out_ref[:, PAIR + low : PAIR + high] = key_grad.astype(BF)
        out_ref[:, 2 * PAIR + low : 2 * PAIR + high] = value_grad.astype(BF)
    sums_ref[0] = jnp.sum(out_ref[...].astype(F32), axis=0, keepdims=True)


def attend_back(qkv, key_bias, attended, lse, pieces):
    length, columns = qkv.shape
    pairs = columns // (3 * PAIR)
    size = pieces[0].shape[0]
    return pl.pallas_call(
        attend_back_kernel,
        grid=(pairs,),
        in_specs=[
            pl.BlockSpec((length, 3 * PAIR), lambda p: (0, p)),
            pl.BlockSpec((length, 1), lambda p: (0, 0)),
            pl.BlockSpec((length, PAIR), lambda p: (0, p)),
            pl.BlockSpec((1, 2, length), lambda p: (p, 0, 0)),
        ]
        + [pl.BlockSpec((size, PAIR), lambda p: (0, p))] * len(pieces),
        out_specs=[
            pl.BlockSpec((length, 3 * PAIR), lambda p: (0, p)),
            pl.BlockSpec((1, 1, 3 * PAIR), lambda p: (p, 0, 0)),
        ],
        out_shape=[shaped((length, columns), BF), shaped((pairs, 1, 3 * PAIR), F32)],
        scratch_shapes=[pltpu.VMEM((length, PAIR), F32)],
        compiler_params=PARAMS,
        cost_estimate=pl.CostEstimate(
            flops=pairs * 2 * 10 * length * length * 256,
            bytes_accessed=length * columns * 6,
            transcendentals=pairs * 2 * length * length,
        ),
        name="attend_back",
    )(qkv, key_bias, attended, lse, *pieces)


def middle_kernel(group, rows_ref, tokens_ref, *rest):
    parts, weights, (branch_ref, middle_ref, normed_ref, unit_ref, inv_ref) = (
        rest[:group], rest[group : 2 * group], rest[2 * group :]
    )
    branch = dot(parts[0][...], weights[0][...], 1, 1)
    for part, weight in zip(parts[1:], weights[1:]):
        branch = branch + dot(part[...], weight[...], 1, 1)
    branch = branch + rows_ref[4:5, :]
    branch_ref[...] = branch
    middle = tokens_ref[...].astype(F32) + rows_ref[5:6, :] * branch
    middle_ref[...] = middle
    unit, inverse = unit_rows(middle)
    unit_ref[...] = unit
    inv_ref[...] = inverse
    normed_ref[...] = (unit * rows_ref[6:7, :] + rows_ref[7:8, :]).astype(BF)


def middle_step(rows, tokens, parts, weights):
    length, width = tokens.shape
    group = len(parts)
    full = shaped((length, width), F32)
    return pl.pallas_call(
        lambda *refs: middle_kernel(group, *refs),
        in_specs=[VMEM] * (2 + 2 * group),
        out_specs=[VMEM] * 5,
        out_shape=[full, full, shaped((length, width), BF), full, shaped((length, 1), F32)],
        compiler_params=PARAMS,
        cost_estimate=pl.CostEstimate(
            flops=2 * length * width * width, bytes_accessed=8_000_000, transcendentals=0
        ),
        name="middle",
    )(rows, tokens, *parts, *weights)


def turn_kernel(group, terms, rows_ref, live_ref, cot_ref, unit_ref, inv_ref, branch_ref, *rest):
    backs, weights, outs = rest[:terms], rest[terms : terms + group], rest[terms + group :]
    middle_ref, grad_ref, sums_ref = outs[:3]
    norm_grad = backs[0][...].astype(F32)
    for ref in backs[1:]:
        norm_grad = norm_grad + ref[...].astype(F32)
    unit = unit_ref[...]
    out_grad = cot_ref[...].astype(F32) * live_ref[...]
    middle = out_grad + norm_back(norm_grad, unit, inv_ref[...], rows_ref[6:7, :])
    middle_ref[...] = middle
    low = (middle * rows_ref[5:6, :]).astype(BF)
    grad_ref[...] = low
    sums_ref[...] = jnp.zeros(sums_ref.shape, F32)
    sums_ref[0:1, :] = jnp.sum(low.astype(F32), axis=0, keepdims=True)
    sums_ref[1:2, :] = jnp.sum(middle * branch_ref[...], axis=0, keepdims=True)
    sums_ref[2:3, :] = jnp.sum(norm_grad * unit, axis=0, keepdims=True)
    sums_ref[3:4, :] = jnp.sum(norm_grad, axis=0, keepdims=True)
    for out, weight in zip(outs[3:], weights):
        out[...] = dot(low, weight[...], 1, 0).astype(BF)


def turn(rows, live, cotangent, unit, inverse, branch, backs, weights):
    length, width = cotangent.shape
    part = weights[0].shape[1]
    group = len(weights)
    return pl.pallas_call(
        lambda *refs: turn_kernel(group, len(backs), *refs),
        in_specs=[VMEM] * (6 + len(backs) + group),
        out_specs=[VMEM] * (3 + group),
        out_shape=[shaped((length, width), F32), shaped((length, width), BF), shaped((8, width), F32)]
        + [shaped((length, part), BF)] * group,
        compiler_params=PARAMS,
        cost_estimate=pl.CostEstimate(
            flops=2 * length * width * width, bytes_accessed=10_000_000, transcendentals=0
        ),
        name="turn",
    )(rows, live, cotangent, unit, inverse, branch, *backs, *weights)


def proj_weights_kernel(grad_ref, *rest):
    half = len(rest) // 2
    for part, out in zip(rest[:half], rest[half:]):
        out[...] = dot(grad_ref[...], part[...], 0, 0).astype(BF)


def proj_weights(grads, parts):
    length, width = grads.shape
    part = parts[0].shape[1]
    return pl.pallas_call(
        proj_weights_kernel,
        in_specs=[VMEM] * (1 + len(parts)),
        out_specs=[VMEM] * len(parts),
        out_shape=[shaped((width, part), BF)] * len(parts),
        compiler_params=PARAMS,
        cost_estimate=pl.CostEstimate(
            flops=2 * length * width * width, bytes_accessed=4_000_000, transcendentals=0
        ),
        name="proj_weights",
    )(grads, *parts)


def mlp_kernel(count, rows_ref, *rest):
    normed_in, cots, lives = rest[:count], rest[count : 2 * count], rest[2 * count : 3 * count]
    fc1_ref, fc2_ref, bias_ref = rest[3 * count : 3 * count + 3]
    backs = rest[3 * count + 3 : 4 * count + 3]
    normed_ref, grad_ref, act_ref, pre_ref, sums_ref, fbias_ref, back_acc = rest[4 * count + 3 :]
    step = pl.program_id(0)
    size = cots[0].shape[0]

    @pl.when(step == 0)
    def _():
        normed_ref[...] = jnp.concatenate([ref[...].astype(F32) for ref in normed_in]).astype(BF)
        scale = rows_ref[9:10, :]
        grads = [cot[...].astype(F32) * live[...] * scale for cot, live in zip(cots, lives)]
        grad_ref[...] = jnp.concatenate(grads).astype(BF)
        fbias_ref[...] = jnp.sum(grads[0].astype(BF).astype(F32), axis=0, keepdims=True)

    chunk = fc1_ref.shape[1] // 2
    for cols in (slice(0, chunk), slice(chunk, 2 * chunk)):
        pre = dot(normed_ref[...], fc1_ref[:, cols], 1, 0) + bias_ref[:, cols]
        act_grad = dot(grad_ref[...], fc2_ref[:, cols], 1, 0)
        cdf = 0.5 * (1.0 + lax.erf(pre * SQRT_HALF))
        act_ref[:, cols] = (pre * cdf).astype(BF)
        slope = cdf + pre * (jnp.exp(-0.5 * pre * pre) * INV_ROOT_TWO_PI)
        pre_grad = (act_grad * slope).astype(BF)
        pre_ref[:, cols] = pre_grad
        sums_ref[:, cols] = jnp.sum(pre_grad.astype(F32), axis=0, keepdims=True)
    back = dot(pre_ref[...], fc1_ref[...], 1, 1)

    @pl.when(step == 0)
    def _():
        back_acc[...] = back

    @pl.when(step == pl.num_programs(0) - 1)
    def _():
        whole = back_acc[...] + back
        for j, ref in enumerate(backs):
            ref[...] = whole[j * size : (j + 1) * size].astype(BF)


def mlp(rows, normed, cots, lives, weights, bias):
    size, width = normed[0].shape
    count = len(normed)
    length = count * size
    hidden = weights.shape[1] // 2
    step = hidden // 2

    def whole(*shape):
        return pl.BlockSpec(shape, lambda i: (0, 0))

    cols = pl.BlockSpec((length, step), lambda i: (0, i))
    return pl.pallas_call(
        lambda *refs: mlp_kernel(count, *refs),
        grid=(2,),
        in_specs=[whole(*rows.shape)]
        + [whole(size, width)] * (2 * count)
        + [whole(size, 1)] * count
        + [
            pl.BlockSpec((width, step), lambda i: (0, i)),
            pl.BlockSpec((width, step), lambda i: (0, 2 + i)),
            pl.BlockSpec((1, step), lambda i: (0, i)),
        ],
        out_specs=[whole(size, width)] * count
        + [whole(length, width)] * 2
        + [cols, cols, pl.BlockSpec((1, step), lambda i: (0, i)), whole(1, width)],
        out_shape=[shaped((size, width), BF)] * count
        + [shaped((length, width), BF)] * 2
        + [shaped((length, hidden), BF)] * 2
        + [shaped((1, hidden), F32), shaped((1, width), F32)],
        scratch_shapes=[pltpu.VMEM((length, width), F32)],
        compiler_params=PARAMS,
        cost_estimate=pl.CostEstimate(
            flops=6 * length * width * hidden,
            bytes_accessed=12_000_000,
            transcendentals=2 * length * hidden,
        ),
        name="mlp",
    )(rows, *normed, *cots, *lives, weights, weights, bias)


def mlp_weights_kernel(
    norm_a, norm_b, grad_a, grad_b, fc2_ref, pre_a, pre_b, act_a, act_b, out_ref, *branches
):
    hidden = pre_a.shape[1]
    first = dot(norm_a[...], pre_a[...], 0, 0) + dot(norm_b[...], pre_b[...], 0, 0)
    out_ref[:, :hidden] = first.astype(BF)
    second = dot(grad_a[...], act_a[...], 0, 0) + dot(grad_b[...], act_b[...], 0, 0)
    out_ref[:, hidden:] = second.astype(BF)
    count = len(branches) // 2
    size = branches[0].shape[0]
    for half, act in enumerate((act_a, act_b)):
        branch = dot(act[...], fc2_ref[...], 1, 1)
        for j in range(count):
            branches[half * count + j][...] = branch[j * size : (j + 1) * size].astype(BF)


def mlp_weights(normed, grads, pres, acts, weights, group):
    length, width = normed[0].shape
    hidden = pres[0].shape[1]
    size = 2 * length // group
    step = 256
    cols = pl.BlockSpec((length, step), lambda i: (0, i))
    whole = pl.BlockSpec((length, hidden), lambda i: (0, 0))
    return pl.pallas_call(
        mlp_weights_kernel,
        grid=(width // step,),
        in_specs=[cols] * 4 + [pl.BlockSpec((step, hidden), lambda i: (i, 1))] + [whole] * 4,
        out_specs=[pl.BlockSpec((step, 2 * hidden), lambda i: (i, 0))]
        + [pl.BlockSpec((size, step), lambda i: (0, i))] * group,
        out_shape=[shaped((width, 2 * hidden), BF)] + [shaped((size, width), BF)] * group,
        compiler_params=PARAMS,
        cost_estimate=pl.CostEstimate(
            flops=12 * length * width * hidden, bytes_accessed=20_000_000, transcendentals=0
        ),
        name="mlp_weights",
    )(*normed, *grads, weights, *pres, *acts)


def finish_kernel(rows_ref, live_ref, cot_ref, middle_ref, *rest):
    terms, (out_ref, sums_ref) = rest[:-2], rest[-2:]
    branch = terms[0][...].astype(F32)
    for ref in terms[1:]:
        branch = branch + ref[...].astype(F32)
    branch = branch + rows_ref[8:9, :]
    out_ref[...] = (middle_ref[...] + rows_ref[9:10, :] * branch).astype(BF)
    grads = cot_ref[...].astype(F32) * live_ref[...]
    sums_ref[...] = jnp.sum(grads * branch, axis=0, keepdims=True)


def finish(rows, live, cotangent, middle, terms):
    length, width = cotangent.shape
    return pl.pallas_call(
        finish_kernel,
        in_specs=[VMEM] * (4 + len(terms)),
        out_specs=[VMEM] * 2,
        out_shape=[shaped((length, width), BF), shaped((1, width), F32)],
        compiler_params=PARAMS,
        name="finish",
    )(rows, live, cotangent, middle, *terms)


def begin_kernel(rows_ref, tokens_ref, mean_ref, inv_ref, middle_ref, *rest):
    terms, out_ref = rest[:-1], rest[-1]
    grads = terms[0][...].astype(F32)
    for ref in terms[1:]:
        grads = grads + ref[...].astype(F32)
    inverse = inv_ref[...]
    unit = (tokens_ref[...].astype(F32) - mean_ref[...]) * inverse
    out_ref[...] = (middle_ref[...] + norm_back(grads, unit, inverse, rows_ref[0:1, :])).astype(BF)


def begin(rows, tokens, mean, inverse, middle_grad, terms):
    length, width = tokens.shape
    column = pl.BlockSpec((length, 1), lambda i: (0, 0))
    whole = pl.BlockSpec((length, width), lambda i: (0, 0))
    return pl.pallas_call(
        begin_kernel,
        grid=(1,),
        in_specs=[pl.BlockSpec(rows.shape, lambda i: (0, 0)), whole, column, column, whole]
        + [whole] * len(terms),
        out_specs=whole,
        out_shape=shaped((length, width), BF),
        compiler_params=PARAMS,
        name="begin",
    )(rows, tokens, mean, inverse, middle_grad, *terms)


def qkv_back_kernel(group, grad_ref, weight_ref, mean_ref, inv_ref, *rest):
    tokens, outs, sums_ref = rest[:group], rest[group:-1], rest[-1]
    size = tokens[0].shape[0]
    gain = shift = 0.0
    for first in range(0, group, 2):
        span = slice(first * size, (first + 2) * size)
        part = dot(grad_ref[span, :], weight_ref[...], 1, 1)
        inputs = jnp.concatenate([tokens[first][...].astype(F32), tokens[first + 1][...].astype(F32)])
        unit = (inputs - mean_ref[span, :]) * inv_ref[span, :]
        outs[first][...] = part[:size].astype(BF)
        outs[first + 1][...] = part[size:].astype(BF)
        gain = gain + jnp.sum(part * unit, axis=0, keepdims=True)
        shift = shift + jnp.sum(part, axis=0, keepdims=True)
    sums_ref[...] = jnp.zeros(sums_ref.shape, F32)
    sums_ref[0:1, :] = gain
    sums_ref[1:2, :] = shift


def qkv_back(qkv_grad, weight, tokens, mean, inverse):
    size, width = tokens[0].shape
    group = len(tokens)
    return pl.pallas_call(
        lambda *refs: qkv_back_kernel(group, *refs),
        in_specs=[VMEM] * (4 + group),
        out_specs=[VMEM] * (group + 1),
        out_shape=[shaped((size, width), BF)] * group + [shaped((8, width), F32)],
        compiler_params=PARAMS,
        cost_estimate=pl.CostEstimate(
            flops=2 * group * size * width * qkv_grad.shape[1],
            bytes_accessed=10_000_000,
            transcendentals=0,
        ),
        name="qkv_back",
    )(qkv_grad, weight, mean, inverse, *tokens)


def attn_weights_kernel(
    direct, shard, terms, ids_ref, normed_ref, grad_ref, norm1_ref, sums_ref, turn_ref, fbias_ref,
    scale2_ref, bias_a_ref, bias_b_ref, *rest,
):
    projs, outs = rest[:terms], rest[terms:-4]
    rows_ref, turned_ref, block_ref, small_ref = rest[-4:]
    place, row = ids_ref[0], ids_ref[1]
    width = normed_ref.shape[1]
    part = projs[0].shape[1]
    rows_ref[...] = jnp.zeros(rows_ref.shape, F32)
    rows_ref[0:2, :] = norm1_ref[0:2, :]
    for pair in range(part // PAIR):
        where = lanes(place * part + pair * PAIR, PAIR)
        rows_ref[2:3, where] = sums_ref[pair, :, :PAIR]
        rows_ref[3:4, where] = sums_ref[pair, :, 2 * PAIR :]
    rows_ref[4:8, :] = turn_ref[0:4, :]
    rows_ref[8:9, :] = fbias_ref[...]
    rows_ref[9:10, :] = scale2_ref[...]
    cols = bias_a_ref.shape[1] // part
    for owner in range(part // shard):
        for line in range(cols):
            spot = (owner * cols + line) * shard
            small_ref[line : line + 1, owner * shard : (owner + 1) * shard] = (
                bias_a_ref[0:1, spot : spot + shard] + bias_b_ref[0:1, spot : spot + shard]
            )
    rows_ref[10 : 10 + cols, lanes(place * part, part)] = small_ref[0:cols, :]
    turned_ref[...] = rows_ref[...].T
    step = block_ref.shape[0]
    for k in range(width // step):
        start = pl.multiple_of(((row >> 1) ^ k) * step, step) if direct else k * step
        cols = pl.ds(start, step)
        block_ref[:, : 3 * part] = dot(normed_ref[:, cols], grad_ref[...], 0, 0)
        proj = projs[0][cols, :].astype(F32)
        for ref in projs[1:]:
            proj = proj + ref[cols, :].astype(F32)
        block_ref[:, 3 * part : 4 * part] = proj
        block_ref[:, 4 * part :] = turned_ref[cols, :]
        if direct:
            size = step // 2
            side = row & 1
            outs[2 * k][...] = block_ref[pl.ds(pl.multiple_of(side * size, size), size), :].astype(BF)
            outs[2 * k + 1][...] = block_ref[
                pl.ds(pl.multiple_of((1 - side) * size, size), size), :
            ].astype(BF)
        else:
            outs[0][k * step : (k + 1) * step, :] = block_ref[...].astype(BF)


def attn_weights(ids, normed1, qkv_grad, sums, projs, blocks, shard):
    length, width = normed1.shape
    part = projs[0].shape[1]
    columns = 4 * part + EXTRA
    direct = blocks > 0
    step = 2 * (width // blocks) if direct else 256
    out_shape = [shaped((width // blocks, columns), BF)] * blocks if direct else [
        shaped((width, columns), BF)
    ]
    return pl.pallas_call(
        lambda *refs: attn_weights_kernel(direct, shard, len(projs), *refs),
        in_specs=[SMEM] + [VMEM] * (2 + len(sums) + len(projs)),
        out_specs=[VMEM] * len(out_shape),
        out_shape=out_shape,
        scratch_shapes=[
            pltpu.VMEM((EXTRA, width), F32),
            pltpu.VMEM((width, EXTRA), F32),
            pltpu.VMEM((step, columns), F32),
            pltpu.VMEM((8, part), F32),
        ],
        compiler_params=PARAMS,
        cost_estimate=pl.CostEstimate(
            flops=6 * length * width * part, bytes_accessed=12_000_000, transcendentals=0
        ),
        name="attn_weights",
    )(ids, normed1, qkv_grad, *sums, *projs)


def total(ids, terms, group):
    size, columns = terms[0].shape
    rows = size // group

    def kernel(ids_ref, *refs):
        ins, outs, sum_ref = refs[: len(terms)], refs[len(terms) : -1], refs[-1]
        value = ins[0][...].astype(F32)
        for ref in ins[1:]:
            value = value + ref[...].astype(F32)
        sum_ref[...] = value
        for k, out in enumerate(outs):
            start = pl.multiple_of((ids_ref[0] ^ k) * rows, rows)
            out[...] = sum_ref[pl.ds(start, rows), :].astype(BF)

    return pl.pallas_call(
        kernel,
        in_specs=[SMEM] + [VMEM] * len(terms),
        out_specs=[VMEM] * group,
        out_shape=[shaped((rows, columns), BF)] * group,
        scratch_shapes=[pltpu.VMEM((size, columns), F32)],
        compiler_params=PARAMS,
        name="total",
    )(ids, *terms)


def place_attn_kernel(ids_ref, *refs):
    group = len(refs) - 3
    blocks, (qkv_ref, proj_ref, extra_ref) = refs[:group], refs[group:]
    width = proj_ref.shape[1]
    part = width // group
    extra = jnp.zeros(extra_ref.shape[::-1], F32)
    for k, block in enumerate(blocks):
        source = ids_ref[0] ^ k
        for third in range(3):
            for pair in range(part // PAIR):
                spot = (pair * 3 + third) * PAIR
                where = lanes(third * width + source * part + pair * PAIR, PAIR)
                qkv_ref[:, where] = block[:, spot : spot + PAIR].astype(F32)
        proj_ref[:, lanes(source * part, part)] = block[:, 3 * part : 4 * part].astype(F32)
        extra = extra + block[:, 4 * part :].astype(F32)
    extra_ref[...] = extra.T


def place_attn(ids, blocks, width):
    rows = blocks[0].shape[0]
    return pl.pallas_call(
        place_attn_kernel,
        in_specs=[SMEM] + [VMEM] * len(blocks),
        out_specs=[VMEM] * 3,
        out_shape=[
            shaped((rows, 3 * width), F32),
            shaped((rows, width), F32),
            shaped((EXTRA, rows), F32),
        ],
        compiler_params=PARAMS,
        name="place_attn",
    )(ids, *blocks)


def place_mlp_kernel(ids_ref, *refs):
    group = len(refs) - 2
    blocks, (fc1_ref, fc2_ref) = refs[:group], refs[group:]
    part = fc1_ref.shape[1] // group
    for k, block in enumerate(blocks):
        where = lanes((ids_ref[0] ^ k) * part, part)
        fc1_ref[:, where] = block[:, :part].astype(F32)
        fc2_ref[:, where] = block[:, part:].astype(F32)


def place_mlp(ids, blocks, hidden):
    rows = blocks[0].shape[0]
    return pl.pallas_call(
        place_mlp_kernel,
        in_specs=[SMEM] + [VMEM] * len(blocks),
        out_specs=[VMEM] * 2,
        out_shape=[shaped((rows, hidden), F32)] * 2,
        compiler_params=PARAMS,
        name="place_mlp",
    )(ids, *blocks)


def local(tokens, counts, w_qkv, w_proj, w_fc1, fc1_bias, w_fc2, vectors, cotangent):
    _, capacity, width = tokens.shape
    hidden = w_fc1.shape[1]
    rows = w_qkv.shape[0]
    group, replicas = lax.axis_size("ctx"), lax.axis_size("dp")
    place, replica = lax.axis_index("ctx"), lax.axis_index("dp")
    ids = jnp.stack([place, replica]).astype(jnp.int32)
    head_width = width // group
    hidden_part = hidden // group
    bias_cols = hidden // width
    vector_count = vectors.shape[0]
    direct = replicas <= 8

    def swap(value, bit, axis="ctx"):
        size = group if axis == "ctx" else replicas
        return lax.ppermute(value, axis, [(i, i ^ bit) for i in range(size)])

    def after(value, *before):
        return lax.optimization_barrier((value,) + before)[0]

    def gather(own, *before):
        pieces = [own]
        for j in range(1, group):
            bit = j & -j
            source = pieces[j ^ bit]
            pieces.append(swap(after(source, *before) if j ^ bit else source, bit))
        return pieces

    def scatter(parts, *before, mids=None):
        pieces = {j: [part] for j, part in enumerate(parts)}

        def added(terms):
            if len(terms) == 1:
                return terms[0]
            return sum(term.astype(F32) for term in terms).astype(BF)

        bit = 1
        while bit < group:
            for j in sorted((j for j in pieces if j & bit), reverse=True):
                value = added(pieces.pop(j))
                if bit > 1:
                    if mids is not None:
                        mids.append(value)
                    value = after(value, *before)
                pieces[j ^ bit].append(swap(value, bit))
            bit *= 2
        return pieces[0]

    def split(whole):
        return [whole[j * capacity : (j + 1) * capacity] for j in range(whole.shape[0] // capacity)]

    def exchange(relative):
        return [relative[0]] + [swap(relative[k], k) for k in range(1, group)]

    def in_order(relative):
        stacked = jnp.stack(relative)
        return jnp.concatenate(
            [lax.dynamic_index_in_dim(stacked, place ^ s, 0, False) for s in range(group)], axis=0
        )

    cuts = cut(
        ids, counts, w_qkv, w_proj.T, w_fc1, w_fc2.T, vectors, fc1_bias.reshape(bias_cols, rows), group
    )
    first = exchange(cuts[:group])
    tokens_far = swap(after(tokens[0], *first), group // 2)
    if direct:
        shards = {0: jnp.concatenate(first, axis=0)}
        for m in range(replicas - 2, 0, -2):
            shards[m] = swap(shards[0], m, "dp")
        shards[1] = swap(shards[0], 1, "dp")
        arrived = [tokens_far] + [shards[m] for m in sorted(shards) if m]
        for m in range(3, replicas, 2):
            shards[m] = swap(after(shards[m - 1], *arrived), 1, "dp")
        first_pieces = [shards[m] for m in range(replicas)]
    else:
        first_pieces = [lax.all_gather(in_order(first), "dp", axis=0, tiled=True)]
        arrived = [tokens_far]
    tokens_pieces = [tokens[0]]
    for j in range(1, group):
        source = tokens_pieces[j ^ (j & -j)]
        if j == group // 2:
            tokens_pieces.append(tokens_far)
        else:
            tokens_pieces.append(swap(after(source, *arrived), j & -j))
    second = exchange([after(block, *arrived) for block in cuts[group:]])
    second_shard = in_order(second)
    second_all = lax.all_gather(second_shard, "dp", axis=0, tiled=True)

    count_column = 4 * head_width + vector_count + bias_cols
    live = []
    for block in first:
        piece = block[0, count_column : count_column + 2].astype(F32)
        bound = piece[0] * 128.0 + piece[1]
        slot = lax.broadcasted_iota(jnp.int32, (capacity, 1), 0).astype(F32)
        live.append((slot < bound).astype(F32))
    key_bias = jnp.where(jnp.concatenate(live, axis=0) > 0.0, 0.0, MASKED_SCORE).astype(F32)

    tokens_own = after(tokens[0], second_shard)
    (
        weight_qkv, weight_proj, vector_rows, normed1, qkv, mean1, inverse1, bias_fc1
    ) = project(
        ids, [tokens_own] + tokens_pieces[1:], first_pieces, hidden_part, 0 if direct else rows
    )

    cotangent_pieces = gather(after(cotangent[0], *second, *first_pieces), qkv)
    attended, attended_low, lse = attend(qkv, key_bias)
    projs = gather(weight_proj, attended_low)
    attended_own = exchange(split(attended_low))
    branch1, middle, normed2_own, unit2, inverse2 = middle_step(
        vector_rows, tokens[0], attended_own, projs
    )
    normed2 = gather(normed2_own)
    half = group // 2

    def feed(where, bias):
        return mlp(
            vector_rows, normed2[where], cotangent_pieces[where], live[where], second_all, bias
        )

    *backs_near, norm_near, grad_near, act_near, pre_near, sums_near, fbias = feed(
        slice(0, half), bias_fc1
    )
    *backs_far, norm_far, grad_far, act_far, pre_far, sums_far, _ = feed(
        slice(half, group), after(bias_fc1, sums_near)
    )
    mids = []
    norm2_terms = scatter(backs_near + backs_far, mids=mids)
    grad_mlp, *branches = mlp_weights(
        [norm_near, norm_far], [grad_near, grad_far], [after(pre_near, *mids), pre_far],
        [act_near, act_far], second_all, group,
    )
    owned_mlp = lax.psum_scatter(grad_mlp, "dp", scatter_dimension=0, tiled=True)

    middle_grad, branch_grad, turn_sums, *att_grads = turn(
        vector_rows, live[0], cotangent[0], unit2, inverse2, branch1, norm2_terms, projs
    )
    att_grads = exchange(att_grads)
    mids = []
    proj_terms = scatter(proj_weights(branch_grad, attended_own), mids=mids)
    branch2_terms = scatter(branches, *att_grads, mids=mids)
    qkv_grad, qkv_sums = attend_back(qkv, key_bias, attended, after(lse, *mids), att_grads)
    *norm1_parts, norm1_sums = qkv_back(qkv_grad, weight_qkv, tokens_pieces, mean1, inverse1)
    output, grad_scale2 = finish(vector_rows, live[0], cotangent[0], middle, branch2_terms)
    parts = attn_weights(
        ids, normed1, qkv_grad,
        [norm1_sums, qkv_sums, turn_sums, fbias, grad_scale2, sums_near, sums_far],
        proj_terms, replicas if direct else 0, rows,
    )
    if direct:
        terms, last = [], []
        for k in list(range(replicas // 2 - 1, -1, -1)):
            other = swap(after(parts[2 * k + 1], *last), 1, "dp")
            if k == 0:
                terms += [parts[0], other]
            else:
                summed = (parts[2 * k].astype(F32) + other.astype(F32)).astype(BF)
                terms.append(swap(summed, 2 * k, "dp"))
            last = [other]
        cuts_mlp = total(ids, [owned_mlp], group)
    else:
        owned_attn = lax.psum_scatter(parts[0], "dp", scatter_dimension=0, tiled=True)

        def relative(owned):
            blocks = owned.reshape(group, rows, -1)
            return [lax.dynamic_index_in_dim(blocks, place ^ k, 0, False) for k in range(group)]

        cuts_mlp = relative(owned_mlp)
    out_fc1, out_fc2 = place_mlp(ids, exchange(cuts_mlp), hidden)
    if direct:
        cuts_attn = total(after(ids, out_fc1), terms, group)
    else:
        cuts_attn = relative(owned_attn)
    input_grad = begin(
        vector_rows, tokens[0], mean1, inverse1, middle_grad, scatter(norm1_parts)
    )

    out_qkv, out_proj, out_extra = place_attn(ids, exchange(cuts_attn), width)
    return (
        output[None],
        input_grad[None],
        out_qkv,
        out_proj.T,
        out_fc1,
        out_extra[vector_count : vector_count + bias_cols].reshape(-1),
        out_fc2.T,
        out_extra[:vector_count],
    )


def solution(mesh):
    both = ("dp", "ctx")
    in_specs = (
        P("dp", "ctx", None),
        P("dp", "ctx"),
        P(both, None),
        P(None, both),
        P(both, None),
        P(both),
        P(None, both),
        P(None, both),
        P("dp", "ctx", None),
    )
    out_specs = (
        P("dp", "ctx", None),
        P("dp", "ctx", None),
        P(both, None),
        P(None, both),
        P(both, None),
        P(both),
        P(None, both),
        P(None, both),
    )
    return jax.shard_map(local, mesh=mesh, in_specs=in_specs, out_specs=out_specs, check_vma=False)
```

profile of v0, /device:TPU:0, one launch (start us, length us, event | category | flops | bytes accessed | tf_op | source)
XLA Modules:
  0.0 369.0 jit_solution(2793687086708389809)
XLA Ops:
  30.0 6.7 %collective-permute-done.5.refs_7_ = bf16[128,1152]{1,0:T(8,128)(2,1)S(1)} collective-permute-done((bf16[128,1152]{1,0:T(8,128)(2,1)S(1)}, bf16[128,1152]{1,0:T(8,128)(2,1)S(1)}, u32[]{:S(2)}, u32[]{:S(2)}) %collective-permute-start.5) | collective-permute-done | bytes 294944 | tf_op jit(solution)/shard_map/ppermute | solution.py:772
  36.8 10.9 %collective-permute-done.6.refs_9_ = bf16[128,1152]{1,0:T(8,128)(2,1)S(1)} collective-permute-done((bf16[128,1152]{1,0:T(8,128)(2,1)S(1)}, bf16[128,1152]{1,0:T(8,128)(2,1)S(1)}, u32[]{:S(2)}, u32[]{:S(2)}) %collective-permute-start.6) | collective-permute-done | bytes 294944 | tf_op jit(solution)/shard_map/ppermute | solution.py:772
  50.3 4.6 %collective-permute-done.9 = bf16[32,2048]{1,0:T(8,128)(2,1)S(1)} collective-permute-done((bf16[32,2048]{1,0:T(8,128)(2,1)}, bf16[32,2048]{1,0:T(8,128)(2,1)S(1)}, u32[]{:S(2)}, u32[]{:S(2)}) %collective-permute-start.9) | collective-permute-done | bytes 131104 | tf_op jit(solution)/shard_map/ppermute | solution.py:772
  72.1 11.3 %collective-permute-done.15.refs_12_ = bf16[128,1152]{1,0:T(8,128)(2,1)S(1)} collective-permute-done((bf16[128,1152]{1,0:T(8,128)(2,1)}, bf16[128,1152]{1,0:T(8,128)(2,1)S(1)}, u32[]{:S(2)}, u32[]{:S(2)}) %collective-permute-start.15) | collective-permute-done | bytes 294944 | tf_op jit(solution)/shard_map/ppermute | solution.py:772
  83.4 6.3 %collective-permute-done.14.refs_10_ = bf16[128,1152]{1,0:T(8,128)(2,1)S(1)} collective-permute-done((bf16[128,1152]{1,0:T(8,128)(2,1)}, bf16[128,1152]{1,0:T(8,128)(2,1)S(1)}, u32[]{:S(2)}, u32[]{:S(2)}) %collective-permute-start.14) | collective-permute-done | bytes 294944 | tf_op jit(solution)/shard_map/ppermute | solution.py:772
  89.7 6.1 %collective-permute-done.13.refs_8_ = bf16[128,1152]{1,0:T(8,128)(2,1)S(1)} collective-permute-done((bf16[128,1152]{1,0:T(8,128)(2,1)S(1)}, bf16[128,1152]{1,0:T(8,128)(2,1)S(1)}, u32[]{:S(2)}, u32[]{:S(2)}) %collective-permute-start.13) | collective-permute-done | bytes 294944 | tf_op jit(solution)/shard_map/ppermute | solution.py:772
  98.3 7.6 %project.1 = (bf16[1024,768]{1,0:T(8,128)(2,1)}, bf16[1024,256]{1,0:T(8,128)(2,1)}, f32[16,1024]{1,0:T(8,128)}, bf16[1376,1024]{1,0:T(8,128)(2,1)}, bf16[1376,76...) custom-call(s32[2]{0:T(128)} %pad_add_fusion.ids_ref.refs_0_, ...), custom_call_target="tpu_custom_call" | custom-call | flops 2164260864 | bytes 12000000 | tf_op jit(solution)/shard_map/project/pallas_call | solution.py:160
  107.2 15.6 %attend.1 = (f32[1376,256]{1,0:T(8,128)}, bf16[1376,256]{1,0:T(8,128)(2,1)}, f32[2,2,1376]{2,1,0:T(2,128)}) custom-call(bf16[1376,768]{1,0:T(8,128)(2,1)} %get-tuple-element.135.qkv_ref, f32[1376,1]{1,0:T(8,128)} %broadcast_select_fusion.bias_ref), custom_call_target="tpu_custom_call" | custom-call | flops 7755268096 | bytes 4227072 | tf_op jit(solution)/shard_map/attend/pallas_call | solution.py:214
  128.0 4.7 %collective-permute-done.17.refs_4_.rest_2_ = bf16[344,256]{1,0:T(8,128)(2,1)S(1)} collective-permute-done((bf16[344,256]{1,0:T(8,128)(2,1)S(1)}, bf16[344,256]{1,0:T(8,128)(2,1)S(1)}, u32[]{:S(2)}, u32[]{:S(2)}) %collective-permute-start.17) | collective-permute-done | bytes 176160 | tf_op jit(solution)/shard_map/ppermute | solution.py:772
  136.3 5.2 %middle.1 = (f32[344,1024]{1,0:T(8,128)}, f32[344,1024]{1,0:T(8,128)}, bf16[344,1024]{1,0:T(8,128)(2,1)}, f32[344,1024]{1,0:T(8,128)}, f32[344,1]{1,0:T(8,128)}) custom-call(f32[16,1024]{1,0:T(8,128)} %get-tuple-element.134.refs_0_.rows_ref, bf16[344,1024]{1,0:T(8,128)(2,1)} %bitcast.28, bf16[344,256]{1,0:T(8,128)(2,1)} %get-tuple-element.225.refs_2_.rest_0_, ...), custom_call_target="tpu_custom_call" | custom-call | flops 721420288 | bytes 8000000 | tf_op jit(solution)/shard_map/middle/pallas_call | solution.py:324
  144.5 7.3 %collective-permute-done.26.refs_3_ = bf16[344,1024]{1,0:T(8,128)(2,1)} collective-permute-done((bf16[344,1024]{1,0:T(8,128)(2,1)S(1)}, bf16[344,1024]{1,0:T(8,128)(2,1)}, u32[]{:S(2)}, u32[]{:S(2)}) %collective-permute-start.26) | collective-permute-done | bytes 704544 | tf_op jit(solution)/shard_map/ppermute | solution.py:772
  151.8 14.3 %collective-permute-done.24.refs_1_ = bf16[344,1024]{1,0:T(8,128)(2,1)S(1)} collective-permute-done((bf16[344,1024]{1,0:T(8,128)(2,1)}, bf16[344,1024]{1,0:T(8,128)(2,1)S(1)}, u32[]{:S(2)}, u32[]{:S(2)}) %collective-permute-start.24) | collective-permute-done | bytes 704544 | tf_op jit(solution)/shard_map/ppermute | solution.py:772
  169.7 12.1 %mlp.2 = (bf16[344,1024]{1,0:T(8,128)(2,1)}, bf16[344,1024]{1,0:T(8,128)(2,1)}, bf16[688,1024]{1,0:T(8,128)(2,1)}, bf16[688,1024]{1,0:T(8,128)(2,1)}, bf16[688,1...) custom-call(f32[16,1024]{1,0:T(8,128)} %get-tuple-element.134.refs_0_.rows_ref, ...), custom_call_target="tpu_custom_call" | custom-call | flops 4328521728 | bytes 12000000 | tf_op jit(solution)/shard_map/mlp/pallas_call | solution.py:448
  182.7 11.9 %mlp.3 = (bf16[344,1024]{1,0:T(8,128)(2,1)}, bf16[344,1024]{1,0:T(8,128)(2,1)}, bf16[688,1024]{1,0:T(8,128)(2,1)}, bf16[688,1024]{1,0:T(8,128)(2,1)}, bf16[688,1...) custom-call(f32[16,1024]{1,0:T(8,128)} %get-tuple-element.134.refs_0_.rows_ref, ...), custom_call_target="tpu_custom_call" | custom-call | flops 4328521728 | bytes 12000000 | tf_op jit(solution)/shard_map/mlp/pallas_call | solution.py:448
  198.5 15.0 %mlp_weights.1 = (bf16[1024,2048]{1,0:T(8,128)(2,1)}, bf16[344,1024]{1,0:T(8,128)(2,1)}, bf16[344,1024]{1,0:T(8,128)(2,1)}, bf16[344,1024]{1,0:T(8,128)(2,1)}, bf16[344,1024]{1,0:T(8,128)(2,1)}) custom-call(bf16[688,1024]{1,0:T(8,128)(2,1)} %get-tuple-element.143.norm_a, bf16[688,1024]{1,0:T(8,128)(2,1)} %get-tuple-element.147.norm_b, ...), custom_call_target="tpu_custom_call" | custom-call | flops 8657043456 | bytes 20000000 | tf_op jit(solution)/shard_map/mlp_weights/pallas_call | solution.py:500
  216.0 15.8 %collective-permute-done.32.refs_8_ = bf16[344,1024]{1,0:T(8,128)(2,1)S(1)} collective-permute-done((bf16[344,1024]{1,0:T(8,128)(2,1)S(1)}, bf16[344,1024]{1,0:T(8,128)(2,1)S(1)}, u32[]{:S(2)}, u32[]{:S(2)}) %collective-permute-start.32) | collective-permute-done | bytes 704544 | tf_op jit(solution)/shard_map/ppermute | solution.py:772
  232.7 6.1 %turn.1 = (f32[344,1024]{1,0:T(8,128)}, bf16[344,1024]{1,0:T(8,128)(2,1)}, f32[8,1024]{1,0:T(8,128)}, bf16[344,256]{1,0:T(8,128)(2,1)}, bf16[344,256]{1,0:T(8,12...) custom-call(f32[16,1024]{1,0:T(8,128)} %get-tuple-element.134.refs_0_.rows_ref, ...), custom_call_target="tpu_custom_call" | custom-call | flops 721420288 | bytes 10000000 | tf_op jit(solution)/shard_map/turn/pallas_call | solution.py:362
  246.0 4.6 %collective-permute-done.34.rest_2_ = bf16[344,256]{1,0:T(8,128)(2,1)S(1)} collective-permute-done((bf16[344,256]{1,0:T(8,128)(2,1)S(1)}, bf16[344,256]{1,0:T(8,128)(2,1)S(1)}, u32[]{:S(2)}, u32[]{:S(2)}) %collective-permute-start.34) | collective-permute-done | bytes 176160 | tf_op jit(solution)/shard_map/ppermute | solution.py:772
  255.7 24.5 %attend_back.1 = (bf16[1376,768]{1,0:T(8,128)(2,1)}, f32[2,1,384]{2,1,0:T(1,128)}) custom-call(bf16[1376,768]{1,0:T(8,128)(2,1)} %get-tuple-element.135.qkv_ref, f32[1376,1]{1,0:T(8,128)} %broadcast_select_fusion.bias_ref, f32[1376,256]{1,0:T(8,128)} %get-tuple-element.175.att_ref, f32[2,2,1376]{2,1,0:T(2,128)} %get-tuple-element.180.lse_ref, ...), custom_call_target="tpu_custom_call" | custom-call | flops 19388170240 | bytes 6340608 | tf_op jit(solution)/shard_map/attend_back/pallas_call | solution.py:277
  280.2 7.0 %qkv_back.1 = (bf16[344,1024]{1,0:T(8,128)(2,1)}, bf16[344,1024]{1,0:T(8,128)(2,1)}, bf16[344,1024]{1,0:T(8,128)(2,1)}, bf16[344,1024]{1,0:T(8,128)(2,1)}, f32[8,1024]{1,0:T(8,128)}) custom-call(bf16[1376,768]{1,0:T(8,128)(2,1)} %get-tuple-element.181.refs_0_.refs_2_, bf16[1024,768]{1,0:T(8,128)(2,1)} %get-tuple-element.182.refs_1_, ...), custom_call_target="tpu_custom_call" | custom-call | flops 2164260864 | bytes 10000000 | tf_op jit(solution)/shard_map/qkv_back/pallas_call | solution.py:585
  292.1 7.7 %attn_weights.1 = (bf16[128,1152]{1,0:T(8,128)(2,1)}, bf16[128,1152]{1,0:T(8,128)(2,1)}, bf16[128,1152]{1,0:T(8,128)(2,1)}, bf16[128,1152]{1,0:T(8,128)(2,1)}, b...) custom-call(s32[2]{0:T(128)} %pad_add_fusion.ids_ref.refs_0_, ...), custom_call_target="tpu_custom_call" | custom-call | flops 2164260864 | bytes 12000000 | tf_op jit(solution)/shard_map/attn_weights/pallas_call | solution.py:657
  301.9 7.5 %collective-permute-done.46 = bf16[128,1152]{1,0:T(8,128)(2,1)S(1)} collective-permute-done((bf16[128,1152]{1,0:T(8,128)(2,1)}, bf16[128,1152]{1,0:T(8,128)(2,1)S(1)}, u32[]{:S(2)}, u32[]{:S(2)}) %collective-permute-start.46) | collective-permute-done | bytes 294944 | tf_op jit(solution)/shard_map/ppermute | solution.py:772
  313.0 4.7 %collective-permute-done.48 = bf16[128,1152]{1,0:T(8,128)(2,1)S(1)} collective-permute-done((bf16[128,1152]{1,0:T(8,128)(2,1)S(1)}, bf16[128,1152]{1,0:T(8,128)(2,1)S(1)}, u32[]{:S(2)}, u32[]{:S(2)}) %collective-permute-start.48) | collective-permute-done | bytes 294944 | tf_op jit(solution)/shard_map/ppermute | solution.py:772
  336.7 5.7 %collective-permute-done.49.refs_1_ = bf16[128,1152]{1,0:T(8,128)(2,1)S(1)} collective-permute-done((bf16[128,1152]{1,0:T(8,128)(2,1)S(1)}, bf16[128,1152]{1,0:T(8,128)(2,1)S(1)}, u32[]{:S(2)}, u32[]{:S(2)}) %collective-permute-start.49) | collective-permute-done | bytes 294944 | tf_op jit(solution)/shard_map/ppermute | solution.py:772
  (266 shorter events, 125.0 us)
Async XLA Ops:
  7.2 161.7 %all-gather.2.cloned.1.call-start = ((), (), s32[]{:S(2)}) async-start(), calls=%async_computation.1 | async-start | bytes 4718592 | tf_op jit(solution)/shard_map/all_gather | solution.py:843
  19.6 28.2 %collective-permute-start.3 = (bf16[344,1024]{1,0:T(8,128)(2,1)}, bf16[344,1024]{1,0:T(8,128)(2,1)S(1)}, u32[]{:S(2)}, u32[]{:S(2)}) collective-permute-start(bf16[344,1024]{1,0:T(8,128)(2,1)} %bitcast.26), channel_id=1, source_target_pairs={{0,2},{1,3},{2,0},{3,1},{4,6},{5,7},{6,4},{7,5},{8,10},{9,11},{10,... | collective-permute-start | bytes 2113544 | tf_op jit(solution)/shard_map/ppermute | solution.py:772
  24.2 23.5 %collective-permute-start.6 = (bf16[128,1152]{1,0:T(8,128)(2,1)S(1)}, bf16[128,1152]{1,0:T(8,128)(2,1)S(1)}, u32[]{:S(2)}, u32[]{:S(2)}) collective-permute-start(bf16[128,1152]{1,0:T(8,128)(2,1)S(1)} %constant_dynamic-update-slice_fusion.refs_5_), channel_id=1, source_target_pairs={{0,16},{4,20},{8,24},{12,28},{16,0},{20,4},{24,8},{28,12},{1,17},{... | collective-permute-start | bytes 884744 | tf_op jit(solution)/shard_map/ppermute | solution.py:772
  26.8 20.9 %collective-permute-start.7 = (bf16[128,1152]{1,0:T(8,128)(2,1)S(1)}, bf16[128,1152]{1,0:T(8,128)(2,1)S(1)}, u32[]{:S(2)}, u32[]{:S(2)}) collective-permute-start(bf16[128,1152]{1,0:T(8,128)(2,1)S(1)} %constant_dynamic-update-slice_fusion.refs_5_), channel_id=1, source_target_pairs={{0,24},{4,28},{8,16},{12,20},{16,8},{20,12},{24,0},{28,4},{1,25},{... | collective-permute-start | bytes 884744 | tf_op jit(solution)/shard_map/ppermute | solution.py:772
  58.9 259.9 %reduce-scatter.2.cloned.1.call-start = ((), (), s32[]{:S(2)}) async-start(), calls=%async_computation.2 | async-start | bytes 4718592 | tf_op jit(solution)/shard_map/reduce_scatter | solution.py:888
  67.6 28.3 %collective-permute-start.12 = (bf16[344,1024]{1,0:T(8,128)(2,1)S(1)}, bf16[344,1024]{1,0:T(8,128)(2,1)S(1)}, u32[]{:S(2)}, u32[]{:S(2)}) collective-permute-start(bf16[344,1024]{1,0:T(8,128)(2,1)S(1)} %collective-permute-done.3.refs_3_.refs_6_), channel_id=1, source_target_pairs={{0,1},{1,0},{2,3},{3,2},{4,5},{5,4},{6,7},{7,6},{8,9},{9,8},{10,11... | collective-permute-start | bytes 2113544 | tf_op jit(solution)/shard_map/ppermute | solution.py:772
  67.9 28.7 %collective-permute-start.11 = (bf16[344,1024]{1,0:T(8,128)(2,1)S(1)}, bf16[344,1024]{1,0:T(8,128)(2,1)S(1)}, u32[]{:S(2)}, u32[]{:S(2)}) collective-permute-start(bf16[344,1024]{1,0:T(8,128)(2,1)S(1)} %bitcast.31), channel_id=1, source_target_pairs={{0,1},{1,0},{2,3},{3,2},{4,5},{5,4},{6,7},{7,6},{8,9},{9,8},{10,11... | collective-permute-start | bytes 2113544 | tf_op jit(solution)/shard_map/ppermute | solution.py:772
  69.2 20.6 %collective-permute-start.14 = (bf16[128,1152]{1,0:T(8,128)(2,1)}, bf16[128,1152]{1,0:T(8,128)(2,1)S(1)}, u32[]{:S(2)}, u32[]{:S(2)}) collective-permute-start(bf16[128,1152]{1,0:T(8,128)(2,1)} %copy-done.39), channel_id=1, source_target_pairs={{0,4},{4,0},{8,12},{12,8},{16,20},{20,16},{24,28},{28,24},{1,5},{5... | collective-permute-start | bytes 884744 | tf_op jit(solution)/shard_map/ppermute | solution.py:772
  70.7 25.2 %collective-permute-start.13 = (bf16[128,1152]{1,0:T(8,128)(2,1)S(1)}, bf16[128,1152]{1,0:T(8,128)(2,1)S(1)}, u32[]{:S(2)}, u32[]{:S(2)}) collective-permute-start(bf16[128,1152]{1,0:T(8,128)(2,1)S(1)} %collective-permute-done.5.refs_7_), channel_id=1, source_target_pairs={{0,4},{4,0},{8,12},{12,8},{16,20},{20,16},{24,28},{28,24},{1,5},{5... | collective-permute-start | bytes 884744 | tf_op jit(solution)/shard_map/ppermute | solution.py:772
  105.9 16.8 %collective-permute-start.20 = (bf16[1024,256]{1,0:T(8,128)(2,1)}, bf16[1024,256]{1,0:T(8,128)(2,1)S(1)}, u32[]{:S(2)}, u32[]{:S(2)}) collective-permute-start(bf16[1024,256]{1,0:T(8,128)(2,1)} %get-tuple-element.137.refs_6_.refs_9_), channel_id=1, source_target_pairs={{0,2},{1,3},{2,0},{3,1},{4,6},{5,7},{6,4},{7,5},{8,10},{9,11},{10,... | collective-permute-start | bytes 1572872 | tf_op jit(solution)/shard_map/ppermute | solution.py:772
  107.2 28.1 %collective-permute-start.19 = (bf16[1024,256]{1,0:T(8,128)(2,1)}, bf16[1024,256]{1,0:T(8,128)(2,1)S(1)}, u32[]{:S(2)}, u32[]{:S(2)}) collective-permute-start(bf16[1024,256]{1,0:T(8,128)(2,1)} %get-tuple-element.137.refs_6_.refs_9_), channel_id=1, source_target_pairs={{0,1},{1,0},{2,3},{3,2},{4,5},{5,4},{6,7},{7,6},{8,9},{9,8},{10,11... | collective-permute-start | bytes 1572872 | tf_op jit(solution)/shard_map/ppermute | solution.py:772
  127.1 24.6 %collective-permute-start.26 = (bf16[344,1024]{1,0:T(8,128)(2,1)S(1)}, bf16[344,1024]{1,0:T(8,128)(2,1)}, u32[]{:S(2)}, u32[]{:S(2)}) collective-permute-start(bf16[344,1024]{1,0:T(8,128)(2,1)S(1)} %bitcast.35), channel_id=1, source_target_pairs={{0,2},{1,3},{2,0},{3,1},{4,6},{5,7},{6,4},{7,5},{8,10},{9,11},{10,... | collective-permute-start | bytes 2113544 | tf_op jit(solution)/shard_map/ppermute | solution.py:772
  141.5 24.6 %collective-permute-start.24 = (bf16[344,1024]{1,0:T(8,128)(2,1)}, bf16[344,1024]{1,0:T(8,128)(2,1)S(1)}, u32[]{:S(2)}, u32[]{:S(2)}) collective-permute-start(bf16[344,1024]{1,0:T(8,128)(2,1)} %get-tuple-element.140.refs_1_), channel_id=1, source_target_pairs={{0,2},{1,3},{2,0},{3,1},{4,6},{5,7},{6,4},{7,5},{8,10},{9,11},{10,... | collective-permute-start | bytes 2113544 | tf_op jit(solution)/shard_map/ppermute | solution.py:772
  142.4 26.4 %collective-permute-start.23 = (bf16[344,1024]{1,0:T(8,128)(2,1)S(1)}, bf16[344,1024]{1,0:T(8,128)(2,1)S(1)}, u32[]{:S(2)}, u32[]{:S(2)}) collective-permute-start(bf16[344,1024]{1,0:T(8,128)(2,1)S(1)} %bitcast.36), channel_id=1, source_target_pairs={{0,1},{1,0},{2,3},{3,2},{4,5},{5,4},{6,7},{7,6},{8,9},{9,8},{10,11... | collective-permute-start | bytes 2113544 | tf_op jit(solution)/shard_map/ppermute | solution.py:772
  143.6 25.2 %collective-permute-start.22 = (bf16[344,1024]{1,0:T(8,128)(2,1)}, bf16[344,1024]{1,0:T(8,128)(2,1)}, u32[]{:S(2)}, u32[]{:S(2)}) collective-permute-start(bf16[344,1024]{1,0:T(8,128)(2,1)} %get-tuple-element.140.refs_1_), channel_id=1, source_target_pairs={{0,1},{1,0},{2,3},{3,2},{4,5},{5,4},{6,7},{7,6},{8,9},{9,8},{10,11... | collective-permute-start | bytes 2113544 | tf_op jit(solution)/shard_map/ppermute | solution.py:772
  151.8 30.0 %collective-permute-start.27 = (bf16[344,1024]{1,0:T(8,128)(2,1)}, bf16[344,1024]{1,0:T(8,128)(2,1)S(1)}, u32[]{:S(2)}, u32[]{:S(2)}) collective-permute-start(bf16[344,1024]{1,0:T(8,128)(2,1)} %collective-permute-done.26.refs_3_), channel_id=1, source_target_pairs={{0,1},{1,0},{2,3},{3,2},{4,5},{5,4},{6,7},{7,6},{8,9},{9,8},{10,11... | collective-permute-start | bytes 2113544 | tf_op jit(solution)/shard_map/ppermute | solution.py:772
  214.0 17.8 %collective-permute-start.32 = (bf16[344,1024]{1,0:T(8,128)(2,1)S(1)}, bf16[344,1024]{1,0:T(8,128)(2,1)S(1)}, u32[]{:S(2)}, u32[]{:S(2)}) collective-permute-start(bf16[344,1024]{1,0:T(8,128)(2,1)S(1)} %add_convert_fusion.2), channel_id=1, source_target_pairs={{0,2},{1,3},{2,0},{3,1},{4,6},{5,7},{6,4},{7,5},{8,10},{9,11},{10,... | collective-permute-start | bytes 2113544 | tf_op jit(solution)/shard_map/ppermute | solution.py:772
  214.9 29.2 %collective-permute-start.30 = (bf16[344,1024]{1,0:T(8,128)(2,1)}, bf16[344,1024]{1,0:T(8,128)(2,1)S(1)}, u32[]{:S(2)}, u32[]{:S(2)}) collective-permute-start(bf16[344,1024]{1,0:T(8,128)(2,1)} %get-tuple-element.160), channel_id=1, source_target_pairs={{0,1},{1,0},{2,3},{3,2},{4,5},{5,4},{6,7},{7,6},{8,9},{9,8},{10,11... | collective-permute-start | bytes 2113544 | tf_op jit(solution)/shard_map/ppermute | solution.py:772
  242.7 44.6 %collective-permute-start.29 = (bf16[344,1024]{1,0:T(8,128)(2,1)S(1)}, bf16[344,1024]{1,0:T(8,128)(2,1)S(1)}, u32[]{:S(2)}, u32[]{:S(2)}) collective-permute-start(bf16[344,1024]{1,0:T(8,128)(2,1)S(1)} %copy-done.33), channel_id=1, source_target_pairs={{0,1},{1,0},{2,3},{3,2},{4,5},{5,4},{6,7},{7,6},{8,9},{9,8},{10,11... | collective-permute-start | bytes 2113544 | tf_op jit(solution)/shard_map/ppermute | solution.py:772
  245.9 46.3 %collective-permute-start.44 = (bf16[1024,256]{1,0:T(8,128)(2,1)}, bf16[1024,256]{1,0:T(8,128)(2,1)}, u32[]{:S(2)}, u32[]{:S(2)}) collective-permute-start(bf16[1024,256]{1,0:T(8,128)(2,1)} %get-tuple-element.202), channel_id=1, source_target_pairs={{0,1},{1,0},{2,3},{3,2},{4,5},{5,4},{6,7},{7,6},{8,9},{9,8},{10,11... | collective-permute-start | bytes 1572872 | tf_op jit(solution)/shard_map/ppermute | solution.py:772
  253.4 33.9 %collective-permute-start.36 = (bf16[344,1024]{1,0:T(8,128)(2,1)S(1)}, bf16[344,1024]{1,0:T(8,128)(2,1)S(1)}, u32[]{:S(2)}, u32[]{:S(2)}) collective-permute-start(bf16[344,1024]{1,0:T(8,128)(2,1)S(1)} %add_convert_fusion.1), channel_id=1, source_target_pairs={{0,2},{1,3},{2,0},{3,1},{4,6},{5,7},{6,4},{7,5},{8,10},{9,11},{10,... | collective-permute-start | bytes 2113544 | tf_op jit(solution)/shard_map/ppermute | solution.py:772
  254.4 37.8 %collective-permute-start.45 = (bf16[1024,256]{1,0:T(8,128)(2,1)S(1)}, bf16[1024,256]{1,0:T(8,128)(2,1)}, u32[]{:S(2)}, u32[]{:S(2)}) collective-permute-start(bf16[1024,256]{1,0:T(8,128)(2,1)S(1)} %add_convert_fusion.3), channel_id=1, source_target_pairs={{0,2},{1,3},{2,0},{3,1},{4,6},{5,7},{6,4},{7,5},{8,10},{9,11},{10,... | collective-permute-start | bytes 1572872 | tf_op jit(solution)/shard_map/ppermute | solution.py:772
  300.7 50.9 %collective-permute-start.38 = (bf16[344,1024]{1,0:T(8,128)(2,1)}, bf16[344,1024]{1,0:T(8,128)(2,1)S(1)}, u32[]{:S(2)}, u32[]{:S(2)}) collective-permute-start(bf16[344,1024]{1,0:T(8,128)(2,1)} %get-tuple-element.184), channel_id=1, source_target_pairs={{0,1},{1,0},{2,3},{3,2},{4,5},{5,4},{6,7},{7,6},{8,9},{9,8},{10,11... | collective-permute-start | bytes 2113544 | tf_op jit(solution)/shard_map/ppermute | solution.py:772
  301.1 50.6 %collective-permute-start.40 = (bf16[344,1024]{1,0:T(8,128)(2,1)S(1)}, bf16[344,1024]{1,0:T(8,128)(2,1)S(1)}, u32[]{:S(2)}, u32[]{:S(2)}) collective-permute-start(bf16[344,1024]{1,0:T(8,128)(2,1)S(1)} %add_convert_fusion), channel_id=1, source_target_pairs={{0,2},{1,3},{2,0},{3,1},{4,6},{5,7},{6,4},{7,5},{8,10},{9,11},{10,... | collective-permute-start | bytes 2113544 | tf_op jit(solution)/shard_map/ppermute | solution.py:772
  (85 other events, 686.6 us)
Sparse Core Ops, SparseCore 0:
  59.0 77.8 all-gather.1
  213.7 87.3 reduce-scatter.1
where the time goes:
time: 374 us; the launch traced here: 369 us
  waiting for transfers between devices  138 us (37%)
  Pallas kernels  135 us (36%)
  starting transfers between devices  45.4 us (12%)
  between operations  20.7 us (6%)
  local copies, waits for them, and re-layouts  20.6 us (6%)
  other arithmetic  9.44 us (3%)
    ppermute x56, waiting for transfers between devices, swap(): return lax.ppermute(value, axis, [(i, i ^ bit) for i in range(size)])  138 us
    ppermute x56, starting transfers between devices, swap(): return lax.ppermute(value, axis, [(i, i ^ bit) for i in range(size)])  45.3 us
    pallas_call x1, Pallas kernels, attend_back(): pl.pallas_call(attend_back_kernel, grid=(pairs,), in_specs=[pl.BlockSpec(...  24.5 us
    pallas_call x2, Pallas kernels, mlp(): pl.pallas_call(lambda *refs: mlp_kernel(count, *refs), grid=(2,), in_spec...  24 us
    pallas_call x1, Pallas kernels, attend(): pl.pallas_call(attend_kernel, grid=(pairs,), in_specs=[pl.BlockSpec((leng...  15.6 us
    pallas_call x1, Pallas kernels, mlp_weights(): pl.pallas_call(mlp_weights_kernel, grid=(width // step,), in_specs=[cols]...  15 us
    unnamed x105, local copies, waits for them, and re-layouts  11.2 us
    pallas_call x1, Pallas kernels, attn_weights(): pl.pallas_call(lambda *refs: attn_weights_kernel(direct, shard, len(projs...  7.65 us
  transfers between devices with their start and end apart: 58, of which 26 were waited for; matrix products, arithmetic and copies ran while one was open for 3% of the time, Pallas kernels for 28%

commit v1 on v0

--- a/solution.py
+++ b/solution.py
@@ -97,10 +97,13 @@
     )(ids, counts, w_qkv, w_proj_t, w_fc1, w_fc2_t, vectors, bias)
 
 
-def project_kernel(ordered, group, ids_ref, *rest):
-    tokens, pieces, outs = rest[:group], rest[group:-11], rest[-11:]
-    qkv_w, proj_w, rows_ref, normed_ref, out_ref, mean_ref, inv_ref, fc1_ref = outs[:8]
-    extra_ref, bias_ref, small_ref = outs[8:]
+def project_kernel(ordered, group, count_column, ids_ref, *rest):
+    tokens, blocks, rest = rest[:group], rest[group : 2 * group], rest[2 * group :]
+    pieces, outs, lives, scratch = (
+        rest[: -12 - group], rest[-12 - group : -3 - group], rest[-3 - group : -3], rest[-3:]
+    )
+    qkv_w, proj_w, rows_ref, normed_ref, out_ref, mean_ref, inv_ref, fc1_ref, key_ref = outs
+    extra_ref, bias_ref, small_ref = scratch
     place, row = ids_ref[0], ids_ref[1]
     capacity, width = tokens[0].shape
     part = proj_w.shape[1]
@@ -121,6 +124,14 @@
             for j in range(group):
                 start = (row ^ m) * size + (place ^ j) * sub
                 lay(piece.at[j * sub : (j + 1) * sub], pl.multiple_of(start, sub), sub)
+    slot = lax.broadcasted_iota(jnp.int32, (capacity, 1), 0).astype(F32)
+    for j, (block, live_ref) in enumerate(zip(blocks, lives)):
+        extra = block[:, 4 * part :].astype(F32)[0:1, :]
+        bound = extra[:, count_column : count_column + 1] * 128.0
+        bound = bound + extra[:, count_column + 1 : count_column + 2]
+        live = jnp.where(slot < bound, 1.0, 0.0)
+        live_ref[...] = live
+        key_ref[j * capacity : (j + 1) * capacity, :] = (1.0 - live) * MASKED_SCORE
     turned = extra_ref[...].T
     rows_ref[...] = turned[: rows_ref.shape[0]]
     bias_ref[...] = jnp.zeros(bias_ref.shape, F32)
@@ -152,15 +163,15 @@
         out_ref[span, :] = (dot(normed, qkv_w[...], 1, 0) + bias).astype(BF)
 
 
-def project(ids, tokens, pieces, hidden_part, ordered):
+def project(ids, tokens, blocks, pieces, hidden_part, count_column, ordered):
     capacity, width = tokens[0].shape
     group = len(tokens)
     length = group * capacity
     part = width // group
     return pl.pallas_call(
-        lambda *refs: project_kernel(ordered, group, *refs),
-        in_specs=[SMEM] + [VMEM] * (group + len(pieces)),
-        out_specs=[VMEM] * 8,
+        lambda *refs: project_kernel(ordered, group, count_column, *refs),
+        in_specs=[SMEM] + [VMEM] * (2 * group + len(pieces)),
+        out_specs=[VMEM] * (9 + group),
         out_shape=[
             shaped((width, 3 * part), BF),
             shaped((width, part), BF),
@@ -170,7 +181,9 @@
             shaped((length, 1), F32),
             shaped((length, 1), F32),
             shaped((1, hidden_part), F32),
-        ],
+            shaped((length, 1), F32),
+        ]
+        + [shaped((capacity, 1), F32)] * group,
         scratch_shapes=[
             pltpu.VMEM((width, EXTRA), F32),
             pltpu.VMEM((8, 3 * part), F32),
@@ -181,7 +194,7 @@
             flops=6 * length * width * part, bytes_accessed=12_000_000, transcendentals=0
         ),
         name="project",
-    )(ids, *tokens, *pieces)
+    )(ids, *tokens, *blocks, *pieces)
 
 
 def query_chunks(length):
@@ -189,7 +202,7 @@
     return [(start, min(step, length - start)) for start in range(0, length, step)]
 
 
-def attend_kernel(qkv_ref, bias_ref, out_ref, low_ref, lse_ref):
+def attend_kernel(qkv_ref, bias_ref, out_ref, lse_ref, *lows):
     length = qkv_ref.shape[0]
     key_bias = bias_ref[...]
     for head in range(2):
@@ -204,11 +217,13 @@
             total = jnp.sum(expo, axis=0, keepdims=True)
             mixed = (dot(values, expo.astype(BF), 0, 0) / total).T
             out_ref[start : start + size, head * HD : (head + 1) * HD] = mixed
-            low_ref[start : start + size, head * HD : (head + 1) * HD] = mixed.astype(BF)
             lse_ref[0, head : head + 1, start : start + size] = top + jnp.log(total)
-
-
-def attend(qkv, key_bias):
+    for j, low in enumerate(lows):
+        size = low.shape[0]
+        low[...] = out_ref[j * size : (j + 1) * size, :].astype(BF)
+
+
+def attend(qkv, key_bias, group):
     length, columns = qkv.shape
     pairs = columns // (3 * PAIR)
     return pl.pallas_call(
@@ -220,14 +235,14 @@
         ],
         out_specs=[
             pl.BlockSpec((length, PAIR), lambda p: (0, p)),
-            pl.BlockSpec((length, PAIR), lambda p: (0, p)),
             pl.BlockSpec((1, 2, length), lambda p: (p, 0, 0)),
-        ],
+        ]
+        + [pl.BlockSpec((length // group, PAIR), lambda p: (0, p))] * group,
         out_shape=[
             shaped((length, pairs * PAIR), F32),
-            shaped((length, pairs * PAIR), BF),
             shaped((pairs, 2, length), F32),
-        ],
+        ]
+        + [shaped((length // group, pairs * PAIR), BF)] * group,
         compiler_params=PARAMS,
         cost_estimate=pl.CostEstimate(
             flops=pairs * 2 * 4 * length * length * 256,
@@ -399,7 +414,9 @@
     normed_in, cots, lives = rest[:count], rest[count : 2 * count], rest[2 * count : 3 * count]
     fc1_ref, fc2_ref, bias_ref = rest[3 * count : 3 * count + 3]
     backs = rest[3 * count + 3 : 4 * count + 3]
-    normed_ref, grad_ref, act_ref, pre_ref, sums_ref, fbias_ref, back_acc = rest[4 * count + 3 :]
+    (
+        normed_ref, out_ref, act_ref, pre_ref, sums_ref, own_ref, grad_ref, back_acc
+    ) = rest[4 * count + 3 :]
     step = pl.program_id(0)
     size = cots[0].shape[0]
 
@@ -407,9 +424,13 @@
     def _():
         normed_ref[...] = jnp.concatenate([ref[...].astype(F32) for ref in normed_in]).astype(BF)
         scale = rows_ref[9:10, :]
-        grads = [cot[...].astype(F32) * live[...] * scale for cot, live in zip(cots, lives)]
-        grad_ref[...] = jnp.concatenate(grads).astype(BF)
-        fbias_ref[...] = jnp.sum(grads[0].astype(BF).astype(F32), axis=0, keepdims=True)
+        grads = [cot[...].astype(F32) * live[...] for cot, live in zip(cots, lives)]
+        whole_grad = jnp.concatenate(grads)
+        out_ref[...] = whole_grad.astype(BF)
+        scaled = (whole_grad * scale).astype(BF)
+        grad_ref[...] = scaled
+        own_ref[0:1, :] = jnp.sum(scaled.astype(F32)[:size], axis=0, keepdims=True)
+        own_ref[1:2, :] = jnp.sum(grads[0], axis=0, keepdims=True)
 
     chunk = fc1_ref.shape[1] // 2
     for cols in (slice(0, chunk), slice(chunk, 2 * chunk)):
@@ -458,12 +479,12 @@
         ],
         out_specs=[whole(size, width)] * count
         + [whole(length, width)] * 2
-        + [cols, cols, pl.BlockSpec((1, step), lambda i: (0, i)), whole(1, width)],
+        + [cols, cols, pl.BlockSpec((1, step), lambda i: (0, i)), whole(8, width)],
         out_shape=[shaped((size, width), BF)] * count
         + [shaped((length, width), BF)] * 2
         + [shaped((length, hidden), BF)] * 2
-        + [shaped((1, hidden), F32), shaped((1, width), F32)],
-        scratch_shapes=[pltpu.VMEM((length, width), F32)],
+        + [shaped((1, hidden), F32), shaped((8, width), F32)],
+        scratch_shapes=[pltpu.VMEM((length, width), BF), pltpu.VMEM((length, width), F32)],
         compiler_params=PARAMS,
         cost_estimate=pl.CostEstimate(
             flops=6 * length * width * hidden,
@@ -475,22 +496,28 @@
 
 
 def mlp_weights_kernel(
-    norm_a, norm_b, grad_a, grad_b, fc2_ref, pre_a, pre_b, act_a, act_b, out_ref, *branches
+    norm_a, norm_b, grad_a, grad_b, rows_ref, fc2_ref, pre_a, pre_b, act_a, act_b, own_ref,
+    out_ref, scale2_ref, *branches
 ):
     hidden = pre_a.shape[1]
     first = dot(norm_a[...], pre_a[...], 0, 0) + dot(norm_b[...], pre_b[...], 0, 0)
     out_ref[:, :hidden] = first.astype(BF)
-    second = dot(grad_a[...], act_a[...], 0, 0) + dot(grad_b[...], act_b[...], 0, 0)
+    outs = [grad_a[...].astype(F32), grad_b[...].astype(F32)]
+    scaled = [(out * rows_ref[9:10, :]).astype(BF) for out in outs]
+    second = dot(scaled[0], act_a[...], 0, 0) + dot(scaled[1], act_b[...], 0, 0)
     out_ref[:, hidden:] = second.astype(BF)
+    scale2 = own_ref[1:2, :] * rows_ref[8:9, :]
     count = len(branches) // 2
     size = branches[0].shape[0]
     for half, act in enumerate((act_a, act_b)):
         branch = dot(act[...], fc2_ref[...], 1, 1)
+        scale2 = scale2 + jnp.sum(outs[half] * branch, axis=0, keepdims=True)
         for j in range(count):
             branches[half * count + j][...] = branch[j * size : (j + 1) * size].astype(BF)
-
-
-def mlp_weights(normed, grads, pres, acts, weights, group):
+    scale2_ref[...] = scale2
+
+
+def mlp_weights(rows, own, normed, grads, pres, acts, weights, group):
     length, width = normed[0].shape
     hidden = pres[0].shape[1]
     size = 2 * length // group
@@ -500,39 +527,42 @@
     return pl.pallas_call(
         mlp_weights_kernel,
         grid=(width // step,),
-        in_specs=[cols] * 4 + [pl.BlockSpec((step, hidden), lambda i: (i, 1))] + [whole] * 4,
+        in_specs=[cols] * 4
+        + [pl.BlockSpec((rows.shape[0], step), lambda i: (0, i))]
+        + [pl.BlockSpec((step, hidden), lambda i: (i, 1))]
+        + [whole] * 4
+        + [pl.BlockSpec((own.shape[0], step), lambda i: (0, i))],
         out_specs=[pl.BlockSpec((step, 2 * hidden), lambda i: (i, 0))]
+        + [pl.BlockSpec((1, step), lambda i: (0, i))]
         + [pl.BlockSpec((size, step), lambda i: (0, i))] * group,
-        out_shape=[shaped((width, 2 * hidden), BF)] + [shaped((size, width), BF)] * group,
+        out_shape=[shaped((width, 2 * hidden), BF), shaped((1, width), F32)]
+        + [shaped((size, width), BF)] * group,
         compiler_params=PARAMS,
         cost_estimate=pl.CostEstimate(
             flops=12 * length * width * hidden, bytes_accessed=20_000_000, transcendentals=0
         ),
         name="mlp_weights",
-    )(*normed, *grads, weights, *pres, *acts)
-
-
-def finish_kernel(rows_ref, live_ref, cot_ref, middle_ref, *rest):
-    terms, (out_ref, sums_ref) = rest[:-2], rest[-2:]
+    )(*normed, *grads, rows, weights, *pres, *acts, own)
+
+
+def finish_kernel(rows_ref, middle_ref, *rest):
+    terms, out_ref = rest[:-1], rest[-1]
     branch = terms[0][...].astype(F32)
     for ref in terms[1:]:
         branch = branch + ref[...].astype(F32)
     branch = branch + rows_ref[8:9, :]
     out_ref[...] = (middle_ref[...] + rows_ref[9:10, :] * branch).astype(BF)
-    grads = cot_ref[...].astype(F32) * live_ref[...]
-    sums_ref[...] = jnp.sum(grads * branch, axis=0, keepdims=True)
-
-
-def finish(rows, live, cotangent, middle, terms):
-    length, width = cotangent.shape
+
+
+def finish(rows, middle, terms):
     return pl.pallas_call(
         finish_kernel,
-        in_specs=[VMEM] * (4 + len(terms)),
-        out_specs=[VMEM] * 2,
-        out_shape=[shaped((length, width), BF), shaped((1, width), F32)],
+        in_specs=[VMEM] * (2 + len(terms)),
+        out_specs=VMEM,
+        out_shape=shaped(middle.shape, BF),
         compiler_params=PARAMS,
         name="finish",
-    )(rows, live, cotangent, middle, *terms)
+    )(rows, middle, *terms)
 
 
 def begin_kernel(rows_ref, tokens_ref, mean_ref, inv_ref, middle_ref, *rest):
@@ -613,7 +643,7 @@
         rows_ref[2:3, where] = sums_ref[pair, :, :PAIR]
         rows_ref[3:4, where] = sums_ref[pair, :, 2 * PAIR :]
     rows_ref[4:8, :] = turn_ref[0:4, :]
-    rows_ref[8:9, :] = fbias_ref[...]
+    rows_ref[8:9, :] = fbias_ref[0:1, :]
     rows_ref[9:10, :] = scale2_ref[...]
     cols = bias_a_ref.shape[1] // part
     for owner in range(part // shard):
@@ -699,11 +729,11 @@
 
 
 def place_attn_kernel(ids_ref, *refs):
-    group = len(refs) - 3
-    blocks, (qkv_ref, proj_ref, extra_ref) = refs[:group], refs[group:]
+    group = len(refs) - 4
+    blocks, (qkv_ref, proj_ref, vec_ref, bias_ref) = refs[:group], refs[group:]
     width = proj_ref.shape[1]
     part = width // group
-    extra = jnp.zeros(extra_ref.shape[::-1], F32)
+    extra = jnp.zeros((qkv_ref.shape[0], EXTRA), F32)
     for k, block in enumerate(blocks):
         source = ids_ref[0] ^ k
         for third in range(3):
@@ -713,19 +743,23 @@
                 qkv_ref[:, where] = block[:, spot : spot + PAIR].astype(F32)
         proj_ref[:, lanes(source * part, part)] = block[:, 3 * part : 4 * part].astype(F32)
         extra = extra + block[:, 4 * part :].astype(F32)
-    extra_ref[...] = extra.T
-
-
-def place_attn(ids, blocks, width):
+    turned = extra.T
+    count = vec_ref.shape[0]
+    vec_ref[...] = turned[:count]
+    bias_ref[...] = turned[count : count + bias_ref.shape[0]]
+
+
+def place_attn(ids, blocks, width, vector_count, bias_cols):
     rows = blocks[0].shape[0]
     return pl.pallas_call(
         place_attn_kernel,
         in_specs=[SMEM] + [VMEM] * len(blocks),
-        out_specs=[VMEM] * 3,
+        out_specs=[VMEM] * 4,
         out_shape=[
             shaped((rows, 3 * width), F32),
             shaped((rows, width), F32),
-            shaped((EXTRA, rows), F32),
+            shaped((vector_count, rows), F32),
+            shaped((bias_cols, rows), F32),
         ],
         compiler_params=PARAMS,
         name="place_attn",
@@ -802,9 +836,6 @@
             bit *= 2
         return pieces[0]
 
-    def split(whole):
-        return [whole[j * capacity : (j + 1) * capacity] for j in range(whole.shape[0] // capacity)]
-
     def exchange(relative):
         return [relative[0]] + [swap(relative[k], k) for k in range(1, group)]
 
@@ -819,13 +850,13 @@
     )
     first = exchange(cuts[:group])
     tokens_far = swap(after(tokens[0], *first), group // 2)
+    second = exchange([after(block, *first) for block in cuts[group:]])
     if direct:
         shards = {0: jnp.concatenate(first, axis=0)}
         for m in range(replicas - 2, 0, -2):
             shards[m] = swap(shards[0], m, "dp")
-        shards[1] = swap(shards[0], 1, "dp")
-        arrived = [tokens_far] + [shards[m] for m in sorted(shards) if m]
-        for m in range(3, replicas, 2):
+        arrived = [tokens_far] + [shards[m] for m in sorted(shards) if m] + second[1:]
+        for m in range(1, replicas, 2):
             shards[m] = swap(after(shards[m - 1], *arrived), 1, "dp")
         first_pieces = [shards[m] for m in range(replicas)]
     else:
@@ -838,30 +869,30 @@
             tokens_pieces.append(tokens_far)
         else:
             tokens_pieces.append(swap(after(source, *arrived), j & -j))
-    second = exchange([after(block, *arrived) for block in cuts[group:]])
-    second_shard = in_order(second)
+    second_shard = after(in_order(second), *arrived)
     second_all = lax.all_gather(second_shard, "dp", axis=0, tiled=True)
-
-    count_column = 4 * head_width + vector_count + bias_cols
-    live = []
-    for block in first:
-        piece = block[0, count_column : count_column + 2].astype(F32)
-        bound = piece[0] * 128.0 + piece[1]
-        slot = lax.broadcasted_iota(jnp.int32, (capacity, 1), 0).astype(F32)
-        live.append((slot < bound).astype(F32))
-    key_bias = jnp.where(jnp.concatenate(live, axis=0) > 0.0, 0.0, MASKED_SCORE).astype(F32)
-
-    tokens_own = after(tokens[0], second_shard)
+    cotangent_far = swap(after(cotangent[0], *arrived), group // 2)
+
+    tokens_own = after(tokens[0], second_shard, cotangent_far)
+    count_column = vector_count + bias_cols
     (
-        weight_qkv, weight_proj, vector_rows, normed1, qkv, mean1, inverse1, bias_fc1
+        weight_qkv, weight_proj, vector_rows, normed1, qkv, mean1, inverse1, bias_fc1, key_bias,
+        *live,
     ) = project(
-        ids, [tokens_own] + tokens_pieces[1:], first_pieces, hidden_part, 0 if direct else rows
-    )
-
-    cotangent_pieces = gather(after(cotangent[0], *second, *first_pieces), qkv)
-    attended, attended_low, lse = attend(qkv, key_bias)
-    projs = gather(weight_proj, attended_low)
-    attended_own = exchange(split(attended_low))
+        ids, [tokens_own] + tokens_pieces[1:], first, first_pieces, hidden_part, count_column,
+        0 if direct else rows,
+    )
+
+    cotangent_pieces = [cotangent[0]]
+    for j in range(1, group):
+        source = cotangent_pieces[j ^ (j & -j)]
+        if j == group // 2:
+            cotangent_pieces.append(cotangent_far)
+        else:
+            cotangent_pieces.append(swap(after(source, qkv), j & -j))
+    attended, lse, *attended_low = attend(qkv, key_bias, group)
+    projs = gather(weight_proj, lse)
+    attended_own = exchange(attended_low)
     branch1, middle, normed2_own, unit2, inverse2 = middle_step(
         vector_rows, tokens[0], attended_own, projs
     )
@@ -873,7 +904,7 @@
             vector_rows, normed2[where], cotangent_pieces[where], live[where], second_all, bias
         )
 
-    *backs_near, norm_near, grad_near, act_near, pre_near, sums_near, fbias = feed(
+    *backs_near, norm_near, grad_near, act_near, pre_near, sums_near, own_sums = feed(
         slice(0, half), bias_fc1
     )
     *backs_far, norm_far, grad_far, act_far, pre_far, sums_far, _ = feed(
@@ -881,11 +912,13 @@
     )
     mids = []
     norm2_terms = scatter(backs_near + backs_far, mids=mids)
-    grad_mlp, *branches = mlp_weights(
-        [norm_near, norm_far], [grad_near, grad_far], [after(pre_near, *mids), pre_far],
+    grad_mlp, grad_scale2, *branches = mlp_weights(
+        vector_rows, own_sums, [norm_near, norm_far], [grad_near, grad_far], [after(pre_near, *mids), pre_far],
         [act_near, act_far], second_all, group,
     )
-    owned_mlp = lax.psum_scatter(grad_mlp, "dp", scatter_dimension=0, tiled=True)
+    owned_mlp = lax.psum_scatter(
+        after(grad_mlp, *norm2_terms), "dp", scatter_dimension=0, tiled=True
+    )
 
     middle_grad, branch_grad, turn_sums, *att_grads = turn(
         vector_rows, live[0], cotangent[0], unit2, inverse2, branch1, norm2_terms, projs
@@ -896,23 +929,23 @@
     branch2_terms = scatter(branches, *att_grads, mids=mids)
     qkv_grad, qkv_sums = attend_back(qkv, key_bias, attended, after(lse, *mids), att_grads)
     *norm1_parts, norm1_sums = qkv_back(qkv_grad, weight_qkv, tokens_pieces, mean1, inverse1)
-    output, grad_scale2 = finish(vector_rows, live[0], cotangent[0], middle, branch2_terms)
     parts = attn_weights(
         ids, normed1, qkv_grad,
-        [norm1_sums, qkv_sums, turn_sums, fbias, grad_scale2, sums_near, sums_far],
+        [norm1_sums, qkv_sums, turn_sums, own_sums, grad_scale2, sums_near, sums_far],
         proj_terms, replicas if direct else 0, rows,
     )
+    norm1_terms = scatter(norm1_parts)
     if direct:
-        terms, last = [], []
-        for k in list(range(replicas // 2 - 1, -1, -1)):
-            other = swap(after(parts[2 * k + 1], *last), 1, "dp")
-            if k == 0:
-                terms += [parts[0], other]
-            else:
-                summed = (parts[2 * k].astype(F32) + other.astype(F32)).astype(BF)
-                terms.append(swap(summed, 2 * k, "dp"))
-            last = [other]
-        cuts_mlp = total(ids, [owned_mlp], group)
+        order = list(range(replicas // 2 - 1, -1, -1))
+        others = []
+        for k in order:
+            others.append(swap(after(parts[2 * k + 1], *others[-2:-1]), 1, "dp"))
+        terms = [parts[0], others[-1]]
+        for k, other in zip(order[:-1], others):
+            summed = (parts[2 * k].astype(F32) + other.astype(F32)).astype(BF)
+            terms.append(swap(summed, 2 * k, "dp"))
+        ids_late = after(ids, *others)
+        cuts_mlp = total(ids_late, [owned_mlp], group)
     else:
         owned_attn = lax.psum_scatter(parts[0], "dp", scatter_dimension=0, tiled=True)
 
@@ -921,25 +954,29 @@
             return [lax.dynamic_index_in_dim(blocks, place ^ k, 0, False) for k in range(group)]
 
         cuts_mlp = relative(owned_mlp)
+        ids_late = ids
     out_fc1, out_fc2 = place_mlp(ids, exchange(cuts_mlp), hidden)
     if direct:
-        cuts_attn = total(after(ids, out_fc1), terms, group)
+        cuts_attn = total(after(ids, out_fc1, *norm1_terms, *branch2_terms), terms, group)
     else:
         cuts_attn = relative(owned_attn)
+
     input_grad = begin(
-        vector_rows, tokens[0], mean1, inverse1, middle_grad, scatter(norm1_parts)
-    )
-
-    out_qkv, out_proj, out_extra = place_attn(ids, exchange(cuts_attn), width)
+        vector_rows, after(tokens[0], *cuts_attn), mean1, inverse1, middle_grad, norm1_terms
+    )
+    output = finish(after(vector_rows, *cuts_attn), middle, branch2_terms)
+    out_qkv, out_proj, out_vectors, out_bias = place_attn(
+        ids, exchange(cuts_attn), width, vector_count, bias_cols
+    )
     return (
         output[None],
         input_grad[None],
         out_qkv,
         out_proj.T,
         out_fc1,
-        out_extra[vector_count : vector_count + bias_cols].reshape(-1),
+        out_bias.reshape(-1),
         out_fc2.T,
-        out_extra[:vector_count],
+        out_vectors,
     )
 
 

time: 374 us -> 354 us (0.947)
  waiting for transfers between devices: 138 us -> 124 us
  starting transfers between devices: 45.4 us -> 55.4 us
  local copies, waits for them, and re-layouts: 20.6 us -> 12.8 us
  between operations: 20.7 us -> 15.5 us
    ppermute x56, waiting for transfers between devices: 138 us -> 124 us  [swap(): return lax.ppermute(value, axis, [(i, i ^ bit) for i in range(size)])]
    ppermute x56, starting transfers between devices: 45.3 us -> 55.3 us  [swap(): return lax.ppermute(value, axis, [(i, i ^ bit) for i in range(size)])]
    slice x7 -> x0, local copies, waits for them, and re-layouts: 6.22 us -> none  [the longest x4 2.34 us: local(): bound = piece[0] * 128.0 + piece[1]]
    unnamed x105 -> x109, local copies, waits for them, and re-layouts: 11.2 us -> 10.2 us
  transfers between devices with their start and end apart: 58 -> 58, of which waited for: 26 -> 26; matrix products, arithmetic and copies ran while one was open for 3% -> 2% of each run, Pallas kernels for 28% -> 33%
where the time goes in v1:
time: 354 us; the launch traced here: 349 us
  Pallas kernels  135 us (38%)
  waiting for transfers between devices  124 us (35%)
  starting transfers between devices  55.4 us (16%)
  between operations  15.5 us (4%)
  local copies, waits for them, and re-layouts  12.8 us (4%)
  other arithmetic  6.32 us (2%)
    ppermute x56, waiting for transfers between devices, swap(): return lax.ppermute(value, axis, [(i, i ^ bit) for i in range(size)])  124 us
    ppermute x56, starting transfers between devices, swap(): return lax.ppermute(value, axis, [(i, i ^ bit) for i in range(size)])  55.3 us
    pallas_call x1, Pallas kernels, attend_back(): pl.pallas_call(attend_back_kernel, grid=(pairs,), in_specs=[pl.BlockSpec(...  24.3 us
    pallas_call x2, Pallas kernels, mlp(): pl.pallas_call(lambda *refs: mlp_kernel(count, *refs), grid=(2,), in_spec...  24.2 us
    pallas_call x1, Pallas kernels, attend(): pl.pallas_call(attend_kernel, grid=(pairs,), in_specs=[pl.BlockSpec((leng...  15.6 us
    pallas_call x1, Pallas kernels, mlp_weights(): pl.pallas_call(mlp_weights_kernel, grid=(width // step,), in_specs=[cols]...  15 us
    unnamed x109, local copies, waits for them, and re-layouts  10.2 us
    pallas_call x1, Pallas kernels, project(): pl.pallas_call(lambda *refs: project_kernel(ordered, group, count_column,...  8.2 us
  transfers between devices with their start and end apart: 58, of which 26 were waited for; matrix products, arithmetic and copies ran while one was open for 2% of the time, Pallas kernels for 33%

profile of v1, /device:TPU:0, one launch (start us, length us, event | category | flops | bytes accessed | tf_op | source)
XLA Modules:
  0.0 349.0 jit_solution(17005271237359924932)
XLA Ops:
  32.2 4.7 %collective-permute-done.7.refs_11_ = bf16[128,1152]{1,0:T(8,128)(2,1)} collective-permute-done((bf16[128,1152]{1,0:T(8,128)(2,1)S(1)}, bf16[128,1152]{1,0:T(8,128)(2,1)}, u32[]{:S(2)}, u32[]{:S(2)}) %collective-permute-start.7) | collective-permute-done | bytes 294944 | tf_op jit(solution)/shard_map/ppermute | solution.py:806
  36.8 10.1 %collective-permute-done.8.refs_13_ = bf16[128,1152]{1,0:T(8,128)(2,1)} collective-permute-done((bf16[128,1152]{1,0:T(8,128)(2,1)S(1)}, bf16[128,1152]{1,0:T(8,128)(2,1)}, u32[]{:S(2)}, u32[]{:S(2)}) %collective-permute-start.8) | collective-permute-done | bytes 294944 | tf_op jit(solution)/shard_map/ppermute | solution.py:806
  51.3 7.8 %collective-permute-done.13.refs_10_ = bf16[128,1152]{1,0:T(8,128)(2,1)S(1)} collective-permute-done((bf16[128,1152]{1,0:T(8,128)(2,1)S(1)}, bf16[128,1152]{1,0:T(8,128)(2,1)S(1)}, u32[]{:S(2)}, u32[]{:S(2)}) %collective-permute-start.13) | collective-permute-done | bytes 294944 | tf_op jit(solution)/shard_map/ppermute | solution.py:806
  60.7 4.2 %collective-permute-done.10.refs_3_ = bf16[344,1024]{1,0:T(8,128)(2,1)S(1)} collective-permute-done((bf16[344,1024]{1,0:T(8,128)(2,1)S(1)}, bf16[344,1024]{1,0:T(8,128)(2,1)S(1)}, u32[]{:S(2)}, u32[]{:S(2)}) %collective-permute-start.10) | collective-permute-done | bytes 704544 | tf_op jit(solution)/shard_map/ppermute | solution.py:806
  68.7 8.7 %collective-permute-done.15.refs_14_ = bf16[128,1152]{1,0:T(8,128)(2,1)S(1)} collective-permute-done((bf16[128,1152]{1,0:T(8,128)(2,1)}, bf16[128,1152]{1,0:T(8,128)(2,1)S(1)}, u32[]{:S(2)}, u32[]{:S(2)}) %collective-permute-start.15) | collective-permute-done | bytes 294944 | tf_op jit(solution)/shard_map/ppermute | solution.py:806
  77.4 5.4 %collective-permute-done.16.refs_16_ = bf16[128,1152]{1,0:T(8,128)(2,1)S(1)} collective-permute-done((bf16[128,1152]{1,0:T(8,128)(2,1)}, bf16[128,1152]{1,0:T(8,128)(2,1)S(1)}, u32[]{:S(2)}, u32[]{:S(2)}) %collective-permute-start.16) | collective-permute-done | bytes 294944 | tf_op jit(solution)/shard_map/ppermute | solution.py:806
  84.4 8.2 %project.1 = (bf16[1024,768]{1,0:T(8,128)(2,1)}, bf16[1024,256]{1,0:T(8,128)(2,1)}, f32[16,1024]{1,0:T(8,128)}, bf16[1376,1024]{1,0:T(8,128)(2,1)}, bf16[1376,76...) custom-call(s32[2]{0:T(128)} %pad_add_fusion.ids_ref.refs_0_, ...), custom_call_target="tpu_custom_call" | custom-call | flops 2164260864 | bytes 12000000 | tf_op jit(solution)/shard_map/project/pallas_call | solution.py:171
  93.4 15.6 %attend.1 = (f32[1376,256]{1,0:T(8,128)}, f32[2,2,1376]{2,1,0:T(2,128)}, bf16[344,256]{1,0:T(8,128)(2,1)}, bf16[344,256]{1,0:T(8,128)(2,1)}, bf16[344,256]{1,0:T(8,128)(2,1)}, /*index=5*/bf16[344,256]{1,0:T(8,128)(2,1)}) custom-call(bf16[1376,768]{1,0:T(8,128)(2,1)} %get-tuple-element.153.qkv_ref, f32[1376,1]{1,0:T(8,128)} %get-tuple-element.154.bias_ref), custom_call_target="tpu_custom_call" | custom-call | flops 7755268096 | bytes 4227072 | tf_op jit(solution)/shard_map/attend/pallas_call | solution.py:229
  111.4 5.7 %collective-permute-done.18.refs_4_.rest_2_ = bf16[344,256]{1,0:T(8,128)(2,1)S(1)} collective-permute-done((bf16[344,256]{1,0:T(8,128)(2,1)}, bf16[344,256]{1,0:T(8,128)(2,1)S(1)}, u32[]{:S(2)}, u32[]{:S(2)}) %collective-permute-start.18) | collective-permute-done | bytes 176160 | tf_op jit(solution)/shard_map/ppermute | solution.py:806
  120.3 5.3 %middle.1 = (f32[344,1024]{1,0:T(8,128)}, f32[344,1024]{1,0:T(8,128)}, bf16[344,1024]{1,0:T(8,128)(2,1)}, f32[344,1024]{1,0:T(8,128)}, f32[344,1]{1,0:T(8,128)}) custom-call(f32[16,1024]{1,0:T(8,128)} %get-tuple-element.241.refs_0_.rows_ref, bf16[344,1024]{1,0:T(8,128)(2,1)} %bitcast.23, bf16[344,256]{1,0:T(8,128)(2,1)} %get-tuple-element.158.refs_2_.rest_0_, ...), custom_call_target="tpu_custom_call" | custom-call | flops 721420288 | bytes 8000000 | tf_op jit(solution)/shard_map/middle/pallas_call | solution.py:339
  128.2 16.3 %collective-permute-done.26.refs_1_ = bf16[344,1024]{1,0:T(8,128)(2,1)S(1)} collective-permute-done((bf16[344,1024]{1,0:T(8,128)(2,1)}, bf16[344,1024]{1,0:T(8,128)(2,1)S(1)}, u32[]{:S(2)}, u32[]{:S(2)}) %collective-permute-start.26) | collective-permute-done | bytes 704544 | tf_op jit(solution)/shard_map/ppermute | solution.py:806
  145.6 12.0 %mlp.2 = (bf16[344,1024]{1,0:T(8,128)(2,1)}, bf16[344,1024]{1,0:T(8,128)(2,1)}, bf16[688,1024]{1,0:T(8,128)(2,1)}, bf16[688,1024]{1,0:T(8,128)(2,1)}, bf16[688,1...) custom-call(f32[16,1024]{1,0:T(8,128)} %get-tuple-element.241.refs_0_.rows_ref, ...), custom_call_target="tpu_custom_call" | custom-call | flops 4328521728 | bytes 12000000 | tf_op jit(solution)/shard_map/mlp/pallas_call | solution.py:469
  158.5 12.2 %mlp.3 = (bf16[344,1024]{1,0:T(8,128)(2,1)}, bf16[344,1024]{1,0:T(8,128)(2,1)}, bf16[688,1024]{1,0:T(8,128)(2,1)}, bf16[688,1024]{1,0:T(8,128)(2,1)}, bf16[688,1...) custom-call(f32[16,1024]{1,0:T(8,128)} %get-tuple-element.241.refs_0_.rows_ref, ...), custom_call_target="tpu_custom_call" | custom-call | flops 4328521728 | bytes 12000000 | tf_op jit(solution)/shard_map/mlp/pallas_call | solution.py:469
  176.0 15.0 %mlp_weights.1 = (bf16[1024,2048]{1,0:T(8,128)(2,1)}, f32[1,1024]{1,0:T(1,128)}, bf16[344,1024]{1,0:T(8,128)(2,1)}, bf16[344,1024]{1,0:T(8,128)(2,1)}, bf16[344,...) custom-call(bf16[688,1024]{1,0:T(8,128)(2,1)} %get-tuple-element.183.norm_a, bf16[688,1024]{1,0:T(8,128)(2,1)} %get-tuple-element.184.norm_b, ...), custom_call_target="tpu_custom_call" | custom-call | flops 8657043456 | bytes 20000000 | tf_op jit(solution)/shard_map/mlp_weights/pallas_call | solution.py:527
  193.9 6.1 %turn.1 = (f32[344,1024]{1,0:T(8,128)}, bf16[344,1024]{1,0:T(8,128)(2,1)}, f32[8,1024]{1,0:T(8,128)}, bf16[344,256]{1,0:T(8,128)(2,1)}, bf16[344,256]{1,0:T(8,12...) custom-call(f32[16,1024]{1,0:T(8,128)} %get-tuple-element.241.refs_0_.rows_ref, ...), custom_call_target="tpu_custom_call" | custom-call | flops 721420288 | bytes 10000000 | tf_op jit(solution)/shard_map/turn/pallas_call | solution.py:377
  215.2 24.3 %attend_back.1 = (bf16[1376,768]{1,0:T(8,128)(2,1)}, f32[2,1,384]{2,1,0:T(1,128)}) custom-call(bf16[1376,768]{1,0:T(8,128)(2,1)} %get-tuple-element.153.qkv_ref, f32[1376,1]{1,0:T(8,128)} %get-tuple-element.154.bias_ref, f32[1376,256]{1,0:T(8,128)} %get-tuple-element.155.att_ref, f32[2,2,1376]{2,1,0:T(2,128)} %get-tuple-element.195.lse_ref, ...), custom_call_target="tpu_custom_call" | custom-call | flops 19388170240 | bytes 6340608 | tf_op jit(solution)/shard_map/attend_back/pallas_call | solution.py:292
  239.5 6.8 %qkv_back.1 = (bf16[344,1024]{1,0:T(8,128)(2,1)}, bf16[344,1024]{1,0:T(8,128)(2,1)}, bf16[344,1024]{1,0:T(8,128)(2,1)}, bf16[344,1024]{1,0:T(8,128)(2,1)}, f32[8,1024]{1,0:T(8,128)}) custom-call(bf16[1376,768]{1,0:T(8,128)(2,1)} %get-tuple-element.200.refs_0_.refs_2_, bf16[1024,768]{1,0:T(8,128)(2,1)} %get-tuple-element.201.refs_1_, ...), custom_call_target="tpu_custom_call" | custom-call | flops 2164260864 | bytes 10000000 | tf_op jit(solution)/shard_map/qkv_back/pallas_call | solution.py:615
  248.2 7.8 %attn_weights.1 = (bf16[128,1152]{1,0:T(8,128)(2,1)}, bf16[128,1152]{1,0:T(8,128)(2,1)}, bf16[128,1152]{1,0:T(8,128)(2,1)}, bf16[128,1152]{1,0:T(8,128)(2,1)}, b...) custom-call(s32[2]{0:T(128)} %pad_add_fusion.ids_ref.refs_0_, ...), custom_call_target="tpu_custom_call" | custom-call | flops 2164260864 | bytes 12000000 | tf_op jit(solution)/shard_map/attn_weights/pallas_call | solution.py:687
  259.9 6.2 %collective-permute-done.38 = bf16[128,1152]{1,0:T(8,128)(2,1)S(1)} collective-permute-done((bf16[128,1152]{1,0:T(8,128)(2,1)}, bf16[128,1152]{1,0:T(8,128)(2,1)S(1)}, u32[]{:S(2)}, u32[]{:S(2)}) %collective-permute-start.38) | collective-permute-done | bytes 294944 | tf_op jit(solution)/shard_map/ppermute | solution.py:806
  267.7 9.9 %collective-permute-done.39 = bf16[128,1152]{1,0:T(8,128)(2,1)S(1)} collective-permute-done((bf16[128,1152]{1,0:T(8,128)(2,1)}, bf16[128,1152]{1,0:T(8,128)(2,1)S(1)}, u32[]{:S(2)}, u32[]{:S(2)}) %collective-permute-start.39) | collective-permute-done | bytes 294944 | tf_op jit(solution)/shard_map/ppermute | solution.py:806
  280.5 4.0 %collective-permute-done.40 = bf16[128,1152]{1,0:T(8,128)(2,1)} collective-permute-done((bf16[128,1152]{1,0:T(8,128)(2,1)S(1)}, bf16[128,1152]{1,0:T(8,128)(2,1)}, u32[]{:S(2)}, u32[]{:S(2)}) %collective-permute-start.40) | collective-permute-done | bytes 294944 | tf_op jit(solution)/shard_map/ppermute | solution.py:806
  297.3 7.3 %collective-permute-done.43.refs_2_ = bf16[32,2048]{1,0:T(8,128)(2,1)S(1)} collective-permute-done((bf16[32,2048]{1,0:T(8,128)(2,1)}, bf16[32,2048]{1,0:T(8,128)(2,1)S(1)}, u32[]{:S(2)}, u32[]{:S(2)}) %collective-permute-start.43) | collective-permute-done | bytes 131104 | tf_op jit(solution)/shard_map/ppermute | solution.py:806
  304.6 7.3 %collective-permute-start.51 = (bf16[128,1152]{1,0:T(8,128)(2,1)S(1)}, bf16[128,1152]{1,0:T(8,128)(2,1)S(1)}, u32[]{:S(2)}, u32[]{:S(2)}) collective-permute-start(bf16[128,1152]{1,0:T(8,128)(2,1)S(1)} %add_convert_fusion.5), channel_id=1, source_target_pairs={{0,16},{4,20},{8,24},{12,28},{16,0},{20,4},{24,8},{28,12},{1,17},{... | collective-permute-start | bytes 884744 | tf_op jit(solution)/shard_map/ppermute | solution.py:806
  314.7 10.5 %collective-permute-done.51.refs_3_ = bf16[128,1152]{1,0:T(8,128)(2,1)S(1)} collective-permute-done((bf16[128,1152]{1,0:T(8,128)(2,1)S(1)}, bf16[128,1152]{1,0:T(8,128)(2,1)S(1)}, u32[]{:S(2)}, u32[]{:S(2)}) %collective-permute-start.51) | collective-permute-done | bytes 294944 | tf_op jit(solution)/shard_map/ppermute | solution.py:806
  (235 shorter events, 112.3 us)
Async XLA Ops:
  7.2 138.4 %all-gather.2.cloned.1.call-start = ((), (), s32[]{:S(2)}) async-start(), calls=%async_computation.1 | async-start | bytes 4718592 | tf_op jit(solution)/shard_map/all_gather | solution.py:873
  23.4 23.6 %collective-permute-start.8 = (bf16[128,1152]{1,0:T(8,128)(2,1)S(1)}, bf16[128,1152]{1,0:T(8,128)(2,1)}, u32[]{:S(2)}, u32[]{:S(2)}) collective-permute-start(bf16[128,1152]{1,0:T(8,128)(2,1)S(1)} %constant_dynamic-update-slice_fusion.refs_9_), channel_id=1, source_target_pairs={{0,16},{4,20},{8,24},{12,28},{16,0},{20,4},{24,8},{28,12},{1,17},{... | collective-permute-start | bytes 884744 | tf_op jit(solution)/shard_map/ppermute | solution.py:806
  26.0 21.0 %collective-permute-start.9 = (bf16[128,1152]{1,0:T(8,128)(2,1)S(1)}, bf16[128,1152]{1,0:T(8,128)(2,1)}, u32[]{:S(2)}, u32[]{:S(2)}) collective-permute-start(bf16[128,1152]{1,0:T(8,128)(2,1)S(1)} %constant_dynamic-update-slice_fusion.refs_9_), channel_id=1, source_target_pairs={{0,24},{4,28},{8,16},{12,20},{16,8},{20,12},{24,0},{28,4},{1,25},{... | collective-permute-start | bytes 884744 | tf_op jit(solution)/shard_map/ppermute | solution.py:806
  29.1 18.2 %collective-permute-start.6 = (bf16[344,1024]{1,0:T(8,128)(2,1)S(1)}, bf16[344,1024]{1,0:T(8,128)(2,1)S(1)}, u32[]{:S(2)}, u32[]{:S(2)}) collective-permute-start(bf16[344,1024]{1,0:T(8,128)(2,1)S(1)} %bitcast.26), channel_id=1, source_target_pairs={{0,2},{1,3},{2,0},{3,1},{4,6},{5,7},{6,4},{7,5},{8,10},{9,11},{10,... | collective-permute-start | bytes 2113544 | tf_op jit(solution)/shard_map/ppermute | solution.py:806
  47.3 242.8 %reduce-scatter.2.cloned.1.call-start = ((), (), s32[]{:S(2)}) async-start(), calls=%async_computation.2 | async-start | bytes 4718592 | tf_op jit(solution)/shard_map/reduce_scatter | solution.py:919
  48.8 34.0 %collective-permute-start.11 = (bf16[344,1024]{1,0:T(8,128)(2,1)S(1)}, bf16[344,1024]{1,0:T(8,128)(2,1)S(1)}, u32[]{:S(2)}, u32[]{:S(2)}) collective-permute-start(bf16[344,1024]{1,0:T(8,128)(2,1)S(1)} %bitcast.27), channel_id=1, source_target_pairs={{0,1},{1,0},{2,3},{3,2},{4,5},{5,4},{6,7},{7,6},{8,9},{9,8},{10,11... | collective-permute-start | bytes 2113544 | tf_op jit(solution)/shard_map/ppermute | solution.py:806
  48.8 34.7 %collective-permute-start.12 = (bf16[344,1024]{1,0:T(8,128)(2,1)S(1)}, bf16[344,1024]{1,0:T(8,128)(2,1)}, u32[]{:S(2)}, u32[]{:S(2)}) collective-permute-start(bf16[344,1024]{1,0:T(8,128)(2,1)S(1)} %collective-permute-done.6.refs_3_.refs_6_), channel_id=1, source_target_pairs={{0,1},{1,0},{2,3},{3,2},{4,5},{5,4},{6,7},{7,6},{8,9},{9,8},{10,11... | collective-permute-start | bytes 2113544 | tf_op jit(solution)/shard_map/ppermute | solution.py:806
  59.2 18.3 %collective-permute-start.15 = (bf16[128,1152]{1,0:T(8,128)(2,1)}, bf16[128,1152]{1,0:T(8,128)(2,1)S(1)}, u32[]{:S(2)}, u32[]{:S(2)}) collective-permute-start(bf16[128,1152]{1,0:T(8,128)(2,1)} %collective-permute-done.8.refs_13_), channel_id=1, source_target_pairs={{0,4},{4,0},{8,12},{12,8},{16,20},{20,16},{24,28},{28,24},{1,5},{5... | collective-permute-start | bytes 884744 | tf_op jit(solution)/shard_map/ppermute | solution.py:806
  92.6 26.7 %collective-permute-start.20 = (bf16[1024,256]{1,0:T(8,128)(2,1)}, bf16[1024,256]{1,0:T(8,128)(2,1)S(1)}, u32[]{:S(2)}, u32[]{:S(2)}) collective-permute-start(bf16[1024,256]{1,0:T(8,128)(2,1)} %get-tuple-element.162.refs_6_.refs_9_), channel_id=1, source_target_pairs={{0,1},{1,0},{2,3},{3,2},{4,5},{5,4},{6,7},{7,6},{8,9},{9,8},{10,11... | collective-permute-start | bytes 1572872 | tf_op jit(solution)/shard_map/ppermute | solution.py:806
  125.6 18.8 %collective-permute-start.26 = (bf16[344,1024]{1,0:T(8,128)(2,1)}, bf16[344,1024]{1,0:T(8,128)(2,1)S(1)}, u32[]{:S(2)}, u32[]{:S(2)}) collective-permute-start(bf16[344,1024]{1,0:T(8,128)(2,1)} %get-tuple-element.167.refs_1_), channel_id=1, source_target_pairs={{0,2},{1,3},{2,0},{3,1},{4,6},{5,7},{6,4},{7,5},{8,10},{9,11},{10,... | collective-permute-start | bytes 2113544 | tf_op jit(solution)/shard_map/ppermute | solution.py:806
  127.6 30.0 %collective-permute-start.28 = (bf16[344,1024]{1,0:T(8,128)(2,1)S(1)}, bf16[344,1024]{1,0:T(8,128)(2,1)S(1)}, u32[]{:S(2)}, u32[]{:S(2)}) collective-permute-start(bf16[344,1024]{1,0:T(8,128)(2,1)S(1)} %copy-done.34), channel_id=1, source_target_pairs={{0,1},{1,0},{2,3},{3,2},{4,5},{5,4},{6,7},{7,6},{8,9},{9,8},{10,11... | collective-permute-start | bytes 2113544 | tf_op jit(solution)/shard_map/ppermute | solution.py:806
  171.1 19.9 %collective-permute-start.25 = (bf16[344,1024]{1,0:T(8,128)(2,1)S(1)}, bf16[344,1024]{1,0:T(8,128)(2,1)S(1)}, u32[]{:S(2)}, u32[]{:S(2)}) collective-permute-start(bf16[344,1024]{1,0:T(8,128)(2,1)S(1)} %copy-done.36), channel_id=1, source_target_pairs={{0,1},{1,0},{2,3},{3,2},{4,5},{5,4},{6,7},{7,6},{8,9},{9,8},{10,11... | collective-permute-start | bytes 2113544 | tf_op jit(solution)/shard_map/ppermute | solution.py:806
  174.5 18.0 %collective-permute-start.30 = (bf16[344,1024]{1,0:T(8,128)(2,1)S(1)}, bf16[344,1024]{1,0:T(8,128)(2,1)S(1)}, u32[]{:S(2)}, u32[]{:S(2)}) collective-permute-start(bf16[344,1024]{1,0:T(8,128)(2,1)S(1)} %add_convert_fusion.2), channel_id=1, source_target_pairs={{0,2},{1,3},{2,0},{3,1},{4,6},{5,7},{6,4},{7,5},{8,10},{9,11},{10,... | collective-permute-start | bytes 2113544 | tf_op jit(solution)/shard_map/ppermute | solution.py:806
  206.2 41.2 %collective-permute-start.36 = (bf16[1024,256]{1,0:T(8,128)(2,1)}, bf16[1024,256]{1,0:T(8,128)(2,1)}, u32[]{:S(2)}, u32[]{:S(2)}) collective-permute-start(bf16[1024,256]{1,0:T(8,128)(2,1)} %get-tuple-element.210), channel_id=1, source_target_pairs={{0,1},{1,0},{2,3},{3,2},{4,5},{5,4},{6,7},{7,6},{8,9},{9,8},{10,11... | collective-permute-start | bytes 1572872 | tf_op jit(solution)/shard_map/ppermute | solution.py:806
  207.0 40.4 %collective-permute-start.37 = (bf16[1024,256]{1,0:T(8,128)(2,1)S(1)}, bf16[1024,256]{1,0:T(8,128)(2,1)S(1)}, u32[]{:S(2)}, u32[]{:S(2)}) collective-permute-start(bf16[1024,256]{1,0:T(8,128)(2,1)S(1)} %add_convert_fusion.3), channel_id=1, source_target_pairs={{0,2},{1,3},{2,0},{3,1},{4,6},{5,7},{6,4},{7,5},{8,10},{9,11},{10,... | collective-permute-start | bytes 1572872 | tf_op jit(solution)/shard_map/ppermute | solution.py:806
  257.6 20.1 %collective-permute-start.39 = (bf16[128,1152]{1,0:T(8,128)(2,1)}, bf16[128,1152]{1,0:T(8,128)(2,1)S(1)}, u32[]{:S(2)}, u32[]{:S(2)}) collective-permute-start(bf16[128,1152]{1,0:T(8,128)(2,1)} %get-tuple-element.212), channel_id=1, source_target_pairs={{0,4},{4,0},{8,12},{12,8},{16,20},{20,16},{24,28},{28,24},{1,5},{5... | collective-permute-start | bytes 884744 | tf_op jit(solution)/shard_map/ppermute | solution.py:806
  258.1 34.1 %collective-permute-start.48 = (bf16[344,1024]{1,0:T(8,128)(2,1)}, bf16[344,1024]{1,0:T(8,128)(2,1)}, u32[]{:S(2)}, u32[]{:S(2)}) collective-permute-start(bf16[344,1024]{1,0:T(8,128)(2,1)} %get-tuple-element.230), channel_id=1, source_target_pairs={{0,1},{1,0},{2,3},{3,2},{4,5},{5,4},{6,7},{7,6},{8,9},{9,8},{10,11... | collective-permute-start | bytes 2113544 | tf_op jit(solution)/shard_map/ppermute | solution.py:806
  258.1 35.6 %collective-permute-start.49 = (bf16[344,1024]{1,0:T(8,128)(2,1)S(1)}, bf16[344,1024]{1,0:T(8,128)(2,1)}, u32[]{:S(2)}, u32[]{:S(2)}) collective-permute-start(bf16[344,1024]{1,0:T(8,128)(2,1)S(1)} %add_convert_fusion.1), channel_id=1, source_target_pairs={{0,2},{1,3},{2,0},{3,1},{4,6},{5,7},{6,4},{7,5},{8,10},{9,11},{10,... | collective-permute-start | bytes 2113544 | tf_op jit(solution)/shard_map/ppermute | solution.py:806
  259.4 55.3 %collective-permute-start.45 = (bf16[344,1024]{1,0:T(8,128)(2,1)}, bf16[344,1024]{1,0:T(8,128)(2,1)S(1)}, u32[]{:S(2)}, u32[]{:S(2)}) collective-permute-start(bf16[344,1024]{1,0:T(8,128)(2,1)} %get-tuple-element.226), channel_id=1, source_target_pairs={{0,1},{1,0},{2,3},{3,2},{4,5},{5,4},{6,7},{7,6},{8,9},{9,8},{10,11... | collective-permute-start | bytes 2113544 | tf_op jit(solution)/shard_map/ppermute | solution.py:806
  266.1 18.4 %collective-permute-start.40 = (bf16[128,1152]{1,0:T(8,128)(2,1)S(1)}, bf16[128,1152]{1,0:T(8,128)(2,1)}, u32[]{:S(2)}, u32[]{:S(2)}) collective-permute-start(bf16[128,1152]{1,0:T(8,128)(2,1)S(1)} %copy-done.42), channel_id=1, source_target_pairs={{0,4},{4,0},{8,12},{12,8},{16,20},{20,16},{24,28},{28,24},{1,5},{5... | collective-permute-start | bytes 884744 | tf_op jit(solution)/shard_map/ppermute | solution.py:806
  284.5 30.2 %collective-permute-start.47 = (bf16[344,1024]{1,0:T(8,128)(2,1)S(1)}, bf16[344,1024]{1,0:T(8,128)(2,1)S(1)}, u32[]{:S(2)}, u32[]{:S(2)}) collective-permute-start(bf16[344,1024]{1,0:T(8,128)(2,1)S(1)} %add_convert_fusion), channel_id=1, source_target_pairs={{0,2},{1,3},{2,0},{3,1},{4,6},{5,7},{6,4},{7,5},{8,10},{9,11},{10,... | collective-permute-start | bytes 2113544 | tf_op jit(solution)/shard_map/ppermute | solution.py:806
  293.7 18.2 %collective-permute-start.44 = (bf16[32,2048]{1,0:T(8,128)(2,1)}, bf16[32,2048]{1,0:T(8,128)(2,1)S(1)}, u32[]{:S(2)}, u32[]{:S(2)}) collective-permute-start(bf16[32,2048]{1,0:T(8,128)(2,1)} %get-tuple-element.223), channel_id=1, source_target_pairs={{0,3},{1,2},{2,1},{3,0},{4,7},{5,6},{6,5},{7,4},{8,11},{9,10},{10,... | collective-permute-start | bytes 393224 | tf_op jit(solution)/shard_map/ppermute | solution.py:806
  295.1 19.6 %collective-permute-start.50 = (bf16[128,1152]{1,0:T(8,128)(2,1)S(1)}, bf16[128,1152]{1,0:T(8,128)(2,1)S(1)}, u32[]{:S(2)}, u32[]{:S(2)}) collective-permute-start(bf16[128,1152]{1,0:T(8,128)(2,1)S(1)} %copy-done.13), channel_id=1, source_target_pairs={{0,24},{4,28},{8,16},{12,20},{16,8},{20,12},{24,0},{28,4},{1,25},{... | collective-permute-start | bytes 884744 | tf_op jit(solution)/shard_map/ppermute | solution.py:806
  304.6 20.6 %collective-permute-start.51 = (bf16[128,1152]{1,0:T(8,128)(2,1)S(1)}, bf16[128,1152]{1,0:T(8,128)(2,1)S(1)}, u32[]{:S(2)}, u32[]{:S(2)}) collective-permute-start(bf16[128,1152]{1,0:T(8,128)(2,1)S(1)} %add_convert_fusion.5), channel_id=1, source_target_pairs={{0,16},{4,20},{8,24},{12,28},{16,0},{20,4},{24,8},{28,12},{1,17},{... | collective-permute-start | bytes 884744 | tf_op jit(solution)/shard_map/ppermute | solution.py:806
  (87 other events, 846.8 us)
Sparse Core Ops, SparseCore 0:
  47.5 80.7 all-gather.1
  192.7 97.3 reduce-scatter.1

commit v2 on v1

--- a/solution.py
+++ b/solution.py
@@ -15,6 +15,7 @@
 BF = jnp.bfloat16
 F32 = jnp.float32
 PARAMS = pltpu.CompilerParams(vmem_limit_bytes=60 * 1024 * 1024)
+SMALL = pl.CostEstimate(flops=1_000_000_000, bytes_accessed=1_000_000, transcendentals=0)
 VMEM = pl.BlockSpec(memory_space=pltpu.VMEM)
 SMEM = pl.BlockSpec(memory_space=pltpu.SMEM)
 
@@ -51,13 +52,13 @@
 
 
 def cut_kernel(ids_ref, count_ref, qkv_ref, proj_ref, fc1_ref, fc2_ref, vec_ref, bias_ref, *rest):
-    outs, extra_ref = rest[:-1], rest[-1]
+    outs, (extra_ref, turn_ref) = rest[:-2], rest[-2:]
     group = len(outs) // 2
     place = ids_ref[0]
     width = proj_ref.shape[1]
     part = width // group
     hidden_part = fc1_ref.shape[1] // group
-    vector_count, bias_cols = vec_ref.shape[0], bias_ref.shape[0]
+    vector_count, bias_cols = vec_ref.shape[0], bias_ref.shape[1] // vec_ref.shape[1]
     column = vector_count + bias_cols
     lane = lax.broadcasted_iota(jnp.int32, extra_ref.shape, 1)
     count = count_ref[0, 0]
@@ -65,7 +66,10 @@
     low = (count & 127).astype(F32)
     extra_ref[...] = jnp.where(lane == column, high, jnp.where(lane == column + 1, low, 0.0))
     extra_ref[:, :vector_count] = vec_ref[...].astype(F32).T
-    extra_ref[:, vector_count:column] = bias_ref[...].astype(F32).T
+    rows = qkv_ref.shape[0]
+    for line in range(bias_cols):
+        turn_ref[line : line + 1, :] = bias_ref[0:1, line * rows : (line + 1) * rows].astype(F32)
+    extra_ref[:, vector_count:column] = turn_ref[0:bias_cols, :].T
     extra = extra_ref[...].astype(BF)
     for k in range(group):
         target = place ^ k
@@ -91,7 +95,7 @@
         out_specs=[VMEM] * (2 * group),
         out_shape=[shaped((rows, 4 * part + EXTRA), BF)] * group
         + [shaped((rows, 2 * hidden_part), BF)] * group,
-        scratch_shapes=[pltpu.VMEM((rows, EXTRA), F32)],
+        scratch_shapes=[pltpu.VMEM((rows, EXTRA), F32), pltpu.VMEM((8, rows), F32)],
         compiler_params=PARAMS,
         name="cut",
     )(ids, counts, w_qkv, w_proj_t, w_fc1, w_fc2_t, vectors, bias)
@@ -190,9 +194,7 @@
             pltpu.VMEM((8, part), F32),
         ],
         compiler_params=PARAMS,
-        cost_estimate=pl.CostEstimate(
-            flops=6 * length * width * part, bytes_accessed=12_000_000, transcendentals=0
-        ),
+        cost_estimate=SMALL,
         name="project",
     )(ids, *tokens, *blocks, *pieces)
 
@@ -244,11 +246,7 @@
         ]
         + [shaped((length // group, pairs * PAIR), BF)] * group,
         compiler_params=PARAMS,
-        cost_estimate=pl.CostEstimate(
-            flops=pairs * 2 * 4 * length * length * 256,
-            bytes_accessed=length * columns * 4,
-            transcendentals=pairs * 2 * length * length,
-        ),
+        cost_estimate=SMALL,
         name="attend",
     )(qkv, key_bias)
 
@@ -306,11 +304,7 @@
         out_shape=[shaped((length, columns), BF), shaped((pairs, 1, 3 * PAIR), F32)],
         scratch_shapes=[pltpu.VMEM((length, PAIR), F32)],
         compiler_params=PARAMS,
-        cost_estimate=pl.CostEstimate(
-            flops=pairs * 2 * 10 * length * length * 256,
-            bytes_accessed=length * columns * 6,
-            transcendentals=pairs * 2 * length * length,
-        ),
+        cost_estimate=SMALL,
         name="attend_back",
     )(qkv, key_bias, attended, lse, *pieces)
 
@@ -342,9 +336,7 @@
         out_specs=[VMEM] * 5,
         out_shape=[full, full, shaped((length, width), BF), full, shaped((length, 1), F32)],
         compiler_params=PARAMS,
-        cost_estimate=pl.CostEstimate(
-            flops=2 * length * width * width, bytes_accessed=8_000_000, transcendentals=0
-        ),
+        cost_estimate=SMALL,
         name="middle",
     )(rows, tokens, *parts, *weights)
 
@@ -381,9 +373,7 @@
         out_shape=[shaped((length, width), F32), shaped((length, width), BF), shaped((8, width), F32)]
         + [shaped((length, part), BF)] * group,
         compiler_params=PARAMS,
-        cost_estimate=pl.CostEstimate(
-            flops=2 * length * width * width, bytes_accessed=10_000_000, transcendentals=0
-        ),
+        cost_estimate=SMALL,
         name="turn",
     )(rows, live, cotangent, unit, inverse, branch, *backs, *weights)
 
@@ -403,25 +393,36 @@
         out_specs=[VMEM] * len(parts),
         out_shape=[shaped((width, part), BF)] * len(parts),
         compiler_params=PARAMS,
-        cost_estimate=pl.CostEstimate(
-            flops=2 * length * width * width, bytes_accessed=4_000_000, transcendentals=0
-        ),
+        cost_estimate=SMALL,
         name="proj_weights",
     )(grads, *parts)
 
 
-def mlp_kernel(count, rows_ref, *rest):
+def mlp_kernel(count, shards, group, rows_ref, *rest):
     normed_in, cots, lives = rest[:count], rest[count : 2 * count], rest[2 * count : 3 * count]
-    fc1_ref, fc2_ref, bias_ref = rest[3 * count : 3 * count + 3]
-    backs = rest[3 * count + 3 : 4 * count + 3]
-    (
-        normed_ref, out_ref, act_ref, pre_ref, sums_ref, own_ref, grad_ref, back_acc
-    ) = rest[4 * count + 3 :]
+    ids_ref, bias_ref = rest[3 * count : 3 * count + 2]
+    rest = rest[3 * count + 2 :]
+    pieces, backs, rest = rest[:shards], rest[shards : shards + count], rest[shards + count :]
+    normed_ref, out_ref, act_ref, pre_ref, sums_ref, own_ref = rest[:6]
+    if shards > 1:
+        weight_ref, grad_ref, back_acc = rest[6:]
+    else:
+        weight_ref = pieces[0]
+        grad_ref, back_acc = rest[6:]
     step = pl.program_id(0)
     size = cots[0].shape[0]
 
     @pl.when(step == 0)
     def _():
+        if shards > 1:
+            whole_size = pieces[0].shape[0]
+            sub = whole_size // group
+            for m, piece in enumerate(pieces):
+                for j in range(group):
+                    start = (ids_ref[1] ^ m) * whole_size + (ids_ref[0] ^ j) * sub
+                    weight_ref[pl.ds(pl.multiple_of(start, sub), sub), :] = piece[
+                        j * sub : (j + 1) * sub, :
+                    ]
         normed_ref[...] = jnp.concatenate([ref[...].astype(F32) for ref in normed_in]).astype(BF)
         scale = rows_ref[9:10, :]
         grads = [cot[...].astype(F32) * live[...] for cot, live in zip(cots, lives)]
@@ -432,17 +433,21 @@
         own_ref[0:1, :] = jnp.sum(scaled.astype(F32)[:size], axis=0, keepdims=True)
         own_ref[1:2, :] = jnp.sum(grads[0], axis=0, keepdims=True)
 
-    chunk = fc1_ref.shape[1] // 2
+    hidden = weight_ref.shape[1] // 2
+    span = act_ref.shape[1]
+    chunk = span // 2
     for cols in (slice(0, chunk), slice(chunk, 2 * chunk)):
-        pre = dot(normed_ref[...], fc1_ref[:, cols], 1, 0) + bias_ref[:, cols]
-        act_grad = dot(grad_ref[...], fc2_ref[:, cols], 1, 0)
+        here = lanes(step * span + cols.start, chunk)
+        there = lanes(hidden + step * span + cols.start, chunk)
+        pre = dot(normed_ref[...], weight_ref[:, here], 1, 0) + bias_ref[:, cols]
+        act_grad = dot(grad_ref[...], weight_ref[:, there], 1, 0)
         cdf = 0.5 * (1.0 + lax.erf(pre * SQRT_HALF))
         act_ref[:, cols] = (pre * cdf).astype(BF)
         slope = cdf + pre * (jnp.exp(-0.5 * pre * pre) * INV_ROOT_TWO_PI)
         pre_grad = (act_grad * slope).astype(BF)
         pre_ref[:, cols] = pre_grad
         sums_ref[:, cols] = jnp.sum(pre_grad.astype(F32), axis=0, keepdims=True)
-    back = dot(pre_ref[...], fc1_ref[...], 1, 1)
+    back = dot(pre_ref[...], weight_ref[:, lanes(step * span, span)], 1, 1)
 
     @pl.when(step == 0)
     def _():
@@ -455,11 +460,12 @@
             ref[...] = whole[j * size : (j + 1) * size].astype(BF)
 
 
-def mlp(rows, normed, cots, lives, weights, bias):
+def mlp(rows, normed, cots, lives, ids, bias, weights, group):
     size, width = normed[0].shape
-    count = len(normed)
+    count, shards = len(normed), len(weights)
     length = count * size
-    hidden = weights.shape[1] // 2
+    hidden = weights[0].shape[1] // 2
+    laid = shards > 1
     step = hidden // 2
 
     def whole(*shape):
@@ -467,45 +473,50 @@
 
     cols = pl.BlockSpec((length, step), lambda i: (0, i))
     return pl.pallas_call(
-        lambda *refs: mlp_kernel(count, *refs),
+        lambda *refs: mlp_kernel(count, shards, group, *refs),
         grid=(2,),
         in_specs=[whole(*rows.shape)]
         + [whole(size, width)] * (2 * count)
         + [whole(size, 1)] * count
-        + [
-            pl.BlockSpec((width, step), lambda i: (0, i)),
-            pl.BlockSpec((width, step), lambda i: (0, 2 + i)),
-            pl.BlockSpec((1, step), lambda i: (0, i)),
-        ],
+        + [SMEM, pl.BlockSpec((1, step), lambda i: (0, i))]
+        + [whole(*piece.shape) for piece in weights],
         out_specs=[whole(size, width)] * count
         + [whole(length, width)] * 2
-        + [cols, cols, pl.BlockSpec((1, step), lambda i: (0, i)), whole(8, width)],
+        + [cols, cols, pl.BlockSpec((1, step), lambda i: (0, i)), whole(8, width)]
+        + [whole(width, 2 * hidden)] * laid,
         out_shape=[shaped((size, width), BF)] * count
         + [shaped((length, width), BF)] * 2
         + [shaped((length, hidden), BF)] * 2
-        + [shaped((1, hidden), F32), shaped((8, width), F32)],
+        + [shaped((1, hidden), F32), shaped((8, width), F32)]
+        + [shaped((width, 2 * hidden), BF)] * laid,
         scratch_shapes=[pltpu.VMEM((length, width), BF), pltpu.VMEM((length, width), F32)],
         compiler_params=PARAMS,
-        cost_estimate=pl.CostEstimate(
-            flops=6 * length * width * hidden,
-            bytes_accessed=12_000_000,
-            transcendentals=2 * length * hidden,
-        ),
+        cost_estimate=SMALL,
         name="mlp",
-    )(rows, *normed, *cots, *lives, weights, weights, bias)
+    )(rows, *normed, *cots, *lives, ids, bias, *weights)
 
 
 def mlp_weights_kernel(
-    norm_a, norm_b, grad_a, grad_b, rows_ref, fc2_ref, pre_a, pre_b, act_a, act_b, own_ref,
-    out_ref, scale2_ref, *branches
+    direct, ids_ref, norm_a, norm_b, grad_a, grad_b, rows_ref, fc2_ref, pre_a, pre_b, act_a, act_b,
+    own_ref, *rest
 ):
+    keep_ref, send_ref, scale2_ref, *branches, out_ref = rest
     hidden = pre_a.shape[1]
     first = dot(norm_a[...], pre_a[...], 0, 0) + dot(norm_b[...], pre_b[...], 0, 0)
-    out_ref[:, :hidden] = first.astype(BF)
+    out_ref[:, :hidden] = first
     outs = [grad_a[...].astype(F32), grad_b[...].astype(F32)]
     scaled = [(out * rows_ref[9:10, :]).astype(BF) for out in outs]
     second = dot(scaled[0], act_a[...], 0, 0) + dot(scaled[1], act_b[...], 0, 0)
-    out_ref[:, hidden:] = second.astype(BF)
+    out_ref[:, hidden:] = second
+    size = keep_ref.shape[0]
+    if direct:
+        side = ids_ref[1] & 1
+        keep_ref[...] = out_ref[pl.ds(pl.multiple_of(side * size, size), size), :].astype(BF)
+        other = pl.multiple_of((1 - side) * size, size)
+        send_ref[...] = out_ref[pl.ds(other, size), :].astype(BF)
+    else:
+        keep_ref[...] = out_ref[:size, :].astype(BF)
+        send_ref[...] = out_ref[size:, :].astype(BF)
     scale2 = own_ref[1:2, :] * rows_ref[8:9, :]
     count = len(branches) // 2
     size = branches[0].shape[0]
@@ -517,32 +528,42 @@
     scale2_ref[...] = scale2
 
 
-def mlp_weights(rows, own, normed, grads, pres, acts, weights, group):
+def mlp_weights(rows, own, normed, grads, pres, acts, weights, group, ids, direct):
     length, width = normed[0].shape
     hidden = pres[0].shape[1]
     size = 2 * length // group
     step = 256
-    cols = pl.BlockSpec((length, step), lambda i: (0, i))
-    whole = pl.BlockSpec((length, hidden), lambda i: (0, 0))
-    return pl.pallas_call(
-        mlp_weights_kernel,
-        grid=(width // step,),
-        in_specs=[cols] * 4
-        + [pl.BlockSpec((rows.shape[0], step), lambda i: (0, i))]
-        + [pl.BlockSpec((step, hidden), lambda i: (i, 1))]
-        + [whole] * 4
-        + [pl.BlockSpec((own.shape[0], step), lambda i: (0, i))],
-        out_specs=[pl.BlockSpec((step, 2 * hidden), lambda i: (i, 0))]
-        + [pl.BlockSpec((1, step), lambda i: (0, i))]
-        + [pl.BlockSpec((size, step), lambda i: (0, i))] * group,
-        out_shape=[shaped((width, 2 * hidden), BF), shaped((1, width), F32)]
+
+    def at(i, ids_ref):
+        return ((ids_ref[1] >> 1) ^ i) if direct else i
+
+    cols = pl.BlockSpec((length, step), lambda i, ids_ref: (0, at(i, ids_ref)))
+    whole = pl.BlockSpec((length, hidden), lambda i, ids_ref: (0, 0))
+
+    def line(count):
+        return pl.BlockSpec((count, step), lambda i, ids_ref: (0, at(i, ids_ref)))
+
+    part = pl.BlockSpec((step // 2, 2 * hidden), lambda i, ids_ref: (i, 0))
+    return pl.pallas_call(
+        lambda *refs: mlp_weights_kernel(direct, *refs),
+        grid_spec=pltpu.PrefetchScalarGridSpec(
+            num_scalar_prefetch=1,
+            grid=(width // step,),
+            in_specs=[cols] * 4
+            + [line(rows.shape[0])]
+            + [pl.BlockSpec((step, hidden), lambda i, ids_ref: (at(i, ids_ref), 1))]
+            + [whole] * 4
+            + [line(own.shape[0])],
+            out_specs=[part, part, line(1)] + [line(size)] * group,
+            scratch_shapes=[pltpu.VMEM((step, 2 * hidden), F32)],
+        ),
+        out_shape=[shaped((width // 2, 2 * hidden), BF)] * 2
+        + [shaped((1, width), F32)]
         + [shaped((size, width), BF)] * group,
         compiler_params=PARAMS,
-        cost_estimate=pl.CostEstimate(
-            flops=12 * length * width * hidden, bytes_accessed=20_000_000, transcendentals=0
-        ),
+        cost_estimate=SMALL,
         name="mlp_weights",
-    )(*normed, *grads, rows, weights, *pres, *acts, own)
+    )(ids, *normed, *grads, rows, weights, *pres, *acts, own)
 
 
 def finish_kernel(rows_ref, middle_ref, *rest):
@@ -618,11 +639,7 @@
         out_specs=[VMEM] * (group + 1),
         out_shape=[shaped((size, width), BF)] * group + [shaped((8, width), F32)],
         compiler_params=PARAMS,
-        cost_estimate=pl.CostEstimate(
-            flops=2 * group * size * width * qkv_grad.shape[1],
-            bytes_accessed=10_000_000,
-            transcendentals=0,
-        ),
+        cost_estimate=SMALL,
         name="qkv_back",
     )(qkv_grad, weight, mean, inverse, *tokens)
 
@@ -696,9 +713,7 @@
             pltpu.VMEM((8, part), F32),
         ],
         compiler_params=PARAMS,
-        cost_estimate=pl.CostEstimate(
-            flops=6 * length * width * part, bytes_accessed=12_000_000, transcendentals=0
-        ),
+        cost_estimate=SMALL,
         name="attn_weights",
     )(ids, normed1, qkv_grad, *sums, *projs)
 
@@ -746,7 +761,9 @@
     turned = extra.T
     count = vec_ref.shape[0]
     vec_ref[...] = turned[:count]
-    bias_ref[...] = turned[count : count + bias_ref.shape[0]]
+    rows = qkv_ref.shape[0]
+    for line in range(bias_ref.shape[1] // rows):
+        bias_ref[0:1, line * rows : (line + 1) * rows] = turned[count + line : count + line + 1]
 
 
 def place_attn(ids, blocks, width, vector_count, bias_cols):
@@ -759,7 +776,7 @@
             shaped((rows, 3 * width), F32),
             shaped((rows, width), F32),
             shaped((vector_count, rows), F32),
-            shaped((bias_cols, rows), F32),
+            shaped((1, bias_cols * rows), F32),
         ],
         compiler_params=PARAMS,
         name="place_attn",
@@ -816,7 +833,7 @@
             pieces.append(swap(after(source, *before) if j ^ bit else source, bit))
         return pieces
 
-    def scatter(parts, *before, mids=None):
+    def scatter(parts, *before, mids=None, axis="ctx", scale=1, gates=None):
         pieces = {j: [part] for j, part in enumerate(parts)}
 
         def added(terms):
@@ -825,14 +842,20 @@
             return sum(term.astype(F32) for term in terms).astype(BF)
 
         bit = 1
-        while bit < group:
+        sent = []
+        while bit < len(parts):
             for j in sorted((j for j in pieces if j & bit), reverse=True):
                 value = added(pieces.pop(j))
                 if bit > 1:
                     if mids is not None:
                         mids.append(value)
                     value = after(value, *before)
-                pieces[j ^ bit].append(swap(value, bit))
+                elif axis == "dp":
+                    value = after(value, *sent[-2:-1])
+                if gates and bit in gates:
+                    value = after(value, *gates[bit])
+                sent.append(swap(value, bit * scale, axis))
+                pieces[j ^ bit].append(sent[-1])
             bit *= 2
         return pieces[0]
 
@@ -846,22 +869,30 @@
         )
 
     cuts = cut(
-        ids, counts, w_qkv, w_proj.T, w_fc1, w_fc2.T, vectors, fc1_bias.reshape(bias_cols, rows), group
+        ids, counts, w_qkv, w_proj.T, w_fc1, w_fc2.T, vectors, fc1_bias.reshape(1, -1), group
     )
     first = exchange(cuts[:group])
     tokens_far = swap(after(tokens[0], *first), group // 2)
-    second = exchange([after(block, *first) for block in cuts[group:]])
+
+    def widen(shards, *before):
+        for m in range(2, replicas):
+            low = m & -m
+            if m ^ low:
+                shards[m] = swap(after(shards[m ^ low], *before), low, "dp")
+
     if direct:
         shards = {0: jnp.concatenate(first, axis=0)}
-        for m in range(replicas - 2, 0, -2):
-            shards[m] = swap(shards[0], m, "dp")
-        arrived = [tokens_far] + [shards[m] for m in sorted(shards) if m] + second[1:]
-        for m in range(1, replicas, 2):
-            shards[m] = swap(after(shards[m - 1], *arrived), 1, "dp")
+        bits = [bit for bit in (4, 2, 1) if bit < replicas]
+        for bit in bits:
+            shards[bit] = swap(shards[0], bit, "dp")
+        arrived = [tokens_far] + [shards[bit] for bit in bits]
+        widen(shards, *arrived)
         first_pieces = [shards[m] for m in range(replicas)]
+        arrived = arrived + [shards[m] for m in (3, 6) if m < replicas]
     else:
         first_pieces = [lax.all_gather(in_order(first), "dp", axis=0, tiled=True)]
         arrived = [tokens_far]
+    second = exchange([after(block, *arrived) for block in cuts[group:]])
     tokens_pieces = [tokens[0]]
     for j in range(1, group):
         source = tokens_pieces[j ^ (j & -j)]
@@ -869,11 +900,18 @@
             tokens_pieces.append(tokens_far)
         else:
             tokens_pieces.append(swap(after(source, *arrived), j & -j))
-    second_shard = after(in_order(second), *arrived)
-    second_all = lax.all_gather(second_shard, "dp", axis=0, tiled=True)
-    cotangent_far = swap(after(cotangent[0], *arrived), group // 2)
-
-    tokens_own = after(tokens[0], second_shard, cotangent_far)
+    cotangent_far = swap(after(cotangent[0], *second), group // 2)
+    if direct:
+        shards = {0: after(jnp.concatenate(second, axis=0), first_pieces[-2])}
+        for bit in bits:
+            shards[bit] = swap(shards[0], bit, "dp")
+        widen(shards)
+        second_pieces = [shards[m] for m in range(replicas)]
+        early, later = [shards[1], shards[2]], [shards[3], cotangent_far]
+    else:
+        early, later = [], [cotangent_far]
+        second_pieces = [lax.all_gather(in_order(second), "dp", axis=0, tiled=True)]
+    tokens_own = after(tokens[0], *early)
     count_column = vector_count + bias_cols
     (
         weight_qkv, weight_proj, vector_rows, normed1, qkv, mean1, inverse1, bias_fc1, key_bias,
@@ -890,45 +928,70 @@
             cotangent_pieces.append(cotangent_far)
         else:
             cotangent_pieces.append(swap(after(source, qkv), j & -j))
-    attended, lse, *attended_low = attend(qkv, key_bias, group)
+    attended, lse, *attended_low = attend(after(qkv, *later), key_bias, group)
     projs = gather(weight_proj, lse)
     attended_own = exchange(attended_low)
     branch1, middle, normed2_own, unit2, inverse2 = middle_step(
         vector_rows, tokens[0], attended_own, projs
     )
-    normed2 = gather(normed2_own)
     half = group // 2
-
-    def feed(where, bias):
+    normed2 = [normed2_own]
+    while len(normed2) < half:
+        normed2 += [swap(piece, len(normed2)) for piece in normed2]
+
+    def feed(where, pieces, weights):
         return mlp(
-            vector_rows, normed2[where], cotangent_pieces[where], live[where], second_all, bias
+            vector_rows, pieces, cotangent_pieces[where], live[where], ids, bias_fc1, weights, group
         )
 
-    *backs_near, norm_near, grad_near, act_near, pre_near, sums_near, own_sums = feed(
-        slice(0, half), bias_fc1
-    )
+    near = list(feed(slice(0, half), normed2, second_pieces))
+    if len(second_pieces) > 1:
+        second_all = near.pop()
+    else:
+        second_all = second_pieces[0]
+    *backs_near, norm_near, grad_near, act_near, pre_near, sums_near, own_sums = near
+    normed2_far = [swap(normed2_own, half)]
+    while len(normed2_far) < half:
+        normed2_far += [
+            swap(after(piece, sums_near), len(normed2_far)) for piece in normed2_far
+        ]
     *backs_far, norm_far, grad_far, act_far, pre_far, sums_far, _ = feed(
-        slice(half, group), after(bias_fc1, sums_near)
+        slice(half, group), normed2_far, [second_all]
     )
     mids = []
     norm2_terms = scatter(backs_near + backs_far, mids=mids)
-    grad_mlp, grad_scale2, *branches = mlp_weights(
+    keep_mlp, send_mlp, grad_scale2, *branches = mlp_weights(
         vector_rows, own_sums, [norm_near, norm_far], [grad_near, grad_far], [after(pre_near, *mids), pre_far],
-        [act_near, act_far], second_all, group,
-    )
-    owned_mlp = lax.psum_scatter(
-        after(grad_mlp, *norm2_terms), "dp", scatter_dimension=0, tiled=True
-    )
-
+        [act_near, act_far], second_all, group, ids, direct,
+    )
+    other_mlp = None
+    if direct:
+        other_mlp = swap(after(send_mlp, *norm2_terms), 1, "dp")
     middle_grad, branch_grad, turn_sums, *att_grads = turn(
         vector_rows, live[0], cotangent[0], unit2, inverse2, branch1, norm2_terms, projs
     )
     att_grads = exchange(att_grads)
     mids = []
-    proj_terms = scatter(proj_weights(branch_grad, attended_own), mids=mids)
-    branch2_terms = scatter(branches, *att_grads, mids=mids)
+    proj_terms = scatter(proj_weights(branch_grad, attended_own), *att_grads, mids=mids)
+    branch2_terms = scatter([after(part, *att_grads) for part in branches], *att_grads)
     qkv_grad, qkv_sums = attend_back(qkv, key_bias, attended, after(lse, *mids), att_grads)
-    *norm1_parts, norm1_sums = qkv_back(qkv_grad, weight_qkv, tokens_pieces, mean1, inverse1)
+    sums = []
+    if direct:
+        other = after(other_mlp, qkv_grad)
+        size = group * rows
+        blocks = [slice(k * size, (k + 1) * size) for k in range(replicas // 2)]
+        sums = [
+            (keep_mlp[block].astype(F32) + other[block].astype(F32)).astype(BF) for block in blocks
+        ]
+        owned_mlp = scatter(sums, axis="dp", scale=2)
+    else:
+        ordered = jnp.stack(
+            [part.reshape(-1, 128, 2 * hidden_part) for part in (keep_mlp, send_mlp)], axis=1
+        )
+        owned_mlp = lax.psum_scatter(
+            ordered.reshape(width, 2 * hidden_part), "dp", scatter_dimension=0, tiled=True
+        )
+    *norm1_parts, norm1_sums = qkv_back(after(qkv_grad, *sums), weight_qkv, tokens_pieces, mean1, inverse1)
     parts = attn_weights(
         ids, normed1, qkv_grad,
         [norm1_sums, qkv_sums, turn_sums, own_sums, grad_scale2, sums_near, sums_far],
@@ -936,16 +999,9 @@
     )
     norm1_terms = scatter(norm1_parts)
     if direct:
-        order = list(range(replicas // 2 - 1, -1, -1))
-        others = []
-        for k in order:
-            others.append(swap(after(parts[2 * k + 1], *others[-2:-1]), 1, "dp"))
-        terms = [parts[0], others[-1]]
-        for k, other in zip(order[:-1], others):
-            summed = (parts[2 * k].astype(F32) + other.astype(F32)).astype(BF)
-            terms.append(swap(summed, 2 * k, "dp"))
-        ids_late = after(ids, *others)
-        cuts_mlp = total(ids_late, [owned_mlp], group)
+        gates = {2: [owned_mlp[1], branch2_terms[-1]], 4: [owned_mlp[-1], norm1_terms[-1]]}
+        terms = scatter(parts, axis="dp", gates=gates)
+        cuts_mlp = total(after(ids, *terms), owned_mlp, group)
     else:
         owned_attn = lax.psum_scatter(parts[0], "dp", scatter_dimension=0, tiled=True)
 
@@ -954,10 +1010,9 @@
             return [lax.dynamic_index_in_dim(blocks, place ^ k, 0, False) for k in range(group)]
 
         cuts_mlp = relative(owned_mlp)
-        ids_late = ids
     out_fc1, out_fc2 = place_mlp(ids, exchange(cuts_mlp), hidden)
     if direct:
-        cuts_attn = total(after(ids, out_fc1, *norm1_terms, *branch2_terms), terms, group)
+        cuts_attn = total(ids, terms, group)
     else:
         cuts_attn = relative(owned_attn)
 

time: 354 us -> 387 us (1.093)
  waiting for transfers between devices: 124 us -> 160 us
  between operations: 15.5 us -> 2.44 us
  Pallas kernels: 135 us -> 140 us
    ppermute x56 -> x67, waiting for transfers between devices: 124 us -> 160 us  [swap(): return lax.ppermute(value, axis, [(i, i ^ bit) for i in range(size)])]
    convert_element_type x4 -> x7, other arithmetic: 2 us -> 6.97 us  [added(): return sum((term.astype(F32) for term in terms)).astype(BF)]
    pallas_call x3, Pallas kernels: 39.2 us -> 44.1 us  [the longest x2 26.8 us: mlp(): pl.pallas_call(lambda *refs: mlp_kernel(count, shards, group, *refs), gri...]
    ppermute x56 -> x67, starting transfers between devices: 55.3 us -> 58.7 us  [swap(): return lax.ppermute(value, axis, [(i, i ^ bit) for i in range(size)])]
    unnamed x109 -> x135, local copies, waits for them, and re-layouts: 10.2 us -> 10.8 us
  transfers between devices with their start and end apart: 58 -> 67, of which waited for: 26 -> 31; matrix products, arithmetic and copies ran while one was open for 2% -> 2% of each run, Pallas kernels for 33% -> 32%
where the time goes in v2:
time: 387 us; the launch traced here: 382 us
  waiting for transfers between devices  160 us (41%)
  Pallas kernels  140 us (36%)
  starting transfers between devices  58.7 us (15%)
  local copies, waits for them, and re-layouts  10.8 us (3%)
  other arithmetic  9.68 us (3%)
    ppermute x67, waiting for transfers between devices, swap(): return lax.ppermute(value, axis, [(i, i ^ bit) for i in range(size)])  160 us
    ppermute x67, starting transfers between devices, swap(): return lax.ppermute(value, axis, [(i, i ^ bit) for i in range(size)])  58.7 us
    pallas_call x2, Pallas kernels, mlp(): pl.pallas_call(lambda *refs: mlp_kernel(count, shards, group, *refs), gri...  26.8 us
    pallas_call x1, Pallas kernels, attend_back(): pl.pallas_call(attend_back_kernel, grid=(pairs,), in_specs=[pl.BlockSpec(...  24.5 us
    pallas_call x1, Pallas kernels, mlp_weights(): pl.pallas_call(lambda *refs: mlp_weights_kernel(direct, *refs), grid_spec...  17.2 us
    pallas_call x1, Pallas kernels, attend(): pl.pallas_call(attend_kernel, grid=(pairs,), in_specs=[pl.BlockSpec((leng...  15.6 us
    unnamed x135, local copies, waits for them, and re-layouts  10.8 us
    pallas_call x1, Pallas kernels, project(): pl.pallas_call(lambda *refs: project_kernel(ordered, group, count_column,...  8.21 us
  transfers between devices with their start and end apart: 67, of which 31 were waited for; matrix products, arithmetic and copies ran while one was open for 2% of the time, Pallas kernels for 32%

profile of v2, /device:TPU:0, one launch (start us, length us, event | category | flops | bytes accessed | tf_op | source)
XLA Modules:
  0.0 381.6 jit_solution(4600510666241126462)
XLA Ops:
  19.1 10.5 %collective-permute-done.4.refs_13_ = bf16[128,1152]{1,0:T(8,128)(2,1)S(1)} collective-permute-done((bf16[128,1152]{1,0:T(8,128)(2,1)S(1)}, bf16[128,1152]{1,0:T(8,128)(2,1)S(1)}, u32[]{:S(2)}, u32[]{:S(2)}) %collective-permute-start.4) | collective-permute-done | bytes 294944 | tf_op jit(solution)/shard_map/ppermute | solution.py:823
  53.5 10.7 %collective-permute-done.12.refs_10_ = bf16[128,2048]{1,0:T(8,128)(2,1)S(1)} collective-permute-done((bf16[128,2048]{1,0:T(8,128)(2,1)S(1)}, bf16[128,2048]{1,0:T(8,128)(2,1)S(1)}, u32[]{:S(2)}, u32[]{:S(2)}) %collective-permute-start.12) | collective-permute-done | bytes 524320 | tf_op jit(solution)/shard_map/ppermute | solution.py:823
  64.5 6.0 %collective-permute-done.16.refs_14_ = bf16[128,1152]{1,0:T(8,128)(2,1)S(1)} collective-permute-done((bf16[128,1152]{1,0:T(8,128)(2,1)S(1)}, bf16[128,1152]{1,0:T(8,128)(2,1)S(1)}, u32[]{:S(2)}, u32[]{:S(2)}) %collective-permute-start.16) | collective-permute-done | bytes 294944 | tf_op jit(solution)/shard_map/ppermute | solution.py:823
  70.8 6.0 %collective-permute-done.17.refs_16_ = bf16[128,1152]{1,0:T(8,128)(2,1)S(1)} collective-permute-done((bf16[128,1152]{1,0:T(8,128)(2,1)S(1)}, bf16[128,1152]{1,0:T(8,128)(2,1)S(1)}, u32[]{:S(2)}, u32[]{:S(2)}) %collective-permute-start.17) | collective-permute-done | bytes 294944 | tf_op jit(solution)/shard_map/ppermute | solution.py:823
  79.2 8.2 %project.1 = (bf16[1024,768]{1,0:T(8,128)(2,1)}, bf16[1024,256]{1,0:T(8,128)(2,1)}, f32[16,1024]{1,0:T(8,128)}, bf16[1376,1024]{1,0:T(8,128)(2,1)}, bf16[1376,76...) custom-call(s32[2]{0:T(128)} %pad_add_fusion.ids_ref.refs_0_.refs_7_, ...), custom_call_target="tpu_custom_call" | custom-call | flops 1000000000 | bytes 1000000 | tf_op jit(solution)/shard_map/project/pallas_call | solution.py:175
  90.3 15.6 %attend.1 = (f32[1376,256]{1,0:T(8,128)}, f32[2,2,1376]{2,1,0:T(2,128)}, bf16[344,256]{1,0:T(8,128)(2,1)}, bf16[344,256]{1,0:T(8,128)(2,1)}, bf16[344,256]{1,0:T(8,128)(2,1)}, /*index=5*/bf16[344,256]{1,0:T(8,128)(2,1)}) custom-call(bf16[1376,768]{1,0:T(8,128)(2,1)} %get-tuple-element.165.qkv_ref, f32[1376,1]{1,0:T(8,128)} %get-tuple-element.163.bias_ref), custom_call_target="tpu_custom_call" | custom-call | flops 1000000000 | bytes 1000000 | tf_op jit(solution)/shard_map/attend/pallas_call | solution.py:231
  106.4 6.3 %collective-permute-done.28.refs_13_ = bf16[128,2048]{1,0:T(8,128)(2,1)} collective-permute-done((bf16[128,2048]{1,0:T(8,128)(2,1)S(1)}, bf16[128,2048]{1,0:T(8,128)(2,1)}, u32[]{:S(2)}, u32[]{:S(2)}) %collective-permute-start.28) | collective-permute-done | bytes 524320 | tf_op jit(solution)/shard_map/ppermute | solution.py:823
  115.5 5.3 %collective-permute-done.21.refs_4_.rest_2_ = bf16[344,256]{1,0:T(8,128)(2,1)S(1)} collective-permute-done((bf16[344,256]{1,0:T(8,128)(2,1)}, bf16[344,256]{1,0:T(8,128)(2,1)S(1)}, u32[]{:S(2)}, u32[]{:S(2)}) %collective-permute-start.21) | collective-permute-done | bytes 176160 | tf_op jit(solution)/shard_map/ppermute | solution.py:823
  124.7 5.3 %middle.1 = (f32[344,1024]{1,0:T(8,128)}, f32[344,1024]{1,0:T(8,128)}, bf16[344,1024]{1,0:T(8,128)(2,1)}, f32[344,1024]{1,0:T(8,128)}, f32[344,1]{1,0:T(8,128)}) custom-call(f32[16,1024]{1,0:T(8,128)} %get-tuple-element.251.refs_0_.refs_5_.rows_ref, bf16[344,1024]{1,0:T(8,128)(2,1)} %bitcast.14, bf16[344,256]{1,0:T(8,128)(2,1)} %get-tuple-element.169.refs_2_.rest_0_, ...), custom_call_target="tpu_custom_call" | custom-call | flops 1000000000 | bytes 1000000 | tf_op jit(solution)/shard_map/middle/pallas_call | solution.py:333
  133.6 13.0 %collective-permute-done.29.refs_14_ = bf16[128,2048]{1,0:T(8,128)(2,1)S(1)} collective-permute-done((bf16[128,2048]{1,0:T(8,128)(2,1)}, bf16[128,2048]{1,0:T(8,128)(2,1)S(1)}, u32[]{:S(2)}, u32[]{:S(2)}) %collective-permute-start.29) | collective-permute-done | bytes 524320 | tf_op jit(solution)/shard_map/ppermute | solution.py:823
  146.7 10.0 %collective-permute-done.31.refs_16_ = bf16[128,2048]{1,0:T(8,128)(2,1)S(1)} collective-permute-done((bf16[128,2048]{1,0:T(8,128)(2,1)}, bf16[128,2048]{1,0:T(8,128)(2,1)S(1)}, u32[]{:S(2)}, u32[]{:S(2)}) %collective-permute-start.31) | collective-permute-done | bytes 524320 | tf_op jit(solution)/shard_map/ppermute | solution.py:823
  158.3 14.2 %mlp.2 = (bf16[344,1024]{1,0:T(8,128)(2,1)}, bf16[344,1024]{1,0:T(8,128)(2,1)}, bf16[688,1024]{1,0:T(8,128)(2,1)}, bf16[688,1024]{1,0:T(8,128)(2,1)}, bf16[688,1...) custom-call(f32[16,1024]{1,0:T(8,128)} %get-tuple-element.251.refs_0, ...), custom_call_target="tpu_custom_call" | custom-call | flops 1000000000 | bytes 1000000 | tf_op jit(solution)/shard_map/mlp/pallas_call | solution.py:475
  175.7 12.6 %mlp.3 = (bf16[344,1024]{1,0:T(8,128)(2,1)}, bf16[344,1024]{1,0:T(8,128)(2,1)}, bf16[688,1024]{1,0:T(8,128)(2,1)}, bf16[688,1024]{1,0:T(8,128)(2,1)}, bf16[688,1...) custom-call(f32[16,1024]{1,0:T(8,128)} %get-tuple-element.251.refs_0_.refs_5_.rows_ref, ...), custom_call_target="tpu_custom_call" | custom-call | flops 1000000000 | bytes 1000000 | tf_op jit(solution)/shard_map/mlp/pallas_call | solution.py:475
  193.2 17.2 %mlp_weights.1 = (bf16[512,2048]{1,0:T(8,128)(2,1)}, bf16[512,2048]{1,0:T(8,128)(2,1)}, f32[1,1024]{1,0:T(1,128)}, bf16[344,1024]{1,0:T(8,128)(2,1)}, bf16[344,1...) custom-call(s32[2]{0:T(128)} %pad_add_fusion.ids_ref.refs_0_.refs_7_, ...), custom_call_target="tpu_custom_call" | custom-call | flops 1000000000 | bytes 1000000 | tf_op jit(solution)/shard_map/mlp_weights/pallas_call | solution.py:547
  211.6 6.1 %turn.1 = (f32[344,1024]{1,0:T(8,128)}, bf16[344,1024]{1,0:T(8,128)(2,1)}, f32[8,1024]{1,0:T(8,128)}, bf16[344,256]{1,0:T(8,128)(2,1)}, bf16[344,256]{1,0:T(8,12...) custom-call(f32[16,1024]{1,0:T(8,128)} %get-tuple-element.251.refs_0_.refs_5_.rows_ref, ...), custom_call_target="tpu_custom_call" | custom-call | flops 1000000000 | bytes 1000000 | tf_op jit(solution)/shard_map/turn/pallas_call | solution.py:369
  231.9 24.5 %attend_back.1 = (bf16[1376,768]{1,0:T(8,128)(2,1)}, f32[2,1,384]{2,1,0:T(1,128)}) custom-call(bf16[1376,768]{1,0:T(8,128)(2,1)} %get-tuple-element.165.qkv_ref, f32[1376,1]{1,0:T(8,128)} %get-tuple-element.163.bias_ref, f32[1376,256]{1,0:T(8,128)} %get-tuple-element.166.att_ref, f32[2,2,1376]{2,1,0:T(2,128)} %get-tuple-element.195.lse_ref, ...), custom_call_target="tpu_custom_call" | custom-call | flops 1000000000 | bytes 1000000 | tf_op jit(solution)/shard_map/attend_back/pallas_call | solution.py:290
  262.5 10.1 %collective-permute-done.54 = bf16[128,2048]{1,0:T(8,128)(2,1)S(1)} collective-permute-done((bf16[128,2048]{1,0:T(8,128)(2,1)S(1)}, bf16[128,2048]{1,0:T(8,128)(2,1)S(1)}, u32[]{:S(2)}, u32[]{:S(2)}) %collective-permute-start.54) | collective-permute-done | bytes 524320 | tf_op jit(solution)/shard_map/ppermute | solution.py:823
  275.4 6.9 %qkv_back.1 = (bf16[344,1024]{1,0:T(8,128)(2,1)}, bf16[344,1024]{1,0:T(8,128)(2,1)}, bf16[344,1024]{1,0:T(8,128)(2,1)}, bf16[344,1024]{1,0:T(8,128)(2,1)}, f32[8,1024]{1,0:T(8,128)}) custom-call(bf16[1376,768]{1,0:T(8,128)(2,1)} %get-tuple-element.215.refs_0_.refs_2_, bf16[1024,768]{1,0:T(8,128)(2,1)} %get-tuple-element.216.refs_1_, ...), custom_call_target="tpu_custom_call" | custom-call | flops 1000000000 | bytes 1000000 | tf_op jit(solution)/shard_map/qkv_back/pallas_call | solution.py:636
  282.3 7.6 %attn_weights.1 = (bf16[128,1152]{1,0:T(8,128)(2,1)}, bf16[128,1152]{1,0:T(8,128)(2,1)}, bf16[128,1152]{1,0:T(8,128)(2,1)}, bf16[128,1152]{1,0:T(8,128)(2,1)}, b...) custom-call(s32[2]{0:T(128)} %pad_add_fusion.ids_ref.refs_0_.refs_7_, ...), custom_call_target="tpu_custom_call" | custom-call | flops 1000000000 | bytes 1000000 | tf_op jit(solution)/shard_map/attn_weights/pallas_call | solution.py:704
  291.1 6.5 %collective-permute-done.47 = bf16[128,1152]{1,0:T(8,128)(2,1)S(1)} collective-permute-done((bf16[128,1152]{1,0:T(8,128)(2,1)}, bf16[128,1152]{1,0:T(8,128)(2,1)S(1)}, u32[]{:S(2)}, u32[]{:S(2)}) %collective-permute-start.47) | collective-permute-done | bytes 294944 | tf_op jit(solution)/shard_map/ppermute | solution.py:823
  306.2 8.7 %collective-permute-done.51.rest_2_ = bf16[344,1024]{1,0:T(8,128)(2,1)S(1)} collective-permute-done((bf16[344,1024]{1,0:T(8,128)(2,1)S(1)}, bf16[344,1024]{1,0:T(8,128)(2,1)S(1)}, u32[]{:S(2)}, u32[]{:S(2)}) %collective-permute-start.51) | collective-permute-done | bytes 704544 | tf_op jit(solution)/shard_map/ppermute | solution.py:823
  321.3 8.2 %collective-permute-done.53 = bf16[128,1152]{1,0:T(8,128)(2,1)S(1)} collective-permute-done((bf16[128,1152]{1,0:T(8,128)(2,1)S(1)}, bf16[128,1152]{1,0:T(8,128)(2,1)S(1)}, u32[]{:S(2)}, u32[]{:S(2)}) %collective-permute-start.53) | collective-permute-done | bytes 294944 | tf_op jit(solution)/shard_map/ppermute | solution.py:823
  331.1 11.5 %collective-permute-done.55.refs_2_ = bf16[128,2048]{1,0:T(8,128)(2,1)S(1)} collective-permute-done((bf16[128,2048]{1,0:T(8,128)(2,1)S(1)}, bf16[128,2048]{1,0:T(8,128)(2,1)S(1)}, u32[]{:S(2)}, u32[]{:S(2)}) %collective-permute-start.55) | collective-permute-done | bytes 524320 | tf_op jit(solution)/shard_map/ppermute | solution.py:823
  346.7 8.8 %collective-permute-done.52.refs_2_ = bf16[128,1152]{1,0:T(8,128)(2,1)S(1)} collective-permute-done((bf16[128,1152]{1,0:T(8,128)(2,1)S(1)}, bf16[128,1152]{1,0:T(8,128)(2,1)S(1)}, u32[]{:S(2)}, u32[]{:S(2)}) %collective-permute-start.52) | collective-permute-done | bytes 294944 | tf_op jit(solution)/shard_map/ppermute | solution.py:823
  (274 shorter events, 139.4 us)
Async XLA Ops:
  51.4 25.4 %collective-permute-start.14 = (bf16[344,1024]{1,0:T(8,128)(2,1)S(1)}, bf16[344,1024]{1,0:T(8,128)(2,1)S(1)}, u32[]{:S(2)}, u32[]{:S(2)}) collective-permute-start(bf16[344,1024]{1,0:T(8,128)(2,1)S(1)} %bitcast.17), channel_id=1, source_target_pairs={{0,1},{1,0},{2,3},{3,2},{4,5},{5,4},{6,7},{7,6},{8,9},{9,8},{10,11... | collective-permute-start | bytes 2113544 | tf_op jit(solution)/shard_map/ppermute | solution.py:823
  51.4 26.1 %collective-permute-start.15 = (bf16[344,1024]{1,0:T(8,128)(2,1)S(1)}, bf16[344,1024]{1,0:T(8,128)(2,1)S(1)}, u32[]{:S(2)}, u32[]{:S(2)}) collective-permute-start(bf16[344,1024]{1,0:T(8,128)(2,1)S(1)} %collective-permute-done.3.refs_3_.refs_6_), channel_id=1, source_target_pairs={{0,1},{1,0},{2,3},{3,2},{4,5},{5,4},{6,7},{7,6},{8,9},{9,8},{10,11... | collective-permute-start | bytes 2113544 | tf_op jit(solution)/shard_map/ppermute | solution.py:823
  51.9 18.5 %collective-permute-start.16 = (bf16[128,1152]{1,0:T(8,128)(2,1)S(1)}, bf16[128,1152]{1,0:T(8,128)(2,1)S(1)}, u32[]{:S(2)}, u32[]{:S(2)}) collective-permute-start(bf16[128,1152]{1,0:T(8,128)(2,1)S(1)} %collective-permute-done.4.refs_13_), channel_id=1, source_target_pairs={{0,4},{4,0},{8,12},{12,8},{16,20},{20,16},{24,28},{28,24},{1,5},{5... | collective-permute-start | bytes 884744 | tf_op jit(solution)/shard_map/ppermute | solution.py:823
  64.5 25.8 %collective-permute-start.19 = (bf16[344,1024]{1,0:T(8,128)(2,1)S(1)}, bf16[344,1024]{1,0:T(8,128)(2,1)}, u32[]{:S(2)}, u32[]{:S(2)}) collective-permute-start(bf16[344,1024]{1,0:T(8,128)(2,1)S(1)} %bitcast.20), channel_id=1, source_target_pairs={{0,2},{1,3},{2,0},{3,1},{4,6},{5,7},{6,4},{7,5},{8,10},{9,11},{10,... | collective-permute-start | bytes 2113544 | tf_op jit(solution)/shard_map/ppermute | solution.py:823
  70.5 19.8 %collective-permute-start.18 = (bf16[128,2048]{1,0:T(8,128)(2,1)}, bf16[128,2048]{1,0:T(8,128)(2,1)}, u32[]{:S(2)}, u32[]{:S(2)}) collective-permute-start(bf16[128,2048]{1,0:T(8,128)(2,1)} %collective-permute-done.13.refs_11_), channel_id=1, source_target_pairs={{0,4},{4,0},{8,12},{12,8},{16,20},{20,16},{24,28},{28,24},{1,5},{5... | collective-permute-start | bytes 1572872 | tf_op jit(solution)/shard_map/ppermute | solution.py:823
  87.4 18.4 %collective-permute-start.24 = (bf16[1024,256]{1,0:T(8,128)(2,1)}, bf16[1024,256]{1,0:T(8,128)(2,1)S(1)}, u32[]{:S(2)}, u32[]{:S(2)}) collective-permute-start(bf16[1024,256]{1,0:T(8,128)(2,1)} %get-tuple-element.173.refs_6_.refs_9_), channel_id=1, source_target_pairs={{0,2},{1,3},{2,0},{3,1},{4,6},{5,7},{6,4},{7,5},{8,10},{9,11},{10,... | collective-permute-start | bytes 1572872 | tf_op jit(solution)/shard_map/ppermute | solution.py:823
  87.5 25.2 %collective-permute-start.28 = (bf16[128,2048]{1,0:T(8,128)(2,1)S(1)}, bf16[128,2048]{1,0:T(8,128)(2,1)}, u32[]{:S(2)}, u32[]{:S(2)}) collective-permute-start(bf16[128,2048]{1,0:T(8,128)(2,1)S(1)} %pad_maximum_fusion.refs_9_), channel_id=1, source_target_pairs={{0,16},{4,20},{8,24},{12,28},{16,0},{20,4},{24,8},{28,12},{1,17},{... | collective-permute-start | bytes 1572872 | tf_op jit(solution)/shard_map/ppermute | solution.py:823
  90.2 24.2 %collective-permute-start.23 = (bf16[1024,256]{1,0:T(8,128)(2,1)}, bf16[1024,256]{1,0:T(8,128)(2,1)S(1)}, u32[]{:S(2)}, u32[]{:S(2)}) collective-permute-start(bf16[1024,256]{1,0:T(8,128)(2,1)} %get-tuple-element.173.refs_6_.refs_9_), channel_id=1, source_target_pairs={{0,1},{1,0},{2,3},{3,2},{4,5},{5,4},{6,7},{7,6},{8,9},{9,8},{10,11... | collective-permute-start | bytes 1572872 | tf_op jit(solution)/shard_map/ppermute | solution.py:823
  112.7 19.4 %collective-permute-start.30 = (bf16[128,2048]{1,0:T(8,128)(2,1)}, bf16[128,2048]{1,0:T(8,128)(2,1)}, u32[]{:S(2)}, u32[]{:S(2)}) collective-permute-start(bf16[128,2048]{1,0:T(8,128)(2,1)} %collective-permute-done.28.refs_13_), channel_id=1, source_target_pairs={{0,8},{4,12},{8,0},{12,4},{16,24},{20,28},{24,16},{28,20},{1,9},{5... | collective-permute-start | bytes 1572872 | tf_op jit(solution)/shard_map/ppermute | solution.py:823
  115.2 31.4 %collective-permute-start.27 = (bf16[344,1024]{1,0:T(8,128)(2,1)S(1)}, bf16[344,1024]{1,0:T(8,128)(2,1)S(1)}, u32[]{:S(2)}, u32[]{:S(2)}) collective-permute-start(bf16[344,1024]{1,0:T(8,128)(2,1)S(1)} %bitcast.21), channel_id=1, source_target_pairs={{0,1},{1,0},{2,3},{3,2},{4,5},{5,4},{6,7},{7,6},{8,9},{9,8},{10,11... | collective-permute-start | bytes 2113544 | tf_op jit(solution)/shard_map/ppermute | solution.py:823
  130.0 26.7 %collective-permute-start.26 = (bf16[344,1024]{1,0:T(8,128)(2,1)}, bf16[344,1024]{1,0:T(8,128)(2,1)S(1)}, u32[]{:S(2)}, u32[]{:S(2)}) collective-permute-start(bf16[344,1024]{1,0:T(8,128)(2,1)} %get-tuple-element.178.refs_1_), channel_id=1, source_target_pairs={{0,1},{1,0},{2,3},{3,2},{4,5},{5,4},{6,7},{7,6},{8,9},{9,8},{10,11... | collective-permute-start | bytes 2113544 | tf_op jit(solution)/shard_map/ppermute | solution.py:823
  130.6 42.0 %collective-permute-start.33 = (bf16[344,1024]{1,0:T(8,128)(2,1)}, bf16[344,1024]{1,0:T(8,128)(2,1)S(1)}, u32[]{:S(2)}, u32[]{:S(2)}) collective-permute-start(bf16[344,1024]{1,0:T(8,128)(2,1)} %get-tuple-element.178.refs_1_), channel_id=1, source_target_pairs={{0,2},{1,3},{2,0},{3,1},{4,6},{5,7},{6,4},{7,5},{8,10},{9,11},{10,... | collective-permute-start | bytes 2113544 | tf_op jit(solution)/shard_map/ppermute | solution.py:823
  132.1 24.6 %collective-permute-start.31 = (bf16[128,2048]{1,0:T(8,128)(2,1)}, bf16[128,2048]{1,0:T(8,128)(2,1)S(1)}, u32[]{:S(2)}, u32[]{:S(2)}) collective-permute-start(bf16[128,2048]{1,0:T(8,128)(2,1)} %collective-permute-done.30.refs_15_), channel_id=1, source_target_pairs={{0,4},{4,0},{8,12},{12,8},{16,20},{20,16},{24,28},{28,24},{1,5},{5... | collective-permute-start | bytes 1572872 | tf_op jit(solution)/shard_map/ppermute | solution.py:823
  146.6 26.0 %collective-permute-start.35 = (bf16[344,1024]{1,0:T(8,128)(2,1)}, bf16[344,1024]{1,0:T(8,128)(2,1)S(1)}, u32[]{:S(2)}, u32[]{:S(2)}) collective-permute-start(bf16[344,1024]{1,0:T(8,128)(2,1)} %collective-permute-done.19.refs_3_), channel_id=1, source_target_pairs={{0,1},{1,0},{2,3},{3,2},{4,5},{5,4},{6,7},{7,6},{8,9},{9,8},{10,11... | collective-permute-start | bytes 2113544 | tf_op jit(solution)/shard_map/ppermute | solution.py:823
  188.6 21.9 %collective-permute-start.32 = (bf16[344,1024]{1,0:T(8,128)(2,1)S(1)}, bf16[344,1024]{1,0:T(8,128)(2,1)S(1)}, u32[]{:S(2)}, u32[]{:S(2)}) collective-permute-start(bf16[344,1024]{1,0:T(8,128)(2,1)S(1)} %copy-done.55), channel_id=1, source_target_pairs={{0,1},{1,0},{2,3},{3,2},{4,5},{5,4},{6,7},{7,6},{8,9},{9,8},{10,11... | collective-permute-start | bytes 2113544 | tf_op jit(solution)/shard_map/ppermute | solution.py:823
  210.5 47.8 %collective-permute-start.42 = (bf16[512,2048]{1,0:T(8,128)(2,1)}, bf16[512,2048]{1,0:T(8,128)(2,1)}, u32[]{:S(2)}, u32[]{:S(2)}) collective-permute-start(bf16[512,2048]{1,0:T(8,128)(2,1)} %get-tuple-element.213), channel_id=1, source_target_pairs={{0,4},{4,0},{8,12},{12,8},{16,20},{20,16},{24,28},{28,24},{1,5},{5... | collective-permute-start | bytes 6291464 | tf_op jit(solution)/shard_map/ppermute | solution.py:823
  260.9 21.4 %collective-permute-start.43 = (bf16[1024,256]{1,0:T(8,128)(2,1)}, bf16[1024,256]{1,0:T(8,128)(2,1)}, u32[]{:S(2)}, u32[]{:S(2)}) collective-permute-start(bf16[1024,256]{1,0:T(8,128)(2,1)} %get-tuple-element.225), channel_id=1, source_target_pairs={{0,1},{1,0},{2,3},{3,2},{4,5},{5,4},{6,7},{7,6},{8,9},{9,8},{10,11... | collective-permute-start | bytes 1572872 | tf_op jit(solution)/shard_map/ppermute | solution.py:823
  260.9 38.2 %collective-permute-start.50 = (bf16[344,1024]{1,0:T(8,128)(2,1)}, bf16[344,1024]{1,0:T(8,128)(2,1)S(1)}, u32[]{:S(2)}, u32[]{:S(2)}) collective-permute-start(bf16[344,1024]{1,0:T(8,128)(2,1)} %get-tuple-element.238), channel_id=1, source_target_pairs={{0,1},{1,0},{2,3},{3,2},{4,5},{5,4},{6,7},{7,6},{8,9},{9,8},{10,11... | collective-permute-start | bytes 2113544 | tf_op jit(solution)/shard_map/ppermute | solution.py:823
  261.4 20.9 %collective-permute-start.44 = (bf16[1024,256]{1,0:T(8,128)(2,1)}, bf16[1024,256]{1,0:T(8,128)(2,1)}, u32[]{:S(2)}, u32[]{:S(2)}) collective-permute-start(bf16[1024,256]{1,0:T(8,128)(2,1)} %add_convert_fusion.8), channel_id=1, source_target_pairs={{0,2},{1,3},{2,0},{3,1},{4,6},{5,7},{6,4},{7,5},{8,10},{9,11},{10,... | collective-permute-start | bytes 1572872 | tf_op jit(solution)/shard_map/ppermute | solution.py:823
  300.5 20.3 %collective-permute-start.45 = (bf16[128,1152]{1,0:T(8,128)(2,1)S(1)}, bf16[128,1152]{1,0:T(8,128)(2,1)S(1)}, u32[]{:S(2)}, u32[]{:S(2)}) collective-permute-start(bf16[128,1152]{1,0:T(8,128)(2,1)S(1)} %copy-done.57), channel_id=1, source_target_pairs={{0,4},{4,0},{8,12},{12,8},{16,20},{20,16},{24,28},{28,24},{1,5},{5... | collective-permute-start | bytes 884744 | tf_op jit(solution)/shard_map/ppermute | solution.py:823
  316.8 26.6 %collective-permute-start.57 = (bf16[344,1024]{1,0:T(8,128)(2,1)S(1)}, bf16[344,1024]{1,0:T(8,128)(2,1)S(1)}, u32[]{:S(2)}, u32[]{:S(2)}) collective-permute-start(bf16[344,1024]{1,0:T(8,128)(2,1)S(1)} %add_convert_fusion), channel_id=1, source_target_pairs={{0,2},{1,3},{2,0},{3,1},{4,6},{5,7},{6,4},{7,5},{8,10},{9,11},{10,... | collective-permute-start | bytes 2113544 | tf_op jit(solution)/shard_map/ppermute | solution.py:823
  317.8 24.8 %collective-permute-start.55 = (bf16[128,2048]{1,0:T(8,128)(2,1)S(1)}, bf16[128,2048]{1,0:T(8,128)(2,1)S(1)}, u32[]{:S(2)}, u32[]{:S(2)}) collective-permute-start(bf16[128,2048]{1,0:T(8,128)(2,1)S(1)} %get-tuple-element.272), channel_id=1, source_target_pairs={{0,16},{4,20},{8,24},{12,28},{16,0},{20,4},{24,8},{28,12},{1,17},{... | collective-permute-start | bytes 1572872 | tf_op jit(solution)/shard_map/ppermute | solution.py:823
  320.7 44.5 %collective-permute-start.59 = (bf16[344,1024]{1,0:T(8,128)(2,1)}, bf16[344,1024]{1,0:T(8,128)(2,1)S(1)}, u32[]{:S(2)}, u32[]{:S(2)}) collective-permute-start(bf16[344,1024]{1,0:T(8,128)(2,1)} %get-tuple-element.256), channel_id=1, source_target_pairs={{0,1},{1,0},{2,3},{3,2},{4,5},{5,4},{6,7},{7,6},{8,9},{9,8},{10,11... | collective-permute-start | bytes 2113544 | tf_op jit(solution)/shard_map/ppermute | solution.py:823
  320.8 44.9 %collective-permute-start.60 = (bf16[344,1024]{1,0:T(8,128)(2,1)}, bf16[344,1024]{1,0:T(8,128)(2,1)S(1)}, u32[]{:S(2)}, u32[]{:S(2)}) collective-permute-start(bf16[344,1024]{1,0:T(8,128)(2,1)} %get-tuple-element.260), channel_id=1, source_target_pairs={{0,1},{1,0},{2,3},{3,2},{4,5},{5,4},{6,7},{7,6},{8,9},{9,8},{10,11... | collective-permute-start | bytes 2113544 | tf_op jit(solution)/shard_map/ppermute | solution.py:823
  (109 other events, 1240.9 us)

commit v3 on v2

--- a/solution.py
+++ b/solution.py
@@ -503,20 +503,17 @@
     keep_ref, send_ref, scale2_ref, *branches, out_ref = rest
     hidden = pre_a.shape[1]
     first = dot(norm_a[...], pre_a[...], 0, 0) + dot(norm_b[...], pre_b[...], 0, 0)
-    out_ref[:, :hidden] = first
+    size = keep_ref.shape[0]
+    out_ref[0, :, :hidden] = first[:size].astype(BF)
+    out_ref[1, :, :hidden] = first[size:].astype(BF)
     outs = [grad_a[...].astype(F32), grad_b[...].astype(F32)]
     scaled = [(out * rows_ref[9:10, :]).astype(BF) for out in outs]
     second = dot(scaled[0], act_a[...], 0, 0) + dot(scaled[1], act_b[...], 0, 0)
-    out_ref[:, hidden:] = second
-    size = keep_ref.shape[0]
-    if direct:
-        side = ids_ref[1] & 1
-        keep_ref[...] = out_ref[pl.ds(pl.multiple_of(side * size, size), size), :].astype(BF)
-        other = pl.multiple_of((1 - side) * size, size)
-        send_ref[...] = out_ref[pl.ds(other, size), :].astype(BF)
-    else:
-        keep_ref[...] = out_ref[:size, :].astype(BF)
-        send_ref[...] = out_ref[size:, :].astype(BF)
+    out_ref[0, :, hidden:] = second[:size].astype(BF)
+    out_ref[1, :, hidden:] = second[size:].astype(BF)
+    side = (ids_ref[1] & 1) if direct else 0
+    keep_ref[...] = out_ref[side]
+    send_ref[...] = out_ref[1 - side]
     scale2 = own_ref[1:2, :] * rows_ref[8:9, :]
     count = len(branches) // 2
     size = branches[0].shape[0]
@@ -534,14 +531,11 @@
     size = 2 * length // group
     step = 256
 
-    def at(i, ids_ref):
-        return ((ids_ref[1] >> 1) ^ i) if direct else i
-
-    cols = pl.BlockSpec((length, step), lambda i, ids_ref: (0, at(i, ids_ref)))
+    cols = pl.BlockSpec((length, step), lambda i, ids_ref: (0, i))
     whole = pl.BlockSpec((length, hidden), lambda i, ids_ref: (0, 0))
 
     def line(count):
-        return pl.BlockSpec((count, step), lambda i, ids_ref: (0, at(i, ids_ref)))
+        return pl.BlockSpec((count, step), lambda i, ids_ref: (0, i))
 
     part = pl.BlockSpec((step // 2, 2 * hidden), lambda i, ids_ref: (i, 0))
     return pl.pallas_call(
@@ -551,11 +545,11 @@
             grid=(width // step,),
             in_specs=[cols] * 4
             + [line(rows.shape[0])]
-            + [pl.BlockSpec((step, hidden), lambda i, ids_ref: (at(i, ids_ref), 1))]
+            + [pl.BlockSpec((step, hidden), lambda i, ids_ref: (i, 1))]
             + [whole] * 4
             + [line(own.shape[0])],
             out_specs=[part, part, line(1)] + [line(size)] * group,
-            scratch_shapes=[pltpu.VMEM((step, 2 * hidden), F32)],
+            scratch_shapes=[pltpu.VMEM((2, step // 2, 2 * hidden), BF)],
         ),
         out_shape=[shaped((width // 2, 2 * hidden), BF)] * 2
         + [shaped((1, width), F32)]
@@ -648,8 +642,8 @@
     direct, shard, terms, ids_ref, normed_ref, grad_ref, norm1_ref, sums_ref, turn_ref, fbias_ref,
     scale2_ref, bias_a_ref, bias_b_ref, *rest,
 ):
-    projs, outs = rest[:terms], rest[terms:-4]
-    rows_ref, turned_ref, block_ref, small_ref = rest[-4:]
+    projs, outs = rest[:terms], rest[terms:-5]
+    rows_ref, turned_ref, block_ref, small_ref, stage_ref = rest[-5:]
     place, row = ids_ref[0], ids_ref[1]
     width = normed_ref.shape[1]
     part = projs[0].shape[1]
@@ -683,11 +677,13 @@
         block_ref[:, 4 * part :] = turned_ref[cols, :]
         if direct:
             size = step // 2
+            stage_ref[0] = block_ref[:size, :].astype(BF)
+            stage_ref[1] = block_ref[size:, :].astype(BF)
             side = row & 1
-            outs[2 * k][...] = block_ref[pl.ds(pl.multiple_of(side * size, size), size), :].astype(BF)
-            outs[2 * k + 1][...] = block_ref[
-                pl.ds(pl.multiple_of((1 - side) * size, size), size), :
-            ].astype(BF)
+            blocks = width // step
+            outs[k][...] = stage_ref[side]
+            spot = (k + 1) % 2 * size
+            outs[blocks + (blocks - 1 - k) // 2][spot : spot + size, :] = stage_ref[1 - side]
         else:
             outs[0][k * step : (k + 1) * step, :] = block_ref[...].astype(BF)
 
@@ -698,9 +694,11 @@
     columns = 4 * part + EXTRA
     direct = blocks > 0
     step = 2 * (width // blocks) if direct else 256
-    out_shape = [shaped((width // blocks, columns), BF)] * blocks if direct else [
-        shaped((width, columns), BF)
-    ]
+    out_shape = [shaped((width, columns), BF)]
+    if direct:
+        size = width // blocks
+        out_shape = [shaped((size, columns), BF)] * (blocks // 2)
+        out_shape += [shaped((2 * size, columns), BF)] * (blocks // 4)
     return pl.pallas_call(
         lambda *refs: attn_weights_kernel(direct, shard, len(projs), *refs),
         in_specs=[SMEM] + [VMEM] * (2 + len(sums) + len(projs)),
@@ -711,6 +709,7 @@
             pltpu.VMEM((width, EXTRA), F32),
             pltpu.VMEM((step, columns), F32),
             pltpu.VMEM((8, part), F32),
+            pltpu.VMEM((2, step // 2, columns), BF),
         ],
         compiler_params=PARAMS,
         cost_estimate=SMALL,
@@ -816,7 +815,7 @@
     hidden_part = hidden // group
     bias_cols = hidden // width
     vector_count = vectors.shape[0]
-    direct = replicas <= 8
+    direct = replicas == 8
 
     def swap(value, bit, axis="ctx"):
         size = group if axis == "ctx" else replicas
@@ -880,19 +879,19 @@
             if m ^ low:
                 shards[m] = swap(after(shards[m ^ low], *before), low, "dp")
 
+    second = exchange([after(block, *first) for block in cuts[group:]])
     if direct:
         shards = {0: jnp.concatenate(first, axis=0)}
-        bits = [bit for bit in (4, 2, 1) if bit < replicas]
-        for bit in bits:
+        for bit in (4, 2, 1):
             shards[bit] = swap(shards[0], bit, "dp")
-        arrived = [tokens_far] + [shards[bit] for bit in bits]
+        arrived = [tokens_far] + [shards[bit] for bit in (4, 2, 1)] + second[1:]
         widen(shards, *arrived)
         first_pieces = [shards[m] for m in range(replicas)]
-        arrived = arrived + [shards[m] for m in (3, 6) if m < replicas]
     else:
         first_pieces = [lax.all_gather(in_order(first), "dp", axis=0, tiled=True)]
         arrived = [tokens_far]
-    second = exchange([after(block, *arrived) for block in cuts[group:]])
+    second_shard = after(in_order(second), *arrived)
+    second_all = lax.all_gather(second_shard, "dp", axis=0, tiled=True)
     tokens_pieces = [tokens[0]]
     for j in range(1, group):
         source = tokens_pieces[j ^ (j & -j)]
@@ -900,18 +899,9 @@
             tokens_pieces.append(tokens_far)
         else:
             tokens_pieces.append(swap(after(source, *arrived), j & -j))
-    cotangent_far = swap(after(cotangent[0], *second), group // 2)
-    if direct:
-        shards = {0: after(jnp.concatenate(second, axis=0), first_pieces[-2])}
-        for bit in bits:
-            shards[bit] = swap(shards[0], bit, "dp")
-        widen(shards)
-        second_pieces = [shards[m] for m in range(replicas)]
-        early, later = [shards[1], shards[2]], [shards[3], cotangent_far]
-    else:
-        early, later = [], [cotangent_far]
-        second_pieces = [lax.all_gather(in_order(second), "dp", axis=0, tiled=True)]
-    tokens_own = after(tokens[0], *early)
+    cotangent_far = swap(after(cotangent[0], *arrived), group // 2)
+
+    tokens_own = after(tokens[0], second_shard)
     count_column = vector_count + bias_cols
     (
         weight_qkv, weight_proj, vector_rows, normed1, qkv, mean1, inverse1, bias_fc1, key_bias,
@@ -928,7 +918,7 @@
             cotangent_pieces.append(cotangent_far)
         else:
             cotangent_pieces.append(swap(after(source, qkv), j & -j))
-    attended, lse, *attended_low = attend(after(qkv, *later), key_bias, group)
+    attended, lse, *attended_low = attend(after(qkv, cotangent_far), key_bias, group)
     projs = gather(weight_proj, lse)
     attended_own = exchange(attended_low)
     branch1, middle, normed2_own, unit2, inverse2 = middle_step(
@@ -944,12 +934,9 @@
             vector_rows, pieces, cotangent_pieces[where], live[where], ids, bias_fc1, weights, group
         )
 
-    near = list(feed(slice(0, half), normed2, second_pieces))
-    if len(second_pieces) > 1:
-        second_all = near.pop()
-    else:
-        second_all = second_pieces[0]
-    *backs_near, norm_near, grad_near, act_near, pre_near, sums_near, own_sums = near
+    *backs_near, norm_near, grad_near, act_near, pre_near, sums_near, own_sums = feed(
+        slice(0, half), normed2, [second_all]
+    )
     normed2_far = [swap(normed2_own, half)]
     while len(normed2_far) < half:
         normed2_far += [
@@ -973,17 +960,17 @@
     att_grads = exchange(att_grads)
     mids = []
     proj_terms = scatter(proj_weights(branch_grad, attended_own), *att_grads, mids=mids)
-    branch2_terms = scatter([after(part, *att_grads) for part in branches], *att_grads)
+    branch2_terms = scatter(branches, *att_grads, mids=mids)
     qkv_grad, qkv_sums = attend_back(qkv, key_bias, attended, after(lse, *mids), att_grads)
-    sums = []
+    pending = [branch2_terms[-1], proj_terms[-1]]
     if direct:
         other = after(other_mlp, qkv_grad)
-        size = group * rows
-        blocks = [slice(k * size, (k + 1) * size) for k in range(replicas // 2)]
-        sums = [
-            (keep_mlp[block].astype(F32) + other[block].astype(F32)).astype(BF) for block in blocks
-        ]
-        owned_mlp = scatter(sums, axis="dp", scale=2)
+        summed = (keep_mlp.astype(F32) + other.astype(F32)).astype(BF)
+        pending.append(summed)
+        lines = [[side + 2 * z for z in range(replicas // 2)] for side in range(2)]
+        owned_mlp = lax.psum_scatter(
+            summed, "dp", scatter_dimension=0, tiled=True, axis_index_groups=lines
+        )
     else:
         ordered = jnp.stack(
             [part.reshape(-1, 128, 2 * hidden_part) for part in (keep_mlp, send_mlp)], axis=1
@@ -991,7 +978,7 @@
         owned_mlp = lax.psum_scatter(
             ordered.reshape(width, 2 * hidden_part), "dp", scatter_dimension=0, tiled=True
         )
-    *norm1_parts, norm1_sums = qkv_back(after(qkv_grad, *sums), weight_qkv, tokens_pieces, mean1, inverse1)
+    *norm1_parts, norm1_sums = qkv_back(after(qkv_grad, *pending), weight_qkv, tokens_pieces, mean1, inverse1)
     parts = attn_weights(
         ids, normed1, qkv_grad,
         [norm1_sums, qkv_sums, turn_sums, own_sums, grad_scale2, sums_near, sums_far],
@@ -999,9 +986,19 @@
     )
     norm1_terms = scatter(norm1_parts)
     if direct:
-        gates = {2: [owned_mlp[1], branch2_terms[-1]], 4: [owned_mlp[-1], norm1_terms[-1]]}
-        terms = scatter(parts, axis="dp", gates=gates)
-        cuts_mlp = total(after(ids, *terms), owned_mlp, group)
+        def add(left, right):
+            return (left.astype(F32) + right.astype(F32)).astype(BF)
+
+        keep0, keep1, keep2, keep3, send32, send10 = parts
+        size = keep0.shape[0]
+        other32 = swap(send32, 1, "dp")
+        other10 = swap(after(send10, other32), 1, "dp")
+        across = swap(add(keep3, other32[:size]), 2, "dp")
+        far = swap(add(add(keep2, other32[size:]), across), 4, "dp")
+        across0 = swap(add(keep1, other10[:size]), 2, "dp")
+        terms = [add(keep0, other10[size:]), across0, far]
+        settled = [across, across0]
+        cuts_mlp = total(after(ids, *settled), [owned_mlp], group)
     else:
         owned_attn = lax.psum_scatter(parts[0], "dp", scatter_dimension=0, tiled=True)
 
@@ -1010,16 +1007,17 @@
             return [lax.dynamic_index_in_dim(blocks, place ^ k, 0, False) for k in range(group)]
 
         cuts_mlp = relative(owned_mlp)
+        settled = []
     out_fc1, out_fc2 = place_mlp(ids, exchange(cuts_mlp), hidden)
+    input_grad = begin(
+        vector_rows, after(tokens[0], *settled), mean1, inverse1, middle_grad, norm1_terms
+    )
+    output = finish(after(vector_rows, *settled), middle, branch2_terms)
     if direct:
-        cuts_attn = total(ids, terms, group)
+        cuts_attn = total(after(ids, input_grad, output, out_fc1), terms, group)
     else:
         cuts_attn = relative(owned_attn)
 
-    input_grad = begin(
-        vector_rows, after(tokens[0], *cuts_attn), mean1, inverse1, middle_grad, norm1_terms
-    )
-    output = finish(after(vector_rows, *cuts_attn), middle, branch2_terms)
     out_qkv, out_proj, out_vectors, out_bias = place_attn(
         ids, exchange(cuts_attn), width, vector_count, bias_cols
     )

time: 387 us -> 354 us (0.915)
  waiting for transfers between devices: 160 us -> 134 us
  starting transfers between devices: 58.7 us -> 42 us
  between operations: 2.44 us -> 15.7 us
    ppermute x67 -> x55, waiting for transfers between devices: 160 us -> 133 us  [swap(): return lax.ppermute(value, axis, [(i, i ^ bit) for i in range(size)])]
    ppermute x67 -> x55, starting transfers between devices: 58.7 us -> 41.9 us  [swap(): return lax.ppermute(value, axis, [(i, i ^ bit) for i in range(size)])]
    convert_element_type x1 -> x4, other arithmetic: 1.17 us -> 6.67 us  [the longest x1 3.9 us: local(): summed = (keep_mlp.astype(F32) + other.astype(F32)).astype(BF)]
    convert_element_type x7 -> x4, other arithmetic: 6.97 us -> 2 us  [added(): return sum((term.astype(F32) for term in terms)).astype(BF)]
    unnamed x135 -> x113, local copies, waits for them, and re-layouts: 10.8 us -> 9.67 us
  transfers between devices with their start and end apart: 67 -> 57, of which waited for: 31 -> 28; matrix products, arithmetic and copies ran while one was open for 2% -> 2% of each run, Pallas kernels for 32% -> 34%
where the time goes in v3:
time: 354 us; the launch traced here: 349 us
  Pallas kernels  137 us (39%)
  waiting for transfers between devices  134 us (38%)
  starting transfers between devices  42 us (12%)
  between operations  15.7 us (4%)
  other arithmetic  11.2 us (3%)
  local copies, waits for them, and re-layouts  9.73 us (3%)
    ppermute x55, waiting for transfers between devices, swap(): return lax.ppermute(value, axis, [(i, i ^ bit) for i in range(size)])  133 us
    ppermute x55, starting transfers between devices, swap(): return lax.ppermute(value, axis, [(i, i ^ bit) for i in range(size)])  41.9 us
    pallas_call x2, Pallas kernels, mlp(): pl.pallas_call(lambda *refs: mlp_kernel(count, shards, group, *refs), gri...  25.5 us
    pallas_call x1, Pallas kernels, attend_back(): pl.pallas_call(attend_back_kernel, grid=(pairs,), in_specs=[pl.BlockSpec(...  24.5 us
    pallas_call x1, Pallas kernels, mlp_weights(): pl.pallas_call(lambda *refs: mlp_weights_kernel(direct, *refs), grid_spec...  16.2 us
    pallas_call x1, Pallas kernels, attend(): pl.pallas_call(attend_kernel, grid=(pairs,), in_specs=[pl.BlockSpec((leng...  15.6 us
    unnamed x113, local copies, waits for them, and re-layouts  9.67 us
    pallas_call x1, Pallas kernels, project(): pl.pallas_call(lambda *refs: project_kernel(ordered, group, count_column,...  8.23 us
  transfers between devices with their start and end apart: 57, of which 28 were waited for; matrix products, arithmetic and copies ran while one was open for 2% of the time, Pallas kernels for 34%

profile of v3, /device:TPU:0, one launch (start us, length us, event | category | flops | bytes accessed | tf_op | source)
XLA Modules:
  0.0 348.9 jit_solution(13816529159215933018)
XLA Ops:
  30.6 6.5 %collective-permute-done.7.refs_13_ = bf16[128,1152]{1,0:T(8,128)(2,1)S(1)} collective-permute-done((bf16[128,1152]{1,0:T(8,128)(2,1)S(1)}, bf16[128,1152]{1,0:T(8,128)(2,1)S(1)}, u32[]{:S(2)}, u32[]{:S(2)}) %collective-permute-start.7) | collective-permute-done | bytes 294944 | tf_op jit(solution)/shard_map/ppermute | solution.py:822
  37.4 7.4 %collective-permute-done.6.refs_3_.refs_6_ = bf16[344,1024]{1,0:T(8,128)(2,1)S(1)} collective-permute-done((bf16[344,1024]{1,0:T(8,128)(2,1)S(1)}, bf16[344,1024]{1,0:T(8,128)(2,1)S(1)}, u32[]{:S(2)}, u32[]{:S(2)}) %collective-permute-start.6) | collective-permute-done | bytes 704544 | tf_op jit(solution)/shard_map/ppermute | solution.py:822
  49.2 5.5 %collective-permute-done.14.refs_15_ = bf16[128,1152]{1,0:T(8,128)(2,1)S(1)} collective-permute-done((bf16[128,1152]{1,0:T(8,128)(2,1)}, bf16[128,1152]{1,0:T(8,128)(2,1)S(1)}, u32[]{:S(2)}, u32[]{:S(2)}) %collective-permute-start.14) | collective-permute-done | bytes 294944 | tf_op jit(solution)/shard_map/ppermute | solution.py:822
  58.5 10.7 %collective-permute-done.13.refs_14_ = bf16[128,1152]{1,0:T(8,128)(2,1)S(1)} collective-permute-done((bf16[128,1152]{1,0:T(8,128)(2,1)}, bf16[128,1152]{1,0:T(8,128)(2,1)S(1)}, u32[]{:S(2)}, u32[]{:S(2)}) %collective-permute-start.13) | collective-permute-done | bytes 294944 | tf_op jit(solution)/shard_map/ppermute | solution.py:822
  69.2 5.1 %collective-permute-done.15.refs_16_ = bf16[128,1152]{1,0:T(8,128)(2,1)S(1)} collective-permute-done((bf16[128,1152]{1,0:T(8,128)(2,1)S(1)}, bf16[128,1152]{1,0:T(8,128)(2,1)S(1)}, u32[]{:S(2)}, u32[]{:S(2)}) %collective-permute-start.15) | collective-permute-done | bytes 294944 | tf_op jit(solution)/shard_map/ppermute | solution.py:822
  76.8 8.2 %project.1 = (bf16[1024,768]{1,0:T(8,128)(2,1)}, bf16[1024,256]{1,0:T(8,128)(2,1)}, f32[16,1024]{1,0:T(8,128)}, bf16[1376,1024]{1,0:T(8,128)(2,1)}, bf16[1376,76...) custom-call(s32[2]{0:T(128)} %pad_add_fusion.ids_ref.refs_0_.refs_7_, ...), custom_call_target="tpu_custom_call" | custom-call | flops 1000000000 | bytes 1000000 | tf_op jit(solution)/shard_map/project/pallas_call | solution.py:175
  86.3 15.6 %attend.1 = (f32[1376,256]{1,0:T(8,128)}, f32[2,2,1376]{2,1,0:T(2,128)}, bf16[344,256]{1,0:T(8,128)(2,1)}, bf16[344,256]{1,0:T(8,128)(2,1)}, bf16[344,256]{1,0:T(8,128)(2,1)}, /*index=5*/bf16[344,256]{1,0:T(8,128)(2,1)}) custom-call(bf16[1376,768]{1,0:T(8,128)(2,1)} %get-tuple-element.155.qkv_ref, f32[1376,1]{1,0:T(8,128)} %get-tuple-element.153.bias_ref), custom_call_target="tpu_custom_call" | custom-call | flops 1000000000 | bytes 1000000 | tf_op jit(solution)/shard_map/attend/pallas_call | solution.py:231
  104.8 5.2 %collective-permute-done.18.refs_4_.rest_2_ = bf16[344,256]{1,0:T(8,128)(2,1)S(1)} collective-permute-done((bf16[344,256]{1,0:T(8,128)(2,1)}, bf16[344,256]{1,0:T(8,128)(2,1)S(1)}, u32[]{:S(2)}, u32[]{:S(2)}) %collective-permute-start.18) | collective-permute-done | bytes 176160 | tf_op jit(solution)/shard_map/ppermute | solution.py:822
  113.9 5.3 %middle.1 = (f32[344,1024]{1,0:T(8,128)}, f32[344,1024]{1,0:T(8,128)}, bf16[344,1024]{1,0:T(8,128)(2,1)}, f32[344,1024]{1,0:T(8,128)}, f32[344,1]{1,0:T(8,128)}) custom-call(f32[16,1024]{1,0:T(8,128)} %get-tuple-element.224.refs_0_.refs_5_.rows_ref, bf16[344,1024]{1,0:T(8,128)(2,1)} %bitcast.25, bf16[344,256]{1,0:T(8,128)(2,1)} %get-tuple-element.159.refs_2_.rest_0_, ...), custom_call_target="tpu_custom_call" | custom-call | flops 1000000000 | bytes 1000000 | tf_op jit(solution)/shard_map/middle/pallas_call | solution.py:333
  122.7 12.6 %mlp.2 = (bf16[344,1024]{1,0:T(8,128)(2,1)}, bf16[344,1024]{1,0:T(8,128)(2,1)}, bf16[688,1024]{1,0:T(8,128)(2,1)}, bf16[688,1024]{1,0:T(8,128)(2,1)}, bf16[688,1...) custom-call(f32[16,1024]{1,0:T(8,128)} %get-tuple-element.224.refs_0_.refs_5_.rows_ref, ...), custom_call_target="tpu_custom_call" | custom-call | flops 1000000000 | bytes 1000000 | tf_op jit(solution)/shard_map/mlp/pallas_call | solution.py:475
  140.8 12.9 %mlp.3 = (bf16[344,1024]{1,0:T(8,128)(2,1)}, bf16[344,1024]{1,0:T(8,128)(2,1)}, bf16[688,1024]{1,0:T(8,128)(2,1)}, bf16[688,1024]{1,0:T(8,128)(2,1)}, bf16[688,1...) custom-call(f32[16,1024]{1,0:T(8,128)} %get-tuple-element.224.refs_0_.refs_5_.rows_ref, ...), custom_call_target="tpu_custom_call" | custom-call | flops 1000000000 | bytes 1000000 | tf_op jit(solution)/shard_map/mlp/pallas_call | solution.py:475
  158.4 16.2 %mlp_weights.1 = (bf16[512,2048]{1,0:T(8,128)(2,1)}, bf16[512,2048]{1,0:T(8,128)(2,1)}, f32[1,1024]{1,0:T(1,128)}, bf16[344,1024]{1,0:T(8,128)(2,1)}, bf16[344,1...) custom-call(s32[2]{0:T(128)} %pad_add_fusion.ids_ref.refs_0_.refs_7_, ...), custom_call_target="tpu_custom_call" | custom-call | flops 1000000000 | bytes 1000000 | tf_op jit(solution)/shard_map/mlp_weights/pallas_call | solution.py:541
  176.9 6.1 %turn.1 = (f32[344,1024]{1,0:T(8,128)}, bf16[344,1024]{1,0:T(8,128)(2,1)}, f32[8,1024]{1,0:T(8,128)}, bf16[344,256]{1,0:T(8,128)(2,1)}, bf16[344,256]{1,0:T(8,12...) custom-call(f32[16,1024]{1,0:T(8,128)} %get-tuple-element.224.refs_0_.refs_5_.rows_ref, ...), custom_call_target="tpu_custom_call" | custom-call | flops 1000000000 | bytes 1000000 | tf_op jit(solution)/shard_map/turn/pallas_call | solution.py:369
  189.5 5.2 %collective-permute-done.34.rest_2_ = bf16[344,256]{1,0:T(8,128)(2,1)S(1)} collective-permute-done((bf16[344,256]{1,0:T(8,128)(2,1)}, bf16[344,256]{1,0:T(8,128)(2,1)S(1)}, u32[]{:S(2)}, u32[]{:S(2)}) %collective-permute-start.34) | collective-permute-done | bytes 176160 | tf_op jit(solution)/shard_map/ppermute | solution.py:822
  198.3 24.5 %attend_back.1 = (bf16[1376,768]{1,0:T(8,128)(2,1)}, f32[2,1,384]{2,1,0:T(1,128)}) custom-call(bf16[1376,768]{1,0:T(8,128)(2,1)} %get-tuple-element.155.qkv_ref, f32[1376,1]{1,0:T(8,128)} %get-tuple-element.153.bias_ref, f32[1376,256]{1,0:T(8,128)} %get-tuple-element.156.att_ref, f32[2,2,1376]{2,1,0:T(2,128)} %get-tuple-element.196.lse_ref, ...), custom_call_target="tpu_custom_call" | custom-call | flops 1000000000 | bytes 1000000 | tf_op jit(solution)/shard_map/attend_back/pallas_call | solution.py:290
  222.7 3.9 %add_convert_fusion = bf16[512,2048]{1,0:T(8,128)(2,1)} fusion(bf16[512,2048]{1,0:T(8,128)(2,1)} %collective-permute-done.38, bf16[512,2048]{1,0:T(8,128)(2,1)S(1)} %copy-done.5), kind=kLoop, calls=%fused_computation | loop fusion | flops 4194304 | bytes 6291456 | tf_op jit(solution)/shard_map/convert_element_type | solution.py:968
  228.9 16.5 %collective-permute-done.36.rest_2_ = bf16[344,1024]{1,0:T(8,128)(2,1)S(1)} collective-permute-done((bf16[344,1024]{1,0:T(8,128)(2,1)S(1)}, bf16[344,1024]{1,0:T(8,128)(2,1)S(1)}, u32[]{:S(2)}, u32[]{:S(2)}) %collective-permute-start.36) | collective-permute-done | bytes 704544 | tf_op jit(solution)/shard_map/ppermute | solution.py:822
  245.4 11.0 %collective-permute-done.37.refs_12_ = bf16[1024,256]{1,0:T(8,128)(2,1)S(1)} collective-permute-done((bf16[1024,256]{1,0:T(8,128)(2,1)S(1)}, bf16[1024,256]{1,0:T(8,128)(2,1)S(1)}, u32[]{:S(2)}, u32[]{:S(2)}) %collective-permute-start.37) | collective-permute-done | bytes 524320 | tf_op jit(solution)/shard_map/ppermute | solution.py:822
  256.3 6.9 %qkv_back.1 = (bf16[344,1024]{1,0:T(8,128)(2,1)}, bf16[344,1024]{1,0:T(8,128)(2,1)}, bf16[344,1024]{1,0:T(8,128)(2,1)}, bf16[344,1024]{1,0:T(8,128)(2,1)}, f32[8,1024]{1,0:T(8,128)}) custom-call(bf16[1376,768]{1,0:T(8,128)(2,1)} %get-tuple-element.208.refs_0_.refs_2_, bf16[1024,768]{1,0:T(8,128)(2,1)} %get-tuple-element.209.refs_1_, ...), custom_call_target="tpu_custom_call" | custom-call | flops 1000000000 | bytes 1000000 | tf_op jit(solution)/shard_map/qkv_back/pallas_call | solution.py:630
  264.0 7.5 %attn_weights.1 = (bf16[128,1152]{1,0:T(8,128)(2,1)}, bf16[128,1152]{1,0:T(8,128)(2,1)}, bf16[128,1152]{1,0:T(8,128)(2,1)}, bf16[128,1152]{1,0:T(8,128)(2,1)}, b...) custom-call(s32[2]{0:T(128)} %pad_add_fusion.ids_ref.refs_0_.refs_7_, bf16[1376,1024]{1,0:T(8,128)(2,1)} %get-tuple-element.151.refs_1_, ...), custom_call_target="tpu_custom_call" | custom-call | flops 1000000000 | bytes 1000000 | tf_op jit(solution)/shard_map/attn_weights/pallas_call | solution.py:702
  272.6 14.3 %collective-permute-done.40 = bf16[256,1152]{1,0:T(8,128)(2,1)S(1)} collective-permute-done((bf16[256,1152]{1,0:T(8,128)(2,1)}, bf16[256,1152]{1,0:T(8,128)(2,1)S(1)}, u32[]{:S(2)}, u32[]{:S(2)}) %collective-permute-start.40) | collective-permute-done | bytes 589856 | tf_op jit(solution)/shard_map/ppermute | solution.py:822
  290.1 11.3 %collective-permute-done.42 = bf16[256,1152]{1,0:T(8,128)(2,1)S(1)} collective-permute-done((bf16[256,1152]{1,0:T(8,128)(2,1)}, bf16[256,1152]{1,0:T(8,128)(2,1)S(1)}, u32[]{:S(2)}, u32[]{:S(2)}) %collective-permute-start.42) | collective-permute-done | bytes 589856 | tf_op jit(solution)/shard_map/ppermute | solution.py:822
  306.2 9.2 %collective-permute-done.43.refs_1_ = bf16[128,1152]{1,0:T(8,128)(2,1)S(1)} collective-permute-done((bf16[128,1152]{1,0:T(8,128)(2,1)S(1)}, bf16[128,1152]{1,0:T(8,128)(2,1)S(1)}, u32[]{:S(2)}, u32[]{:S(2)}) %collective-permute-start.43) | collective-permute-done | bytes 294944 | tf_op jit(solution)/shard_map/ppermute | solution.py:822
  323.4 4.0 %begin.1 = bf16[344,1024]{1,0:T(8,128)(2,1)} custom-call(f32[16,1024]{1,0:T(8,128)} %get-tuple-element.224.refs_0_.refs_5_.rows_ref, bf16[344,1024]{1,0:T(8,128)(2,1)} %bitcast.27, f32[1376,1]{1,0:T(8,128)} %get-tuple-element.210.refs_2_.mean_ref, f32[1376,1]{1,0:T(8,128)} %get-tuple-element.211.refs_3_.inv_ref, f32[344,1024]{1,0:T(8,128)} %get-tuple-element.229.middle_ref, ...), custom_call_target="tpu_custom_call" | custom-call | tf_op jit(solution)/shard_map/begin/pallas_call | solution.py:597
  (236 shorter events, 101.9 us)
Async XLA Ops:
  7.2 115.5 %all-gather.2.cloned.1.call-start = ((), (), s32[]{:S(2)}) async-start(), calls=%async_computation.1 | async-start | bytes 4718592 | tf_op jit(solution)/shard_map/all_gather | solution.py:894
  20.3 16.8 %collective-permute-start.7 = (bf16[128,1152]{1,0:T(8,128)(2,1)S(1)}, bf16[128,1152]{1,0:T(8,128)(2,1)S(1)}, u32[]{:S(2)}, u32[]{:S(2)}) collective-permute-start(bf16[128,1152]{1,0:T(8,128)(2,1)S(1)} %constant_dynamic-update-slice_fusion.refs_9_), channel_id=1, source_target_pairs={{0,16},{4,20},{8,24},{12,28},{16,0},{20,4},{24,8},{28,12},{1,17},{... | collective-permute-start | bytes 884744 | tf_op jit(solution)/shard_map/ppermute | solution.py:822
  27.2 17.6 %collective-permute-start.6 = (bf16[344,1024]{1,0:T(8,128)(2,1)S(1)}, bf16[344,1024]{1,0:T(8,128)(2,1)S(1)}, u32[]{:S(2)}, u32[]{:S(2)}) collective-permute-start(bf16[344,1024]{1,0:T(8,128)(2,1)S(1)} %bitcast.28), channel_id=1, source_target_pairs={{0,2},{1,3},{2,0},{3,1},{4,6},{5,7},{6,4},{7,5},{8,10},{9,11},{10,... | collective-permute-start | bytes 2113544 | tf_op jit(solution)/shard_map/ppermute | solution.py:822
  44.9 270.5 %reduce-scatter.2.cloned.1.call-start = ((), (), s32[]{:S(2)}) async-start(), calls=%async_computation.2 | async-start | bytes 2621440 | tf_op jit(solution)/shard_map/reduce_scatter | solution.py:971
  44.9 29.4 %collective-permute-start.10 = (bf16[344,1024]{1,0:T(8,128)(2,1)S(1)}, bf16[344,1024]{1,0:T(8,128)(2,1)S(1)}, u32[]{:S(2)}, u32[]{:S(2)}) collective-permute-start(bf16[344,1024]{1,0:T(8,128)(2,1)S(1)} %bitcast.29), channel_id=1, source_target_pairs={{0,1},{1,0},{2,3},{3,2},{4,5},{5,4},{6,7},{7,6},{8,9},{9,8},{10,11... | collective-permute-start | bytes 2113544 | tf_op jit(solution)/shard_map/ppermute | solution.py:822
  45.0 30.1 %collective-permute-start.11 = (bf16[344,1024]{1,0:T(8,128)(2,1)S(1)}, bf16[344,1024]{1,0:T(8,128)(2,1)S(1)}, u32[]{:S(2)}, u32[]{:S(2)}) collective-permute-start(bf16[344,1024]{1,0:T(8,128)(2,1)S(1)} %collective-permute-done.6.refs_3_.refs_6_), channel_id=1, source_target_pairs={{0,1},{1,0},{2,3},{3,2},{4,5},{5,4},{6,7},{7,6},{8,9},{9,8},{10,11... | collective-permute-start | bytes 2113544 | tf_op jit(solution)/shard_map/ppermute | solution.py:822
  48.7 20.5 %collective-permute-start.13 = (bf16[128,1152]{1,0:T(8,128)(2,1)}, bf16[128,1152]{1,0:T(8,128)(2,1)S(1)}, u32[]{:S(2)}, u32[]{:S(2)}) collective-permute-start(bf16[128,1152]{1,0:T(8,128)(2,1)} %copy-done.26), channel_id=1, source_target_pairs={{0,4},{4,0},{8,12},{12,8},{16,20},{20,16},{24,28},{28,24},{1,5},{5... | collective-permute-start | bytes 884744 | tf_op jit(solution)/shard_map/ppermute | solution.py:822
  54.7 19.6 %collective-permute-start.15 = (bf16[128,1152]{1,0:T(8,128)(2,1)S(1)}, bf16[128,1152]{1,0:T(8,128)(2,1)S(1)}, u32[]{:S(2)}, u32[]{:S(2)}) collective-permute-start(bf16[128,1152]{1,0:T(8,128)(2,1)S(1)} %collective-permute-done.14.refs_15_), channel_id=1, source_target_pairs={{0,4},{4,0},{8,12},{12,8},{16,20},{20,16},{24,28},{28,24},{1,5},{5... | collective-permute-start | bytes 884744 | tf_op jit(solution)/shard_map/ppermute | solution.py:822
  57.9 28.4 %collective-permute-start.16 = (bf16[344,1024]{1,0:T(8,128)(2,1)S(1)}, bf16[344,1024]{1,0:T(8,128)(2,1)}, u32[]{:S(2)}, u32[]{:S(2)}) collective-permute-start(bf16[344,1024]{1,0:T(8,128)(2,1)S(1)} %bitcast.32), channel_id=1, source_target_pairs={{0,2},{1,3},{2,0},{3,1},{4,6},{5,7},{6,4},{7,5},{8,10},{9,11},{10,... | collective-permute-start | bytes 2113544 | tf_op jit(solution)/shard_map/ppermute | solution.py:822
  85.0 16.8 %collective-permute-start.21 = (bf16[1024,256]{1,0:T(8,128)(2,1)}, bf16[1024,256]{1,0:T(8,128)(2,1)S(1)}, u32[]{:S(2)}, u32[]{:S(2)}) collective-permute-start(bf16[1024,256]{1,0:T(8,128)(2,1)} %get-tuple-element.163.refs_6_.refs_9_), channel_id=1, source_target_pairs={{0,2},{1,3},{2,0},{3,1},{4,6},{5,7},{6,4},{7,5},{8,10},{9,11},{10,... | collective-permute-start | bytes 1572872 | tf_op jit(solution)/shard_map/ppermute | solution.py:822
  86.2 26.6 %collective-permute-start.20 = (bf16[1024,256]{1,0:T(8,128)(2,1)}, bf16[1024,256]{1,0:T(8,128)(2,1)S(1)}, u32[]{:S(2)}, u32[]{:S(2)}) collective-permute-start(bf16[1024,256]{1,0:T(8,128)(2,1)} %get-tuple-element.163.refs_6_.refs_9_), channel_id=1, source_target_pairs={{0,1},{1,0},{2,3},{3,2},{4,5},{5,4},{6,7},{7,6},{8,9},{9,8},{10,11... | collective-permute-start | bytes 1572872 | tf_op jit(solution)/shard_map/ppermute | solution.py:822
  119.8 18.0 %collective-permute-start.26 = (bf16[344,1024]{1,0:T(8,128)(2,1)}, bf16[344,1024]{1,0:T(8,128)(2,1)S(1)}, u32[]{:S(2)}, u32[]{:S(2)}) collective-permute-start(bf16[344,1024]{1,0:T(8,128)(2,1)} %get-tuple-element.168.refs_1_), channel_id=1, source_target_pairs={{0,2},{1,3},{2,0},{3,1},{4,6},{5,7},{6,4},{7,5},{8,10},{9,11},{10,... | collective-permute-start | bytes 2113544 | tf_op jit(solution)/shard_map/ppermute | solution.py:822
  120.7 17.1 %collective-permute-start.28 = (bf16[344,1024]{1,0:T(8,128)(2,1)}, bf16[344,1024]{1,0:T(8,128)(2,1)S(1)}, u32[]{:S(2)}, u32[]{:S(2)}) collective-permute-start(bf16[344,1024]{1,0:T(8,128)(2,1)} %collective-permute-done.16.refs_3_), channel_id=1, source_target_pairs={{0,1},{1,0},{2,3},{3,2},{4,5},{5,4},{6,7},{7,6},{8,9},{9,8},{10,11... | collective-permute-start | bytes 2113544 | tf_op jit(solution)/shard_map/ppermute | solution.py:822
  153.9 20.7 %collective-permute-start.25 = (bf16[344,1024]{1,0:T(8,128)(2,1)S(1)}, bf16[344,1024]{1,0:T(8,128)(2,1)S(1)}, u32[]{:S(2)}, u32[]{:S(2)}) collective-permute-start(bf16[344,1024]{1,0:T(8,128)(2,1)S(1)} %copy-done.49), channel_id=1, source_target_pairs={{0,1},{1,0},{2,3},{3,2},{4,5},{5,4},{6,7},{7,6},{8,9},{9,8},{10,11... | collective-permute-start | bytes 2113544 | tf_op jit(solution)/shard_map/ppermute | solution.py:822
  157.5 17.9 %collective-permute-start.30 = (bf16[344,1024]{1,0:T(8,128)(2,1)S(1)}, bf16[344,1024]{1,0:T(8,128)(2,1)S(1)}, u32[]{:S(2)}, u32[]{:S(2)}) collective-permute-start(bf16[344,1024]{1,0:T(8,128)(2,1)S(1)} %add_convert_fusion.3), channel_id=1, source_target_pairs={{0,2},{1,3},{2,0},{3,1},{4,6},{5,7},{6,4},{7,5},{8,10},{9,11},{10,... | collective-permute-start | bytes 2113544 | tf_op jit(solution)/shard_map/ppermute | solution.py:822
  175.4 47.3 %collective-permute-start.38 = (bf16[512,2048]{1,0:T(8,128)(2,1)}, bf16[512,2048]{1,0:T(8,128)(2,1)}, u32[]{:S(2)}, u32[]{:S(2)}) collective-permute-start(bf16[512,2048]{1,0:T(8,128)(2,1)} %get-tuple-element.206), channel_id=1, source_target_pairs={{0,4},{4,0},{8,12},{12,8},{16,20},{20,16},{24,28},{28,24},{1,5},{5... | collective-permute-start | bytes 6291464 | tf_op jit(solution)/shard_map/ppermute | solution.py:822
  226.7 18.7 %collective-permute-start.36 = (bf16[344,1024]{1,0:T(8,128)(2,1)S(1)}, bf16[344,1024]{1,0:T(8,128)(2,1)S(1)}, u32[]{:S(2)}, u32[]{:S(2)}) collective-permute-start(bf16[344,1024]{1,0:T(8,128)(2,1)S(1)} %add_convert_fusion.2), channel_id=1, source_target_pairs={{0,2},{1,3},{2,0},{3,1},{4,6},{5,7},{6,4},{7,5},{8,10},{9,11},{10,... | collective-permute-start | bytes 2113544 | tf_op jit(solution)/shard_map/ppermute | solution.py:822
  227.6 28.8 %collective-permute-start.37 = (bf16[1024,256]{1,0:T(8,128)(2,1)S(1)}, bf16[1024,256]{1,0:T(8,128)(2,1)S(1)}, u32[]{:S(2)}, u32[]{:S(2)}) collective-permute-start(bf16[1024,256]{1,0:T(8,128)(2,1)S(1)} %add_convert_fusion.4), channel_id=1, source_target_pairs={{0,2},{1,3},{2,0},{3,1},{4,6},{5,7},{6,4},{7,5},{8,10},{9,11},{10,... | collective-permute-start | bytes 1572872 | tf_op jit(solution)/shard_map/ppermute | solution.py:822
  228.8 34.5 %collective-permute-start.39 = (bf16[1024,256]{1,0:T(8,128)(2,1)S(1)}, bf16[1024,256]{1,0:T(8,128)(2,1)S(1)}, u32[]{:S(2)}, u32[]{:S(2)}) collective-permute-start(bf16[1024,256]{1,0:T(8,128)(2,1)S(1)} %copy-done.51), channel_id=1, source_target_pairs={{0,1},{1,0},{2,3},{3,2},{4,5},{5,4},{6,7},{7,6},{8,9},{9,8},{10,11... | collective-permute-start | bytes 1572872 | tf_op jit(solution)/shard_map/ppermute | solution.py:822
  272.1 16.6 %collective-permute-start.46 = (bf16[344,1024]{1,0:T(8,128)(2,1)S(1)}, bf16[344,1024]{1,0:T(8,128)(2,1)S(1)}, u32[]{:S(2)}, u32[]{:S(2)}) collective-permute-start(bf16[344,1024]{1,0:T(8,128)(2,1)S(1)} %copy-done.50), channel_id=1, source_target_pairs={{0,1},{1,0},{2,3},{3,2},{4,5},{5,4},{6,7},{7,6},{8,9},{9,8},{10,11... | collective-permute-start | bytes 2113544 | tf_op jit(solution)/shard_map/ppermute | solution.py:822
  272.1 45.3 %collective-permute-start.44 = (bf16[344,1024]{1,0:T(8,128)(2,1)}, bf16[344,1024]{1,0:T(8,128)(2,1)S(1)}, u32[]{:S(2)}, u32[]{:S(2)}) collective-permute-start(bf16[344,1024]{1,0:T(8,128)(2,1)} %get-tuple-element.227), channel_id=1, source_target_pairs={{0,1},{1,0},{2,3},{3,2},{4,5},{5,4},{6,7},{7,6},{8,9},{9,8},{10,11... | collective-permute-start | bytes 2113544 | tf_op jit(solution)/shard_map/ppermute | solution.py:822
  272.6 46.0 %collective-permute-start.45 = (bf16[344,1024]{1,0:T(8,128)(2,1)}, bf16[344,1024]{1,0:T(8,128)(2,1)S(1)}, u32[]{:S(2)}, u32[]{:S(2)}) collective-permute-start(bf16[344,1024]{1,0:T(8,128)(2,1)} %get-tuple-element.231), channel_id=1, source_target_pairs={{0,1},{1,0},{2,3},{3,2},{4,5},{5,4},{6,7},{7,6},{8,9},{9,8},{10,11... | collective-permute-start | bytes 2113544 | tf_op jit(solution)/shard_map/ppermute | solution.py:822
  289.0 33.5 %collective-permute-start.47 = (bf16[344,1024]{1,0:T(8,128)(2,1)S(1)}, bf16[344,1024]{1,0:T(8,128)(2,1)S(1)}, u32[]{:S(2)}, u32[]{:S(2)}) collective-permute-start(bf16[344,1024]{1,0:T(8,128)(2,1)S(1)} %add_convert_fusion.1), channel_id=1, source_target_pairs={{0,2},{1,3},{2,0},{3,1},{4,6},{5,7},{6,4},{7,5},{8,10},{9,11},{10,... | collective-permute-start | bytes 2113544 | tf_op jit(solution)/shard_map/ppermute | solution.py:822
  303.4 26.9 %collective-permute-start.51 = (bf16[128,1152]{1,0:T(8,128)(2,1)}, bf16[128,1152]{1,0:T(8,128)(2,1)S(1)}, u32[]{:S(2)}, u32[]{:S(2)}) collective-permute-start(bf16[128,1152]{1,0:T(8,128)(2,1)} %add_convert_fusion.5), channel_id=1, source_target_pairs={{0,16},{4,20},{8,24},{12,28},{16,0},{20,4},{24,8},{28,12},{1,17},{... | collective-permute-start | bytes 884744 | tf_op jit(solution)/shard_map/ppermute | solution.py:822
  (88 other events, 672.1 us)
Sparse Core Ops, SparseCore 0:
  45.0 77.6 all-gather.1
  226.8 43.3 reduce-scatter.1

commit v4 on v3

--- a/solution.py
+++ b/solution.py
@@ -884,12 +884,14 @@
         shards = {0: jnp.concatenate(first, axis=0)}
         for bit in (4, 2, 1):
             shards[bit] = swap(shards[0], bit, "dp")
-        arrived = [tokens_far] + [shards[bit] for bit in (4, 2, 1)] + second[1:]
+        arrived = [shards[bit] for bit in (4, 2, 1)] + second[1:]
         widen(shards, *arrived)
+        shards[7] = swap(after(shards[6], tokens_far), 1, "dp")
         first_pieces = [shards[m] for m in range(replicas)]
+        nearly = [shards[6], shards[3], shards[5]]
     else:
         first_pieces = [lax.all_gather(in_order(first), "dp", axis=0, tiled=True)]
-        arrived = [tokens_far]
+        arrived = nearly = [tokens_far]
     second_shard = after(in_order(second), *arrived)
     second_all = lax.all_gather(second_shard, "dp", axis=0, tiled=True)
     tokens_pieces = [tokens[0]]
@@ -898,7 +900,7 @@
         if j == group // 2:
             tokens_pieces.append(tokens_far)
         else:
-            tokens_pieces.append(swap(after(source, *arrived), j & -j))
+            tokens_pieces.append(swap(after(source, *nearly), j & -j))
     cotangent_far = swap(after(cotangent[0], *arrived), group // 2)
 
     tokens_own = after(tokens[0], second_shard)
@@ -960,9 +962,9 @@
     att_grads = exchange(att_grads)
     mids = []
     proj_terms = scatter(proj_weights(branch_grad, attended_own), *att_grads, mids=mids)
-    branch2_terms = scatter(branches, *att_grads, mids=mids)
+    branch2_terms = scatter(branches, *att_grads)
     qkv_grad, qkv_sums = attend_back(qkv, key_bias, attended, after(lse, *mids), att_grads)
-    pending = [branch2_terms[-1], proj_terms[-1]]
+    pending = []
     if direct:
         other = after(other_mlp, qkv_grad)
         summed = (keep_mlp.astype(F32) + other.astype(F32)).astype(BF)
@@ -997,7 +999,7 @@
         far = swap(add(add(keep2, other32[size:]), across), 4, "dp")
         across0 = swap(add(keep1, other10[:size]), 2, "dp")
         terms = [add(keep0, other10[size:]), across0, far]
-        settled = [across, across0]
+        settled = [across]
         cuts_mlp = total(after(ids, *settled), [owned_mlp], group)
     else:
         owned_attn = lax.psum_scatter(parts[0], "dp", scatter_dimension=0, tiled=True)

time: 354 us -> 330 us (0.932)
  waiting for transfers between devices: 134 us -> 105 us
    ppermute x55, waiting for transfers between devices: 133 us -> 105 us  [swap(): return lax.ppermute(value, axis, [(i, i ^ bit) for i in range(size)])]
    unnamed x113 -> x117, local copies, waits for them, and re-layouts: 9.67 us -> 10.7 us
  transfers between devices with their start and end apart: 57 -> 57, of which waited for: 28 -> 25; matrix products, arithmetic and copies ran while one was open for 2% -> 3% of each run, Pallas kernels for 34% -> 36%
where the time goes in v4:
time: 330 us; the launch traced here: 325 us
  Pallas kernels  137 us (42%)
  waiting for transfers between devices  105 us (32%)
  starting transfers between devices  44.6 us (14%)
  between operations  15.6 us (5%)
  other arithmetic  12.2 us (4%)
  local copies, waits for them, and re-layouts  10.7 us (3%)
    ppermute x55, waiting for transfers between devices, swap(): return lax.ppermute(value, axis, [(i, i ^ bit) for i in range(size)])  105 us
    ppermute x55, starting transfers between devices, swap(): return lax.ppermute(value, axis, [(i, i ^ bit) for i in range(size)])  44.6 us
    pallas_call x2, Pallas kernels, mlp(): pl.pallas_call(lambda *refs: mlp_kernel(count, shards, group, *refs), gri...  25.3 us
    pallas_call x1, Pallas kernels, attend_back(): pl.pallas_call(attend_back_kernel, grid=(pairs,), in_specs=[pl.BlockSpec(...  24.4 us
    pallas_call x1, Pallas kernels, mlp_weights(): pl.pallas_call(lambda *refs: mlp_weights_kernel(direct, *refs), grid_spec...  16.1 us
    pallas_call x1, Pallas kernels, attend(): pl.pallas_call(attend_kernel, grid=(pairs,), in_specs=[pl.BlockSpec((leng...  15.6 us
    unnamed x117, local copies, waits for them, and re-layouts  10.7 us
    pallas_call x1, Pallas kernels, project(): pl.pallas_call(lambda *refs: project_kernel(ordered, group, count_column,...  8.76 us
  transfers between devices with their start and end apart: 57, of which 25 were waited for; matrix products, arithmetic and copies ran while one was open for 3% of the time, Pallas kernels for 36%

profile of v4, /device:TPU:0, one launch (start us, length us, event | category | flops | bytes accessed | tf_op | source)
XLA Modules:
  0.0 325.5 jit_solution(10083899847019329224)
XLA Ops:
  29.0 8.0 %collective-permute-done.6.refs_13_ = bf16[128,1152]{1,0:T(8,128)(2,1)S(1)} collective-permute-done((bf16[128,1152]{1,0:T(8,128)(2,1)S(1)}, bf16[128,1152]{1,0:T(8,128)(2,1)S(1)}, u32[]{:S(2)}, u32[]{:S(2)}) %collective-permute-start.6) | collective-permute-done | bytes 294944 | tf_op jit(solution)/shard_map/ppermute | solution.py:822
  42.9 4.7 %collective-permute-done.9.refs_15_ = bf16[128,1152]{1,0:T(8,128)(2,1)S(1)} collective-permute-done((bf16[128,1152]{1,0:T(8,128)(2,1)S(1)}, bf16[128,1152]{1,0:T(8,128)(2,1)S(1)}, u32[]{:S(2)}, u32[]{:S(2)}) %collective-permute-start.9) | collective-permute-done | bytes 294944 | tf_op jit(solution)/shard_map/ppermute | solution.py:822
  47.5 5.2 %collective-permute-done.10.refs_12_ = bf16[128,1152]{1,0:T(8,128)(2,1)S(1)} collective-permute-done((bf16[128,1152]{1,0:T(8,128)(2,1)S(1)}, bf16[128,1152]{1,0:T(8,128)(2,1)S(1)}, u32[]{:S(2)}, u32[]{:S(2)}) %collective-permute-start.10) | collective-permute-done | bytes 294944 | tf_op jit(solution)/shard_map/ppermute | solution.py:822
  52.7 8.2 %collective-permute-done.11.refs_14_ = bf16[128,1152]{1,0:T(8,128)(2,1)S(1)} collective-permute-done((bf16[128,1152]{1,0:T(8,128)(2,1)S(1)}, bf16[128,1152]{1,0:T(8,128)(2,1)S(1)}, u32[]{:S(2)}, u32[]{:S(2)}) %collective-permute-start.11) | collective-permute-done | bytes 294944 | tf_op jit(solution)/shard_map/ppermute | solution.py:822
  63.3 7.0 %collective-permute-done.15.refs_16_ = bf16[128,1152]{1,0:T(8,128)(2,1)S(1)} collective-permute-done((bf16[128,1152]{1,0:T(8,128)(2,1)S(1)}, bf16[128,1152]{1,0:T(8,128)(2,1)S(1)}, u32[]{:S(2)}, u32[]{:S(2)}) %collective-permute-start.15) | collective-permute-done | bytes 294944 | tf_op jit(solution)/shard_map/ppermute | solution.py:822
  72.8 8.8 %project.1 = (bf16[1024,768]{1,0:T(8,128)(2,1)}, bf16[1024,256]{1,0:T(8,128)(2,1)}, f32[16,1024]{1,0:T(8,128)}, bf16[1376,1024]{1,0:T(8,128)(2,1)}, bf16[1376,76...) custom-call(s32[2]{0:T(128)} %pad_add_fusion.ids_ref.refs_0_.refs_7_, ...), custom_call_target="tpu_custom_call" | custom-call | flops 1000000000 | bytes 1000000 | tf_op jit(solution)/shard_map/project/pallas_call | solution.py:175
  81.7 15.6 %attend.1 = (f32[1376,256]{1,0:T(8,128)}, f32[2,2,1376]{2,1,0:T(2,128)}, bf16[344,256]{1,0:T(8,128)(2,1)}, bf16[344,256]{1,0:T(8,128)(2,1)}, bf16[344,256]{1,0:T(8,128)(2,1)}, /*index=5*/bf16[344,256]{1,0:T(8,128)(2,1)}) custom-call(bf16[1376,768]{1,0:T(8,128)(2,1)} %get-tuple-element.155.qkv_ref, f32[1376,1]{1,0:T(8,128)} %get-tuple-element.153.bias_ref), custom_call_target="tpu_custom_call" | custom-call | flops 1000000000 | bytes 1000000 | tf_op jit(solution)/shard_map/attend/pallas_call | solution.py:231
  100.3 5.2 %collective-permute-done.18.refs_4_.rest_2_ = bf16[344,256]{1,0:T(8,128)(2,1)S(1)} collective-permute-done((bf16[344,256]{1,0:T(8,128)(2,1)}, bf16[344,256]{1,0:T(8,128)(2,1)S(1)}, u32[]{:S(2)}, u32[]{:S(2)}) %collective-permute-start.18) | collective-permute-done | bytes 176160 | tf_op jit(solution)/shard_map/ppermute | solution.py:822
  109.7 5.3 %middle.1 = (f32[344,1024]{1,0:T(8,128)}, f32[344,1024]{1,0:T(8,128)}, bf16[344,1024]{1,0:T(8,128)(2,1)}, f32[344,1024]{1,0:T(8,128)}, f32[344,1]{1,0:T(8,128)}) custom-call(f32[16,1024]{1,0:T(8,128)} %get-tuple-element.218.refs_0_.refs_5_.rows_ref, bf16[344,1024]{1,0:T(8,128)(2,1)} %bitcast.25, bf16[344,256]{1,0:T(8,128)(2,1)} %get-tuple-element.159.refs_2_.rest_0_, ...), custom_call_target="tpu_custom_call" | custom-call | flops 1000000000 | bytes 1000000 | tf_op jit(solution)/shard_map/middle/pallas_call | solution.py:333
  118.4 12.5 %mlp.2 = (bf16[344,1024]{1,0:T(8,128)(2,1)}, bf16[344,1024]{1,0:T(8,128)(2,1)}, bf16[688,1024]{1,0:T(8,128)(2,1)}, bf16[688,1024]{1,0:T(8,128)(2,1)}, bf16[688,1...) custom-call(f32[16,1024]{1,0:T(8,128)} %get-tuple-element.218.refs_0_.refs_5_.rows_ref, ...), custom_call_target="tpu_custom_call" | custom-call | flops 1000000000 | bytes 1000000 | tf_op jit(solution)/shard_map/mlp/pallas_call | solution.py:475
  136.6 12.8 %mlp.3 = (bf16[344,1024]{1,0:T(8,128)(2,1)}, bf16[344,1024]{1,0:T(8,128)(2,1)}, bf16[688,1024]{1,0:T(8,128)(2,1)}, bf16[688,1024]{1,0:T(8,128)(2,1)}, bf16[688,1...) custom-call(f32[16,1024]{1,0:T(8,128)} %get-tuple-element.218.refs_0_.refs_5_.rows_ref, ...), custom_call_target="tpu_custom_call" | custom-call | flops 1000000000 | bytes 1000000 | tf_op jit(solution)/shard_map/mlp/pallas_call | solution.py:475
  154.9 16.1 %mlp_weights.1 = (bf16[512,2048]{1,0:T(8,128)(2,1)}, bf16[512,2048]{1,0:T(8,128)(2,1)}, f32[1,1024]{1,0:T(1,128)}, bf16[344,1024]{1,0:T(8,128)(2,1)}, bf16[344,1...) custom-call(s32[2]{0:T(128)} %pad_add_fusion.ids_ref.refs_0_.refs_7_, ...), custom_call_target="tpu_custom_call" | custom-call | flops 1000000000 | bytes 1000000 | tf_op jit(solution)/shard_map/mlp_weights/pallas_call | solution.py:541
  172.6 6.0 %turn.1 = (f32[344,1024]{1,0:T(8,128)}, bf16[344,1024]{1,0:T(8,128)(2,1)}, f32[8,1024]{1,0:T(8,128)}, bf16[344,256]{1,0:T(8,128)(2,1)}, bf16[344,256]{1,0:T(8,12...) custom-call(f32[16,1024]{1,0:T(8,128)} %get-tuple-element.218.refs_0_.refs_5_.rows_ref, ...), custom_call_target="tpu_custom_call" | custom-call | flops 1000000000 | bytes 1000000 | tf_op jit(solution)/shard_map/turn/pallas_call | solution.py:369
  185.8 4.5 %collective-permute-done.33.rest_2_ = bf16[344,256]{1,0:T(8,128)(2,1)S(1)} collective-permute-done((bf16[344,256]{1,0:T(8,128)(2,1)S(1)}, bf16[344,256]{1,0:T(8,128)(2,1)S(1)}, u32[]{:S(2)}, u32[]{:S(2)}) %collective-permute-start.33) | collective-permute-done | bytes 176160 | tf_op jit(solution)/shard_map/ppermute | solution.py:822
  192.9 24.4 %attend_back.1 = (bf16[1376,768]{1,0:T(8,128)(2,1)}, f32[2,1,384]{2,1,0:T(1,128)}) custom-call(bf16[1376,768]{1,0:T(8,128)(2,1)} %get-tuple-element.155.qkv_ref, f32[1376,1]{1,0:T(8,128)} %get-tuple-element.153.bias_ref, f32[1376,256]{1,0:T(8,128)} %get-tuple-element.156.att_ref, f32[2,2,1376]{2,1,0:T(2,128)} %get-tuple-element.184.lse_ref, ...), custom_call_target="tpu_custom_call" | custom-call | flops 1000000000 | bytes 1000000 | tf_op jit(solution)/shard_map/attend_back/pallas_call | solution.py:290
  218.9 3.8 %add_convert_fusion = bf16[512,2048]{1,0:T(8,128)(2,1)} fusion(bf16[512,2048]{1,0:T(8,128)(2,1)} %collective-permute-done.35, bf16[512,2048]{1,0:T(8,128)(2,1)S(1)} %copy-done.5), kind=kLoop, calls=%fused_computation | loop fusion | flops 4194304 | bytes 6291456 | tf_op jit(solution)/shard_map/convert_element_type | solution.py:970
  225.0 6.8 %qkv_back.1 = (bf16[344,1024]{1,0:T(8,128)(2,1)}, bf16[344,1024]{1,0:T(8,128)(2,1)}, bf16[344,1024]{1,0:T(8,128)(2,1)}, bf16[344,1024]{1,0:T(8,128)(2,1)}, f32[8,1024]{1,0:T(8,128)}) custom-call(bf16[1376,768]{1,0:T(8,128)(2,1)} %get-tuple-element.204.refs_0_.refs_2_, bf16[1024,768]{1,0:T(8,128)(2,1)} %get-tuple-element.205.refs_1_, ...), custom_call_target="tpu_custom_call" | custom-call | flops 1000000000 | bytes 1000000 | tf_op jit(solution)/shard_map/qkv_back/pallas_call | solution.py:630
  231.7 6.4 %collective-permute-done.37.refs_12_ = bf16[1024,256]{1,0:T(8,128)(2,1)S(1)} collective-permute-done((bf16[1024,256]{1,0:T(8,128)(2,1)S(1)}, bf16[1024,256]{1,0:T(8,128)(2,1)S(1)}, u32[]{:S(2)}, u32[]{:S(2)}) %collective-permute-start.37) | collective-permute-done | bytes 524320 | tf_op jit(solution)/shard_map/ppermute | solution.py:822
  238.9 7.5 %attn_weights.1 = (bf16[128,1152]{1,0:T(8,128)(2,1)}, bf16[128,1152]{1,0:T(8,128)(2,1)}, bf16[128,1152]{1,0:T(8,128)(2,1)}, bf16[128,1152]{1,0:T(8,128)(2,1)}, b...) custom-call(s32[2]{0:T(128)} %pad_add_fusion.ids_ref.refs_0_.refs_7_, bf16[1376,1024]{1,0:T(8,128)(2,1)} %get-tuple-element.151.refs_1_, ...), custom_call_target="tpu_custom_call" | custom-call | flops 1000000000 | bytes 1000000 | tf_op jit(solution)/shard_map/attn_weights/pallas_call | solution.py:702
  248.4 13.3 %collective-permute-done.38 = bf16[256,1152]{1,0:T(8,128)(2,1)S(1)} collective-permute-done((bf16[256,1152]{1,0:T(8,128)(2,1)}, bf16[256,1152]{1,0:T(8,128)(2,1)S(1)}, u32[]{:S(2)}, u32[]{:S(2)}) %collective-permute-start.38) | collective-permute-done | bytes 589856 | tf_op jit(solution)/shard_map/ppermute | solution.py:822
  266.1 5.6 %collective-permute-done.39 = bf16[128,1152]{1,0:T(8,128)(2,1)S(1)} collective-permute-done((bf16[128,1152]{1,0:T(8,128)(2,1)S(1)}, bf16[128,1152]{1,0:T(8,128)(2,1)S(1)}, u32[]{:S(2)}, u32[]{:S(2)}) %collective-permute-start.39) | collective-permute-done | bytes 294944 | tf_op jit(solution)/shard_map/ppermute | solution.py:822
  273.8 6.1 %collective-permute-done.49 = bf16[256,1152]{1,0:T(8,128)(2,1)S(1)} collective-permute-done((bf16[256,1152]{1,0:T(8,128)(2,1)S(1)}, bf16[256,1152]{1,0:T(8,128)(2,1)S(1)}, u32[]{:S(2)}, u32[]{:S(2)}) %collective-permute-start.49) | collective-permute-done | bytes 589856 | tf_op jit(solution)/shard_map/ppermute | solution.py:822
  288.8 7.9 %collective-permute-done.45.rest_2_ = bf16[344,1024]{1,0:T(8,128)(2,1)S(1)} collective-permute-done((bf16[344,1024]{1,0:T(8,128)(2,1)S(1)}, bf16[344,1024]{1,0:T(8,128)(2,1)S(1)}, u32[]{:S(2)}, u32[]{:S(2)}) %collective-permute-start.45) | collective-permute-done | bytes 704544 | tf_op jit(solution)/shard_map/ppermute | solution.py:822
  300.1 4.0 %begin.1 = bf16[344,1024]{1,0:T(8,128)(2,1)} custom-call(f32[16,1024]{1,0:T(8,128)} %get-tuple-element.218.refs_0_.refs_5_.rows_ref, bf16[344,1024]{1,0:T(8,128)(2,1)} %bitcast.27, f32[1376,1]{1,0:T(8,128)} %get-tuple-element.206.refs_2_.mean_ref, f32[1376,1]{1,0:T(8,128)} %get-tuple-element.207.refs_3_.inv_ref, f32[344,1024]{1,0:T(8,128)} %get-tuple-element.226.middle_ref, ...), custom_call_target="tpu_custom_call" | custom-call | tf_op jit(solution)/shard_map/begin/pallas_call | solution.py:597
  (240 shorter events, 104.1 us)
Async XLA Ops:
  7.2 110.4 %all-gather.2.cloned.1.call-start = ((), (), s32[]{:S(2)}) async-start(), calls=%async_computation.1 | async-start | bytes 4718592 | tf_op jit(solution)/shard_map/all_gather | solution.py:896
  20.2 16.8 %collective-permute-start.6 = (bf16[128,1152]{1,0:T(8,128)(2,1)S(1)}, bf16[128,1152]{1,0:T(8,128)(2,1)S(1)}, u32[]{:S(2)}, u32[]{:S(2)}) collective-permute-start(bf16[128,1152]{1,0:T(8,128)(2,1)S(1)} %constant_dynamic-update-slice_fusion.refs_9_), channel_id=1, source_target_pairs={{0,16},{4,20},{8,24},{12,28},{16,0},{20,4},{24,8},{28,12},{1,17},{... | collective-permute-start | bytes 884744 | tf_op jit(solution)/shard_map/ppermute | solution.py:822
  37.2 248.3 %reduce-scatter.2.cloned.1.call-start = ((), (), s32[]{:S(2)}) async-start(), calls=%async_computation.2 | async-start | bytes 2621440 | tf_op jit(solution)/shard_map/reduce_scatter | solution.py:973
  38.0 22.9 %collective-permute-start.13 = (bf16[344,1024]{1,0:T(8,128)(2,1)S(1)}, bf16[344,1024]{1,0:T(8,128)(2,1)S(1)}, u32[]{:S(2)}, u32[]{:S(2)}) collective-permute-start(bf16[344,1024]{1,0:T(8,128)(2,1)S(1)} %bitcast.28), channel_id=1, source_target_pairs={{0,2},{1,3},{2,0},{3,1},{4,6},{5,7},{6,4},{7,5},{8,10},{9,11},{10,... | collective-permute-start | bytes 2113544 | tf_op jit(solution)/shard_map/ppermute | solution.py:822
  42.4 18.5 %collective-permute-start.11 = (bf16[128,1152]{1,0:T(8,128)(2,1)S(1)}, bf16[128,1152]{1,0:T(8,128)(2,1)S(1)}, u32[]{:S(2)}, u32[]{:S(2)}) collective-permute-start(bf16[128,1152]{1,0:T(8,128)(2,1)S(1)} %collective-permute-done.6.refs_13_), channel_id=1, source_target_pairs={{0,4},{4,0},{8,12},{12,8},{16,20},{20,16},{24,28},{28,24},{1,5},{5... | collective-permute-start | bytes 884744 | tf_op jit(solution)/shard_map/ppermute | solution.py:822
  62.9 18.8 %collective-permute-start.16 = (bf16[344,1024]{1,0:T(8,128)(2,1)S(1)}, bf16[344,1024]{1,0:T(8,128)(2,1)}, u32[]{:S(2)}, u32[]{:S(2)}) collective-permute-start(bf16[344,1024]{1,0:T(8,128)(2,1)S(1)} %bitcast.32), channel_id=1, source_target_pairs={{0,2},{1,3},{2,0},{3,1},{4,6},{5,7},{6,4},{7,5},{8,10},{9,11},{10,... | collective-permute-start | bytes 2113544 | tf_op jit(solution)/shard_map/ppermute | solution.py:822
  81.6 15.7 %collective-permute-start.21 = (bf16[1024,256]{1,0:T(8,128)(2,1)}, bf16[1024,256]{1,0:T(8,128)(2,1)S(1)}, u32[]{:S(2)}, u32[]{:S(2)}) collective-permute-start(bf16[1024,256]{1,0:T(8,128)(2,1)} %get-tuple-element.163.refs_6_.refs_9_), channel_id=1, source_target_pairs={{0,2},{1,3},{2,0},{3,1},{4,6},{5,7},{6,4},{7,5},{8,10},{9,11},{10,... | collective-permute-start | bytes 1572872 | tf_op jit(solution)/shard_map/ppermute | solution.py:822
  81.7 27.0 %collective-permute-start.20 = (bf16[1024,256]{1,0:T(8,128)(2,1)}, bf16[1024,256]{1,0:T(8,128)(2,1)S(1)}, u32[]{:S(2)}, u32[]{:S(2)}) collective-permute-start(bf16[1024,256]{1,0:T(8,128)(2,1)} %get-tuple-element.163.refs_6_.refs_9_), channel_id=1, source_target_pairs={{0,1},{1,0},{2,3},{3,2},{4,5},{5,4},{6,7},{7,6},{8,9},{9,8},{10,11... | collective-permute-start | bytes 1572872 | tf_op jit(solution)/shard_map/ppermute | solution.py:822
  100.0 17.3 %collective-permute-start.24 = (bf16[344,1024]{1,0:T(8,128)(2,1)S(1)}, bf16[344,1024]{1,0:T(8,128)(2,1)S(1)}, u32[]{:S(2)}, u32[]{:S(2)}) collective-permute-start(bf16[344,1024]{1,0:T(8,128)(2,1)S(1)} %bitcast.33), channel_id=1, source_target_pairs={{0,1},{1,0},{2,3},{3,2},{4,5},{5,4},{6,7},{7,6},{8,9},{9,8},{10,11... | collective-permute-start | bytes 2113544 | tf_op jit(solution)/shard_map/ppermute | solution.py:822
  115.5 18.0 %collective-permute-start.26 = (bf16[344,1024]{1,0:T(8,128)(2,1)}, bf16[344,1024]{1,0:T(8,128)(2,1)S(1)}, u32[]{:S(2)}, u32[]{:S(2)}) collective-permute-start(bf16[344,1024]{1,0:T(8,128)(2,1)} %get-tuple-element.168.refs_1_), channel_id=1, source_target_pairs={{0,2},{1,3},{2,0},{3,1},{4,6},{5,7},{6,4},{7,5},{8,10},{9,11},{10,... | collective-permute-start | bytes 2113544 | tf_op jit(solution)/shard_map/ppermute | solution.py:822
  117.3 16.2 %collective-permute-start.28 = (bf16[344,1024]{1,0:T(8,128)(2,1)}, bf16[344,1024]{1,0:T(8,128)(2,1)S(1)}, u32[]{:S(2)}, u32[]{:S(2)}) collective-permute-start(bf16[344,1024]{1,0:T(8,128)(2,1)} %collective-permute-done.16.refs_3_), channel_id=1, source_target_pairs={{0,1},{1,0},{2,3},{3,2},{4,5},{5,4},{6,7},{7,6},{8,9},{9,8},{10,11... | collective-permute-start | bytes 2113544 | tf_op jit(solution)/shard_map/ppermute | solution.py:822
  149.5 21.5 %collective-permute-start.25 = (bf16[344,1024]{1,0:T(8,128)(2,1)S(1)}, bf16[344,1024]{1,0:T(8,128)(2,1)S(1)}, u32[]{:S(2)}, u32[]{:S(2)}) collective-permute-start(bf16[344,1024]{1,0:T(8,128)(2,1)S(1)} %copy-done.48), channel_id=1, source_target_pairs={{0,1},{1,0},{2,3},{3,2},{4,5},{5,4},{6,7},{7,6},{8,9},{9,8},{10,11... | collective-permute-start | bytes 2113544 | tf_op jit(solution)/shard_map/ppermute | solution.py:822
  153.1 18.0 %collective-permute-start.30 = (bf16[344,1024]{1,0:T(8,128)(2,1)S(1)}, bf16[344,1024]{1,0:T(8,128)(2,1)S(1)}, u32[]{:S(2)}, u32[]{:S(2)}) collective-permute-start(bf16[344,1024]{1,0:T(8,128)(2,1)S(1)} %add_convert_fusion.3), channel_id=1, source_target_pairs={{0,2},{1,3},{2,0},{3,1},{4,6},{5,7},{6,4},{7,5},{8,10},{9,11},{10,... | collective-permute-start | bytes 2113544 | tf_op jit(solution)/shard_map/ppermute | solution.py:822
  171.1 47.8 %collective-permute-start.35 = (bf16[512,2048]{1,0:T(8,128)(2,1)}, bf16[512,2048]{1,0:T(8,128)(2,1)}, u32[]{:S(2)}, u32[]{:S(2)}) collective-permute-start(bf16[512,2048]{1,0:T(8,128)(2,1)} %get-tuple-element.202), channel_id=1, source_target_pairs={{0,4},{4,0},{8,12},{12,8},{16,20},{20,16},{24,28},{28,24},{1,5},{5... | collective-permute-start | bytes 6291464 | tf_op jit(solution)/shard_map/ppermute | solution.py:822
  247.9 35.7 %collective-permute-start.40 = (bf16[344,1024]{1,0:T(8,128)(2,1)}, bf16[344,1024]{1,0:T(8,128)(2,1)S(1)}, u32[]{:S(2)}, u32[]{:S(2)}) collective-permute-start(bf16[344,1024]{1,0:T(8,128)(2,1)} %get-tuple-element.221), channel_id=1, source_target_pairs={{0,1},{1,0},{2,3},{3,2},{4,5},{5,4},{6,7},{7,6},{8,9},{9,8},{10,11... | collective-permute-start | bytes 2113544 | tf_op jit(solution)/shard_map/ppermute | solution.py:822
  248.4 15.8 %collective-permute-start.44 = (bf16[344,1024]{1,0:T(8,128)(2,1)S(1)}, bf16[344,1024]{1,0:T(8,128)(2,1)S(1)}, u32[]{:S(2)}, u32[]{:S(2)}) collective-permute-start(bf16[344,1024]{1,0:T(8,128)(2,1)S(1)} %copy-done.47), channel_id=1, source_target_pairs={{0,1},{1,0},{2,3},{3,2},{4,5},{5,4},{6,7},{7,6},{8,9},{9,8},{10,11... | collective-permute-start | bytes 2113544 | tf_op jit(solution)/shard_map/ppermute | solution.py:822
  263.3 24.2 %collective-permute-start.42 = (bf16[344,1024]{1,0:T(8,128)(2,1)S(1)}, bf16[344,1024]{1,0:T(8,128)(2,1)}, u32[]{:S(2)}, u32[]{:S(2)}) collective-permute-start(bf16[344,1024]{1,0:T(8,128)(2,1)S(1)} %add_convert_fusion.2), channel_id=1, source_target_pairs={{0,2},{1,3},{2,0},{3,1},{4,6},{5,7},{6,4},{7,5},{8,10},{9,11},{10,... | collective-permute-start | bytes 2113544 | tf_op jit(solution)/shard_map/ppermute | solution.py:822
  264.2 23.3 %collective-permute-start.43 = (bf16[344,1024]{1,0:T(8,128)(2,1)}, bf16[344,1024]{1,0:T(8,128)(2,1)S(1)}, u32[]{:S(2)}, u32[]{:S(2)}) collective-permute-start(bf16[344,1024]{1,0:T(8,128)(2,1)} %get-tuple-element.228), channel_id=1, source_target_pairs={{0,1},{1,0},{2,3},{3,2},{4,5},{5,4},{6,7},{7,6},{8,9},{9,8},{10,11... | collective-permute-start | bytes 2113544 | tf_op jit(solution)/shard_map/ppermute | solution.py:822
  264.2 15.7 %collective-permute-start.49 = (bf16[256,1152]{1,0:T(8,128)(2,1)S(1)}, bf16[256,1152]{1,0:T(8,128)(2,1)S(1)}, u32[]{:S(2)}, u32[]{:S(2)}) collective-permute-start(bf16[256,1152]{1,0:T(8,128)(2,1)S(1)} %copy-done.49), channel_id=1, source_target_pairs={{0,4},{4,0},{8,12},{12,8},{16,20},{20,16},{24,28},{28,24},{1,5},{5... | collective-permute-start | bytes 1769480 | tf_op jit(solution)/shard_map/ppermute | solution.py:822
  271.7 24.9 %collective-permute-start.45 = (bf16[344,1024]{1,0:T(8,128)(2,1)S(1)}, bf16[344,1024]{1,0:T(8,128)(2,1)S(1)}, u32[]{:S(2)}, u32[]{:S(2)}) collective-permute-start(bf16[344,1024]{1,0:T(8,128)(2,1)S(1)} %add_convert_fusion.1), channel_id=1, source_target_pairs={{0,2},{1,3},{2,0},{3,1},{4,6},{5,7},{6,4},{7,5},{8,10},{9,11},{10,... | collective-permute-start | bytes 2113544 | tf_op jit(solution)/shard_map/ppermute | solution.py:822
  279.9 27.1 %collective-permute-start.51 = (bf16[128,1152]{1,0:T(8,128)(2,1)}, bf16[128,1152]{1,0:T(8,128)(2,1)}, u32[]{:S(2)}, u32[]{:S(2)}) collective-permute-start(bf16[128,1152]{1,0:T(8,128)(2,1)} %add_convert_fusion.5), channel_id=1, source_target_pairs={{0,16},{4,20},{8,24},{12,28},{16,0},{20,4},{24,8},{28,12},{1,17},{... | collective-permute-start | bytes 884744 | tf_op jit(solution)/shard_map/ppermute | solution.py:822
  283.5 23.5 %collective-permute-start.50 = (bf16[128,1152]{1,0:T(8,128)(2,1)}, bf16[128,1152]{1,0:T(8,128)(2,1)}, u32[]{:S(2)}, u32[]{:S(2)}) collective-permute-start(bf16[128,1152]{1,0:T(8,128)(2,1)} %get-tuple-element.252), channel_id=1, source_target_pairs={{0,8},{4,12},{8,0},{12,4},{16,24},{20,28},{24,16},{28,20},{1,9},{5... | collective-permute-start | bytes 884744 | tf_op jit(solution)/shard_map/ppermute | solution.py:822
  287.5 16.7 %collective-permute-start.46 = (bf16[32,2048]{1,0:T(8,128)(2,1)}, bf16[32,2048]{1,0:T(8,128)(2,1)S(1)}, u32[]{:S(2)}, u32[]{:S(2)}) collective-permute-start(bf16[32,2048]{1,0:T(8,128)(2,1)} %get-tuple-element.233), channel_id=1, source_target_pairs={{0,1},{1,0},{2,3},{3,2},{4,5},{5,4},{6,7},{7,6},{8,9},{9,8},{10,11... | collective-permute-start | bytes 393224 | tf_op jit(solution)/shard_map/ppermute | solution.py:822
  287.5 16.7 %collective-permute-start.47 = (bf16[32,2048]{1,0:T(8,128)(2,1)}, bf16[32,2048]{1,0:T(8,128)(2,1)S(1)}, u32[]{:S(2)}, u32[]{:S(2)}) collective-permute-start(bf16[32,2048]{1,0:T(8,128)(2,1)} %get-tuple-element.234), channel_id=1, source_target_pairs={{0,2},{1,3},{2,0},{3,1},{4,6},{5,7},{6,4},{7,5},{8,10},{9,11},{10,... | collective-permute-start | bytes 393224 | tf_op jit(solution)/shard_map/ppermute | solution.py:822
  (90 other events, 664.8 us)
Sparse Core Ops, SparseCore 0:
  37.4 76.5 all-gather.1
  222.9 43.7 reduce-scatter.1

commit v5 on v4

--- a/solution.py
+++ b/solution.py
@@ -886,9 +886,8 @@
             shards[bit] = swap(shards[0], bit, "dp")
         arrived = [shards[bit] for bit in (4, 2, 1)] + second[1:]
         widen(shards, *arrived)
-        shards[7] = swap(after(shards[6], tokens_far), 1, "dp")
         first_pieces = [shards[m] for m in range(replicas)]
-        nearly = [shards[6], shards[3], shards[5]]
+        nearly = [shards[3], shards[5], shards[7]]
     else:
         first_pieces = [lax.all_gather(in_order(first), "dp", axis=0, tiled=True)]
         arrived = nearly = [tokens_far]
@@ -962,13 +961,13 @@
     att_grads = exchange(att_grads)
     mids = []
     proj_terms = scatter(proj_weights(branch_grad, attended_own), *att_grads, mids=mids)
-    branch2_terms = scatter(branches, *att_grads)
+    branch2_mids = []
+    branch2_terms = scatter(branches, *att_grads, mids=branch2_mids)
     qkv_grad, qkv_sums = attend_back(qkv, key_bias, attended, after(lse, *mids), att_grads)
-    pending = []
+    *norm1_parts, norm1_sums = qkv_back(qkv_grad, weight_qkv, tokens_pieces, mean1, inverse1)
     if direct:
-        other = after(other_mlp, qkv_grad)
+        other = after(other_mlp, norm1_sums)
         summed = (keep_mlp.astype(F32) + other.astype(F32)).astype(BF)
-        pending.append(summed)
         lines = [[side + 2 * z for z in range(replicas // 2)] for side in range(2)]
         owned_mlp = lax.psum_scatter(
             summed, "dp", scatter_dimension=0, tiled=True, axis_index_groups=lines
@@ -980,9 +979,9 @@
         owned_mlp = lax.psum_scatter(
             ordered.reshape(width, 2 * hidden_part), "dp", scatter_dimension=0, tiled=True
         )
-    *norm1_parts, norm1_sums = qkv_back(after(qkv_grad, *pending), weight_qkv, tokens_pieces, mean1, inverse1)
+    before = branch2_mids + ([summed] if direct else [])
     parts = attn_weights(
-        ids, normed1, qkv_grad,
+        ids, after(normed1, *before), qkv_grad,
         [norm1_sums, qkv_sums, turn_sums, own_sums, grad_scale2, sums_near, sums_far],
         proj_terms, replicas if direct else 0, rows,
     )
@@ -994,9 +993,10 @@
         keep0, keep1, keep2, keep3, send32, send10 = parts
         size = keep0.shape[0]
         other32 = swap(send32, 1, "dp")
-        other10 = swap(after(send10, other32), 1, "dp")
+        other10 = swap(after(send10, other32, branch2_terms[-1]), 1, "dp")
         across = swap(add(keep3, other32[:size]), 2, "dp")
-        far = swap(add(add(keep2, other32[size:]), across), 4, "dp")
+        near2 = add(add(keep2, other32[size:]), across)
+        far = swap(after(near2, norm1_terms[-1]), 4, "dp")
         across0 = swap(add(keep1, other10[:size]), 2, "dp")
         terms = [add(keep0, other10[size:]), across0, far]
         settled = [across]

time: 330 us -> 333 us (level)
  waiting for transfers between devices: 105 us -> 113 us
  starting transfers between devices: 44.6 us -> 40.5 us
    ppermute x55, waiting for transfers between devices: 105 us -> 113 us  [swap(): return lax.ppermute(value, axis, [(i, i ^ bit) for i in range(size)])]
    ppermute x55, starting transfers between devices: 44.6 us -> 40.5 us  [swap(): return lax.ppermute(value, axis, [(i, i ^ bit) for i in range(size)])]
    unnamed x117 -> x119, local copies, waits for them, and re-layouts: 10.7 us -> 10.1 us
  transfers between devices with their start and end apart: 57 -> 57, of which waited for: 25 -> 31; matrix products, arithmetic and copies ran while one was open for 3% -> 3% of each run, Pallas kernels for 36% -> 36%
where the time goes in v5:
time: 333 us; the launch traced here: 328 us
  Pallas kernels  136 us (41%)
  waiting for transfers between devices  113 us (34%)
  starting transfers between devices  40.5 us (12%)
  between operations  15.6 us (5%)
  other arithmetic  12.2 us (4%)
  local copies, waits for them, and re-layouts  10.1 us (3%)
    ppermute x55, waiting for transfers between devices, swap(): return lax.ppermute(value, axis, [(i, i ^ bit) for i in range(size)])  113 us
    ppermute x55, starting transfers between devices, swap(): return lax.ppermute(value, axis, [(i, i ^ bit) for i in range(size)])  40.5 us
    pallas_call x2, Pallas kernels, mlp(): pl.pallas_call(lambda *refs: mlp_kernel(count, shards, group, *refs), gri...  25.5 us
    pallas_call x1, Pallas kernels, attend_back(): pl.pallas_call(attend_back_kernel, grid=(pairs,), in_specs=[pl.BlockSpec(...  24.3 us
    pallas_call x1, Pallas kernels, mlp_weights(): pl.pallas_call(lambda *refs: mlp_weights_kernel(direct, *refs), grid_spec...  16.1 us
    pallas_call x1, Pallas kernels, attend(): pl.pallas_call(attend_kernel, grid=(pairs,), in_specs=[pl.BlockSpec((leng...  15.5 us
    unnamed x119, local copies, waits for them, and re-layouts  10.1 us
    pallas_call x1, Pallas kernels, project(): pl.pallas_call(lambda *refs: project_kernel(ordered, group, count_column,...  8.22 us
  transfers between devices with their start and end apart: 57, of which 31 were waited for; matrix products, arithmetic and copies ran while one was open for 3% of the time, Pallas kernels for 36%

profile of v5, /device:TPU:0, one launch (start us, length us, event | category | flops | bytes accessed | tf_op | source)
XLA Modules:
  0.0 328.0 jit_solution(6776545966456832022)
XLA Ops:
  28.7 8.5 %collective-permute-done.6.refs_13_ = bf16[128,1152]{1,0:T(8,128)(2,1)S(1)} collective-permute-done((bf16[128,1152]{1,0:T(8,128)(2,1)S(1)}, bf16[128,1152]{1,0:T(8,128)(2,1)S(1)}, u32[]{:S(2)}, u32[]{:S(2)}) %collective-permute-start.6) | collective-permute-done | bytes 294944 | tf_op jit(solution)/shard_map/ppermute | solution.py:822
  43.0 4.7 %collective-permute-done.11.refs_15_ = bf16[128,1152]{1,0:T(8,128)(2,1)S(1)} collective-permute-done((bf16[128,1152]{1,0:T(8,128)(2,1)S(1)}, bf16[128,1152]{1,0:T(8,128)(2,1)S(1)}, u32[]{:S(2)}, u32[]{:S(2)}) %collective-permute-start.11) | collective-permute-done | bytes 294944 | tf_op jit(solution)/shard_map/ppermute | solution.py:822
  49.2 3.6 %collective-permute-done.10.refs_14_ = bf16[128,1152]{1,0:T(8,128)(2,1)S(1)} collective-permute-done((bf16[128,1152]{1,0:T(8,128)(2,1)S(1)}, bf16[128,1152]{1,0:T(8,128)(2,1)S(1)}, u32[]{:S(2)}, u32[]{:S(2)}) %collective-permute-start.10) | collective-permute-done | bytes 294944 | tf_op jit(solution)/shard_map/ppermute | solution.py:822
  52.8 10.0 %collective-permute-done.9.refs_12_ = bf16[128,1152]{1,0:T(8,128)(2,1)S(1)} collective-permute-done((bf16[128,1152]{1,0:T(8,128)(2,1)S(1)}, bf16[128,1152]{1,0:T(8,128)(2,1)S(1)}, u32[]{:S(2)}, u32[]{:S(2)}) %collective-permute-start.9) | collective-permute-done | bytes 294944 | tf_op jit(solution)/shard_map/ppermute | solution.py:822
  62.8 4.5 %collective-permute-done.12.refs_16_ = bf16[128,1152]{1,0:T(8,128)(2,1)S(1)} collective-permute-done((bf16[128,1152]{1,0:T(8,128)(2,1)S(1)}, bf16[128,1152]{1,0:T(8,128)(2,1)S(1)}, u32[]{:S(2)}, u32[]{:S(2)}) %collective-permute-start.12) | collective-permute-done | bytes 294944 | tf_op jit(solution)/shard_map/ppermute | solution.py:822
  71.4 8.2 %project.1 = (bf16[1024,768]{1,0:T(8,128)(2,1)}, bf16[1024,256]{1,0:T(8,128)(2,1)}, f32[16,1024]{1,0:T(8,128)}, bf16[1376,1024]{1,0:T(8,128)(2,1)}, bf16[1376,76...) custom-call(s32[2]{0:T(128)} %pad_add_fusion.ids_ref.refs_0_.refs_7_, ...), custom_call_target="tpu_custom_call" | custom-call | flops 1000000000 | bytes 1000000 | tf_op jit(solution)/shard_map/project/pallas_call | solution.py:175
  80.2 6.4 %collective-permute-done.16.refs_3_ = bf16[344,1024]{1,0:T(8,128)(2,1)} collective-permute-done((bf16[344,1024]{1,0:T(8,128)(2,1)S(1)}, bf16[344,1024]{1,0:T(8,128)(2,1)}, u32[]{:S(2)}, u32[]{:S(2)}) %collective-permute-start.16) | collective-permute-done | bytes 704544 | tf_op jit(solution)/shard_map/ppermute | solution.py:822
  86.6 15.5 %attend.1 = (f32[1376,256]{1,0:T(8,128)}, f32[2,2,1376]{2,1,0:T(2,128)}, bf16[344,256]{1,0:T(8,128)(2,1)}, bf16[344,256]{1,0:T(8,128)(2,1)}, bf16[344,256]{1,0:T(8,128)(2,1)}, /*index=5*/bf16[344,256]{1,0:T(8,128)(2,1)}) custom-call(bf16[1376,768]{1,0:T(8,128)(2,1)} %get-tuple-element.155.qkv_ref, f32[1376,1]{1,0:T(8,128)} %get-tuple-element.156.bias_ref), custom_call_target="tpu_custom_call" | custom-call | flops 1000000000 | bytes 1000000 | tf_op jit(solution)/shard_map/attend/pallas_call | solution.py:231
  104.9 5.4 %collective-permute-done.18.refs_4_.rest_2_ = bf16[344,256]{1,0:T(8,128)(2,1)S(1)} collective-permute-done((bf16[344,256]{1,0:T(8,128)(2,1)}, bf16[344,256]{1,0:T(8,128)(2,1)S(1)}, u32[]{:S(2)}, u32[]{:S(2)}) %collective-permute-start.18) | collective-permute-done | bytes 176160 | tf_op jit(solution)/shard_map/ppermute | solution.py:822
  113.3 5.3 %middle.1 = (f32[344,1024]{1,0:T(8,128)}, f32[344,1024]{1,0:T(8,128)}, bf16[344,1024]{1,0:T(8,128)(2,1)}, f32[344,1024]{1,0:T(8,128)}, f32[344,1]{1,0:T(8,128)}) custom-call(f32[16,1024]{1,0:T(8,128)} %get-tuple-element.221.refs_0_.refs_5_.rows_ref, bf16[344,1024]{1,0:T(8,128)(2,1)} %bitcast.25, bf16[344,256]{1,0:T(8,128)(2,1)} %get-tuple-element.157.refs_2_.rest_0_, ...), custom_call_target="tpu_custom_call" | custom-call | flops 1000000000 | bytes 1000000 | tf_op jit(solution)/shard_map/middle/pallas_call | solution.py:333
  122.5 12.6 %mlp.2 = (bf16[344,1024]{1,0:T(8,128)(2,1)}, bf16[344,1024]{1,0:T(8,128)(2,1)}, bf16[688,1024]{1,0:T(8,128)(2,1)}, bf16[688,1024]{1,0:T(8,128)(2,1)}, bf16[688,1...) custom-call(f32[16,1024]{1,0:T(8,128)} %get-tuple-element.221.refs_0_.refs_5_.rows_ref, ...), custom_call_target="tpu_custom_call" | custom-call | flops 1000000000 | bytes 1000000 | tf_op jit(solution)/shard_map/mlp/pallas_call | solution.py:475
  140.7 12.9 %mlp.3 = (bf16[344,1024]{1,0:T(8,128)(2,1)}, bf16[344,1024]{1,0:T(8,128)(2,1)}, bf16[688,1024]{1,0:T(8,128)(2,1)}, bf16[688,1024]{1,0:T(8,128)(2,1)}, bf16[688,1...) custom-call(f32[16,1024]{1,0:T(8,128)} %get-tuple-element.221.refs_0_.refs_5_.rows_ref, ...), custom_call_target="tpu_custom_call" | custom-call | flops 1000000000 | bytes 1000000 | tf_op jit(solution)/shard_map/mlp/pallas_call | solution.py:475
  158.0 16.1 %mlp_weights.1 = (bf16[512,2048]{1,0:T(8,128)(2,1)}, bf16[512,2048]{1,0:T(8,128)(2,1)}, f32[1,1024]{1,0:T(1,128)}, bf16[344,1024]{1,0:T(8,128)(2,1)}, bf16[344,1...) custom-call(s32[2]{0:T(128)} %pad_add_fusion.ids_ref.refs_0_.refs_7_, ...), custom_call_target="tpu_custom_call" | custom-call | flops 1000000000 | bytes 1000000 | tf_op jit(solution)/shard_map/mlp_weights/pallas_call | solution.py:541
  176.8 6.1 %turn.1 = (f32[344,1024]{1,0:T(8,128)}, bf16[344,1024]{1,0:T(8,128)(2,1)}, f32[8,1024]{1,0:T(8,128)}, bf16[344,256]{1,0:T(8,128)(2,1)}, bf16[344,256]{1,0:T(8,12...) custom-call(f32[16,1024]{1,0:T(8,128)} %get-tuple-element.221.refs_0_.refs_5_.rows_ref, ...), custom_call_target="tpu_custom_call" | custom-call | flops 1000000000 | bytes 1000000 | tf_op jit(solution)/shard_map/turn/pallas_call | solution.py:369
  182.9 3.7 %proj_weights.1 = (bf16[1024,256]{1,0:T(8,128)(2,1)}, bf16[1024,256]{1,0:T(8,128)(2,1)}, bf16[1024,256]{1,0:T(8,128)(2,1)}, bf16[1024,256]{1,0:T(8,128)(2,1)}) custom-call(bf16[344,1024]{1,0:T(8,128)(2,1)} %get-tuple-element.197.grad_ref, bf16[344,256]{1,0:T(8,128)(2,1)} %get-tuple-element.157.refs_2_.rest_0_, bf16[344,256]{1,0:T(8,128)(2,1)} %copy-done.52, ...), custom_call_target="tpu_custom_call" | custom-call | flops 1000000000 | bytes 1000000 | tf_op jit(solution)/shard_map/proj_weights/pallas_call | solution.py:390
  189.9 4.5 %collective-permute-done.35.rest_2_ = bf16[344,256]{1,0:T(8,128)(2,1)S(1)} collective-permute-done((bf16[344,256]{1,0:T(8,128)(2,1)S(1)}, bf16[344,256]{1,0:T(8,128)(2,1)S(1)}, u32[]{:S(2)}, u32[]{:S(2)}) %collective-permute-start.35) | collective-permute-done | bytes 176160 | tf_op jit(solution)/shard_map/ppermute | solution.py:822
  197.1 24.3 %attend_back.1 = (bf16[1376,768]{1,0:T(8,128)(2,1)}, f32[2,1,384]{2,1,0:T(1,128)}) custom-call(bf16[1376,768]{1,0:T(8,128)(2,1)} %get-tuple-element.155.qkv_ref, f32[1376,1]{1,0:T(8,128)} %get-tuple-element.156.bias_ref, f32[1376,256]{1,0:T(8,128)} %get-tuple-element.193.att_ref, f32[2,2,1376]{2,1,0:T(2,128)} %get-tuple-element.200.lse_ref, ...), custom_call_target="tpu_custom_call" | custom-call | flops 1000000000 | bytes 1000000 | tf_op jit(solution)/shard_map/attend_back/pallas_call | solution.py:290
  221.4 6.8 %qkv_back.1 = (bf16[344,1024]{1,0:T(8,128)(2,1)}, bf16[344,1024]{1,0:T(8,128)(2,1)}, bf16[344,1024]{1,0:T(8,128)(2,1)}, bf16[344,1024]{1,0:T(8,128)(2,1)}, f32[8,1024]{1,0:T(8,128)}) custom-call(bf16[1376,768]{1,0:T(8,128)(2,1)} %get-tuple-element.205.refs_0_.refs_2_, bf16[1024,768]{1,0:T(8,128)(2,1)} %get-tuple-element.206.refs_1_, ...), custom_call_target="tpu_custom_call" | custom-call | flops 1000000000 | bytes 1000000 | tf_op jit(solution)/shard_map/qkv_back/pallas_call | solution.py:630
  228.2 3.9 %add_convert_fusion = bf16[512,2048]{1,0:T(8,128)(2,1)} fusion(bf16[512,2048]{1,0:T(8,128)(2,1)} %collective-permute-done.32, bf16[512,2048]{1,0:T(8,128)(2,1)S(1)} %copy-done.5), kind=kLoop, calls=%fused_computation | loop fusion | flops 4194304 | bytes 6291456 | tf_op jit(solution)/shard_map/convert_element_type | solution.py:970
  237.2 11.5 %collective-permute-done.38.refs_12_ = bf16[1024,256]{1,0:T(8,128)(2,1)S(1)} collective-permute-done((bf16[1024,256]{1,0:T(8,128)(2,1)S(1)}, bf16[1024,256]{1,0:T(8,128)(2,1)S(1)}, u32[]{:S(2)}, u32[]{:S(2)}) %collective-permute-start.38) | collective-permute-done | bytes 524320 | tf_op jit(solution)/shard_map/ppermute | solution.py:822
  249.5 7.5 %attn_weights.1 = (bf16[128,1152]{1,0:T(8,128)(2,1)}, bf16[128,1152]{1,0:T(8,128)(2,1)}, bf16[128,1152]{1,0:T(8,128)(2,1)}, bf16[128,1152]{1,0:T(8,128)(2,1)}, b...) custom-call(s32[2]{0:T(128)} %pad_add_fusion.ids_ref.refs_0_.refs_7_, bf16[1376,1024]{1,0:T(8,128)(2,1)} %get-tuple-element.211.refs_1_, ...), custom_call_target="tpu_custom_call" | custom-call | flops 1000000000 | bytes 1000000 | tf_op jit(solution)/shard_map/attn_weights/pallas_call | solution.py:702
  258.5 13.7 %collective-permute-done.39 = bf16[256,1152]{1,0:T(8,128)(2,1)S(1)} collective-permute-done((bf16[256,1152]{1,0:T(8,128)(2,1)}, bf16[256,1152]{1,0:T(8,128)(2,1)S(1)}, u32[]{:S(2)}, u32[]{:S(2)}) %collective-permute-start.39) | collective-permute-done | bytes 589856 | tf_op jit(solution)/shard_map/ppermute | solution.py:822
  282.2 8.9 %collective-permute-done.45.rest_2_ = bf16[344,1024]{1,0:T(8,128)(2,1)S(1)} collective-permute-done((bf16[344,1024]{1,0:T(8,128)(2,1)S(1)}, bf16[344,1024]{1,0:T(8,128)(2,1)S(1)}, u32[]{:S(2)}, u32[]{:S(2)}) %collective-permute-start.45) | collective-permute-done | bytes 704544 | tf_op jit(solution)/shard_map/ppermute | solution.py:822
  299.3 4.0 %begin.1 = bf16[344,1024]{1,0:T(8,128)(2,1)} custom-call(f32[16,1024]{1,0:T(8,128)} %get-tuple-element.221.refs_0_.refs_5_.rows_ref, bf16[344,1024]{1,0:T(8,128)(2,1)} %bitcast.27, f32[1376,1]{1,0:T(8,128)} %get-tuple-element.207.refs_2_.mean_ref, f32[1376,1]{1,0:T(8,128)} %get-tuple-element.208.refs_3_.inv_ref, f32[344,1024]{1,0:T(8,128)} %get-tuple-element.227.middle_ref, ...), custom_call_target="tpu_custom_call" | custom-call | tf_op jit(solution)/shard_map/begin/pallas_call | solution.py:597
  (242 shorter events, 103.8 us)
Async XLA Ops:
  7.2 114.5 %all-gather.2.cloned.1.call-start = ((), (), s32[]{:S(2)}) async-start(), calls=%async_computation.1 | async-start | bytes 4718592 | tf_op jit(solution)/shard_map/all_gather | solution.py:895
  20.3 16.9 %collective-permute-start.6 = (bf16[128,1152]{1,0:T(8,128)(2,1)S(1)}, bf16[128,1152]{1,0:T(8,128)(2,1)S(1)}, u32[]{:S(2)}, u32[]{:S(2)}) collective-permute-start(bf16[128,1152]{1,0:T(8,128)(2,1)S(1)} %constant_dynamic-update-slice_fusion.refs_9_), channel_id=1, source_target_pairs={{0,16},{4,20},{8,24},{12,28},{16,0},{20,4},{24,8},{28,12},{1,17},{... | collective-permute-start | bytes 884744 | tf_op jit(solution)/shard_map/ppermute | solution.py:822
  37.3 258.0 %reduce-scatter.2.cloned.1.call-start = ((), (), s32[]{:S(2)}) async-start(), calls=%async_computation.2 | async-start | bytes 2621440 | tf_op jit(solution)/shard_map/reduce_scatter | solution.py:972
  38.1 24.7 %collective-permute-start.14 = (bf16[344,1024]{1,0:T(8,128)(2,1)S(1)}, bf16[344,1024]{1,0:T(8,128)(2,1)S(1)}, u32[]{:S(2)}, u32[]{:S(2)}) collective-permute-start(bf16[344,1024]{1,0:T(8,128)(2,1)S(1)} %bitcast.28), channel_id=1, source_target_pairs={{0,2},{1,3},{2,0},{3,1},{4,6},{5,7},{6,4},{7,5},{8,10},{9,11},{10,... | collective-permute-start | bytes 2113544 | tf_op jit(solution)/shard_map/ppermute | solution.py:822
  42.4 20.4 %collective-permute-start.9 = (bf16[128,1152]{1,0:T(8,128)(2,1)S(1)}, bf16[128,1152]{1,0:T(8,128)(2,1)S(1)}, u32[]{:S(2)}, u32[]{:S(2)}) collective-permute-start(bf16[128,1152]{1,0:T(8,128)(2,1)S(1)} %collective-permute-done.7.refs_11_), channel_id=1, source_target_pairs={{0,4},{4,0},{8,12},{12,8},{16,20},{20,16},{24,28},{28,24},{1,5},{5... | collective-permute-start | bytes 884744 | tf_op jit(solution)/shard_map/ppermute | solution.py:822
  47.7 19.6 %collective-permute-start.12 = (bf16[128,1152]{1,0:T(8,128)(2,1)S(1)}, bf16[128,1152]{1,0:T(8,128)(2,1)S(1)}, u32[]{:S(2)}, u32[]{:S(2)}) collective-permute-start(bf16[128,1152]{1,0:T(8,128)(2,1)S(1)} %collective-permute-done.11.refs_15_), channel_id=1, source_target_pairs={{0,4},{4,0},{8,12},{12,8},{16,20},{20,16},{24,28},{28,24},{1,5},{5... | collective-permute-start | bytes 884744 | tf_op jit(solution)/shard_map/ppermute | solution.py:822
  67.8 18.8 %collective-permute-start.16 = (bf16[344,1024]{1,0:T(8,128)(2,1)S(1)}, bf16[344,1024]{1,0:T(8,128)(2,1)}, u32[]{:S(2)}, u32[]{:S(2)}) collective-permute-start(bf16[344,1024]{1,0:T(8,128)(2,1)S(1)} %bitcast.32), channel_id=1, source_target_pairs={{0,2},{1,3},{2,0},{3,1},{4,6},{5,7},{6,4},{7,5},{8,10},{9,11},{10,... | collective-permute-start | bytes 2113544 | tf_op jit(solution)/shard_map/ppermute | solution.py:822
  79.6 22.6 %collective-permute-start.21 = (bf16[1024,256]{1,0:T(8,128)(2,1)}, bf16[1024,256]{1,0:T(8,128)(2,1)S(1)}, u32[]{:S(2)}, u32[]{:S(2)}) collective-permute-start(bf16[1024,256]{1,0:T(8,128)(2,1)} %get-tuple-element.161.refs_6_.refs_9_), channel_id=1, source_target_pairs={{0,2},{1,3},{2,0},{3,1},{4,6},{5,7},{6,4},{7,5},{8,10},{9,11},{10,... | collective-permute-start | bytes 1572872 | tf_op jit(solution)/shard_map/ppermute | solution.py:822
  80.2 32.1 %collective-permute-start.20 = (bf16[1024,256]{1,0:T(8,128)(2,1)}, bf16[1024,256]{1,0:T(8,128)(2,1)S(1)}, u32[]{:S(2)}, u32[]{:S(2)}) collective-permute-start(bf16[1024,256]{1,0:T(8,128)(2,1)} %get-tuple-element.161.refs_6_.refs_9_), channel_id=1, source_target_pairs={{0,1},{1,0},{2,3},{3,2},{4,5},{5,4},{6,7},{7,6},{8,9},{9,8},{10,11... | collective-permute-start | bytes 1572872 | tf_op jit(solution)/shard_map/ppermute | solution.py:822
  104.6 15.6 %collective-permute-start.24 = (bf16[344,1024]{1,0:T(8,128)(2,1)S(1)}, bf16[344,1024]{1,0:T(8,128)(2,1)S(1)}, u32[]{:S(2)}, u32[]{:S(2)}) collective-permute-start(bf16[344,1024]{1,0:T(8,128)(2,1)S(1)} %bitcast.33), channel_id=1, source_target_pairs={{0,1},{1,0},{2,3},{3,2},{4,5},{5,4},{6,7},{7,6},{8,9},{9,8},{10,11... | collective-permute-start | bytes 2113544 | tf_op jit(solution)/shard_map/ppermute | solution.py:822
  119.7 18.0 %collective-permute-start.25 = (bf16[344,1024]{1,0:T(8,128)(2,1)}, bf16[344,1024]{1,0:T(8,128)(2,1)S(1)}, u32[]{:S(2)}, u32[]{:S(2)}) collective-permute-start(bf16[344,1024]{1,0:T(8,128)(2,1)} %get-tuple-element.164.refs_1_), channel_id=1, source_target_pairs={{0,2},{1,3},{2,0},{3,1},{4,6},{5,7},{6,4},{7,5},{8,10},{9,11},{10,... | collective-permute-start | bytes 2113544 | tf_op jit(solution)/shard_map/ppermute | solution.py:822
  120.2 17.4 %collective-permute-start.27 = (bf16[344,1024]{1,0:T(8,128)(2,1)}, bf16[344,1024]{1,0:T(8,128)(2,1)S(1)}, u32[]{:S(2)}, u32[]{:S(2)}) collective-permute-start(bf16[344,1024]{1,0:T(8,128)(2,1)} %collective-permute-done.16.refs_3_), channel_id=1, source_target_pairs={{0,1},{1,0},{2,3},{3,2},{4,5},{5,4},{6,7},{7,6},{8,9},{9,8},{10,11... | collective-permute-start | bytes 2113544 | tf_op jit(solution)/shard_map/ppermute | solution.py:822
  153.8 20.4 %collective-permute-start.30 = (bf16[344,1024]{1,0:T(8,128)(2,1)S(1)}, bf16[344,1024]{1,0:T(8,128)(2,1)S(1)}, u32[]{:S(2)}, u32[]{:S(2)}) collective-permute-start(bf16[344,1024]{1,0:T(8,128)(2,1)S(1)} %copy-done.50), channel_id=1, source_target_pairs={{0,1},{1,0},{2,3},{3,2},{4,5},{5,4},{6,7},{7,6},{8,9},{9,8},{10,11... | collective-permute-start | bytes 2113544 | tf_op jit(solution)/shard_map/ppermute | solution.py:822
  157.4 17.9 %collective-permute-start.31 = (bf16[344,1024]{1,0:T(8,128)(2,1)S(1)}, bf16[344,1024]{1,0:T(8,128)(2,1)S(1)}, u32[]{:S(2)}, u32[]{:S(2)}) collective-permute-start(bf16[344,1024]{1,0:T(8,128)(2,1)S(1)} %add_convert_fusion.3), channel_id=1, source_target_pairs={{0,2},{1,3},{2,0},{3,1},{4,6},{5,7},{6,4},{7,5},{8,10},{9,11},{10,... | collective-permute-start | bytes 2113544 | tf_op jit(solution)/shard_map/ppermute | solution.py:822
  175.3 52.9 %collective-permute-start.32 = (bf16[512,2048]{1,0:T(8,128)(2,1)}, bf16[512,2048]{1,0:T(8,128)(2,1)}, u32[]{:S(2)}, u32[]{:S(2)}) collective-permute-start(bf16[512,2048]{1,0:T(8,128)(2,1)} %get-tuple-element.192), channel_id=1, source_target_pairs={{0,4},{4,0},{8,12},{12,8},{16,20},{20,16},{24,28},{28,24},{1,5},{5... | collective-permute-start | bytes 6291464 | tf_op jit(solution)/shard_map/ppermute | solution.py:822
  256.9 15.3 %collective-permute-start.39 = (bf16[256,1152]{1,0:T(8,128)(2,1)}, bf16[256,1152]{1,0:T(8,128)(2,1)S(1)}, u32[]{:S(2)}, u32[]{:S(2)}) collective-permute-start(bf16[256,1152]{1,0:T(8,128)(2,1)} %get-tuple-element.220), channel_id=1, source_target_pairs={{0,4},{4,0},{8,12},{12,8},{16,20},{20,16},{24,28},{28,24},{1,5},{5... | collective-permute-start | bytes 1769480 | tf_op jit(solution)/shard_map/ppermute | solution.py:822
  257.8 16.0 %collective-permute-start.44 = (bf16[344,1024]{1,0:T(8,128)(2,1)}, bf16[344,1024]{1,0:T(8,128)(2,1)S(1)}, u32[]{:S(2)}, u32[]{:S(2)}) collective-permute-start(bf16[344,1024]{1,0:T(8,128)(2,1)} %get-tuple-element.231), channel_id=1, source_target_pairs={{0,1},{1,0},{2,3},{3,2},{4,5},{5,4},{6,7},{7,6},{8,9},{9,8},{10,11... | collective-permute-start | bytes 2113544 | tf_op jit(solution)/shard_map/ppermute | solution.py:822
  257.8 18.6 %collective-permute-start.42 = (bf16[344,1024]{1,0:T(8,128)(2,1)S(1)}, bf16[344,1024]{1,0:T(8,128)(2,1)S(1)}, u32[]{:S(2)}, u32[]{:S(2)}) collective-permute-start(bf16[344,1024]{1,0:T(8,128)(2,1)S(1)} %add_convert_fusion.2), channel_id=1, source_target_pairs={{0,2},{1,3},{2,0},{3,1},{4,6},{5,7},{6,4},{7,5},{8,10},{9,11},{10,... | collective-permute-start | bytes 2113544 | tf_op jit(solution)/shard_map/ppermute | solution.py:822
  274.1 17.1 %collective-permute-start.45 = (bf16[344,1024]{1,0:T(8,128)(2,1)S(1)}, bf16[344,1024]{1,0:T(8,128)(2,1)S(1)}, u32[]{:S(2)}, u32[]{:S(2)}) collective-permute-start(bf16[344,1024]{1,0:T(8,128)(2,1)S(1)} %add_convert_fusion.1), channel_id=1, source_target_pairs={{0,2},{1,3},{2,0},{3,1},{4,6},{5,7},{6,4},{7,5},{8,10},{9,11},{10,... | collective-permute-start | bytes 2113544 | tf_op jit(solution)/shard_map/ppermute | solution.py:822
  276.4 17.0 %collective-permute-start.49 = (bf16[256,1152]{1,0:T(8,128)(2,1)S(1)}, bf16[256,1152]{1,0:T(8,128)(2,1)S(1)}, u32[]{:S(2)}, u32[]{:S(2)}) collective-permute-start(bf16[256,1152]{1,0:T(8,128)(2,1)S(1)} %copy-done.51), channel_id=1, source_target_pairs={{0,4},{4,0},{8,12},{12,8},{16,20},{20,16},{24,28},{28,24},{1,5},{5... | collective-permute-start | bytes 1769480 | tf_op jit(solution)/shard_map/ppermute | solution.py:822
  277.5 19.7 %collective-permute-start.41 = (bf16[344,1024]{1,0:T(8,128)(2,1)}, bf16[344,1024]{1,0:T(8,128)(2,1)S(1)}, u32[]{:S(2)}, u32[]{:S(2)}) collective-permute-start(bf16[344,1024]{1,0:T(8,128)(2,1)} %get-tuple-element.224), channel_id=1, source_target_pairs={{0,1},{1,0},{2,3},{3,2},{4,5},{5,4},{6,7},{7,6},{8,9},{9,8},{10,11... | collective-permute-start | bytes 2113544 | tf_op jit(solution)/shard_map/ppermute | solution.py:822
  277.5 20.9 %collective-permute-start.43 = (bf16[344,1024]{1,0:T(8,128)(2,1)}, bf16[344,1024]{1,0:T(8,128)(2,1)S(1)}, u32[]{:S(2)}, u32[]{:S(2)}) collective-permute-start(bf16[344,1024]{1,0:T(8,128)(2,1)} %get-tuple-element.229), channel_id=1, source_target_pairs={{0,1},{1,0},{2,3},{3,2},{4,5},{5,4},{6,7},{7,6},{8,9},{9,8},{10,11... | collective-permute-start | bytes 2113544 | tf_op jit(solution)/shard_map/ppermute | solution.py:822
  291.1 18.3 %collective-permute-start.51 = (bf16[128,1152]{1,0:T(8,128)(2,1)}, bf16[128,1152]{1,0:T(8,128)(2,1)S(1)}, u32[]{:S(2)}, u32[]{:S(2)}) collective-permute-start(bf16[128,1152]{1,0:T(8,128)(2,1)} %add_convert_fusion.5), channel_id=1, source_target_pairs={{0,16},{4,20},{8,24},{12,28},{16,0},{20,4},{24,8},{28,12},{1,17},{... | collective-permute-start | bytes 884744 | tf_op jit(solution)/shard_map/ppermute | solution.py:822
  294.3 15.1 %collective-permute-start.50 = (bf16[128,1152]{1,0:T(8,128)(2,1)S(1)}, bf16[128,1152]{1,0:T(8,128)(2,1)S(1)}, u32[]{:S(2)}, u32[]{:S(2)}) collective-permute-start(bf16[128,1152]{1,0:T(8,128)(2,1)S(1)} %get-tuple-element.254), channel_id=1, source_target_pairs={{0,8},{4,12},{8,0},{12,4},{16,24},{20,28},{24,16},{28,20},{1,9},{5... | collective-permute-start | bytes 884744 | tf_op jit(solution)/shard_map/ppermute | solution.py:822
  (91 other events, 624.5 us)
Sparse Core Ops, SparseCore 0:
  37.5 77.3 all-gather.1
  232.3 43.4 reduce-scatter.1

commit v6 on v5

--- a/solution.py
+++ b/solution.py
@@ -378,24 +378,24 @@
     )(rows, live, cotangent, unit, inverse, branch, *backs, *weights)
 
 
-def proj_weights_kernel(grad_ref, *rest):
-    half = len(rest) // 2
-    for part, out in zip(rest[:half], rest[half:]):
-        out[...] = dot(grad_ref[...], part[...], 0, 0).astype(BF)
-
-
-def proj_weights(grads, parts):
-    length, width = grads.shape
+def proj_weights_kernel(ids_ref, grad_ref, *rest):
+    parts, out_ref = rest[:-1], rest[-1]
+    for j, part in enumerate(parts):
+        out_ref[ids_ref[0] ^ j] = dot(grad_ref[...], part[...], 0, 0).astype(BF)
+
+
+def proj_weights(ids, grads, parts):
+    width = grads.shape[1]
     part = parts[0].shape[1]
     return pl.pallas_call(
         proj_weights_kernel,
-        in_specs=[VMEM] * (1 + len(parts)),
-        out_specs=[VMEM] * len(parts),
-        out_shape=[shaped((width, part), BF)] * len(parts),
+        in_specs=[SMEM] + [VMEM] * (1 + len(parts)),
+        out_specs=VMEM,
+        out_shape=shaped((len(parts), width, part), BF),
         compiler_params=PARAMS,
         cost_estimate=SMALL,
         name="proj_weights",
-    )(grads, *parts)
+    )(ids, grads, *parts)
 
 
 def mlp_kernel(count, shards, group, rows_ref, *rest):
@@ -893,6 +893,8 @@
         arrived = nearly = [tokens_far]
     second_shard = after(in_order(second), *arrived)
     second_all = lax.all_gather(second_shard, "dp", axis=0, tiled=True)
+    cotangent_far = swap(after(cotangent[0], *arrived), group // 2)
+    nearly = nearly + [cotangent_far]
     tokens_pieces = [tokens[0]]
     for j in range(1, group):
         source = tokens_pieces[j ^ (j & -j)]
@@ -900,8 +902,6 @@
             tokens_pieces.append(tokens_far)
         else:
             tokens_pieces.append(swap(after(source, *nearly), j & -j))
-    cotangent_far = swap(after(cotangent[0], *arrived), group // 2)
-
     tokens_own = after(tokens[0], second_shard)
     count_column = vector_count + bias_cols
     (
@@ -919,7 +919,7 @@
             cotangent_pieces.append(cotangent_far)
         else:
             cotangent_pieces.append(swap(after(source, qkv), j & -j))
-    attended, lse, *attended_low = attend(after(qkv, cotangent_far), key_bias, group)
+    attended, lse, *attended_low = attend(qkv, key_bias, group)
     projs = gather(weight_proj, lse)
     attended_own = exchange(attended_low)
     branch1, middle, normed2_own, unit2, inverse2 = middle_step(
@@ -959,14 +959,15 @@
         vector_rows, live[0], cotangent[0], unit2, inverse2, branch1, norm2_terms, projs
     )
     att_grads = exchange(att_grads)
-    mids = []
-    proj_terms = scatter(proj_weights(branch_grad, attended_own), *att_grads, mids=mids)
+    proj_parts = proj_weights(ids, branch_grad, attended_own).reshape(group * width, -1)
+    proj_grad = lax.psum_scatter(
+        after(proj_parts, *att_grads), "ctx", scatter_dimension=0, tiled=True
+    )
     branch2_mids = []
     branch2_terms = scatter(branches, *att_grads, mids=branch2_mids)
-    qkv_grad, qkv_sums = attend_back(qkv, key_bias, attended, after(lse, *mids), att_grads)
-    *norm1_parts, norm1_sums = qkv_back(qkv_grad, weight_qkv, tokens_pieces, mean1, inverse1)
+    qkv_grad, qkv_sums = attend_back(qkv, key_bias, attended, after(lse, proj_parts), att_grads)
     if direct:
-        other = after(other_mlp, norm1_sums)
+        other = after(other_mlp, qkv_grad)
         summed = (keep_mlp.astype(F32) + other.astype(F32)).astype(BF)
         lines = [[side + 2 * z for z in range(replicas // 2)] for side in range(2)]
         owned_mlp = lax.psum_scatter(
@@ -979,11 +980,12 @@
         owned_mlp = lax.psum_scatter(
             ordered.reshape(width, 2 * hidden_part), "dp", scatter_dimension=0, tiled=True
         )
-    before = branch2_mids + ([summed] if direct else [])
+    *norm1_parts, norm1_sums = qkv_back(after(qkv_grad, summed) if direct else qkv_grad, weight_qkv, tokens_pieces, mean1, inverse1)
+    before = branch2_mids
     parts = attn_weights(
         ids, after(normed1, *before), qkv_grad,
         [norm1_sums, qkv_sums, turn_sums, own_sums, grad_scale2, sums_near, sums_far],
-        proj_terms, replicas if direct else 0, rows,
+        [proj_grad], replicas if direct else 0, rows,
     )
     norm1_terms = scatter(norm1_parts)
     if direct:

time: 333 us -> 354 us (1.063)
  waiting for transfers between devices: 113 us -> 135 us
    ppermute x55 -> x52, waiting for transfers between devices: 113 us -> 135 us  [swap(): return lax.ppermute(value, axis, [(i, i ^ bit) for i in range(size)])]
    unnamed x119 -> x113, local copies, waits for them, and re-layouts: 10.1 us -> 8.55 us
    ppermute x55 -> x52, starting transfers between devices: 40.5 us -> 41.7 us  [swap(): return lax.ppermute(value, axis, [(i, i ^ bit) for i in range(size)])]
  transfers between devices with their start and end apart: 57 -> 55, of which waited for: 31 -> 30; matrix products, arithmetic and copies ran while one was open for 3% -> 3% of each run, Pallas kernels for 36% -> 32%
where the time goes in v6:
time: 354 us; the launch traced here: 349 us
  Pallas kernels  137 us (39%)
  waiting for transfers between devices  135 us (38%)
  starting transfers between devices  41.8 us (12%)
  between operations  15 us (4%)
  other arithmetic  10.9 us (3%)
  local copies, waits for them, and re-layouts  8.61 us (2%)
    ppermute x52, waiting for transfers between devices, swap(): return lax.ppermute(value, axis, [(i, i ^ bit) for i in range(size)])  135 us
    ppermute x52, starting transfers between devices, swap(): return lax.ppermute(value, axis, [(i, i ^ bit) for i in range(size)])  41.7 us
    pallas_call x2, Pallas kernels, mlp(): pl.pallas_call(lambda *refs: mlp_kernel(count, shards, group, *refs), gri...  25.3 us
    pallas_call x1, Pallas kernels, attend_back(): pl.pallas_call(attend_back_kernel, grid=(pairs,), in_specs=[pl.BlockSpec(...  24.4 us
    pallas_call x1, Pallas kernels, mlp_weights(): pl.pallas_call(lambda *refs: mlp_weights_kernel(direct, *refs), grid_spec...  16.2 us
    pallas_call x1, Pallas kernels, attend(): pl.pallas_call(attend_kernel, grid=(pairs,), in_specs=[pl.BlockSpec((leng...  15.6 us
    pallas_call x1, Pallas kernels, project(): pl.pallas_call(lambda *refs: project_kernel(ordered, group, count_column,...  8.74 us
    unnamed x113, local copies, waits for them, and re-layouts  8.55 us
  transfers between devices with their start and end apart: 55, of which 30 were waited for; matrix products, arithmetic and copies ran while one was open for 3% of the time, Pallas kernels for 32%

profile of v6, /device:TPU:0, one launch (start us, length us, event | category | flops | bytes accessed | tf_op | source)
XLA Modules:
  0.0 348.6 jit_solution(9817445549398541488)
XLA Ops:
  28.6 8.5 %collective-permute-done.6.refs_13_ = bf16[128,1152]{1,0:T(8,128)(2,1)S(1)} collective-permute-done((bf16[128,1152]{1,0:T(8,128)(2,1)S(1)}, bf16[128,1152]{1,0:T(8,128)(2,1)S(1)}, u32[]{:S(2)}, u32[]{:S(2)}) %collective-permute-start.6) | collective-permute-done | bytes 294944 | tf_op jit(solution)/shard_map/ppermute | solution.py:822
  43.6 4.4 %collective-permute-done.11.refs_15_ = bf16[128,1152]{1,0:T(8,128)(2,1)S(1)} collective-permute-done((bf16[128,1152]{1,0:T(8,128)(2,1)S(1)}, bf16[128,1152]{1,0:T(8,128)(2,1)S(1)}, u32[]{:S(2)}, u32[]{:S(2)}) %collective-permute-start.11) | collective-permute-done | bytes 294944 | tf_op jit(solution)/shard_map/ppermute | solution.py:822
  49.4 4.7 %collective-permute-done.10.refs_14_ = bf16[128,1152]{1,0:T(8,128)(2,1)S(1)} collective-permute-done((bf16[128,1152]{1,0:T(8,128)(2,1)S(1)}, bf16[128,1152]{1,0:T(8,128)(2,1)S(1)}, u32[]{:S(2)}, u32[]{:S(2)}) %collective-permute-start.10) | collective-permute-done | bytes 294944 | tf_op jit(solution)/shard_map/ppermute | solution.py:822
  54.1 9.3 %collective-permute-done.9.refs_12_ = bf16[128,1152]{1,0:T(8,128)(2,1)S(1)} collective-permute-done((bf16[128,1152]{1,0:T(8,128)(2,1)S(1)}, bf16[128,1152]{1,0:T(8,128)(2,1)S(1)}, u32[]{:S(2)}, u32[]{:S(2)}) %collective-permute-start.9) | collective-permute-done | bytes 294944 | tf_op jit(solution)/shard_map/ppermute | solution.py:822
  63.4 4.1 %collective-permute-done.12.refs_16_ = bf16[128,1152]{1,0:T(8,128)(2,1)S(1)} collective-permute-done((bf16[128,1152]{1,0:T(8,128)(2,1)S(1)}, bf16[128,1152]{1,0:T(8,128)(2,1)S(1)}, u32[]{:S(2)}, u32[]{:S(2)}) %collective-permute-start.12) | collective-permute-done | bytes 294944 | tf_op jit(solution)/shard_map/ppermute | solution.py:822
  74.4 8.7 %project.1 = (bf16[1024,768]{1,0:T(8,128)(2,1)}, bf16[1024,256]{1,0:T(8,128)(2,1)}, f32[16,1024]{1,0:T(8,128)}, bf16[1376,1024]{1,0:T(8,128)(2,1)}, bf16[1376,76...) custom-call(s32[2]{0:T(128)} %pad_add_fusion.ids_ref.refs_0_.refs_7_, ...), custom_call_target="tpu_custom_call" | custom-call | flops 1000000000 | bytes 1000000 | tf_op jit(solution)/shard_map/project/pallas_call | solution.py:175
  84.7 15.6 %attend.1 = (f32[1376,256]{1,0:T(8,128)}, f32[2,2,1376]{2,1,0:T(2,128)}, bf16[344,256]{1,0:T(8,128)(2,1)}, bf16[344,256]{1,0:T(8,128)(2,1)}, bf16[344,256]{1,0:T(8,128)(2,1)}, /*index=5*/bf16[344,256]{1,0:T(8,128)(2,1)}) custom-call(bf16[1376,768]{1,0:T(8,128)(2,1)} %get-tuple-element.150.qkv_ref, f32[1376,1]{1,0:T(8,128)} %get-tuple-element.151.bias_ref), custom_call_target="tpu_custom_call" | custom-call | flops 1000000000 | bytes 1000000 | tf_op jit(solution)/shard_map/attend/pallas_call | solution.py:231
  103.2 5.2 %collective-permute-done.18.refs_4_.rest_2_ = bf16[344,256]{1,0:T(8,128)(2,1)S(1)} collective-permute-done((bf16[344,256]{1,0:T(8,128)(2,1)}, bf16[344,256]{1,0:T(8,128)(2,1)S(1)}, u32[]{:S(2)}, u32[]{:S(2)}) %collective-permute-start.18) | collective-permute-done | bytes 176160 | tf_op jit(solution)/shard_map/ppermute | solution.py:822
  112.2 5.3 %middle.1 = (f32[344,1024]{1,0:T(8,128)}, f32[344,1024]{1,0:T(8,128)}, bf16[344,1024]{1,0:T(8,128)(2,1)}, f32[344,1024]{1,0:T(8,128)}, f32[344,1]{1,0:T(8,128)}) custom-call(f32[16,1024]{1,0:T(8,128)} %get-tuple-element.213.refs_0_.refs_5_.rows_ref, bf16[344,1024]{1,0:T(8,128)(2,1)} %bitcast.26, bf16[344,256]{1,0:T(8,128)(2,1)} %get-tuple-element.152.refs_2_.rest_0_, ...), custom_call_target="tpu_custom_call" | custom-call | flops 1000000000 | bytes 1000000 | tf_op jit(solution)/shard_map/middle/pallas_call | solution.py:333
  120.4 12.5 %mlp.2 = (bf16[344,1024]{1,0:T(8,128)(2,1)}, bf16[344,1024]{1,0:T(8,128)(2,1)}, bf16[688,1024]{1,0:T(8,128)(2,1)}, bf16[688,1024]{1,0:T(8,128)(2,1)}, bf16[688,1...) custom-call(f32[16,1024]{1,0:T(8,128)} %get-tuple-element.213.refs_0_.refs_5_.rows_ref, ...), custom_call_target="tpu_custom_call" | custom-call | flops 1000000000 | bytes 1000000 | tf_op jit(solution)/shard_map/mlp/pallas_call | solution.py:475
  139.2 12.7 %mlp.3 = (bf16[344,1024]{1,0:T(8,128)(2,1)}, bf16[344,1024]{1,0:T(8,128)(2,1)}, bf16[688,1024]{1,0:T(8,128)(2,1)}, bf16[688,1024]{1,0:T(8,128)(2,1)}, bf16[688,1...) custom-call(f32[16,1024]{1,0:T(8,128)} %get-tuple-element.213.refs_0_.refs_5_.rows_ref, ...), custom_call_target="tpu_custom_call" | custom-call | flops 1000000000 | bytes 1000000 | tf_op jit(solution)/shard_map/mlp/pallas_call | solution.py:475
  156.4 17.3 %collective-permute-done.31.refs_8_ = bf16[344,1024]{1,0:T(8,128)(2,1)S(1)} collective-permute-done((bf16[344,1024]{1,0:T(8,128)(2,1)S(1)}, bf16[344,1024]{1,0:T(8,128)(2,1)S(1)}, u32[]{:S(2)}, u32[]{:S(2)}) %collective-permute-start.31) | collective-permute-done | bytes 704544 | tf_op jit(solution)/shard_map/ppermute | solution.py:822
  174.6 6.1 %turn.1 = (f32[344,1024]{1,0:T(8,128)}, bf16[344,1024]{1,0:T(8,128)(2,1)}, f32[8,1024]{1,0:T(8,128)}, bf16[344,256]{1,0:T(8,128)(2,1)}, bf16[344,256]{1,0:T(8,12...) custom-call(f32[16,1024]{1,0:T(8,128)} %get-tuple-element.213.refs_0_.refs_5_.rows_ref, ...), custom_call_target="tpu_custom_call" | custom-call | flops 1000000000 | bytes 1000000 | tf_op jit(solution)/shard_map/turn/pallas_call | solution.py:369
  182.6 4.2 %proj_weights.1 = bf16[4,1024,256]{2,1,0:T(8,128)(2,1)} custom-call(s32[2]{0:T(128)} %pad_add_fusion.ids_ref.refs_0_.refs_7_, bf16[344,1024]{1,0:T(8,128)(2,1)} %get-tuple-element.190.grad_ref, bf16[344,256]{1,0:T(8,128)(2,1)} %get-tuple-element.152.refs_2_.rest_0_, bf16[344,256]{1,0:T(8,128)(2,1)} %copy-done.52, bf16[344,256]{1,0:T(8,128)(2,1)} %copy-done.53, ...), custom_call_target="tpu_custom_call" | custom-call | flops 1000000000 | bytes 1000000 | tf_op jit(solution)/shard_map/proj_weights/pallas_call | solution.py:390
  191.2 16.2 %mlp_weights.1 = (bf16[512,2048]{1,0:T(8,128)(2,1)}, bf16[512,2048]{1,0:T(8,128)(2,1)}, f32[1,1024]{1,0:T(1,128)}, bf16[344,1024]{1,0:T(8,128)(2,1)}, bf16[344,1...) custom-call(s32[2]{0:T(128)} %pad_add_fusion.ids_ref.refs_0_.refs_7_, ...), custom_call_target="tpu_custom_call" | custom-call | flops 1000000000 | bytes 1000000 | tf_op jit(solution)/shard_map/mlp_weights/pallas_call | solution.py:541
  209.0 24.4 %attend_back.1 = (bf16[1376,768]{1,0:T(8,128)(2,1)}, f32[2,1,384]{2,1,0:T(1,128)}) custom-call(bf16[1376,768]{1,0:T(8,128)(2,1)} %get-tuple-element.150.qkv_ref, f32[1376,1]{1,0:T(8,128)} %get-tuple-element.151.bias_ref, f32[1376,256]{1,0:T(8,128)} %get-tuple-element.184.att_ref, f32[2,2,1376]{2,1,0:T(2,128)} %get-tuple-element.191.lse_ref, ...), custom_call_target="tpu_custom_call" | custom-call | flops 1000000000 | bytes 1000000 | tf_op jit(solution)/shard_map/attend_back/pallas_call | solution.py:290
  233.4 22.2 %collective-permute-done.35 = bf16[512,2048]{1,0:T(8,128)(2,1)} collective-permute-done((bf16[512,2048]{1,0:T(8,128)(2,1)}, bf16[512,2048]{1,0:T(8,128)(2,1)}, u32[]{:S(2)}, u32[]{:S(2)}) %collective-permute-start.35) | collective-permute-done | bytes 2097184 | tf_op jit(solution)/shard_map/ppermute | solution.py:822
  255.6 3.8 %add_convert_fusion = bf16[512,2048]{1,0:T(8,128)(2,1)} fusion(bf16[512,2048]{1,0:T(8,128)(2,1)} %collective-permute-done.35, bf16[512,2048]{1,0:T(8,128)(2,1)S(1)} %copy-done.5), kind=kLoop, calls=%fused_computation | loop fusion | flops 4194304 | bytes 6291456 | tf_op jit(solution)/shard_map/convert_element_type | solution.py:971
  263.0 6.8 %qkv_back.1 = (bf16[344,1024]{1,0:T(8,128)(2,1)}, bf16[344,1024]{1,0:T(8,128)(2,1)}, bf16[344,1024]{1,0:T(8,128)(2,1)}, bf16[344,1024]{1,0:T(8,128)(2,1)}, f32[8,1024]{1,0:T(8,128)}) custom-call(bf16[1376,768]{1,0:T(8,128)(2,1)} %get-tuple-element.201.refs_0_.refs_2_, bf16[1024,768]{1,0:T(8,128)(2,1)} %get-tuple-element.202.refs_1_, ...), custom_call_target="tpu_custom_call" | custom-call | flops 1000000000 | bytes 1000000 | tf_op jit(solution)/shard_map/qkv_back/pallas_call | solution.py:630
  269.8 7.0 %attn_weights.1 = (bf16[128,1152]{1,0:T(8,128)(2,1)}, bf16[128,1152]{1,0:T(8,128)(2,1)}, bf16[128,1152]{1,0:T(8,128)(2,1)}, bf16[128,1152]{1,0:T(8,128)(2,1)}, b...) custom-call(s32[2]{0:T(128)} %pad_add_fusion.ids_ref.refs_0_.refs_7_, bf16[1376,1024]{1,0:T(8,128)(2,1)} %get-tuple-element.183.refs_1_, ...), custom_call_target="tpu_custom_call" | custom-call | flops 1000000000 | bytes 1000000 | tf_op jit(solution)/shard_map/attn_weights/pallas_call | solution.py:702
  278.8 13.5 %collective-permute-done.36 = bf16[256,1152]{1,0:T(8,128)(2,1)S(1)} collective-permute-done((bf16[256,1152]{1,0:T(8,128)(2,1)}, bf16[256,1152]{1,0:T(8,128)(2,1)S(1)}, u32[]{:S(2)}, u32[]{:S(2)}) %collective-permute-start.36) | collective-permute-done | bytes 589856 | tf_op jit(solution)/shard_map/ppermute | solution.py:822
  298.2 9.9 %collective-permute-done.37 = bf16[128,1152]{1,0:T(8,128)(2,1)S(1)} collective-permute-done((bf16[128,1152]{1,0:T(8,128)(2,1)S(1)}, bf16[128,1152]{1,0:T(8,128)(2,1)S(1)}, u32[]{:S(2)}, u32[]{:S(2)}) %collective-permute-start.37) | collective-permute-done | bytes 294944 | tf_op jit(solution)/shard_map/ppermute | solution.py:822
  308.9 3.5 %collective-permute-done.42.rest_2_ = bf16[344,1024]{1,0:T(8,128)(2,1)S(1)} collective-permute-done((bf16[344,1024]{1,0:T(8,128)(2,1)S(1)}, bf16[344,1024]{1,0:T(8,128)(2,1)S(1)}, u32[]{:S(2)}, u32[]{:S(2)}) %collective-permute-start.42) | collective-permute-done | bytes 704544 | tf_op jit(solution)/shard_map/ppermute | solution.py:822
  320.3 4.0 %begin.1 = bf16[344,1024]{1,0:T(8,128)(2,1)} custom-call(f32[16,1024]{1,0:T(8,128)} %get-tuple-element.213.refs_0_.refs_5_.rows_ref, bf16[344,1024]{1,0:T(8,128)(2,1)} %bitcast.28, f32[1376,1]{1,0:T(8,128)} %get-tuple-element.203.refs_2_.mean_ref, f32[1376,1]{1,0:T(8,128)} %get-tuple-element.204.refs_3_.inv_ref, f32[344,1024]{1,0:T(8,128)} %get-tuple-element.219.middle_ref, ...), custom_call_target="tpu_custom_call" | custom-call | tf_op jit(solution)/shard_map/begin/pallas_call | solution.py:597
  (232 shorter events, 103.6 us)
Async XLA Ops:
  7.2 113.2 %all-gather.2.cloned.1.call-start = ((), (), s32[]{:S(2)}) async-start(), calls=%async_computation.2 | async-start | bytes 4718592 | tf_op jit(solution)/shard_map/all_gather | solution.py:895
  20.2 16.9 %collective-permute-start.6 = (bf16[128,1152]{1,0:T(8,128)(2,1)S(1)}, bf16[128,1152]{1,0:T(8,128)(2,1)S(1)}, u32[]{:S(2)}, u32[]{:S(2)}) collective-permute-start(bf16[128,1152]{1,0:T(8,128)(2,1)S(1)} %constant_dynamic-update-slice_fusion.refs_9_), channel_id=1, source_target_pairs={{0,16},{4,20},{8,24},{12,28},{16,0},{20,4},{24,8},{28,12},{1,17},{... | collective-permute-start | bytes 884744 | tf_op jit(solution)/shard_map/ppermute | solution.py:822
  37.3 232.5 %reduce-scatter.3.cloned.1.call-start = ((), (), s32[]{:S(2)}) async-start(), calls=%async_computation.3 | async-start | bytes 2621440 | tf_op jit(solution)/shard_map/reduce_scatter | solution.py:963
  38.0 25.4 %collective-permute-start.15 = (bf16[344,1024]{1,0:T(8,128)(2,1)S(1)}, bf16[344,1024]{1,0:T(8,128)(2,1)S(1)}, u32[]{:S(2)}, u32[]{:S(2)}) collective-permute-start(bf16[344,1024]{1,0:T(8,128)(2,1)S(1)} %bitcast.29), channel_id=1, source_target_pairs={{0,2},{1,3},{2,0},{3,1},{4,6},{5,7},{6,4},{7,5},{8,10},{9,11},{10,... | collective-permute-start | bytes 2113544 | tf_op jit(solution)/shard_map/ppermute | solution.py:822
  39.4 30.9 %collective-permute-start.13 = (bf16[344,1024]{1,0:T(8,128)(2,1)S(1)}, bf16[344,1024]{1,0:T(8,128)(2,1)S(1)}, u32[]{:S(2)}, u32[]{:S(2)}) collective-permute-start(bf16[344,1024]{1,0:T(8,128)(2,1)S(1)} %bitcast.33), channel_id=1, source_target_pairs={{0,2},{1,3},{2,0},{3,1},{4,6},{5,7},{6,4},{7,5},{8,10},{9,11},{10,... | collective-permute-start | bytes 2113544 | tf_op jit(solution)/shard_map/ppermute | solution.py:822
  43.1 20.4 %collective-permute-start.9 = (bf16[128,1152]{1,0:T(8,128)(2,1)S(1)}, bf16[128,1152]{1,0:T(8,128)(2,1)S(1)}, u32[]{:S(2)}, u32[]{:S(2)}) collective-permute-start(bf16[128,1152]{1,0:T(8,128)(2,1)S(1)} %collective-permute-done.7.refs_11_), channel_id=1, source_target_pairs={{0,4},{4,0},{8,12},{12,8},{16,20},{20,16},{24,28},{28,24},{1,5},{5... | collective-permute-start | bytes 884744 | tf_op jit(solution)/shard_map/ppermute | solution.py:822
  48.0 19.6 %collective-permute-start.12 = (bf16[128,1152]{1,0:T(8,128)(2,1)S(1)}, bf16[128,1152]{1,0:T(8,128)(2,1)S(1)}, u32[]{:S(2)}, u32[]{:S(2)}) collective-permute-start(bf16[128,1152]{1,0:T(8,128)(2,1)S(1)} %collective-permute-done.11.refs_15_), channel_id=1, source_target_pairs={{0,4},{4,0},{8,12},{12,8},{16,20},{20,16},{24,28},{28,24},{1,5},{5... | collective-permute-start | bytes 884744 | tf_op jit(solution)/shard_map/ppermute | solution.py:822
  83.2 17.1 %collective-permute-start.21 = (bf16[1024,256]{1,0:T(8,128)(2,1)}, bf16[1024,256]{1,0:T(8,128)(2,1)S(1)}, u32[]{:S(2)}, u32[]{:S(2)}) collective-permute-start(bf16[1024,256]{1,0:T(8,128)(2,1)} %get-tuple-element.156.refs_6_.refs_9_), channel_id=1, source_target_pairs={{0,2},{1,3},{2,0},{3,1},{4,6},{5,7},{6,4},{7,5},{8,10},{9,11},{10,... | collective-permute-start | bytes 1572872 | tf_op jit(solution)/shard_map/ppermute | solution.py:822
  84.7 26.5 %collective-permute-start.20 = (bf16[1024,256]{1,0:T(8,128)(2,1)}, bf16[1024,256]{1,0:T(8,128)(2,1)S(1)}, u32[]{:S(2)}, u32[]{:S(2)}) collective-permute-start(bf16[1024,256]{1,0:T(8,128)(2,1)} %get-tuple-element.156.refs_6_.refs_9_), channel_id=1, source_target_pairs={{0,1},{1,0},{2,3},{3,2},{4,5},{5,4},{6,7},{7,6},{8,9},{9,8},{10,11... | collective-permute-start | bytes 1572872 | tf_op jit(solution)/shard_map/ppermute | solution.py:822
  102.8 16.0 %collective-permute-start.24 = (bf16[344,1024]{1,0:T(8,128)(2,1)S(1)}, bf16[344,1024]{1,0:T(8,128)(2,1)S(1)}, u32[]{:S(2)}, u32[]{:S(2)}) collective-permute-start(bf16[344,1024]{1,0:T(8,128)(2,1)S(1)} %bitcast.34), channel_id=1, source_target_pairs={{0,1},{1,0},{2,3},{3,2},{4,5},{5,4},{6,7},{7,6},{8,9},{9,8},{10,11... | collective-permute-start | bytes 2113544 | tf_op jit(solution)/shard_map/ppermute | solution.py:822
  118.2 18.0 %collective-permute-start.25 = (bf16[344,1024]{1,0:T(8,128)(2,1)}, bf16[344,1024]{1,0:T(8,128)(2,1)S(1)}, u32[]{:S(2)}, u32[]{:S(2)}) collective-permute-start(bf16[344,1024]{1,0:T(8,128)(2,1)} %get-tuple-element.159.refs_1_), channel_id=1, source_target_pairs={{0,2},{1,3},{2,0},{3,1},{4,6},{5,7},{6,4},{7,5},{8,10},{9,11},{10,... | collective-permute-start | bytes 2113544 | tf_op jit(solution)/shard_map/ppermute | solution.py:822
  118.8 17.4 %collective-permute-start.27 = (bf16[344,1024]{1,0:T(8,128)(2,1)S(1)}, bf16[344,1024]{1,0:T(8,128)(2,1)S(1)}, u32[]{:S(2)}, u32[]{:S(2)}) collective-permute-start(bf16[344,1024]{1,0:T(8,128)(2,1)S(1)} %copy-done.11), channel_id=1, source_target_pairs={{0,1},{1,0},{2,3},{3,2},{4,5},{5,4},{6,7},{7,6},{8,9},{9,8},{10,11... | collective-permute-start | bytes 2113544 | tf_op jit(solution)/shard_map/ppermute | solution.py:822
  155.8 17.9 %collective-permute-start.31 = (bf16[344,1024]{1,0:T(8,128)(2,1)S(1)}, bf16[344,1024]{1,0:T(8,128)(2,1)S(1)}, u32[]{:S(2)}, u32[]{:S(2)}) collective-permute-start(bf16[344,1024]{1,0:T(8,128)(2,1)S(1)} %add_convert_fusion.3), channel_id=1, source_target_pairs={{0,2},{1,3},{2,0},{3,1},{4,6},{5,7},{6,4},{7,5},{8,10},{9,11},{10,... | collective-permute-start | bytes 2113544 | tf_op jit(solution)/shard_map/ppermute | solution.py:822
  191.1 125.4 %reduce-scatter.5.cloned.1.call-start = ((), (), s32[]{:S(2)}) async-start(), calls=%async_computation.4 | async-start | bytes 2621440 | tf_op jit(solution)/shard_map/reduce_scatter | solution.py:973
  207.4 48.2 %collective-permute-start.35 = (bf16[512,2048]{1,0:T(8,128)(2,1)}, bf16[512,2048]{1,0:T(8,128)(2,1)}, u32[]{:S(2)}, u32[]{:S(2)}) collective-permute-start(bf16[512,2048]{1,0:T(8,128)(2,1)} %get-tuple-element.199), channel_id=1, source_target_pairs={{0,4},{4,0},{8,12},{12,8},{16,20},{20,16},{24,28},{28,24},{1,5},{5... | collective-permute-start | bytes 6291464 | tf_op jit(solution)/shard_map/ppermute | solution.py:822
  276.8 15.5 %collective-permute-start.36 = (bf16[256,1152]{1,0:T(8,128)(2,1)}, bf16[256,1152]{1,0:T(8,128)(2,1)S(1)}, u32[]{:S(2)}, u32[]{:S(2)}) collective-permute-start(bf16[256,1152]{1,0:T(8,128)(2,1)} %get-tuple-element.212), channel_id=1, source_target_pairs={{0,4},{4,0},{8,12},{12,8},{16,20},{20,16},{24,28},{28,24},{1,5},{5... | collective-permute-start | bytes 1769480 | tf_op jit(solution)/shard_map/ppermute | solution.py:822
  278.3 17.0 %collective-permute-start.41 = (bf16[344,1024]{1,0:T(8,128)(2,1)S(1)}, bf16[344,1024]{1,0:T(8,128)(2,1)S(1)}, u32[]{:S(2)}, u32[]{:S(2)}) collective-permute-start(bf16[344,1024]{1,0:T(8,128)(2,1)S(1)} %copy-done.49), channel_id=1, source_target_pairs={{0,1},{1,0},{2,3},{3,2},{4,5},{5,4},{6,7},{7,6},{8,9},{9,8},{10,11... | collective-permute-start | bytes 2113544 | tf_op jit(solution)/shard_map/ppermute | solution.py:822
  278.3 18.2 %collective-permute-start.39 = (bf16[344,1024]{1,0:T(8,128)(2,1)S(1)}, bf16[344,1024]{1,0:T(8,128)(2,1)S(1)}, u32[]{:S(2)}, u32[]{:S(2)}) collective-permute-start(bf16[344,1024]{1,0:T(8,128)(2,1)S(1)} %add_convert_fusion.2), channel_id=1, source_target_pairs={{0,2},{1,3},{2,0},{3,1},{4,6},{5,7},{6,4},{7,5},{8,10},{9,11},{10,... | collective-permute-start | bytes 2113544 | tf_op jit(solution)/shard_map/ppermute | solution.py:822
  293.4 14.7 %collective-permute-start.37 = (bf16[128,1152]{1,0:T(8,128)(2,1)S(1)}, bf16[128,1152]{1,0:T(8,128)(2,1)S(1)}, u32[]{:S(2)}, u32[]{:S(2)}) collective-permute-start(bf16[128,1152]{1,0:T(8,128)(2,1)S(1)} %add_convert_fusion.8), channel_id=1, source_target_pairs={{0,8},{4,12},{8,0},{12,4},{16,24},{20,28},{24,16},{28,20},{1,9},{5... | collective-permute-start | bytes 884744 | tf_op jit(solution)/shard_map/ppermute | solution.py:822
  295.5 16.9 %collective-permute-start.42 = (bf16[344,1024]{1,0:T(8,128)(2,1)S(1)}, bf16[344,1024]{1,0:T(8,128)(2,1)S(1)}, u32[]{:S(2)}, u32[]{:S(2)}) collective-permute-start(bf16[344,1024]{1,0:T(8,128)(2,1)S(1)} %add_convert_fusion.1), channel_id=1, source_target_pairs={{0,2},{1,3},{2,0},{3,1},{4,6},{5,7},{6,4},{7,5},{8,10},{9,11},{10,... | collective-permute-start | bytes 2113544 | tf_op jit(solution)/shard_map/ppermute | solution.py:822
  296.5 18.5 %collective-permute-start.46 = (bf16[256,1152]{1,0:T(8,128)(2,1)S(1)}, bf16[256,1152]{1,0:T(8,128)(2,1)S(1)}, u32[]{:S(2)}, u32[]{:S(2)}) collective-permute-start(bf16[256,1152]{1,0:T(8,128)(2,1)S(1)} %copy-done.51), channel_id=1, source_target_pairs={{0,4},{4,0},{8,12},{12,8},{16,20},{20,16},{24,28},{28,24},{1,5},{5... | collective-permute-start | bytes 1769480 | tf_op jit(solution)/shard_map/ppermute | solution.py:822
  297.7 20.7 %collective-permute-start.38 = (bf16[344,1024]{1,0:T(8,128)(2,1)}, bf16[344,1024]{1,0:T(8,128)(2,1)S(1)}, u32[]{:S(2)}, u32[]{:S(2)}) collective-permute-start(bf16[344,1024]{1,0:T(8,128)(2,1)} %get-tuple-element.216), channel_id=1, source_target_pairs={{0,1},{1,0},{2,3},{3,2},{4,5},{5,4},{6,7},{7,6},{8,9},{9,8},{10,11... | collective-permute-start | bytes 2113544 | tf_op jit(solution)/shard_map/ppermute | solution.py:822
  297.7 21.7 %collective-permute-start.40 = (bf16[344,1024]{1,0:T(8,128)(2,1)}, bf16[344,1024]{1,0:T(8,128)(2,1)S(1)}, u32[]{:S(2)}, u32[]{:S(2)}) collective-permute-start(bf16[344,1024]{1,0:T(8,128)(2,1)} %get-tuple-element.221), channel_id=1, source_target_pairs={{0,1},{1,0},{2,3},{3,2},{4,5},{5,4},{6,7},{7,6},{8,9},{9,8},{10,11... | collective-permute-start | bytes 2113544 | tf_op jit(solution)/shard_map/ppermute | solution.py:822
  312.5 18.0 %collective-permute-start.48 = (bf16[128,1152]{1,0:T(8,128)(2,1)}, bf16[128,1152]{1,0:T(8,128)(2,1)S(1)}, u32[]{:S(2)}, u32[]{:S(2)}) collective-permute-start(bf16[128,1152]{1,0:T(8,128)(2,1)} %add_convert_fusion.4), channel_id=1, source_target_pairs={{0,16},{4,20},{8,24},{12,28},{16,0},{20,4},{24,8},{28,12},{1,17},{... | collective-permute-start | bytes 884744 | tf_op jit(solution)/shard_map/ppermute | solution.py:822
  (86 other events, 716.8 us)
Sparse Core Ops, SparseCore 0:
  37.4 77.3 all-gather.1
  191.2 31.8 reduce-scatter.2
  259.6 49.0 reduce-scatter.4

commit v7 on v6

--- a/solution.py
+++ b/solution.py
@@ -956,7 +956,7 @@
     if direct:
         other_mlp = swap(after(send_mlp, *norm2_terms), 1, "dp")
     middle_grad, branch_grad, turn_sums, *att_grads = turn(
-        vector_rows, live[0], cotangent[0], unit2, inverse2, branch1, norm2_terms, projs
+        after(vector_rows, grad_scale2), live[0], cotangent[0], unit2, inverse2, branch1, norm2_terms, projs
     )
     att_grads = exchange(att_grads)
     proj_parts = proj_weights(ids, branch_grad, attended_own).reshape(group * width, -1)

time: 354 us -> 336 us (0.949)
  waiting for transfers between devices: 135 us -> 123 us
  starting transfers between devices: 41.8 us -> 37.5 us
    ppermute x52, waiting for transfers between devices: 135 us -> 123 us  [swap(): return lax.ppermute(value, axis, [(i, i ^ bit) for i in range(size)])]
    ppermute x52, starting transfers between devices: 41.7 us -> 37.4 us  [swap(): return lax.ppermute(value, axis, [(i, i ^ bit) for i in range(size)])]
  transfers between devices with their start and end apart: 55 -> 55, of which waited for: 30 -> 28; matrix products, arithmetic and copies ran while one was open for 3% -> 3% of each run, Pallas kernels for 32% -> 34%
where the time goes in v7:
time: 336 us; the launch traced here: 331 us
  Pallas kernels  136 us (40%)
  waiting for transfers between devices  123 us (37%)
  starting transfers between devices  37.5 us (11%)
  between operations  15.1 us (4%)
  other arithmetic  10.9 us (3%)
  local copies, waits for them, and re-layouts  7.98 us (2%)
    ppermute x52, waiting for transfers between devices, swap(): return lax.ppermute(value, axis, [(i, i ^ bit) for i in range(size)])  123 us
    ppermute x52, starting transfers between devices, swap(): return lax.ppermute(value, axis, [(i, i ^ bit) for i in range(size)])  37.4 us
    pallas_call x2, Pallas kernels, mlp(): pl.pallas_call(lambda *refs: mlp_kernel(count, shards, group, *refs), gri...  25.3 us
    pallas_call x1, Pallas kernels, attend_back(): pl.pallas_call(attend_back_kernel, grid=(pairs,), in_specs=[pl.BlockSpec(...  24.4 us
    pallas_call x1, Pallas kernels, mlp_weights(): pl.pallas_call(lambda *refs: mlp_weights_kernel(direct, *refs), grid_spec...  16.2 us
    pallas_call x1, Pallas kernels, attend(): pl.pallas_call(attend_kernel, grid=(pairs,), in_specs=[pl.BlockSpec((leng...  15.6 us
    pallas_call x1, Pallas kernels, project(): pl.pallas_call(lambda *refs: project_kernel(ordered, group, count_column,...  8.24 us
    unnamed x113, local copies, waits for them, and re-layouts  7.92 us
  transfers between devices with their start and end apart: 55, of which 28 were waited for; matrix products, arithmetic and copies ran while one was open for 3% of the time, Pallas kernels for 34%

profile of v7, /device:TPU:0, one launch (start us, length us, event | category | flops | bytes accessed | tf_op | source)
XLA Modules:
  0.0 330.6 jit_solution(3498641963006718483)
XLA Ops:
  29.6 7.6 %collective-permute-done.7.refs_11_ = bf16[128,1152]{1,0:T(8,128)(2,1)S(1)} collective-permute-done((bf16[128,1152]{1,0:T(8,128)(2,1)S(1)}, bf16[128,1152]{1,0:T(8,128)(2,1)S(1)}, u32[]{:S(2)}, u32[]{:S(2)}) %collective-permute-start.7) | collective-permute-done | bytes 294944 | tf_op jit(solution)/shard_map/ppermute | solution.py:822
  44.3 4.2 %collective-permute-done.11.refs_15_ = bf16[128,1152]{1,0:T(8,128)(2,1)S(1)} collective-permute-done((bf16[128,1152]{1,0:T(8,128)(2,1)S(1)}, bf16[128,1152]{1,0:T(8,128)(2,1)S(1)}, u32[]{:S(2)}, u32[]{:S(2)}) %collective-permute-start.11) | collective-permute-done | bytes 294944 | tf_op jit(solution)/shard_map/ppermute | solution.py:822
  49.0 15.1 %collective-permute-done.9.refs_12_ = bf16[128,1152]{1,0:T(8,128)(2,1)S(1)} collective-permute-done((bf16[128,1152]{1,0:T(8,128)(2,1)S(1)}, bf16[128,1152]{1,0:T(8,128)(2,1)S(1)}, u32[]{:S(2)}, u32[]{:S(2)}) %collective-permute-start.9) | collective-permute-done | bytes 294944 | tf_op jit(solution)/shard_map/ppermute | solution.py:822
  64.1 3.7 %collective-permute-done.12.refs_16_ = bf16[128,1152]{1,0:T(8,128)(2,1)S(1)} collective-permute-done((bf16[128,1152]{1,0:T(8,128)(2,1)S(1)}, bf16[128,1152]{1,0:T(8,128)(2,1)S(1)}, u32[]{:S(2)}, u32[]{:S(2)}) %collective-permute-start.12) | collective-permute-done | bytes 294944 | tf_op jit(solution)/shard_map/ppermute | solution.py:822
  72.6 8.2 %project.1 = (bf16[1024,768]{1,0:T(8,128)(2,1)}, bf16[1024,256]{1,0:T(8,128)(2,1)}, f32[16,1024]{1,0:T(8,128)}, bf16[1376,1024]{1,0:T(8,128)(2,1)}, bf16[1376,76...) custom-call(s32[2]{0:T(128)} %pad_add_fusion.ids_ref.refs_0_.refs_7_, ...), custom_call_target="tpu_custom_call" | custom-call | flops 1000000000 | bytes 1000000 | tf_op jit(solution)/shard_map/project/pallas_call | solution.py:175
  82.4 15.6 %attend.1 = (f32[1376,256]{1,0:T(8,128)}, f32[2,2,1376]{2,1,0:T(2,128)}, bf16[344,256]{1,0:T(8,128)(2,1)}, bf16[344,256]{1,0:T(8,128)(2,1)}, bf16[344,256]{1,0:T(8,128)(2,1)}, /*index=5*/bf16[344,256]{1,0:T(8,128)(2,1)}) custom-call(bf16[1376,768]{1,0:T(8,128)(2,1)} %get-tuple-element.151.qkv_ref, f32[1376,1]{1,0:T(8,128)} %get-tuple-element.152.bias_ref), custom_call_target="tpu_custom_call" | custom-call | flops 1000000000 | bytes 1000000 | tf_op jit(solution)/shard_map/attend/pallas_call | solution.py:231
  100.9 5.2 %collective-permute-done.18.refs_4_.rest_2_ = bf16[344,256]{1,0:T(8,128)(2,1)S(1)} collective-permute-done((bf16[344,256]{1,0:T(8,128)(2,1)}, bf16[344,256]{1,0:T(8,128)(2,1)S(1)}, u32[]{:S(2)}, u32[]{:S(2)}) %collective-permute-start.18) | collective-permute-done | bytes 176160 | tf_op jit(solution)/shard_map/ppermute | solution.py:822
  110.0 5.3 %middle.1 = (f32[344,1024]{1,0:T(8,128)}, f32[344,1024]{1,0:T(8,128)}, bf16[344,1024]{1,0:T(8,128)(2,1)}, f32[344,1024]{1,0:T(8,128)}, f32[344,1]{1,0:T(8,128)}) custom-call(f32[16,1024]{1,0:T(8,128)} %get-tuple-element.215.refs_0_.refs_5_.rows_ref, bf16[344,1024]{1,0:T(8,128)(2,1)} %bitcast.26, bf16[344,256]{1,0:T(8,128)(2,1)} %get-tuple-element.153.refs_2_.rest_0_, ...), custom_call_target="tpu_custom_call" | custom-call | flops 1000000000 | bytes 1000000 | tf_op jit(solution)/shard_map/middle/pallas_call | solution.py:333
  118.1 12.5 %mlp.2 = (bf16[344,1024]{1,0:T(8,128)(2,1)}, bf16[344,1024]{1,0:T(8,128)(2,1)}, bf16[688,1024]{1,0:T(8,128)(2,1)}, bf16[688,1024]{1,0:T(8,128)(2,1)}, bf16[688,1...) custom-call(f32[16,1024]{1,0:T(8,128)} %get-tuple-element.215.refs_0_.refs_5_.rows_ref, ...), custom_call_target="tpu_custom_call" | custom-call | flops 1000000000 | bytes 1000000 | tf_op jit(solution)/shard_map/mlp/pallas_call | solution.py:475
  136.9 12.8 %mlp.3 = (bf16[344,1024]{1,0:T(8,128)(2,1)}, bf16[344,1024]{1,0:T(8,128)(2,1)}, bf16[688,1024]{1,0:T(8,128)(2,1)}, bf16[688,1024]{1,0:T(8,128)(2,1)}, bf16[688,1...) custom-call(f32[16,1024]{1,0:T(8,128)} %get-tuple-element.215.refs_0_.refs_5_.rows_ref, ...), custom_call_target="tpu_custom_call" | custom-call | flops 1000000000 | bytes 1000000 | tf_op jit(solution)/shard_map/mlp/pallas_call | solution.py:475
  154.1 16.2 %mlp_weights.1 = (bf16[512,2048]{1,0:T(8,128)(2,1)}, bf16[512,2048]{1,0:T(8,128)(2,1)}, f32[1,1024]{1,0:T(1,128)}, bf16[344,1024]{1,0:T(8,128)(2,1)}, bf16[344,1...) custom-call(s32[2]{0:T(128)} %pad_add_fusion.ids_ref.refs_0_.refs_7_, ...), custom_call_target="tpu_custom_call" | custom-call | flops 1000000000 | bytes 1000000 | tf_op jit(solution)/shard_map/mlp_weights/pallas_call | solution.py:541
  172.2 6.0 %turn.1 = (f32[344,1024]{1,0:T(8,128)}, bf16[344,1024]{1,0:T(8,128)(2,1)}, f32[8,1024]{1,0:T(8,128)}, bf16[344,256]{1,0:T(8,128)(2,1)}, bf16[344,256]{1,0:T(8,12...) custom-call(f32[16,1024]{1,0:T(8,128)} %get-tuple-element.215.refs_0_.refs_5_.rows_ref, ...), custom_call_target="tpu_custom_call" | custom-call | flops 1000000000 | bytes 1000000 | tf_op jit(solution)/shard_map/turn/pallas_call | solution.py:369
  180.1 4.1 %proj_weights.1 = bf16[4,1024,256]{2,1,0:T(8,128)(2,1)} custom-call(s32[2]{0:T(128)} %pad_add_fusion.ids_ref.refs_0_.refs_7_, bf16[344,1024]{1,0:T(8,128)(2,1)} %get-tuple-element.193.grad_ref, bf16[344,256]{1,0:T(8,128)(2,1)} %get-tuple-element.153.refs_2_.rest_0_, bf16[344,256]{1,0:T(8,128)(2,1)} %copy-done.52, bf16[344,256]{1,0:T(8,128)(2,1)} %copy-done.53, ...), custom_call_target="tpu_custom_call" | custom-call | flops 1000000000 | bytes 1000000 | tf_op jit(solution)/shard_map/proj_weights/pallas_call | solution.py:390
  189.3 24.4 %attend_back.1 = (bf16[1376,768]{1,0:T(8,128)(2,1)}, f32[2,1,384]{2,1,0:T(1,128)}) custom-call(bf16[1376,768]{1,0:T(8,128)(2,1)} %get-tuple-element.151.qkv_ref, f32[1376,1]{1,0:T(8,128)} %get-tuple-element.152.bias_ref, f32[1376,256]{1,0:T(8,128)} %get-tuple-element.185.att_ref, f32[2,2,1376]{2,1,0:T(2,128)} %get-tuple-element.194.lse_ref, ...), custom_call_target="tpu_custom_call" | custom-call | flops 1000000000 | bytes 1000000 | tf_op jit(solution)/shard_map/attend_back/pallas_call | solution.py:290
  213.8 23.2 %collective-permute-done.35 = bf16[512,2048]{1,0:T(8,128)(2,1)} collective-permute-done((bf16[512,2048]{1,0:T(8,128)(2,1)}, bf16[512,2048]{1,0:T(8,128)(2,1)}, u32[]{:S(2)}, u32[]{:S(2)}) %collective-permute-start.35) | collective-permute-done | bytes 2097184 | tf_op jit(solution)/shard_map/ppermute | solution.py:822
  236.9 3.8 %add_convert_fusion = bf16[512,2048]{1,0:T(8,128)(2,1)} fusion(bf16[512,2048]{1,0:T(8,128)(2,1)} %collective-permute-done.35, bf16[512,2048]{1,0:T(8,128)(2,1)S(1)} %copy-done.5), kind=kLoop, calls=%fused_computation | loop fusion | flops 4194304 | bytes 6291456 | tf_op jit(solution)/shard_map/convert_element_type | solution.py:971
  244.3 6.8 %qkv_back.1 = (bf16[344,1024]{1,0:T(8,128)(2,1)}, bf16[344,1024]{1,0:T(8,128)(2,1)}, bf16[344,1024]{1,0:T(8,128)(2,1)}, bf16[344,1024]{1,0:T(8,128)(2,1)}, f32[8,1024]{1,0:T(8,128)}) custom-call(bf16[1376,768]{1,0:T(8,128)(2,1)} %get-tuple-element.204.refs_0_.refs_2_, bf16[1024,768]{1,0:T(8,128)(2,1)} %get-tuple-element.205.refs_1_, ...), custom_call_target="tpu_custom_call" | custom-call | flops 1000000000 | bytes 1000000 | tf_op jit(solution)/shard_map/qkv_back/pallas_call | solution.py:630
  251.1 7.0 %attn_weights.1 = (bf16[128,1152]{1,0:T(8,128)(2,1)}, bf16[128,1152]{1,0:T(8,128)(2,1)}, bf16[128,1152]{1,0:T(8,128)(2,1)}, bf16[128,1152]{1,0:T(8,128)(2,1)}, b...) custom-call(s32[2]{0:T(128)} %pad_add_fusion.ids_ref.refs_0_.refs_7_, bf16[1376,1024]{1,0:T(8,128)(2,1)} %get-tuple-element.184.refs_1_, ...), custom_call_target="tpu_custom_call" | custom-call | flops 1000000000 | bytes 1000000 | tf_op jit(solution)/shard_map/attn_weights/pallas_call | solution.py:702
  259.1 14.5 %collective-permute-done.36 = bf16[256,1152]{1,0:T(8,128)(2,1)S(1)} collective-permute-done((bf16[256,1152]{1,0:T(8,128)(2,1)}, bf16[256,1152]{1,0:T(8,128)(2,1)S(1)}, u32[]{:S(2)}, u32[]{:S(2)}) %collective-permute-start.36) | collective-permute-done | bytes 589856 | tf_op jit(solution)/shard_map/ppermute | solution.py:822
  274.7 3.4 %collective-permute-start.37 = (bf16[128,1152]{1,0:T(8,128)(2,1)S(1)}, bf16[128,1152]{1,0:T(8,128)(2,1)S(1)}, u32[]{:S(2)}, u32[]{:S(2)}) collective-permute-start(bf16[128,1152]{1,0:T(8,128)(2,1)S(1)} %add_convert_fusion.8), channel_id=1, source_target_pairs={{0,8},{4,12},{8,0},{12,4},{16,24},{20,28},{24,16},{28,20},{1,9},{5... | collective-permute-start | bytes 884744 | tf_op jit(solution)/shard_map/ppermute | solution.py:822
  279.8 9.6 %collective-permute-done.37 = bf16[128,1152]{1,0:T(8,128)(2,1)S(1)} collective-permute-done((bf16[128,1152]{1,0:T(8,128)(2,1)S(1)}, bf16[128,1152]{1,0:T(8,128)(2,1)S(1)}, u32[]{:S(2)}, u32[]{:S(2)}) %collective-permute-start.37) | collective-permute-done | bytes 294944 | tf_op jit(solution)/shard_map/ppermute | solution.py:822
  290.3 5.0 %collective-permute-done.42.rest_2_ = bf16[344,1024]{1,0:T(8,128)(2,1)S(1)} collective-permute-done((bf16[344,1024]{1,0:T(8,128)(2,1)S(1)}, bf16[344,1024]{1,0:T(8,128)(2,1)S(1)}, u32[]{:S(2)}, u32[]{:S(2)}) %collective-permute-start.42) | collective-permute-done | bytes 704544 | tf_op jit(solution)/shard_map/ppermute | solution.py:822
  305.8 4.0 %begin.1 = bf16[344,1024]{1,0:T(8,128)(2,1)} custom-call(f32[16,1024]{1,0:T(8,128)} %get-tuple-element.215.refs_0_.refs_5_.rows_ref, bf16[344,1024]{1,0:T(8,128)(2,1)} %bitcast.28, f32[1376,1]{1,0:T(8,128)} %get-tuple-element.206.refs_2_.mean_ref, f32[1376,1]{1,0:T(8,128)} %get-tuple-element.207.refs_3_.inv_ref, f32[344,1024]{1,0:T(8,128)} %get-tuple-element.221.middle_ref, ...), custom_call_target="tpu_custom_call" | custom-call | tf_op jit(solution)/shard_map/begin/pallas_call | solution.py:597
  317.4 3.8 %collective-permute-done.50.refs_2_ = bf16[32,1152]{1,0:T(8,128)(2,1)S(1)} collective-permute-done((bf16[32,1152]{1,0:T(8,128)(2,1)}, bf16[32,1152]{1,0:T(8,128)(2,1)S(1)}, u32[]{:S(2)}, u32[]{:S(2)}) %collective-permute-start.50) | collective-permute-done | bytes 73760 | tf_op jit(solution)/shard_map/ppermute | solution.py:822
  (232 shorter events, 93.4 us)
Async XLA Ops:
  7.2 110.9 %all-gather.2.cloned.1.call-start = ((), (), s32[]{:S(2)}) async-start(), calls=%async_computation.2 | async-start | bytes 4718592 | tf_op jit(solution)/shard_map/all_gather | solution.py:895
  23.5 16.1 %collective-permute-start.6 = (bf16[128,1152]{1,0:T(8,128)(2,1)S(1)}, bf16[128,1152]{1,0:T(8,128)(2,1)S(1)}, u32[]{:S(2)}, u32[]{:S(2)}) collective-permute-start(bf16[128,1152]{1,0:T(8,128)(2,1)S(1)} %constant_dynamic-update-slice_fusion.refs_9_), channel_id=1, source_target_pairs={{0,16},{4,20},{8,24},{12,28},{16,0},{20,4},{24,8},{28,12},{1,17},{... | collective-permute-start | bytes 884744 | tf_op jit(solution)/shard_map/ppermute | solution.py:822
  39.6 211.5 %reduce-scatter.3.cloned.1.call-start = ((), (), s32[]{:S(2)}) async-start(), calls=%async_computation.3 | async-start | bytes 2621440 | tf_op jit(solution)/shard_map/reduce_scatter | solution.py:963
  39.7 28.2 %collective-permute-start.13 = (bf16[344,1024]{1,0:T(8,128)(2,1)S(1)}, bf16[344,1024]{1,0:T(8,128)(2,1)S(1)}, u32[]{:S(2)}, u32[]{:S(2)}) collective-permute-start(bf16[344,1024]{1,0:T(8,128)(2,1)S(1)} %bitcast.33), channel_id=1, source_target_pairs={{0,2},{1,3},{2,0},{3,1},{4,6},{5,7},{6,4},{7,5},{8,10},{9,11},{10,... | collective-permute-start | bytes 2113544 | tf_op jit(solution)/shard_map/ppermute | solution.py:822
  41.1 28.4 %collective-permute-start.15 = (bf16[344,1024]{1,0:T(8,128)(2,1)S(1)}, bf16[344,1024]{1,0:T(8,128)(2,1)S(1)}, u32[]{:S(2)}, u32[]{:S(2)}) collective-permute-start(bf16[344,1024]{1,0:T(8,128)(2,1)S(1)} %bitcast.29), channel_id=1, source_target_pairs={{0,2},{1,3},{2,0},{3,1},{4,6},{5,7},{6,4},{7,5},{8,10},{9,11},{10,... | collective-permute-start | bytes 2113544 | tf_op jit(solution)/shard_map/ppermute | solution.py:822
  42.2 21.9 %collective-permute-start.10 = (bf16[128,1152]{1,0:T(8,128)(2,1)S(1)}, bf16[128,1152]{1,0:T(8,128)(2,1)S(1)}, u32[]{:S(2)}, u32[]{:S(2)}) collective-permute-start(bf16[128,1152]{1,0:T(8,128)(2,1)S(1)} %collective-permute-done.6.refs_13_), channel_id=1, source_target_pairs={{0,4},{4,0},{8,12},{12,8},{16,20},{20,16},{24,28},{28,24},{1,5},{5... | collective-permute-start | bytes 884744 | tf_op jit(solution)/shard_map/ppermute | solution.py:822
  42.7 21.4 %collective-permute-start.9 = (bf16[128,1152]{1,0:T(8,128)(2,1)S(1)}, bf16[128,1152]{1,0:T(8,128)(2,1)S(1)}, u32[]{:S(2)}, u32[]{:S(2)}) collective-permute-start(bf16[128,1152]{1,0:T(8,128)(2,1)S(1)} %collective-permute-done.7.refs_11_), channel_id=1, source_target_pairs={{0,4},{4,0},{8,12},{12,8},{16,20},{20,16},{24,28},{28,24},{1,5},{5... | collective-permute-start | bytes 884744 | tf_op jit(solution)/shard_map/ppermute | solution.py:822
  48.5 19.3 %collective-permute-start.12 = (bf16[128,1152]{1,0:T(8,128)(2,1)S(1)}, bf16[128,1152]{1,0:T(8,128)(2,1)S(1)}, u32[]{:S(2)}, u32[]{:S(2)}) collective-permute-start(bf16[128,1152]{1,0:T(8,128)(2,1)S(1)} %collective-permute-done.11.refs_15_), channel_id=1, source_target_pairs={{0,4},{4,0},{8,12},{12,8},{16,20},{20,16},{24,28},{28,24},{1,5},{5... | collective-permute-start | bytes 884744 | tf_op jit(solution)/shard_map/ppermute | solution.py:822
  80.8 17.1 %collective-permute-start.21 = (bf16[1024,256]{1,0:T(8,128)(2,1)}, bf16[1024,256]{1,0:T(8,128)(2,1)S(1)}, u32[]{:S(2)}, u32[]{:S(2)}) collective-permute-start(bf16[1024,256]{1,0:T(8,128)(2,1)} %get-tuple-element.157.refs_6_.refs_9_), channel_id=1, source_target_pairs={{0,2},{1,3},{2,0},{3,1},{4,6},{5,7},{6,4},{7,5},{8,10},{9,11},{10,... | collective-permute-start | bytes 1572872 | tf_op jit(solution)/shard_map/ppermute | solution.py:822
  82.4 26.6 %collective-permute-start.20 = (bf16[1024,256]{1,0:T(8,128)(2,1)}, bf16[1024,256]{1,0:T(8,128)(2,1)S(1)}, u32[]{:S(2)}, u32[]{:S(2)}) collective-permute-start(bf16[1024,256]{1,0:T(8,128)(2,1)} %get-tuple-element.157.refs_6_.refs_9_), channel_id=1, source_target_pairs={{0,1},{1,0},{2,3},{3,2},{4,5},{5,4},{6,7},{7,6},{8,9},{9,8},{10,11... | collective-permute-start | bytes 1572872 | tf_op jit(solution)/shard_map/ppermute | solution.py:822
  100.5 15.9 %collective-permute-start.24 = (bf16[344,1024]{1,0:T(8,128)(2,1)S(1)}, bf16[344,1024]{1,0:T(8,128)(2,1)S(1)}, u32[]{:S(2)}, u32[]{:S(2)}) collective-permute-start(bf16[344,1024]{1,0:T(8,128)(2,1)S(1)} %bitcast.34), channel_id=1, source_target_pairs={{0,1},{1,0},{2,3},{3,2},{4,5},{5,4},{6,7},{7,6},{8,9},{9,8},{10,11... | collective-permute-start | bytes 2113544 | tf_op jit(solution)/shard_map/ppermute | solution.py:822
  115.9 18.0 %collective-permute-start.25 = (bf16[344,1024]{1,0:T(8,128)(2,1)}, bf16[344,1024]{1,0:T(8,128)(2,1)S(1)}, u32[]{:S(2)}, u32[]{:S(2)}) collective-permute-start(bf16[344,1024]{1,0:T(8,128)(2,1)} %get-tuple-element.160.refs_1_), channel_id=1, source_target_pairs={{0,2},{1,3},{2,0},{3,1},{4,6},{5,7},{6,4},{7,5},{8,10},{9,11},{10,... | collective-permute-start | bytes 2113544 | tf_op jit(solution)/shard_map/ppermute | solution.py:822
  116.4 17.5 %collective-permute-start.27 = (bf16[344,1024]{1,0:T(8,128)(2,1)S(1)}, bf16[344,1024]{1,0:T(8,128)(2,1)S(1)}, u32[]{:S(2)}, u32[]{:S(2)}) collective-permute-start(bf16[344,1024]{1,0:T(8,128)(2,1)S(1)} %copy-done.11), channel_id=1, source_target_pairs={{0,1},{1,0},{2,3},{3,2},{4,5},{5,4},{6,7},{7,6},{8,9},{9,8},{10,11... | collective-permute-start | bytes 2113544 | tf_op jit(solution)/shard_map/ppermute | solution.py:822
  149.9 20.4 %collective-permute-start.30 = (bf16[344,1024]{1,0:T(8,128)(2,1)S(1)}, bf16[344,1024]{1,0:T(8,128)(2,1)S(1)}, u32[]{:S(2)}, u32[]{:S(2)}) collective-permute-start(bf16[344,1024]{1,0:T(8,128)(2,1)S(1)} %copy-done.49), channel_id=1, source_target_pairs={{0,1},{1,0},{2,3},{3,2},{4,5},{5,4},{6,7},{7,6},{8,9},{9,8},{10,11... | collective-permute-start | bytes 2113544 | tf_op jit(solution)/shard_map/ppermute | solution.py:822
  153.5 17.9 %collective-permute-start.31 = (bf16[344,1024]{1,0:T(8,128)(2,1)S(1)}, bf16[344,1024]{1,0:T(8,128)(2,1)S(1)}, u32[]{:S(2)}, u32[]{:S(2)}) collective-permute-start(bf16[344,1024]{1,0:T(8,128)(2,1)S(1)} %add_convert_fusion.3), channel_id=1, source_target_pairs={{0,2},{1,3},{2,0},{3,1},{4,6},{5,7},{6,4},{7,5},{8,10},{9,11},{10,... | collective-permute-start | bytes 2113544 | tf_op jit(solution)/shard_map/ppermute | solution.py:822
  188.7 110.1 %reduce-scatter.5.cloned.1.call-start = ((), (), s32[]{:S(2)}) async-start(), calls=%async_computation.4 | async-start | bytes 2621440 | tf_op jit(solution)/shard_map/reduce_scatter | solution.py:973
  188.7 48.2 %collective-permute-start.35 = (bf16[512,2048]{1,0:T(8,128)(2,1)}, bf16[512,2048]{1,0:T(8,128)(2,1)}, u32[]{:S(2)}, u32[]{:S(2)}) collective-permute-start(bf16[512,2048]{1,0:T(8,128)(2,1)} %get-tuple-element.202), channel_id=1, source_target_pairs={{0,4},{4,0},{8,12},{12,8},{16,20},{20,16},{24,28},{28,24},{1,5},{5... | collective-permute-start | bytes 6291464 | tf_op jit(solution)/shard_map/ppermute | solution.py:822
  258.5 19.7 %collective-permute-start.41 = (bf16[344,1024]{1,0:T(8,128)(2,1)S(1)}, bf16[344,1024]{1,0:T(8,128)(2,1)S(1)}, u32[]{:S(2)}, u32[]{:S(2)}) collective-permute-start(bf16[344,1024]{1,0:T(8,128)(2,1)S(1)} %copy-done.50), channel_id=1, source_target_pairs={{0,1},{1,0},{2,3},{3,2},{4,5},{5,4},{6,7},{7,6},{8,9},{9,8},{10,11... | collective-permute-start | bytes 2113544 | tf_op jit(solution)/shard_map/ppermute | solution.py:822
  258.5 20.5 %collective-permute-start.39 = (bf16[344,1024]{1,0:T(8,128)(2,1)S(1)}, bf16[344,1024]{1,0:T(8,128)(2,1)S(1)}, u32[]{:S(2)}, u32[]{:S(2)}) collective-permute-start(bf16[344,1024]{1,0:T(8,128)(2,1)S(1)} %add_convert_fusion.2), channel_id=1, source_target_pairs={{0,2},{1,3},{2,0},{3,1},{4,6},{5,7},{6,4},{7,5},{8,10},{9,11},{10,... | collective-permute-start | bytes 2113544 | tf_op jit(solution)/shard_map/ppermute | solution.py:822
  278.4 16.9 %collective-permute-start.42 = (bf16[344,1024]{1,0:T(8,128)(2,1)S(1)}, bf16[344,1024]{1,0:T(8,128)(2,1)S(1)}, u32[]{:S(2)}, u32[]{:S(2)}) collective-permute-start(bf16[344,1024]{1,0:T(8,128)(2,1)S(1)} %add_convert_fusion.1), channel_id=1, source_target_pairs={{0,2},{1,3},{2,0},{3,1},{4,6},{5,7},{6,4},{7,5},{8,10},{9,11},{10,... | collective-permute-start | bytes 2113544 | tf_op jit(solution)/shard_map/ppermute | solution.py:822
  279.0 18.6 %collective-permute-start.46 = (bf16[256,1152]{1,0:T(8,128)(2,1)S(1)}, bf16[256,1152]{1,0:T(8,128)(2,1)S(1)}, u32[]{:S(2)}, u32[]{:S(2)}) collective-permute-start(bf16[256,1152]{1,0:T(8,128)(2,1)S(1)} %copy-done.51), channel_id=1, source_target_pairs={{0,4},{4,0},{8,12},{12,8},{16,20},{20,16},{24,28},{28,24},{1,5},{5... | collective-permute-start | bytes 1769480 | tf_op jit(solution)/shard_map/ppermute | solution.py:822
  279.3 21.4 %collective-permute-start.38 = (bf16[344,1024]{1,0:T(8,128)(2,1)}, bf16[344,1024]{1,0:T(8,128)(2,1)S(1)}, u32[]{:S(2)}, u32[]{:S(2)}) collective-permute-start(bf16[344,1024]{1,0:T(8,128)(2,1)} %get-tuple-element.218), channel_id=1, source_target_pairs={{0,1},{1,0},{2,3},{3,2},{4,5},{5,4},{6,7},{7,6},{8,9},{9,8},{10,11... | collective-permute-start | bytes 2113544 | tf_op jit(solution)/shard_map/ppermute | solution.py:822
  279.3 21.8 %collective-permute-start.40 = (bf16[344,1024]{1,0:T(8,128)(2,1)}, bf16[344,1024]{1,0:T(8,128)(2,1)S(1)}, u32[]{:S(2)}, u32[]{:S(2)}) collective-permute-start(bf16[344,1024]{1,0:T(8,128)(2,1)} %get-tuple-element.223), channel_id=1, source_target_pairs={{0,1},{1,0},{2,3},{3,2},{4,5},{5,4},{6,7},{7,6},{8,9},{9,8},{10,11... | collective-permute-start | bytes 2113544 | tf_op jit(solution)/shard_map/ppermute | solution.py:822
  295.3 17.5 %collective-permute-start.48 = (bf16[128,1152]{1,0:T(8,128)(2,1)}, bf16[128,1152]{1,0:T(8,128)(2,1)S(1)}, u32[]{:S(2)}, u32[]{:S(2)}) collective-permute-start(bf16[128,1152]{1,0:T(8,128)(2,1)} %add_convert_fusion.4), channel_id=1, source_target_pairs={{0,16},{4,20},{8,24},{12,28},{16,0},{20,4},{24,8},{28,12},{1,17},{... | collective-permute-start | bytes 884744 | tf_op jit(solution)/shard_map/ppermute | solution.py:822
  (86 other events, 651.4 us)
Sparse Core Ops, SparseCore 0:
  39.8 75.5 all-gather.1
  188.8 31.9 reduce-scatter.2
  240.9 47.7 reduce-scatter.4

commit v8 on v7

--- a/solution.py
+++ b/solution.py
@@ -16,6 +16,7 @@
 F32 = jnp.float32
 PARAMS = pltpu.CompilerParams(vmem_limit_bytes=60 * 1024 * 1024)
 SMALL = pl.CostEstimate(flops=1_000_000_000, bytes_accessed=1_000_000, transcendentals=0)
+TINY = pl.CostEstimate(flops=1_000, bytes_accessed=1_000, transcendentals=0)
 VMEM = pl.BlockSpec(memory_space=pltpu.VMEM)
 SMEM = pl.BlockSpec(memory_space=pltpu.SMEM)
 
@@ -304,7 +305,7 @@
         out_shape=[shaped((length, columns), BF), shaped((pairs, 1, 3 * PAIR), F32)],
         scratch_shapes=[pltpu.VMEM((length, PAIR), F32)],
         compiler_params=PARAMS,
-        cost_estimate=SMALL,
+        cost_estimate=TINY,
         name="attend_back",
     )(qkv, key_bias, attended, lse, *pieces)
 
@@ -373,7 +374,7 @@
         out_shape=[shaped((length, width), F32), shaped((length, width), BF), shaped((8, width), F32)]
         + [shaped((length, part), BF)] * group,
         compiler_params=PARAMS,
-        cost_estimate=SMALL,
+        cost_estimate=TINY,
         name="turn",
     )(rows, live, cotangent, unit, inverse, branch, *backs, *weights)
 
@@ -393,7 +394,7 @@
         out_specs=VMEM,
         out_shape=shaped((len(parts), width, part), BF),
         compiler_params=PARAMS,
-        cost_estimate=SMALL,
+        cost_estimate=TINY,
         name="proj_weights",
     )(ids, grads, *parts)
 
@@ -633,7 +634,7 @@
         out_specs=[VMEM] * (group + 1),
         out_shape=[shaped((size, width), BF)] * group + [shaped((8, width), F32)],
         compiler_params=PARAMS,
-        cost_estimate=SMALL,
+        cost_estimate=TINY,
         name="qkv_back",
     )(qkv_grad, weight, mean, inverse, *tokens)
 
@@ -966,8 +967,9 @@
     branch2_mids = []
     branch2_terms = scatter(branches, *att_grads, mids=branch2_mids)
     qkv_grad, qkv_sums = attend_back(qkv, key_bias, attended, after(lse, proj_parts), att_grads)
+    *norm1_parts, norm1_sums = qkv_back(qkv_grad, weight_qkv, tokens_pieces, mean1, inverse1)
     if direct:
-        other = after(other_mlp, qkv_grad)
+        other = after(other_mlp, norm1_sums)
         summed = (keep_mlp.astype(F32) + other.astype(F32)).astype(BF)
         lines = [[side + 2 * z for z in range(replicas // 2)] for side in range(2)]
         owned_mlp = lax.psum_scatter(
@@ -980,8 +982,7 @@
         owned_mlp = lax.psum_scatter(
             ordered.reshape(width, 2 * hidden_part), "dp", scatter_dimension=0, tiled=True
         )
-    *norm1_parts, norm1_sums = qkv_back(after(qkv_grad, summed) if direct else qkv_grad, weight_qkv, tokens_pieces, mean1, inverse1)
-    before = branch2_mids
+    before = branch2_mids + ([summed] if direct else [])
     parts = attn_weights(
         ids, after(normed1, *before), qkv_grad,
         [norm1_sums, qkv_sums, turn_sums, own_sums, grad_scale2, sums_near, sums_far],

time: 336 us -> 331 us (0.985)
  waiting for transfers between devices: 123 us -> 117 us
    ppermute x52, waiting for transfers between devices: 123 us -> 117 us  [swap(): return lax.ppermute(value, axis, [(i, i ^ bit) for i in range(size)])]
where the time goes in v8:
time: 331 us; the launch traced here: 325 us
  Pallas kernels  136 us (41%)
  waiting for transfers between devices  117 us (35%)
  starting transfers between devices  37.7 us (11%)
  between operations  15.1 us (5%)
  other arithmetic  11 us (3%)
  local copies, waits for them, and re-layouts  8.53 us (3%)
    ppermute x52, waiting for transfers between devices, swap(): return lax.ppermute(value, axis, [(i, i ^ bit) for i in range(size)])  117 us
    ppermute x52, starting transfers between devices, swap(): return lax.ppermute(value, axis, [(i, i ^ bit) for i in range(size)])  37.6 us
    pallas_call x2, Pallas kernels, mlp(): pl.pallas_call(lambda *refs: mlp_kernel(count, shards, group, *refs), gri...  25.4 us
    pallas_call x1, Pallas kernels, attend_back(): pl.pallas_call(attend_back_kernel, grid=(pairs,), in_specs=[pl.BlockSpec(...  24.3 us
    pallas_call x1, Pallas kernels, mlp_weights(): pl.pallas_call(lambda *refs: mlp_weights_kernel(direct, *refs), grid_spec...  16.2 us
    pallas_call x1, Pallas kernels, attend(): pl.pallas_call(attend_kernel, grid=(pairs,), in_specs=[pl.BlockSpec((leng...  15.5 us
    unnamed x113, local copies, waits for them, and re-layouts  8.47 us
    pallas_call x1, Pallas kernels, project(): pl.pallas_call(lambda *refs: project_kernel(ordered, group, count_column,...  8.24 us
  transfers between devices with their start and end apart: 55, of which 28 were waited for; matrix products, arithmetic and copies ran while one was open for 3% of the time, Pallas kernels for 34%

profile of v8, /device:TPU:0, one launch (start us, length us, event | category | flops | bytes accessed | tf_op | source)
XLA Modules:
  0.0 325.5 jit_solution(13336030998864469890)
XLA Ops:
  29.6 7.6 %collective-permute-done.7.refs_11_ = bf16[128,1152]{1,0:T(8,128)(2,1)S(1)} collective-permute-done((bf16[128,1152]{1,0:T(8,128)(2,1)S(1)}, bf16[128,1152]{1,0:T(8,128)(2,1)S(1)}, u32[]{:S(2)}, u32[]{:S(2)}) %collective-permute-start.7) | collective-permute-done | bytes 294944 | tf_op jit(solution)/shard_map/ppermute | solution.py:823
  44.3 4.2 %collective-permute-done.11.refs_15_ = bf16[128,1152]{1,0:T(8,128)(2,1)S(1)} collective-permute-done((bf16[128,1152]{1,0:T(8,128)(2,1)S(1)}, bf16[128,1152]{1,0:T(8,128)(2,1)S(1)}, u32[]{:S(2)}, u32[]{:S(2)}) %collective-permute-start.11) | collective-permute-done | bytes 294944 | tf_op jit(solution)/shard_map/ppermute | solution.py:823
  49.0 15.1 %collective-permute-done.9.refs_12_ = bf16[128,1152]{1,0:T(8,128)(2,1)S(1)} collective-permute-done((bf16[128,1152]{1,0:T(8,128)(2,1)S(1)}, bf16[128,1152]{1,0:T(8,128)(2,1)S(1)}, u32[]{:S(2)}, u32[]{:S(2)}) %collective-permute-start.9) | collective-permute-done | bytes 294944 | tf_op jit(solution)/shard_map/ppermute | solution.py:823
  64.1 3.7 %collective-permute-done.12.refs_16_ = bf16[128,1152]{1,0:T(8,128)(2,1)S(1)} collective-permute-done((bf16[128,1152]{1,0:T(8,128)(2,1)S(1)}, bf16[128,1152]{1,0:T(8,128)(2,1)S(1)}, u32[]{:S(2)}, u32[]{:S(2)}) %collective-permute-start.12) | collective-permute-done | bytes 294944 | tf_op jit(solution)/shard_map/ppermute | solution.py:823
  72.6 8.2 %project.1 = (bf16[1024,768]{1,0:T(8,128)(2,1)}, bf16[1024,256]{1,0:T(8,128)(2,1)}, f32[16,1024]{1,0:T(8,128)}, bf16[1376,1024]{1,0:T(8,128)(2,1)}, bf16[1376,76...) custom-call(s32[2]{0:T(128)} %pad_add_fusion.ids_ref.refs_0_.refs_7_, ...), custom_call_target="tpu_custom_call" | custom-call | flops 1000000000 | bytes 1000000 | tf_op jit(solution)/shard_map/project/pallas_call | solution.py:176
  82.4 15.5 %attend.1 = (f32[1376,256]{1,0:T(8,128)}, f32[2,2,1376]{2,1,0:T(2,128)}, bf16[344,256]{1,0:T(8,128)(2,1)}, bf16[344,256]{1,0:T(8,128)(2,1)}, bf16[344,256]{1,0:T(8,128)(2,1)}, /*index=5*/bf16[344,256]{1,0:T(8,128)(2,1)}) custom-call(bf16[1376,768]{1,0:T(8,128)(2,1)} %get-tuple-element.150.qkv_ref, f32[1376,1]{1,0:T(8,128)} %get-tuple-element.151.bias_ref), custom_call_target="tpu_custom_call" | custom-call | flops 1000000000 | bytes 1000000 | tf_op jit(solution)/shard_map/attend/pallas_call | solution.py:232
  100.9 5.2 %collective-permute-done.18.refs_4_.rest_2_ = bf16[344,256]{1,0:T(8,128)(2,1)S(1)} collective-permute-done((bf16[344,256]{1,0:T(8,128)(2,1)}, bf16[344,256]{1,0:T(8,128)(2,1)S(1)}, u32[]{:S(2)}, u32[]{:S(2)}) %collective-permute-start.18) | collective-permute-done | bytes 176160 | tf_op jit(solution)/shard_map/ppermute | solution.py:823
  110.0 5.3 %middle.1 = (f32[344,1024]{1,0:T(8,128)}, f32[344,1024]{1,0:T(8,128)}, bf16[344,1024]{1,0:T(8,128)(2,1)}, f32[344,1024]{1,0:T(8,128)}, f32[344,1]{1,0:T(8,128)}) custom-call(f32[16,1024]{1,0:T(8,128)} %get-tuple-element.213.refs_0_.refs_5_.rows_ref, bf16[344,1024]{1,0:T(8,128)(2,1)} %bitcast.27, bf16[344,256]{1,0:T(8,128)(2,1)} %get-tuple-element.152.refs_2_.rest_0_, ...), custom_call_target="tpu_custom_call" | custom-call | flops 1000000000 | bytes 1000000 | tf_op jit(solution)/shard_map/middle/pallas_call | solution.py:334
  118.1 12.6 %mlp.2 = (bf16[344,1024]{1,0:T(8,128)(2,1)}, bf16[344,1024]{1,0:T(8,128)(2,1)}, bf16[688,1024]{1,0:T(8,128)(2,1)}, bf16[688,1024]{1,0:T(8,128)(2,1)}, bf16[688,1...) custom-call(f32[16,1024]{1,0:T(8,128)} %get-tuple-element.213.refs_0_.refs_5_.rows_ref, ...), custom_call_target="tpu_custom_call" | custom-call | flops 1000000000 | bytes 1000000 | tf_op jit(solution)/shard_map/mlp/pallas_call | solution.py:476
  130.7 3.2 collective-permute-done.25.refs_1_
  137.0 12.8 %mlp.3 = (bf16[344,1024]{1,0:T(8,128)(2,1)}, bf16[344,1024]{1,0:T(8,128)(2,1)}, bf16[688,1024]{1,0:T(8,128)(2,1)}, bf16[688,1024]{1,0:T(8,128)(2,1)}, bf16[688,1...) custom-call(f32[16,1024]{1,0:T(8,128)} %get-tuple-element.213.refs_0_.refs_5_.rows_ref, ...), custom_call_target="tpu_custom_call" | custom-call | flops 1000000000 | bytes 1000000 | tf_op jit(solution)/shard_map/mlp/pallas_call | solution.py:476
  154.2 16.2 %mlp_weights.1 = (bf16[512,2048]{1,0:T(8,128)(2,1)}, bf16[512,2048]{1,0:T(8,128)(2,1)}, f32[1,1024]{1,0:T(1,128)}, bf16[344,1024]{1,0:T(8,128)(2,1)}, bf16[344,1...) custom-call(s32[2]{0:T(128)} %pad_add_fusion.ids_ref.refs_0_.refs_7_, ...), custom_call_target="tpu_custom_call" | custom-call | flops 1000000000 | bytes 1000000 | tf_op jit(solution)/shard_map/mlp_weights/pallas_call | solution.py:542
  172.4 6.0 %turn.1 = (f32[344,1024]{1,0:T(8,128)}, bf16[344,1024]{1,0:T(8,128)(2,1)}, f32[8,1024]{1,0:T(8,128)}, bf16[344,256]{1,0:T(8,128)(2,1)}, bf16[344,256]{1,0:T(8,12...) custom-call(f32[16,1024]{1,0:T(8,128)} %get-tuple-element.213.refs_0_.refs_5_.rows_ref, ...), custom_call_target="tpu_custom_call" | custom-call | flops 1000 | bytes 1000 | tf_op jit(solution)/shard_map/turn/pallas_call | solution.py:370
  180.3 4.1 %proj_weights.1 = bf16[4,1024,256]{2,1,0:T(8,128)(2,1)} custom-call(s32[2]{0:T(128)} %pad_add_fusion.ids_ref.refs_0_.refs_7_, bf16[344,1024]{1,0:T(8,128)(2,1)} %get-tuple-element.194.grad_ref, bf16[344,256]{1,0:T(8,128)(2,1)} %get-tuple-element.152.refs_2_.rest_0_, bf16[344,256]{1,0:T(8,128)(2,1)} %copy-done.39, bf16[344,256]{1,0:T(8,128)(2,1)} %copy-done.40, ...), custom_call_target="tpu_custom_call" | custom-call | flops 1000 | bytes 1000 | tf_op jit(solution)/shard_map/proj_weights/pallas_call | solution.py:391
  189.5 24.3 %attend_back.1 = (bf16[1376,768]{1,0:T(8,128)(2,1)}, f32[2,1,384]{2,1,0:T(1,128)}) custom-call(bf16[1376,768]{1,0:T(8,128)(2,1)} %get-tuple-element.150.qkv_ref, f32[1376,1]{1,0:T(8,128)} %get-tuple-element.151.bias_ref, f32[1376,256]{1,0:T(8,128)} %get-tuple-element.188.att_ref, f32[2,2,1376]{2,1,0:T(2,128)} %get-tuple-element.195.lse_ref, ...), custom_call_target="tpu_custom_call" | custom-call | flops 1000 | bytes 1000 | tf_op jit(solution)/shard_map/attend_back/pallas_call | solution.py:291
  213.8 6.9 %qkv_back.1 = (bf16[344,1024]{1,0:T(8,128)(2,1)}, bf16[344,1024]{1,0:T(8,128)(2,1)}, bf16[344,1024]{1,0:T(8,128)(2,1)}, bf16[344,1024]{1,0:T(8,128)(2,1)}, f32[8,1024]{1,0:T(8,128)}) custom-call(bf16[1376,768]{1,0:T(8,128)(2,1)} %get-tuple-element.200.refs_0_.refs_2_, bf16[1024,768]{1,0:T(8,128)(2,1)} %get-tuple-element.201.refs_1_, ...), custom_call_target="tpu_custom_call" | custom-call | flops 1000 | bytes 1000 | tf_op jit(solution)/shard_map/qkv_back/pallas_call | solution.py:631
  220.7 16.4 %collective-permute-done.32 = bf16[512,2048]{1,0:T(8,128)(2,1)} collective-permute-done((bf16[512,2048]{1,0:T(8,128)(2,1)}, bf16[512,2048]{1,0:T(8,128)(2,1)}, u32[]{:S(2)}, u32[]{:S(2)}) %collective-permute-start.32) | collective-permute-done | bytes 2097184 | tf_op jit(solution)/shard_map/ppermute | solution.py:823
  237.1 3.8 %add_convert_fusion = bf16[512,2048]{1,0:T(8,128)(2,1)} fusion(bf16[512,2048]{1,0:T(8,128)(2,1)} %collective-permute-done.32, bf16[512,2048]{1,0:T(8,128)(2,1)S(1)} %copy-done.5), kind=kLoop, calls=%fused_computation | loop fusion | flops 4194304 | bytes 6291456 | tf_op jit(solution)/shard_map/convert_element_type | solution.py:973
  244.5 7.0 %attn_weights.1 = (bf16[128,1152]{1,0:T(8,128)(2,1)}, bf16[128,1152]{1,0:T(8,128)(2,1)}, bf16[128,1152]{1,0:T(8,128)(2,1)}, bf16[128,1152]{1,0:T(8,128)(2,1)}, b...) custom-call(s32[2]{0:T(128)} %pad_add_fusion.ids_ref.refs_0_.refs_7_, bf16[1376,1024]{1,0:T(8,128)(2,1)} %get-tuple-element.206.refs_1_, ...), custom_call_target="tpu_custom_call" | custom-call | flops 1000000000 | bytes 1000000 | tf_op jit(solution)/shard_map/attn_weights/pallas_call | solution.py:703
  252.6 14.5 %collective-permute-done.36 = bf16[256,1152]{1,0:T(8,128)(2,1)S(1)} collective-permute-done((bf16[256,1152]{1,0:T(8,128)(2,1)}, bf16[256,1152]{1,0:T(8,128)(2,1)S(1)}, u32[]{:S(2)}, u32[]{:S(2)}) %collective-permute-start.36) | collective-permute-done | bytes 589856 | tf_op jit(solution)/shard_map/ppermute | solution.py:823
  268.2 3.5 %collective-permute-start.37 = (bf16[128,1152]{1,0:T(8,128)(2,1)S(1)}, bf16[128,1152]{1,0:T(8,128)(2,1)S(1)}, u32[]{:S(2)}, u32[]{:S(2)}) collective-permute-start(bf16[128,1152]{1,0:T(8,128)(2,1)S(1)} %add_convert_fusion.8), channel_id=1, source_target_pairs={{0,8},{4,12},{8,0},{12,4},{16,24},{20,28},{24,16},{28,20},{1,9},{5... | collective-permute-start | bytes 884744 | tf_op jit(solution)/shard_map/ppermute | solution.py:823
  273.1 15.1 %collective-permute-done.37 = bf16[128,1152]{1,0:T(8,128)(2,1)S(1)} collective-permute-done((bf16[128,1152]{1,0:T(8,128)(2,1)S(1)}, bf16[128,1152]{1,0:T(8,128)(2,1)S(1)}, u32[]{:S(2)}, u32[]{:S(2)}) %collective-permute-start.37) | collective-permute-done | bytes 294944 | tf_op jit(solution)/shard_map/ppermute | solution.py:823
  297.2 4.0 %begin.1 = bf16[344,1024]{1,0:T(8,128)(2,1)} custom-call(f32[16,1024]{1,0:T(8,128)} %get-tuple-element.213.refs_0_.refs_5_.rows_ref, bf16[344,1024]{1,0:T(8,128)(2,1)} %bitcast.29, f32[1376,1]{1,0:T(8,128)} %get-tuple-element.202.refs_2_.mean_ref, f32[1376,1]{1,0:T(8,128)} %get-tuple-element.203.refs_3_.inv_ref, f32[344,1024]{1,0:T(8,128)} %get-tuple-element.219.middle_ref, ...), custom_call_target="tpu_custom_call" | custom-call | tf_op jit(solution)/shard_map/begin/pallas_call | solution.py:598
  312.0 3.5 %collective-permute-done.50.refs_2_ = bf16[32,1152]{1,0:T(8,128)(2,1)S(1)} collective-permute-done((bf16[32,1152]{1,0:T(8,128)(2,1)}, bf16[32,1152]{1,0:T(8,128)(2,1)S(1)}, u32[]{:S(2)}, u32[]{:S(2)}) %collective-permute-start.50) | collective-permute-done | bytes 73760 | tf_op jit(solution)/shard_map/ppermute | solution.py:823
  (232 shorter events, 91.5 us)
Async XLA Ops:
  7.2 111.0 %all-gather.2.cloned.1.call-start = ((), (), s32[]{:S(2)}) async-start(), calls=%async_computation.2 | async-start | bytes 4718592 | tf_op jit(solution)/shard_map/all_gather | solution.py:896
  23.5 16.1 %collective-permute-start.6 = (bf16[128,1152]{1,0:T(8,128)(2,1)S(1)}, bf16[128,1152]{1,0:T(8,128)(2,1)S(1)}, u32[]{:S(2)}, u32[]{:S(2)}) collective-permute-start(bf16[128,1152]{1,0:T(8,128)(2,1)S(1)} %constant_dynamic-update-slice_fusion.refs_9_), channel_id=1, source_target_pairs={{0,16},{4,20},{8,24},{12,28},{16,0},{20,4},{24,8},{28,12},{1,17},{... | collective-permute-start | bytes 884744 | tf_op jit(solution)/shard_map/ppermute | solution.py:823
  39.6 204.9 %reduce-scatter.3.cloned.1.call-start = ((), (), s32[]{:S(2)}) async-start(), calls=%async_computation.3 | async-start | bytes 2621440 | tf_op jit(solution)/shard_map/reduce_scatter | solution.py:964
  39.7 28.2 %collective-permute-start.13 = (bf16[344,1024]{1,0:T(8,128)(2,1)S(1)}, bf16[344,1024]{1,0:T(8,128)(2,1)S(1)}, u32[]{:S(2)}, u32[]{:S(2)}) collective-permute-start(bf16[344,1024]{1,0:T(8,128)(2,1)S(1)} %bitcast.34), channel_id=1, source_target_pairs={{0,2},{1,3},{2,0},{3,1},{4,6},{5,7},{6,4},{7,5},{8,10},{9,11},{10,... | collective-permute-start | bytes 2113544 | tf_op jit(solution)/shard_map/ppermute | solution.py:823
  41.1 28.4 %collective-permute-start.15 = (bf16[344,1024]{1,0:T(8,128)(2,1)S(1)}, bf16[344,1024]{1,0:T(8,128)(2,1)S(1)}, u32[]{:S(2)}, u32[]{:S(2)}) collective-permute-start(bf16[344,1024]{1,0:T(8,128)(2,1)S(1)} %bitcast.30), channel_id=1, source_target_pairs={{0,2},{1,3},{2,0},{3,1},{4,6},{5,7},{6,4},{7,5},{8,10},{9,11},{10,... | collective-permute-start | bytes 2113544 | tf_op jit(solution)/shard_map/ppermute | solution.py:823
  42.2 21.9 %collective-permute-start.10 = (bf16[128,1152]{1,0:T(8,128)(2,1)S(1)}, bf16[128,1152]{1,0:T(8,128)(2,1)S(1)}, u32[]{:S(2)}, u32[]{:S(2)}) collective-permute-start(bf16[128,1152]{1,0:T(8,128)(2,1)S(1)} %collective-permute-done.6.refs_13_), channel_id=1, source_target_pairs={{0,4},{4,0},{8,12},{12,8},{16,20},{20,16},{24,28},{28,24},{1,5},{5... | collective-permute-start | bytes 884744 | tf_op jit(solution)/shard_map/ppermute | solution.py:823
  42.7 21.4 %collective-permute-start.9 = (bf16[128,1152]{1,0:T(8,128)(2,1)S(1)}, bf16[128,1152]{1,0:T(8,128)(2,1)S(1)}, u32[]{:S(2)}, u32[]{:S(2)}) collective-permute-start(bf16[128,1152]{1,0:T(8,128)(2,1)S(1)} %collective-permute-done.7.refs_11_), channel_id=1, source_target_pairs={{0,4},{4,0},{8,12},{12,8},{16,20},{20,16},{24,28},{28,24},{1,5},{5... | collective-permute-start | bytes 884744 | tf_op jit(solution)/shard_map/ppermute | solution.py:823
  48.5 19.3 %collective-permute-start.12 = (bf16[128,1152]{1,0:T(8,128)(2,1)S(1)}, bf16[128,1152]{1,0:T(8,128)(2,1)S(1)}, u32[]{:S(2)}, u32[]{:S(2)}) collective-permute-start(bf16[128,1152]{1,0:T(8,128)(2,1)S(1)} %collective-permute-done.11.refs_15_), channel_id=1, source_target_pairs={{0,4},{4,0},{8,12},{12,8},{16,20},{20,16},{24,28},{28,24},{1,5},{5... | collective-permute-start | bytes 884744 | tf_op jit(solution)/shard_map/ppermute | solution.py:823
  80.8 17.1 %collective-permute-start.21 = (bf16[1024,256]{1,0:T(8,128)(2,1)}, bf16[1024,256]{1,0:T(8,128)(2,1)S(1)}, u32[]{:S(2)}, u32[]{:S(2)}) collective-permute-start(bf16[1024,256]{1,0:T(8,128)(2,1)} %get-tuple-element.156.refs_6_.refs_9_), channel_id=1, source_target_pairs={{0,2},{1,3},{2,0},{3,1},{4,6},{5,7},{6,4},{7,5},{8,10},{9,11},{10,... | collective-permute-start | bytes 1572872 | tf_op jit(solution)/shard_map/ppermute | solution.py:823
  82.4 26.6 %collective-permute-start.20 = (bf16[1024,256]{1,0:T(8,128)(2,1)}, bf16[1024,256]{1,0:T(8,128)(2,1)S(1)}, u32[]{:S(2)}, u32[]{:S(2)}) collective-permute-start(bf16[1024,256]{1,0:T(8,128)(2,1)} %get-tuple-element.156.refs_6_.refs_9_), channel_id=1, source_target_pairs={{0,1},{1,0},{2,3},{3,2},{4,5},{5,4},{6,7},{7,6},{8,9},{9,8},{10,11... | collective-permute-start | bytes 1572872 | tf_op jit(solution)/shard_map/ppermute | solution.py:823
  116.0 18.0 %collective-permute-start.25 = (bf16[344,1024]{1,0:T(8,128)(2,1)}, bf16[344,1024]{1,0:T(8,128)(2,1)S(1)}, u32[]{:S(2)}, u32[]{:S(2)}) collective-permute-start(bf16[344,1024]{1,0:T(8,128)(2,1)} %get-tuple-element.159.refs_1_), channel_id=1, source_target_pairs={{0,2},{1,3},{2,0},{3,1},{4,6},{5,7},{6,4},{7,5},{8,10},{9,11},{10,... | collective-permute-start | bytes 2113544 | tf_op jit(solution)/shard_map/ppermute | solution.py:823
  116.5 17.5 %collective-permute-start.27 = (bf16[344,1024]{1,0:T(8,128)(2,1)S(1)}, bf16[344,1024]{1,0:T(8,128)(2,1)S(1)}, u32[]{:S(2)}, u32[]{:S(2)}) collective-permute-start(bf16[344,1024]{1,0:T(8,128)(2,1)S(1)} %copy-done.11), channel_id=1, source_target_pairs={{0,1},{1,0},{2,3},{3,2},{4,5},{5,4},{6,7},{7,6},{8,9},{9,8},{10,11... | collective-permute-start | bytes 2113544 | tf_op jit(solution)/shard_map/ppermute | solution.py:823
  150.0 20.4 %collective-permute-start.30 = (bf16[344,1024]{1,0:T(8,128)(2,1)S(1)}, bf16[344,1024]{1,0:T(8,128)(2,1)S(1)}, u32[]{:S(2)}, u32[]{:S(2)}) collective-permute-start(bf16[344,1024]{1,0:T(8,128)(2,1)S(1)} %copy-done.53), channel_id=1, source_target_pairs={{0,1},{1,0},{2,3},{3,2},{4,5},{5,4},{6,7},{7,6},{8,9},{9,8},{10,11... | collective-permute-start | bytes 2113544 | tf_op jit(solution)/shard_map/ppermute | solution.py:823
  153.6 17.9 %collective-permute-start.31 = (bf16[344,1024]{1,0:T(8,128)(2,1)S(1)}, bf16[344,1024]{1,0:T(8,128)(2,1)S(1)}, u32[]{:S(2)}, u32[]{:S(2)}) collective-permute-start(bf16[344,1024]{1,0:T(8,128)(2,1)S(1)} %add_convert_fusion.3), channel_id=1, source_target_pairs={{0,2},{1,3},{2,0},{3,1},{4,6},{5,7},{6,4},{7,5},{8,10},{9,11},{10,... | collective-permute-start | bytes 2113544 | tf_op jit(solution)/shard_map/ppermute | solution.py:823
  188.9 104.0 %reduce-scatter.5.cloned.1.call-start = ((), (), s32[]{:S(2)}) async-start(), calls=%async_computation.4 | async-start | bytes 2621440 | tf_op jit(solution)/shard_map/reduce_scatter | solution.py:975
  188.9 48.2 %collective-permute-start.32 = (bf16[512,2048]{1,0:T(8,128)(2,1)}, bf16[512,2048]{1,0:T(8,128)(2,1)}, u32[]{:S(2)}, u32[]{:S(2)}) collective-permute-start(bf16[512,2048]{1,0:T(8,128)(2,1)} %get-tuple-element.187), channel_id=1, source_target_pairs={{0,4},{4,0},{8,12},{12,8},{16,20},{20,16},{24,28},{28,24},{1,5},{5... | collective-permute-start | bytes 6291464 | tf_op jit(solution)/shard_map/ppermute | solution.py:823
  252.0 19.7 %collective-permute-start.41 = (bf16[344,1024]{1,0:T(8,128)(2,1)S(1)}, bf16[344,1024]{1,0:T(8,128)(2,1)S(1)}, u32[]{:S(2)}, u32[]{:S(2)}) collective-permute-start(bf16[344,1024]{1,0:T(8,128)(2,1)S(1)} %copy-done.52), channel_id=1, source_target_pairs={{0,1},{1,0},{2,3},{3,2},{4,5},{5,4},{6,7},{7,6},{8,9},{9,8},{10,11... | collective-permute-start | bytes 2113544 | tf_op jit(solution)/shard_map/ppermute | solution.py:823
  252.0 20.3 %collective-permute-start.39 = (bf16[344,1024]{1,0:T(8,128)(2,1)S(1)}, bf16[344,1024]{1,0:T(8,128)(2,1)S(1)}, u32[]{:S(2)}, u32[]{:S(2)}) collective-permute-start(bf16[344,1024]{1,0:T(8,128)(2,1)S(1)} %add_convert_fusion.2), channel_id=1, source_target_pairs={{0,2},{1,3},{2,0},{3,1},{4,6},{5,7},{6,4},{7,5},{8,10},{9,11},{10,... | collective-permute-start | bytes 2113544 | tf_op jit(solution)/shard_map/ppermute | solution.py:823
  268.2 20.0 %collective-permute-start.37 = (bf16[128,1152]{1,0:T(8,128)(2,1)S(1)}, bf16[128,1152]{1,0:T(8,128)(2,1)S(1)}, u32[]{:S(2)}, u32[]{:S(2)}) collective-permute-start(bf16[128,1152]{1,0:T(8,128)(2,1)S(1)} %add_convert_fusion.8), channel_id=1, source_target_pairs={{0,8},{4,12},{8,0},{12,4},{16,24},{20,28},{24,16},{28,20},{1,9},{5... | collective-permute-start | bytes 884744 | tf_op jit(solution)/shard_map/ppermute | solution.py:823
  271.9 17.1 %collective-permute-start.42 = (bf16[344,1024]{1,0:T(8,128)(2,1)S(1)}, bf16[344,1024]{1,0:T(8,128)(2,1)S(1)}, u32[]{:S(2)}, u32[]{:S(2)}) collective-permute-start(bf16[344,1024]{1,0:T(8,128)(2,1)S(1)} %add_convert_fusion.1), channel_id=1, source_target_pairs={{0,2},{1,3},{2,0},{3,1},{4,6},{5,7},{6,4},{7,5},{8,10},{9,11},{10,... | collective-permute-start | bytes 2113544 | tf_op jit(solution)/shard_map/ppermute | solution.py:823
  272.3 18.9 %collective-permute-start.46 = (bf16[256,1152]{1,0:T(8,128)(2,1)S(1)}, bf16[256,1152]{1,0:T(8,128)(2,1)S(1)}, u32[]{:S(2)}, u32[]{:S(2)}) collective-permute-start(bf16[256,1152]{1,0:T(8,128)(2,1)S(1)} %copy-done.54), channel_id=1, source_target_pairs={{0,4},{4,0},{8,12},{12,8},{16,20},{20,16},{24,28},{28,24},{1,5},{5... | collective-permute-start | bytes 1769480 | tf_op jit(solution)/shard_map/ppermute | solution.py:823
  272.6 22.2 %collective-permute-start.38 = (bf16[344,1024]{1,0:T(8,128)(2,1)}, bf16[344,1024]{1,0:T(8,128)(2,1)S(1)}, u32[]{:S(2)}, u32[]{:S(2)}) collective-permute-start(bf16[344,1024]{1,0:T(8,128)(2,1)} %get-tuple-element.216), channel_id=1, source_target_pairs={{0,1},{1,0},{2,3},{3,2},{4,5},{5,4},{6,7},{7,6},{8,9},{9,8},{10,11... | collective-permute-start | bytes 2113544 | tf_op jit(solution)/shard_map/ppermute | solution.py:823
  272.6 23.8 %collective-permute-start.40 = (bf16[344,1024]{1,0:T(8,128)(2,1)}, bf16[344,1024]{1,0:T(8,128)(2,1)S(1)}, u32[]{:S(2)}, u32[]{:S(2)}) collective-permute-start(bf16[344,1024]{1,0:T(8,128)(2,1)} %get-tuple-element.221), channel_id=1, source_target_pairs={{0,1},{1,0},{2,3},{3,2},{4,5},{5,4},{6,7},{7,6},{8,9},{9,8},{10,11... | collective-permute-start | bytes 2113544 | tf_op jit(solution)/shard_map/ppermute | solution.py:823
  289.1 18.3 %collective-permute-start.48 = (bf16[128,1152]{1,0:T(8,128)(2,1)}, bf16[128,1152]{1,0:T(8,128)(2,1)S(1)}, u32[]{:S(2)}, u32[]{:S(2)}) collective-permute-start(bf16[128,1152]{1,0:T(8,128)(2,1)} %add_convert_fusion.4), channel_id=1, source_target_pairs={{0,16},{4,20},{8,24},{12,28},{16,0},{20,4},{24,8},{28,12},{1,17},{... | collective-permute-start | bytes 884744 | tf_op jit(solution)/shard_map/ppermute | solution.py:823
  (86 other events, 633.3 us)
Sparse Core Ops, SparseCore 0:
  39.8 75.5 all-gather.1
  189.0 31.9 reduce-scatter.2
  241.1 50.5 reduce-scatter.4

commit v9 on v8

--- a/solution.py
+++ b/solution.py
@@ -968,8 +968,14 @@
     branch2_terms = scatter(branches, *att_grads, mids=branch2_mids)
     qkv_grad, qkv_sums = attend_back(qkv, key_bias, attended, after(lse, proj_parts), att_grads)
     *norm1_parts, norm1_sums = qkv_back(qkv_grad, weight_qkv, tokens_pieces, mean1, inverse1)
+    before = branch2_mids
+    parts = attn_weights(
+        ids, after(normed1, *before), qkv_grad,
+        [norm1_sums, qkv_sums, turn_sums, own_sums, grad_scale2, sums_near, sums_far],
+        [proj_grad], replicas if direct else 0, rows,
+    )
     if direct:
-        other = after(other_mlp, norm1_sums)
+        other = after(other_mlp, parts[0])
         summed = (keep_mlp.astype(F32) + other.astype(F32)).astype(BF)
         lines = [[side + 2 * z for z in range(replicas // 2)] for side in range(2)]
         owned_mlp = lax.psum_scatter(
@@ -982,12 +988,6 @@
         owned_mlp = lax.psum_scatter(
             ordered.reshape(width, 2 * hidden_part), "dp", scatter_dimension=0, tiled=True
         )
-    before = branch2_mids + ([summed] if direct else [])
-    parts = attn_weights(
-        ids, after(normed1, *before), qkv_grad,
-        [norm1_sums, qkv_sums, turn_sums, own_sums, grad_scale2, sums_near, sums_far],
-        [proj_grad], replicas if direct else 0, rows,
-    )
     norm1_terms = scatter(norm1_parts)
     if direct:
         def add(left, right):
@@ -1003,7 +1003,6 @@
         across0 = swap(add(keep1, other10[:size]), 2, "dp")
         terms = [add(keep0, other10[size:]), across0, far]
         settled = [across]
-        cuts_mlp = total(after(ids, *settled), [owned_mlp], group)
     else:
         owned_attn = lax.psum_scatter(parts[0], "dp", scatter_dimension=0, tiled=True)
 
@@ -1013,16 +1012,17 @@
 
         cuts_mlp = relative(owned_mlp)
         settled = []
-    out_fc1, out_fc2 = place_mlp(ids, exchange(cuts_mlp), hidden)
     input_grad = begin(
         vector_rows, after(tokens[0], *settled), mean1, inverse1, middle_grad, norm1_terms
     )
     output = finish(after(vector_rows, *settled), middle, branch2_terms)
     if direct:
-        cuts_attn = total(after(ids, input_grad, output, out_fc1), terms, group)
+        cuts_attn = total(after(ids, input_grad, output), terms, group)
+        cuts_mlp = total(after(ids, *cuts_attn), [owned_mlp], group)
     else:
         cuts_attn = relative(owned_attn)
 
+    out_fc1, out_fc2 = place_mlp(ids, exchange(cuts_mlp), hidden)
     out_qkv, out_proj, out_vectors, out_bias = place_attn(
         ids, exchange(cuts_attn), width, vector_count, bias_cols
     )

time: 331 us -> 336 us (1.015)
  starting transfers between devices: 37.7 us -> 41.4 us
    ppermute x52, starting transfers between devices: 37.6 us -> 41.2 us  [swap(): return lax.ppermute(value, axis, [(i, i ^ bit) for i in range(size)])]
    unnamed x113 -> x115, local copies, waits for them, and re-layouts: 8.47 us -> 9.08 us
  transfers between devices with their start and end apart: 55 -> 55, of which waited for: 28 -> 29; matrix products, arithmetic and copies ran while one was open for 3% -> 2% of each run, Pallas kernels for 34% -> 34%
where the time goes in v9:
time: 336 us; the launch traced here: 331 us
  Pallas kernels  136 us (40%)
  waiting for transfers between devices  119 us (35%)
  starting transfers between devices  41.4 us (12%)
  between operations  15.1 us (4%)
  other arithmetic  9.96 us (3%)
  local copies, waits for them, and re-layouts  9.14 us (3%)
    ppermute x52, waiting for transfers between devices, swap(): return lax.ppermute(value, axis, [(i, i ^ bit) for i in range(size)])  119 us
    ppermute x52, starting transfers between devices, swap(): return lax.ppermute(value, axis, [(i, i ^ bit) for i in range(size)])  41.2 us
    pallas_call x2, Pallas kernels, mlp(): pl.pallas_call(lambda *refs: mlp_kernel(count, shards, group, *refs), gri...  25.4 us
    pallas_call x1, Pallas kernels, attend_back(): pl.pallas_call(attend_back_kernel, grid=(pairs,), in_specs=[pl.BlockSpec(...  24.3 us
    pallas_call x1, Pallas kernels, mlp_weights(): pl.pallas_call(lambda *refs: mlp_weights_kernel(direct, *refs), grid_spec...  16.2 us
    pallas_call x1, Pallas kernels, attend(): pl.pallas_call(attend_kernel, grid=(pairs,), in_specs=[pl.BlockSpec((leng...  15.6 us
    unnamed x115, local copies, waits for them, and re-layouts  9.08 us
    pallas_call x1, Pallas kernels, project(): pl.pallas_call(lambda *refs: project_kernel(ordered, group, count_column,...  8.23 us
  transfers between devices with their start and end apart: 55, of which 29 were waited for; matrix products, arithmetic and copies ran while one was open for 2% of the time, Pallas kernels for 34%

profile of v9, /device:TPU:0, one launch (start us, length us, event | category | flops | bytes accessed | tf_op | source)
XLA Modules:
  0.0 331.1 jit_solution(1997102615189099728)
XLA Ops:
  29.6 7.6 %collective-permute-done.7.refs_11_ = bf16[128,1152]{1,0:T(8,128)(2,1)S(1)} collective-permute-done((bf16[128,1152]{1,0:T(8,128)(2,1)S(1)}, bf16[128,1152]{1,0:T(8,128)(2,1)S(1)}, u32[]{:S(2)}, u32[]{:S(2)}) %collective-permute-start.7) | collective-permute-done | bytes 294944 | tf_op jit(solution)/shard_map/ppermute | solution.py:823
  44.3 4.2 %collective-permute-done.11.refs_15_ = bf16[128,1152]{1,0:T(8,128)(2,1)S(1)} collective-permute-done((bf16[128,1152]{1,0:T(8,128)(2,1)S(1)}, bf16[128,1152]{1,0:T(8,128)(2,1)S(1)}, u32[]{:S(2)}, u32[]{:S(2)}) %collective-permute-start.11) | collective-permute-done | bytes 294944 | tf_op jit(solution)/shard_map/ppermute | solution.py:823
  49.0 15.1 %collective-permute-done.9.refs_12_ = bf16[128,1152]{1,0:T(8,128)(2,1)S(1)} collective-permute-done((bf16[128,1152]{1,0:T(8,128)(2,1)S(1)}, bf16[128,1152]{1,0:T(8,128)(2,1)S(1)}, u32[]{:S(2)}, u32[]{:S(2)}) %collective-permute-start.9) | collective-permute-done | bytes 294944 | tf_op jit(solution)/shard_map/ppermute | solution.py:823
  64.2 3.7 %collective-permute-done.12.refs_16_ = bf16[128,1152]{1,0:T(8,128)(2,1)S(1)} collective-permute-done((bf16[128,1152]{1,0:T(8,128)(2,1)S(1)}, bf16[128,1152]{1,0:T(8,128)(2,1)S(1)}, u32[]{:S(2)}, u32[]{:S(2)}) %collective-permute-start.12) | collective-permute-done | bytes 294944 | tf_op jit(solution)/shard_map/ppermute | solution.py:823
  72.6 8.2 %project.1 = (bf16[1024,768]{1,0:T(8,128)(2,1)}, bf16[1024,256]{1,0:T(8,128)(2,1)}, f32[16,1024]{1,0:T(8,128)}, bf16[1376,1024]{1,0:T(8,128)(2,1)}, bf16[1376,76...) custom-call(s32[2]{0:T(128)} %pad_add_fusion.ids_ref.refs_0_.refs_7_, ...), custom_call_target="tpu_custom_call" | custom-call | flops 1000000000 | bytes 1000000 | tf_op jit(solution)/shard_map/project/pallas_call | solution.py:176
  82.4 15.6 %attend.1 = (f32[1376,256]{1,0:T(8,128)}, f32[2,2,1376]{2,1,0:T(2,128)}, bf16[344,256]{1,0:T(8,128)(2,1)}, bf16[344,256]{1,0:T(8,128)(2,1)}, bf16[344,256]{1,0:T(8,128)(2,1)}, /*index=5*/bf16[344,256]{1,0:T(8,128)(2,1)}) custom-call(bf16[1376,768]{1,0:T(8,128)(2,1)} %get-tuple-element.150.qkv_ref, f32[1376,1]{1,0:T(8,128)} %get-tuple-element.151.bias_ref), custom_call_target="tpu_custom_call" | custom-call | flops 1000000000 | bytes 1000000 | tf_op jit(solution)/shard_map/attend/pallas_call | solution.py:232
  100.9 5.2 %collective-permute-done.18.refs_4_.rest_2_ = bf16[344,256]{1,0:T(8,128)(2,1)S(1)} collective-permute-done((bf16[344,256]{1,0:T(8,128)(2,1)}, bf16[344,256]{1,0:T(8,128)(2,1)S(1)}, u32[]{:S(2)}, u32[]{:S(2)}) %collective-permute-start.18) | collective-permute-done | bytes 176160 | tf_op jit(solution)/shard_map/ppermute | solution.py:823
  110.0 5.3 %middle.1 = (f32[344,1024]{1,0:T(8,128)}, f32[344,1024]{1,0:T(8,128)}, bf16[344,1024]{1,0:T(8,128)(2,1)}, f32[344,1024]{1,0:T(8,128)}, f32[344,1]{1,0:T(8,128)}) custom-call(f32[16,1024]{1,0:T(8,128)} %get-tuple-element.209.refs_0_.refs_5_.rows_ref, bf16[344,1024]{1,0:T(8,128)(2,1)} %bitcast.27, bf16[344,256]{1,0:T(8,128)(2,1)} %get-tuple-element.152.refs_2_.rest_0_, ...), custom_call_target="tpu_custom_call" | custom-call | flops 1000000000 | bytes 1000000 | tf_op jit(solution)/shard_map/middle/pallas_call | solution.py:334
  118.1 12.6 %mlp.2 = (bf16[344,1024]{1,0:T(8,128)(2,1)}, bf16[344,1024]{1,0:T(8,128)(2,1)}, bf16[688,1024]{1,0:T(8,128)(2,1)}, bf16[688,1024]{1,0:T(8,128)(2,1)}, bf16[688,1...) custom-call(f32[16,1024]{1,0:T(8,128)} %get-tuple-element.209.refs_0_.refs_5_.rows_ref, ...), custom_call_target="tpu_custom_call" | custom-call | flops 1000000000 | bytes 1000000 | tf_op jit(solution)/shard_map/mlp/pallas_call | solution.py:476
  137.0 12.8 %mlp.3 = (bf16[344,1024]{1,0:T(8,128)(2,1)}, bf16[344,1024]{1,0:T(8,128)(2,1)}, bf16[688,1024]{1,0:T(8,128)(2,1)}, bf16[688,1024]{1,0:T(8,128)(2,1)}, bf16[688,1...) custom-call(f32[16,1024]{1,0:T(8,128)} %get-tuple-element.209.refs_0_.refs_5_.rows_ref, ...), custom_call_target="tpu_custom_call" | custom-call | flops 1000000000 | bytes 1000000 | tf_op jit(solution)/shard_map/mlp/pallas_call | solution.py:476
  154.2 16.2 %mlp_weights.1 = (bf16[512,2048]{1,0:T(8,128)(2,1)}, bf16[512,2048]{1,0:T(8,128)(2,1)}, f32[1,1024]{1,0:T(1,128)}, bf16[344,1024]{1,0:T(8,128)(2,1)}, bf16[344,1...) custom-call(s32[2]{0:T(128)} %pad_add_fusion.ids_ref.refs_0_.refs_7_, ...), custom_call_target="tpu_custom_call" | custom-call | flops 1000000000 | bytes 1000000 | tf_op jit(solution)/shard_map/mlp_weights/pallas_call | solution.py:542
  172.3 6.1 %turn.1 = (f32[344,1024]{1,0:T(8,128)}, bf16[344,1024]{1,0:T(8,128)(2,1)}, f32[8,1024]{1,0:T(8,128)}, bf16[344,256]{1,0:T(8,128)(2,1)}, bf16[344,256]{1,0:T(8,12...) custom-call(f32[16,1024]{1,0:T(8,128)} %get-tuple-element.209.refs_0_.refs_5_.rows_ref, ...), custom_call_target="tpu_custom_call" | custom-call | flops 1000 | bytes 1000 | tf_op jit(solution)/shard_map/turn/pallas_call | solution.py:370
  180.3 4.1 %proj_weights.1 = bf16[4,1024,256]{2,1,0:T(8,128)(2,1)} custom-call(s32[2]{0:T(128)} %pad_add_fusion.ids_ref.refs_0_.refs_7_, bf16[344,1024]{1,0:T(8,128)(2,1)} %get-tuple-element.192.grad_ref, bf16[344,256]{1,0:T(8,128)(2,1)} %get-tuple-element.152.refs_2_.rest_0_, bf16[344,256]{1,0:T(8,128)(2,1)} %copy-done.40, bf16[344,256]{1,0:T(8,128)(2,1)} %copy-done.41, ...), custom_call_target="tpu_custom_call" | custom-call | flops 1000 | bytes 1000 | tf_op jit(solution)/shard_map/proj_weights/pallas_call | solution.py:391
  191.9 24.3 %attend_back.1 = (bf16[1376,768]{1,0:T(8,128)(2,1)}, f32[2,1,384]{2,1,0:T(1,128)}) custom-call(bf16[1376,768]{1,0:T(8,128)(2,1)} %get-tuple-element.150.qkv_ref, f32[1376,1]{1,0:T(8,128)} %get-tuple-element.151.bias_ref, f32[1376,256]{1,0:T(8,128)} %get-tuple-element.184.att_ref, f32[2,2,1376]{2,1,0:T(2,128)} %get-tuple-element.193.lse_ref, ...), custom_call_target="tpu_custom_call" | custom-call | flops 1000 | bytes 1000 | tf_op jit(solution)/shard_map/attend_back/pallas_call | solution.py:291
  216.2 6.7 %qkv_back.1 = (bf16[344,1024]{1,0:T(8,128)(2,1)}, bf16[344,1024]{1,0:T(8,128)(2,1)}, bf16[344,1024]{1,0:T(8,128)(2,1)}, bf16[344,1024]{1,0:T(8,128)(2,1)}, f32[8,1024]{1,0:T(8,128)}) custom-call(bf16[1376,768]{1,0:T(8,128)(2,1)} %get-tuple-element.198.refs_0_.refs_2_, bf16[1024,768]{1,0:T(8,128)(2,1)} %get-tuple-element.199.refs_1_, ...), custom_call_target="tpu_custom_call" | custom-call | flops 1000 | bytes 1000 | tf_op jit(solution)/shard_map/qkv_back/pallas_call | solution.py:631
  223.0 7.0 %attn_weights.1 = (bf16[128,1152]{1,0:T(8,128)(2,1)}, bf16[128,1152]{1,0:T(8,128)(2,1)}, bf16[128,1152]{1,0:T(8,128)(2,1)}, bf16[128,1152]{1,0:T(8,128)(2,1)}, b...) custom-call(s32[2]{0:T(128)} %pad_add_fusion.ids_ref.refs_0_.refs_7_, bf16[1376,1024]{1,0:T(8,128)(2,1)} %get-tuple-element.183.refs_1_, ...), custom_call_target="tpu_custom_call" | custom-call | flops 1000000000 | bytes 1000000 | tf_op jit(solution)/shard_map/attn_weights/pallas_call | solution.py:703
  230.0 7.1 %collective-permute-done.48 = bf16[512,2048]{1,0:T(8,128)(2,1)} collective-permute-done((bf16[512,2048]{1,0:T(8,128)(2,1)}, bf16[512,2048]{1,0:T(8,128)(2,1)}, u32[]{:S(2)}, u32[]{:S(2)}) %collective-permute-start.48) | collective-permute-done | bytes 2097184 | tf_op jit(solution)/shard_map/ppermute | solution.py:823
  237.1 3.9 %add_convert_fusion = bf16[512,2048]{1,0:T(8,128)(2,1)} fusion(bf16[512,2048]{1,0:T(8,128)(2,1)} %collective-permute-done.48, bf16[512,2048]{1,0:T(8,128)(2,1)S(1)} %copy-done.5), kind=kLoop, calls=%fused_computation | loop fusion | flops 4194304 | bytes 6291456 | tf_op jit(solution)/shard_map/convert_element_type | solution.py:979
  242.2 13.8 %collective-permute-done.35 = bf16[256,1152]{1,0:T(8,128)(2,1)S(1)} collective-permute-done((bf16[256,1152]{1,0:T(8,128)(2,1)}, bf16[256,1152]{1,0:T(8,128)(2,1)S(1)}, u32[]{:S(2)}, u32[]{:S(2)}) %collective-permute-start.35) | collective-permute-done | bytes 589856 | tf_op jit(solution)/shard_map/ppermute | solution.py:823
  262.2 17.1 %collective-permute-done.36 = bf16[128,1152]{1,0:T(8,128)(2,1)S(1)} collective-permute-done((bf16[128,1152]{1,0:T(8,128)(2,1)S(1)}, bf16[128,1152]{1,0:T(8,128)(2,1)S(1)}, u32[]{:S(2)}, u32[]{:S(2)}) %collective-permute-start.36) | collective-permute-done | bytes 294944 | tf_op jit(solution)/shard_map/ppermute | solution.py:823
  282.0 4.0 %collective-permute-start.43 = (bf16[128,1152]{1,0:T(8,128)(2,1)S(1)}, bf16[128,1152]{1,0:T(8,128)(2,1)S(1)}, u32[]{:S(2)}, u32[]{:S(2)}) collective-permute-start(bf16[128,1152]{1,0:T(8,128)(2,1)S(1)} %get-tuple-element.246), channel_id=1, source_target_pairs={{0,8},{4,12},{8,0},{12,4},{16,24},{20,28},{24,16},{28,20},{1,9},{5... | collective-permute-start | bytes 884744 | tf_op jit(solution)/shard_map/ppermute | solution.py:823
  286.8 4.0 %begin.1 = bf16[344,1024]{1,0:T(8,128)(2,1)} custom-call(f32[16,1024]{1,0:T(8,128)} %get-tuple-element.209.refs_0_.refs_5_.rows_ref, bf16[344,1024]{1,0:T(8,128)(2,1)} %bitcast.29, f32[1376,1]{1,0:T(8,128)} %get-tuple-element.200.refs_2_.mean_ref, f32[1376,1]{1,0:T(8,128)} %get-tuple-element.201.refs_3_.inv_ref, f32[344,1024]{1,0:T(8,128)} %get-tuple-element.215.middle_ref, ...), custom_call_target="tpu_custom_call" | custom-call | tf_op jit(solution)/shard_map/begin/pallas_call | solution.py:598
  295.0 5.6 %collective-permute-done.44.refs_2_ = bf16[128,1152]{1,0:T(8,128)(2,1)S(1)} collective-permute-done((bf16[128,1152]{1,0:T(8,128)(2,1)}, bf16[128,1152]{1,0:T(8,128)(2,1)S(1)}, u32[]{:S(2)}, u32[]{:S(2)}) %collective-permute-start.44) | collective-permute-done | bytes 294944 | tf_op jit(solution)/shard_map/ppermute | solution.py:823
  311.0 7.3 %collective-permute-done.46.refs_2_ = bf16[32,1152]{1,0:T(8,128)(2,1)S(1)} collective-permute-done((bf16[32,1152]{1,0:T(8,128)(2,1)}, bf16[32,1152]{1,0:T(8,128)(2,1)S(1)}, u32[]{:S(2)}, u32[]{:S(2)}) %collective-permute-start.46) | collective-permute-done | bytes 73760 | tf_op jit(solution)/shard_map/ppermute | solution.py:823
  (234 shorter events, 98.6 us)
Async XLA Ops:
  7.2 110.9 %all-gather.2.cloned.1.call-start = ((), (), s32[]{:S(2)}) async-start(), calls=%async_computation.2 | async-start | bytes 4718592 | tf_op jit(solution)/shard_map/all_gather | solution.py:896
  39.7 183.3 %reduce-scatter.3.cloned.1.call-start = ((), (), s32[]{:S(2)}) async-start(), calls=%async_computation.3 | async-start | bytes 2621440 | tf_op jit(solution)/shard_map/reduce_scatter | solution.py:964
  39.7 28.2 %collective-permute-start.13 = (bf16[344,1024]{1,0:T(8,128)(2,1)S(1)}, bf16[344,1024]{1,0:T(8,128)(2,1)S(1)}, u32[]{:S(2)}, u32[]{:S(2)}) collective-permute-start(bf16[344,1024]{1,0:T(8,128)(2,1)S(1)} %bitcast.34), channel_id=1, source_target_pairs={{0,2},{1,3},{2,0},{3,1},{4,6},{5,7},{6,4},{7,5},{8,10},{9,11},{10,... | collective-permute-start | bytes 2113544 | tf_op jit(solution)/shard_map/ppermute | solution.py:823
  41.1 28.4 %collective-permute-start.15 = (bf16[344,1024]{1,0:T(8,128)(2,1)S(1)}, bf16[344,1024]{1,0:T(8,128)(2,1)S(1)}, u32[]{:S(2)}, u32[]{:S(2)}) collective-permute-start(bf16[344,1024]{1,0:T(8,128)(2,1)S(1)} %bitcast.30), channel_id=1, source_target_pairs={{0,2},{1,3},{2,0},{3,1},{4,6},{5,7},{6,4},{7,5},{8,10},{9,11},{10,... | collective-permute-start | bytes 2113544 | tf_op jit(solution)/shard_map/ppermute | solution.py:823
  42.3 21.9 %collective-permute-start.10 = (bf16[128,1152]{1,0:T(8,128)(2,1)S(1)}, bf16[128,1152]{1,0:T(8,128)(2,1)S(1)}, u32[]{:S(2)}, u32[]{:S(2)}) collective-permute-start(bf16[128,1152]{1,0:T(8,128)(2,1)S(1)} %collective-permute-done.6.refs_13_), channel_id=1, source_target_pairs={{0,4},{4,0},{8,12},{12,8},{16,20},{20,16},{24,28},{28,24},{1,5},{5... | collective-permute-start | bytes 884744 | tf_op jit(solution)/shard_map/ppermute | solution.py:823
  42.8 21.4 %collective-permute-start.9 = (bf16[128,1152]{1,0:T(8,128)(2,1)S(1)}, bf16[128,1152]{1,0:T(8,128)(2,1)S(1)}, u32[]{:S(2)}, u32[]{:S(2)}) collective-permute-start(bf16[128,1152]{1,0:T(8,128)(2,1)S(1)} %collective-permute-done.7.refs_11_), channel_id=1, source_target_pairs={{0,4},{4,0},{8,12},{12,8},{16,20},{20,16},{24,28},{28,24},{1,5},{5... | collective-permute-start | bytes 884744 | tf_op jit(solution)/shard_map/ppermute | solution.py:823
  48.5 19.3 %collective-permute-start.12 = (bf16[128,1152]{1,0:T(8,128)(2,1)S(1)}, bf16[128,1152]{1,0:T(8,128)(2,1)S(1)}, u32[]{:S(2)}, u32[]{:S(2)}) collective-permute-start(bf16[128,1152]{1,0:T(8,128)(2,1)S(1)} %collective-permute-done.11.refs_15_), channel_id=1, source_target_pairs={{0,4},{4,0},{8,12},{12,8},{16,20},{20,16},{24,28},{28,24},{1,5},{5... | collective-permute-start | bytes 884744 | tf_op jit(solution)/shard_map/ppermute | solution.py:823
  80.8 17.1 %collective-permute-start.21 = (bf16[1024,256]{1,0:T(8,128)(2,1)}, bf16[1024,256]{1,0:T(8,128)(2,1)S(1)}, u32[]{:S(2)}, u32[]{:S(2)}) collective-permute-start(bf16[1024,256]{1,0:T(8,128)(2,1)} %get-tuple-element.156.refs_6_.refs_9_), channel_id=1, source_target_pairs={{0,2},{1,3},{2,0},{3,1},{4,6},{5,7},{6,4},{7,5},{8,10},{9,11},{10,... | collective-permute-start | bytes 1572872 | tf_op jit(solution)/shard_map/ppermute | solution.py:823
  82.4 26.6 %collective-permute-start.20 = (bf16[1024,256]{1,0:T(8,128)(2,1)}, bf16[1024,256]{1,0:T(8,128)(2,1)S(1)}, u32[]{:S(2)}, u32[]{:S(2)}) collective-permute-start(bf16[1024,256]{1,0:T(8,128)(2,1)} %get-tuple-element.156.refs_6_.refs_9_), channel_id=1, source_target_pairs={{0,1},{1,0},{2,3},{3,2},{4,5},{5,4},{6,7},{7,6},{8,9},{9,8},{10,11... | collective-permute-start | bytes 1572872 | tf_op jit(solution)/shard_map/ppermute | solution.py:823
  116.0 18.0 %collective-permute-start.25 = (bf16[344,1024]{1,0:T(8,128)(2,1)}, bf16[344,1024]{1,0:T(8,128)(2,1)S(1)}, u32[]{:S(2)}, u32[]{:S(2)}) collective-permute-start(bf16[344,1024]{1,0:T(8,128)(2,1)} %get-tuple-element.159.refs_1_), channel_id=1, source_target_pairs={{0,2},{1,3},{2,0},{3,1},{4,6},{5,7},{6,4},{7,5},{8,10},{9,11},{10,... | collective-permute-start | bytes 2113544 | tf_op jit(solution)/shard_map/ppermute | solution.py:823
  116.5 17.5 %collective-permute-start.27 = (bf16[344,1024]{1,0:T(8,128)(2,1)S(1)}, bf16[344,1024]{1,0:T(8,128)(2,1)S(1)}, u32[]{:S(2)}, u32[]{:S(2)}) collective-permute-start(bf16[344,1024]{1,0:T(8,128)(2,1)S(1)} %copy-done.11), channel_id=1, source_target_pairs={{0,1},{1,0},{2,3},{3,2},{4,5},{5,4},{6,7},{7,6},{8,9},{9,8},{10,11... | collective-permute-start | bytes 2113544 | tf_op jit(solution)/shard_map/ppermute | solution.py:823
  150.0 20.4 %collective-permute-start.30 = (bf16[344,1024]{1,0:T(8,128)(2,1)S(1)}, bf16[344,1024]{1,0:T(8,128)(2,1)S(1)}, u32[]{:S(2)}, u32[]{:S(2)}) collective-permute-start(bf16[344,1024]{1,0:T(8,128)(2,1)S(1)} %copy-done.54), channel_id=1, source_target_pairs={{0,1},{1,0},{2,3},{3,2},{4,5},{5,4},{6,7},{7,6},{8,9},{9,8},{10,11... | collective-permute-start | bytes 2113544 | tf_op jit(solution)/shard_map/ppermute | solution.py:823
  153.6 17.9 %collective-permute-start.31 = (bf16[344,1024]{1,0:T(8,128)(2,1)S(1)}, bf16[344,1024]{1,0:T(8,128)(2,1)S(1)}, u32[]{:S(2)}, u32[]{:S(2)}) collective-permute-start(bf16[344,1024]{1,0:T(8,128)(2,1)S(1)} %add_convert_fusion.3), channel_id=1, source_target_pairs={{0,2},{1,3},{2,0},{3,1},{4,6},{5,7},{6,4},{7,5},{8,10},{9,11},{10,... | collective-permute-start | bytes 2113544 | tf_op jit(solution)/shard_map/ppermute | solution.py:823
  188.8 116.2 %reduce-scatter.5.cloned.1.call-start = ((), (), s32[]{:S(2)}) async-start(), calls=%async_computation.4 | async-start | bytes 2621440 | tf_op jit(solution)/shard_map/reduce_scatter | solution.py:981
  188.9 48.2 %collective-permute-start.48 = (bf16[512,2048]{1,0:T(8,128)(2,1)}, bf16[512,2048]{1,0:T(8,128)(2,1)}, u32[]{:S(2)}, u32[]{:S(2)}) collective-permute-start(bf16[512,2048]{1,0:T(8,128)(2,1)} %get-tuple-element.236), channel_id=1, source_target_pairs={{0,4},{4,0},{8,12},{12,8},{16,20},{20,16},{24,28},{28,24},{1,5},{5... | collective-permute-start | bytes 6291464 | tf_op jit(solution)/shard_map/ppermute | solution.py:823
  241.6 17.5 %collective-permute-start.40 = (bf16[344,1024]{1,0:T(8,128)(2,1)}, bf16[344,1024]{1,0:T(8,128)(2,1)S(1)}, u32[]{:S(2)}, u32[]{:S(2)}) collective-permute-start(bf16[344,1024]{1,0:T(8,128)(2,1)} %get-tuple-element.219), channel_id=1, source_target_pairs={{0,1},{1,0},{2,3},{3,2},{4,5},{5,4},{6,7},{7,6},{8,9},{9,8},{10,11... | collective-permute-start | bytes 2113544 | tf_op jit(solution)/shard_map/ppermute | solution.py:823
  241.6 18.5 %collective-permute-start.38 = (bf16[344,1024]{1,0:T(8,128)(2,1)S(1)}, bf16[344,1024]{1,0:T(8,128)(2,1)S(1)}, u32[]{:S(2)}, u32[]{:S(2)}) collective-permute-start(bf16[344,1024]{1,0:T(8,128)(2,1)S(1)} %add_convert_fusion.2), channel_id=1, source_target_pairs={{0,2},{1,3},{2,0},{3,1},{4,6},{5,7},{6,4},{7,5},{8,10},{9,11},{10,... | collective-permute-start | bytes 2113544 | tf_op jit(solution)/shard_map/ppermute | solution.py:823
  256.1 23.2 %collective-permute-start.36 = (bf16[128,1152]{1,0:T(8,128)(2,1)S(1)}, bf16[128,1152]{1,0:T(8,128)(2,1)S(1)}, u32[]{:S(2)}, u32[]{:S(2)}) collective-permute-start(bf16[128,1152]{1,0:T(8,128)(2,1)S(1)} %add_convert_fusion.8), channel_id=1, source_target_pairs={{0,8},{4,12},{8,0},{12,4},{16,24},{20,28},{24,16},{28,20},{1,9},{5... | collective-permute-start | bytes 884744 | tf_op jit(solution)/shard_map/ppermute | solution.py:823
  259.4 20.7 %collective-permute-start.41 = (bf16[344,1024]{1,0:T(8,128)(2,1)S(1)}, bf16[344,1024]{1,0:T(8,128)(2,1)S(1)}, u32[]{:S(2)}, u32[]{:S(2)}) collective-permute-start(bf16[344,1024]{1,0:T(8,128)(2,1)S(1)} %add_convert_fusion.1), channel_id=1, source_target_pairs={{0,2},{1,3},{2,0},{3,1},{4,6},{5,7},{6,4},{7,5},{8,10},{9,11},{10,... | collective-permute-start | bytes 2113544 | tf_op jit(solution)/shard_map/ppermute | solution.py:823
  260.1 21.1 %collective-permute-start.42 = (bf16[256,1152]{1,0:T(8,128)(2,1)S(1)}, bf16[256,1152]{1,0:T(8,128)(2,1)S(1)}, u32[]{:S(2)}, u32[]{:S(2)}) collective-permute-start(bf16[256,1152]{1,0:T(8,128)(2,1)S(1)} %copy-done.55), channel_id=1, source_target_pairs={{0,4},{4,0},{8,12},{12,8},{16,20},{20,16},{24,28},{28,24},{1,5},{5... | collective-permute-start | bytes 1769480 | tf_op jit(solution)/shard_map/ppermute | solution.py:823
  261.7 29.2 %collective-permute-start.37 = (bf16[344,1024]{1,0:T(8,128)(2,1)}, bf16[344,1024]{1,0:T(8,128)(2,1)S(1)}, u32[]{:S(2)}, u32[]{:S(2)}) collective-permute-start(bf16[344,1024]{1,0:T(8,128)(2,1)} %get-tuple-element.212), channel_id=1, source_target_pairs={{0,1},{1,0},{2,3},{3,2},{4,5},{5,4},{6,7},{7,6},{8,9},{9,8},{10,11... | collective-permute-start | bytes 2113544 | tf_op jit(solution)/shard_map/ppermute | solution.py:823
  261.7 24.3 %collective-permute-start.39 = (bf16[344,1024]{1,0:T(8,128)(2,1)S(1)}, bf16[344,1024]{1,0:T(8,128)(2,1)S(1)}, u32[]{:S(2)}, u32[]{:S(2)}) collective-permute-start(bf16[344,1024]{1,0:T(8,128)(2,1)S(1)} %copy-done.52), channel_id=1, source_target_pairs={{0,1},{1,0},{2,3},{3,2},{4,5},{5,4},{6,7},{7,6},{8,9},{9,8},{10,11... | collective-permute-start | bytes 2113544 | tf_op jit(solution)/shard_map/ppermute | solution.py:823
  280.1 20.4 %collective-permute-start.44 = (bf16[128,1152]{1,0:T(8,128)(2,1)}, bf16[128,1152]{1,0:T(8,128)(2,1)S(1)}, u32[]{:S(2)}, u32[]{:S(2)}) collective-permute-start(bf16[128,1152]{1,0:T(8,128)(2,1)} %add_convert_fusion.4), channel_id=1, source_target_pairs={{0,16},{4,20},{8,24},{12,28},{16,0},{20,4},{24,8},{28,12},{1,17},{... | collective-permute-start | bytes 884744 | tf_op jit(solution)/shard_map/ppermute | solution.py:823
  282.0 20.3 %collective-permute-start.43 = (bf16[128,1152]{1,0:T(8,128)(2,1)S(1)}, bf16[128,1152]{1,0:T(8,128)(2,1)S(1)}, u32[]{:S(2)}, u32[]{:S(2)}) collective-permute-start(bf16[128,1152]{1,0:T(8,128)(2,1)S(1)} %get-tuple-element.246), channel_id=1, source_target_pairs={{0,8},{4,12},{8,0},{12,4},{16,24},{20,28},{24,16},{28,20},{1,9},{5... | collective-permute-start | bytes 884744 | tf_op jit(solution)/shard_map/ppermute | solution.py:823
  (87 other events, 673.7 us)
Sparse Core Ops, SparseCore 0:
  39.8 75.5 all-gather.1
  188.9 31.9 reduce-scatter.2
  241.1 56.6 reduce-scatter.4
